TPU v7x, 128 devices: a whole 4x4x4 slice. The times are simulated.
128 devices in a mesh: member: 8 (over y, x_hi), grid: 16 (over x_lo, z, core).
Axes of the slice: x: 4 (x_hi: 2, x_lo: 2; x = x_hi * 2 + x_lo), y: 4, z: 4, core: 2. Of those that a mesh axis runs over, the one named last changes fastest.
Arguments:
- latents: bfloat16 [8, 32768, 1024], P('member', 'grid'), may hold values from -6 to 6
- hidden_weight: bfloat16 [1024, 1024], replicated, may hold values from -0.1875 to 0.1875
- output_weight: bfloat16 [1024, 100], replicated, may hold values from -0.1875 to 0.1875
- observed: float32 [100, 32768], P(None, 'grid'), may hold values from -6 to 6
- node_area_weight: float32 [32768], P('grid'), may hold values from 0.3 to 3
Outputs:
- grad_latents: bfloat16 [8, 32768, 1024], P('member', 'grid')
- grad_first: float32 [1024, 1024], P('grid')
- grad_second: float32 [1024, 100], P('grid')
All inputs are finite; a program needn't handle non-finite values.
Results may differ from a plain program's by a relative error of at most 0.018.
Values may be sent and summed in bfloat16 or wider, within the bound.
No kernel may reach another device: no remote copies, remote signals or barrier semaphores. Data moves between devices by JAX's collectives and lax.ppermute only.
A program may use at most 128 MiB of HBM per device.

v0:
```python
import math

import jax
import jax.numpy as jnp
from jax import lax
from jax.sharding import PartitionSpec as P

smooth_sq = 0.0025


def slope_function(diff):
    return diff / jnp.sqrt(diff * diff + smooth_sq)


def body(latents, hidden_weight, output_weight, observed, node_area_weight):
    latent_state = latents[0]
    member_list = lax.axis_size("member")
    groups = lax.axis_size("grid")
    node_count = latent_state.shape[0]
    pre_activation = jnp.dot(latent_state, hidden_weight, preferred_element_type=jnp.float32)
    gate_sigmoid = jax.nn.sigmoid(pre_activation)
    hidden_activation = (pre_activation * gate_sigmoid).astype(jnp.bfloat16)
    single_prediction = lax.dot_general(
        output_weight,
        hidden_activation,
        (((0,), (1,)), ((), ())),
        preferred_element_type=jnp.float32,
    )
    every_member_set = lax.all_gather(single_prediction[None], "member", axis=0, tiled=True)
    pairwise_sum = jnp.sum(slope_function(single_prediction[None] - every_member_set), axis=0)
    field_gradient = node_area_weight[None, :] * (
        slope_function(single_prediction - observed) - pairwise_sum / (member_list - 1)
    )
    grad_low = field_gradient.astype(jnp.bfloat16)
    grad_hidden = lax.dot_general(
        grad_low, output_weight, (((0,), (1,)), ((), ())), preferred_element_type=jnp.float32
    )
    grad_pre = (grad_hidden * gate_sigmoid * (1.0 + pre_activation * (1.0 - gate_sigmoid))).astype(
        jnp.bfloat16
    )
    part_second = lax.dot_general(
        hidden_activation, grad_low, (((0,), (1,)), ((), ())), preferred_element_type=jnp.float32
    )
    part_first = lax.dot_general(
        latent_state, grad_pre, (((0,), (0,)), ((), ())), preferred_element_type=jnp.float32
    )
    grad_latent = lax.dot_general(
        grad_pre, hidden_weight, (((1,), (1,)), ((), ())), preferred_element_type=jnp.float32
    ).astype(jnp.bfloat16)
    row_sums = (
        lax.psum_scatter(
            part_first.astype(jnp.bfloat16), "grid", scatter_dimension=0, tiled=True
        ).astype(jnp.float32),
        lax.psum_scatter(
            part_second.astype(jnp.bfloat16), "grid", scatter_dimension=0, tiled=True
        ).astype(jnp.float32),
    )
    sum_first, sum_second = (
        lax.psum(row_sums[0].astype(jnp.bfloat16), "member").astype(jnp.float32),
        lax.psum(row_sums[1].astype(jnp.bfloat16), "member").astype(jnp.float32),
    )
    factor = 1.0 / math.sqrt(member_list * node_count * groups)
    return (grad_latent[None], sum_first * factor, sum_second * factor)


def solution(mesh):
    in_specs = (P("member", "grid", None), P(), P(), P(None, "grid"), P("grid"))
    out_specs = (P("member", "grid", None), P("grid", None), P("grid", None))
    return jax.shard_map(body, mesh=mesh, in_specs=in_specs, out_specs=out_specs, check_vma=False)
```

profile of v0, /device:TPU:0, one launch (start us, length us, event | category | flops | bytes accessed | tf_op | source)
XLA Modules:
  0.0 350.5 jit_solution(18207945630226371425)
XLA Ops:
  7.2 0.0 copy-start
  7.2 0.0 copy-start.5
  7.2 0.0 all-gather.4.cloned.1.call-start
  7.2 1.5 copy-done
  8.8 10.1 %multiply_convert_fusion.1 = (bf16[2048,1024]{1,0:T(8,128)(2,1)S(1)}, f32[2048,1024]{1,0:T(8,128)}) fusion(bf16[1024,1024]{1,0:T(8,128)(2,1)S(1)} %copy-done, bf16[1,2048,1024]{2,1,0:T(8,128)(2,1)} %param.5), kind=kOutput, calls=%fused_computation.1 | convolution fusion | flops 4305453056 | bytes 18874368 | tf_op jit(solution)/shard_map/dot_general | solution.py:20
  18.8 0.0 copy-start.2
  18.8 2.0 copy-done.2
  20.8 0.0 copy-done.5
  20.9 2.4 fusion.6
  23.2 0.0 all-gather.4.cloned.1.call-update
  23.3 0.0 reduce-scatter.5.cloned.1.call-start
  23.3 95.7 %all-gather.4.cloned.1.call-done = f32[8,100,2048]{2,1,0:T(8,128)} async-done(((f32[1,100,2048]{2,1,0:T(8,128)}), f32[8,100,2048]{2,1,0:T(8,128)}) %all-gather.4.cloned.1.call-update) | async-done | bytes 6553616 | tf_op jit(solution)/shard_map/all_gather | solution.py:29
  119.0 0.0 copy-start.1
  119.0 0.0 copy-start.4
  119.0 0.0 copy-start.6
  119.0 0.0 copy-start.3
  119.0 4.7 %multiply_reduce_fusion = f32[100,2048]{1,0:T(8,128)S(1)} fusion(f32[8,100,2048]{2,1,0:T(8,128)} %all-gather.4.cloned.1.call-done, f32[100,2048]{1,0:T(8,128)} %bitcast.29), kind=kLoop, calls=%fused_computation.3 | loop fusion | flops 7987200 | bytes 8192000 | tf_op jit(solution)/shard_map/reduce_sum | solution.py:30
  123.8 0.0 copy-done.1
  123.8 0.0 copy-done.4
  123.8 0.0 copy-done.6
  123.8 0.3 multiply_convert_fusion.2
  124.1 0.0 copy-done.3
  124.1 2.0 convolution_convert_fusion
  126.1 7.0 %multiply_convert_fusion = bf16[2048,1024]{1,0:T(8,128)(2,1)} fusion(f32[2048,1024]{1,0:T(8,128)} %get-tuple-element.10, bf16[100,2048]{1,0:T(8,128)(2,1)S(1)} %multiply_convert_fusion.2, bf16[1024,100]{0,1:T(8,128)(2,1)S(1)} %copy-done.5), kind=kOutput, calls=%fused_computation | convolution fusion | flops 438304768 | bytes 13197312 | tf_op jit(solution)/shard_map/dot_general | solution.py:35
  133.0 0.0 reduce-scatter.5.cloned.1.call-update
  133.1 0.2 reduce-scatter.7.cloned.1.call-start
  133.3 9.4 %convert_bitcast_fusion.1 = bf16[1024,1024]{0,1:T(8,128)(2,1)} fusion(bf16[2048,1024]{1,0:T(8,128)(2,1)} %multiply_convert_fusion, bf16[1,2048,1024]{2,1,0:T(8,128)(2,1)} %param.5), kind=kOutput, calls=%fused_computation.9 | convolution fusion | flops 4296015872 | bytes 10485760 | tf_op jit(solution)/shard_map/dot_general | solution.py:44
  142.7 3.9 %copy.10 = bf16[1024,1024]{1,0:T(8,128)(2,1)} copy(bf16[1024,1024]{0,1:T(8,128)(2,1)} %convert_bitcast_fusion.1) | data formatting | bytes 4194304
  146.6 0.0 reduce-scatter.7.cloned.1.call-update
  146.6 0.0 all-reduce.2.cloned.1.call-start
  146.7 8.3 %convert_bitcast_fusion = bf16[1,2048,1024]{2,1,0:T(8,128)(2,1)} fusion(bf16[2048,1024]{1,0:T(8,128)(2,1)} %multiply_convert_fusion, bf16[1024,1024]{1,0:T(8,128)(2,1)S(1)} %copy-done), kind=kOutput, calls=%fused_computation.8 | convolution fusion | flops 4297064448 | bytes 10485760 | tf_op jit(solution)/shard_map/dot_general | solution.py:47
  155.0 36.4 %reduce-scatter.5.cloned.1.call-done = bf16[64,100]{1,0:T(8,128)(2,1)} async-done(((bf16[1024,100]{1,0:T(8,128)(2,1)}), bf16[64,100]{1,0:T(8,128)(2,1)}) %reduce-scatter.5.cloned.1.call-update) | async-done | bytes 12816 | tf_op jit(solution)/shard_map/reduce_scatter | solution.py:54
  191.4 41.5 %psum.15 = bf16[64,100]{1,0:T(8,128)(2,1)S(1)} all-reduce(bf16[64,100]{1,0:T(8,128)(2,1)} %reduce-scatter.5.cloned.1.call-done), channel_id=1, replica_groups=mesh['member'=8,'grid'=16] {'member'}, use_global_device_ids=true, to_apply=%region_4.0 | all-reduce | flops 6400 | bytes 25600 | tf_op jit(solution)/shard_map/psum | solution.py:60
  232.9 23.2 %reduce-scatter.7.cloned.1.call-done = bf16[64,1024]{1,0:T(8,128)(2,1)} async-done(((bf16[1024,1024]{1,0:T(8,128)(2,1)}), bf16[64,1024]{1,0:T(8,128)(2,1)}) %reduce-scatter.7.cloned.1.call-update) | async-done | bytes 131088
  256.1 1.7 copy.11
  257.9 0.0 all-reduce.2.cloned.1.call-update
  257.9 0.6 convert_multiply_fusion.1
  258.5 83.6 %all-reduce.2.cloned.1.call-done = bf16[64,1024]{0,1:T(8,128)(2,1)} async-done(((bf16[64,1024]{0,1:T(8,128)(2,1)}), bf16[64,1024]{0,1:T(8,128)(2,1)}) %all-reduce.2.cloned.1.call-update) | async-done | bytes 131088 | tf_op jit(solution)/shard_map/psum | solution.py:59
  342.1 1.0 convert_multiply_fusion
  343.1 0.9 copy.9
Async XLA Ops:
  7.2 1.6 copy-start
  7.2 13.7 %copy-start.5 = (bf16[1024,100]{0,1:T(8,128)(2,1)S(1)}, bf16[1024,100]{0,1:T(8,128)(2,1)}, u32[]{:S(2)}) copy-start(bf16[1024,100]{0,1:T(8,128)(2,1)} %param.7) | copy-start | bytes 614404
  7.2 111.8 %all-gather.4.cloned.1.call-start = ((), (), s32[]{:S(2)}) async-start(), calls=%async_computation.4 | async-start | bytes 7667712 | tf_op jit(solution)/shard_map/all_gather | solution.py:29
  18.8 2.0 copy-start.2
  23.3 168.1 %reduce-scatter.5.cloned.1.call-start = ((), (), s32[]{:S(2)}) async-start(), calls=%async_computation.3 | async-start | bytes 278528 | tf_op jit(solution)/shard_map/reduce_scatter | solution.py:54
  119.0 4.7 %copy-start.1 = (f32[2048,100]{0,1:T(8,128)S(1)}, f32[2048,100]{0,1:T(8,128)}, u32[]{:S(2)}) copy-start(f32[2048,100]{0,1:T(8,128)} %fusion.6) | copy-start | bytes 2457604
  119.0 4.7 %copy-start.4 = (f32[100,2048]{1,0:T(8,128)S(1)}, f32[100,2048]{1,0:T(8,128)}, u32[]{:S(2)}) copy-start(f32[100,2048]{1,0:T(8,128)} %param.8) | copy-start | bytes 2457604
  119.0 4.7 %copy-start.6 = (f32[2048]{0:T(1024)S(1)}, f32[2048]{0:T(1024)}, u32[]{:S(2)}) copy-start(f32[2048]{0:T(1024)} %param.9) | copy-start | bytes 24580
  119.0 5.0 %copy-start.3 = (bf16[2048,1024]{1,0:T(8,128)(2,1)S(1)}, bf16[2048,1024]{1,0:T(8,128)(2,1)}, u32[]{:S(2)}) copy-start(bf16[2048,1024]{1,0:T(8,128)(2,1)} %copy-done.2) | copy-start | bytes 12582916
  133.1 123.1 %reduce-scatter.7.cloned.1.call-start = ((), (), s32[]{:S(2)}) async-start(), calls=%async_computation.5 | async-start | bytes 2228224
  146.6 195.5 %all-reduce.2.cloned.1.call-start = ((), (), s32[]{:S(2)}) async-start(), calls=%async_computation.2 | async-start | bytes 524288 | tf_op jit(solution)/shard_map/psum | solution.py:59
Sparse Core Ops, SparseCore 0:
  23.4 95.6 all-gather.3
  133.2 58.1 reduce-scatter.4
  193.9 62.1 reduce-scatter.6
  259.2 82.8 all-reduce.1
where the time goes:
time: 351 us
  waiting for transfers between devices  239 us (68%)
  blocking collectives  41.5 us (12%)
  matrix products  39.1 us (11%)
  between operations  13.8 us (4%)
  local copies, waits for them, and re-layouts  10.1 us (3%)
  other arithmetic  6.57 us (2%)
    all_gather x1, waiting for transfers between devices, body(): lax.all_gather(single_prediction[None], 'member', axis=0, tiled=True)  95.7 us
    psum x1, waiting for transfers between devices, body(): lax.psum(row_sums[0].astype(jnp.bfloat16), 'member').astype(jnp.float32)  83.6 us
    psum x1, blocking collectives, body(): lax.psum(row_sums[1].astype(jnp.bfloat16), 'member').astype(jnp.float32)  41.5 us
    reduce_scatter x1, waiting for transfers between devices, body(): lax.psum_scatter(part_second.astype(jnp.bfloat16), 'grid', scatter_dimens...  36.4 us
    unnamed x5, waiting for transfers between devices  23.3 us
    unnamed x17, local copies, waits for them, and re-layouts  10.1 us
    dot_general x1, matrix products, body(): jnp.dot(latent_state, hidden_weight, preferred_element_type=jnp.float32)  10.1 us
    dot_general x1, matrix products, body(): lax.dot_general(latent_state, grad_pre, (((0,), (0,)), ((), ())), preferr...  9.37 us
  transfers between devices with their start and end apart: 4, of which 4 were waited for; matrix products, arithmetic and copies ran while one was open for 6% of the time, Pallas kernels for 0%

commit v1 on v0

v1 whole, which is shorter than its diff:
```python
import math

import jax
import jax.numpy as jnp
from jax import lax
from jax.sharding import PartitionSpec as P

smooth_sq = 0.0025
bf16 = jnp.bfloat16
f32 = jnp.float32


def slope_function(diff):
    return diff * lax.rsqrt(diff * diff + smooth_sq)


def moved(value, move):
    pairs = []
    for member in range(8):
        for grid in range(16):
            y, x_hi, x_lo, z, core = member // 2, member % 2, grid // 8, (grid // 2) % 4, grid % 2
            y, x, z, core = move(y, x_hi * 2 + x_lo, z, core)
            target = (y * 2 + x // 2) * 16 + ((x % 2) * 4 + z) * 2 + core
            pairs.append((member * 16 + grid, target))
    return lax.ppermute(value, ("member", "grid"), pairs)


def summed(own, others):
    total = own.astype(f32)
    for other in others:
        total = total + other.astype(f32)
    return total


def reduced(part):
    grid = lax.axis_index("grid")
    x_lo, z, core = grid // 8, (grid // 2) % 4, grid % 2
    columns = part.shape[1]
    blocks = part.reshape(2, 4, 2, 64, columns)

    def pick(array, index, axis):
        return lax.dynamic_index_in_dim(array, index, axis, keepdims=False)

    got = moved(pick(blocks, 1 - core, 2), lambda y, x, z, c: (y, x, z, 1 - c))
    blocks = summed(pick(blocks, core, 2), [got]).astype(bf16)
    got = [
        moved(pick(blocks, (z + k) % 4, 1), lambda y, x, z, c, k=k: (y, x, (z + k) % 4, c))
        for k in (1, 2, 3)
    ]
    blocks = summed(pick(blocks, z, 1), got).astype(bf16)
    mine, theirs = pick(blocks, x_lo, 0), pick(blocks, 1 - x_lo, 0)
    got = [
        moved(mine if k == 2 else theirs, lambda y, x, z, c, k=k: (y, x ^ k, z, c))
        for k in (1, 2, 3)
    ]
    block = summed(mine, got).astype(bf16)
    got = [moved(block, lambda y, x, z, c, k=k: ((y + k) % 4, x, z, c)) for k in (1, 2, 3)]
    return summed(block, got)


def body(latents, hidden_weight, output_weight, observed, node_area_weight):
    latent_state = latents[0]
    member_list = lax.axis_size("member")
    groups = lax.axis_size("grid")
    node_count = latent_state.shape[0]
    variables = output_weight.shape[1]
    pre_activation = jnp.dot(latent_state, hidden_weight, preferred_element_type=f32)
    gate_sigmoid = jax.nn.sigmoid(pre_activation)
    hidden_activation = (pre_activation * gate_sigmoid).astype(bf16)
    forecast = lax.dot_general(
        output_weight, hidden_activation, (((0,), (1,)), ((), ())), preferred_element_type=f32
    )
    share = node_count // member_list
    blocks = forecast.reshape(variables, member_list, share).transpose(1, 0, 2)
    blocks = (0.25 * blocks).astype(jnp.float16)
    blocks = lax.all_to_all(blocks, "member", 0, 0, tiled=True)
    blocks = 4.0 * blocks.astype(f32)
    place = lax.axis_index("member") * share
    here = lax.dynamic_slice_in_dim(observed, place, share, 1)
    weight = lax.dynamic_slice_in_dim(node_area_weight, place, share, 0)
    pairwise = [0.0] * member_list
    for a in range(member_list):
        for b in range(a + 1, member_list):
            slope = slope_function(blocks[a] - blocks[b])
            pairwise[a] = pairwise[a] + slope
            pairwise[b] = pairwise[b] - slope
    low = jnp.stack(
        [
            weight[None, :] * (slope_function(blocks[a] - here) - pairwise[a] / (member_list - 1))
            for a in range(member_list)
        ]
    ).astype(bf16)
    low = lax.all_to_all(low, "member", 0, 0, tiled=True)
    grad_low = low.transpose(1, 0, 2).reshape(variables, node_count)
    grad_hidden = lax.dot_general(
        grad_low, output_weight, (((0,), (1,)), ((), ())), preferred_element_type=f32
    )
    grad_pre = (grad_hidden * gate_sigmoid * (1.0 + pre_activation * (1.0 - gate_sigmoid))).astype(
        bf16
    )
    part_second = lax.dot_general(
        hidden_activation, grad_low, (((0,), (1,)), ((), ())), preferred_element_type=f32
    )
    part_first = lax.dot_general(
        latent_state, grad_pre, (((0,), (0,)), ((), ())), preferred_element_type=f32
    )
    part = jnp.concatenate(
        [part_first.astype(bf16), jnp.pad(part_second.astype(bf16), ((0, 0), (0, 128 - variables)))], axis=1
    )
    total = reduced(part)
    grad_latent = lax.dot_general(
        grad_pre, hidden_weight, (((1,), (1,)), ((), ())), preferred_element_type=f32
    ).astype(bf16)
    factor = 1.0 / math.sqrt(member_list * node_count * groups)
    width = part_first.shape[1]
    return (grad_latent[None], total[:, :width] * factor, total[:, width : width + variables] * factor)


def solution(mesh):
    in_specs = (P("member", "grid", None), P(), P(), P(None, "grid"), P("grid"))
    out_specs = (P("member", "grid", None), P("grid", None), P("grid", None))
    return jax.shard_map(body, mesh=mesh, in_specs=in_specs, out_specs=out_specs, check_vma=False)
```

time: 351 us -> 124 us (0.35)
  waiting for transfers between devices: 239 us -> 40.7 us
  blocking collectives: 41.5 us -> 0 us
  starting transfers between devices: 0.34 us -> 25.6 us
  between operations: 13.8 us -> 0.95 us
  other arithmetic: 6.57 us -> 12.8 us
  matrix products: 39.1 us -> 33.3 us
    all_gather x1 -> x0, waiting for transfers between devices: 95.7 us -> none  [body(): lax.all_gather(single_prediction[None], 'member', axis=0, tiled=True)]
    psum x1 -> x0, waiting for transfers between devices: 83.6 us -> none  [body(): lax.psum(row_sums[0].astype(jnp.bfloat16), 'member').astype(jnp.float32)]
    psum x1 -> x0, blocking collectives: 41.5 us -> none  [body(): lax.psum(row_sums[1].astype(jnp.bfloat16), 'member').astype(jnp.float32)]
    reduce_scatter x1 -> x0, waiting for transfers between devices: 36.4 us -> none  [body(): lax.psum_scatter(part_second.astype(jnp.bfloat16), 'grid', scatter_dimens...]
    unnamed x5 -> x0, waiting for transfers between devices: 23.3 us -> none
    ppermute x0 -> x10, waiting for transfers between devices: none -> 21.3 us  [moved(): return lax.ppermute(value, ('member', 'grid'), pairs)]
    all_to_all x0 -> x2, waiting for transfers between devices: none -> 19.4 us  [the longest x1 9.77 us: body(): blocks = lax.all_to_all(blocks, 'member', 0, 0, tiled=True)]
    ppermute x0 -> x10, starting transfers between devices: none -> 14.9 us  [moved(): return lax.ppermute(value, ('member', 'grid'), pairs)]
  transfers between devices with their start and end apart: 4 -> 12, of which waited for: 4 -> 8; matrix products, arithmetic and copies ran while one was open for 6% -> 7% of each run, Pallas kernels for 0% -> 0%
where the time goes in v1:
time: 124 us
  waiting for transfers between devices  40.7 us (33%)
  matrix products  33.3 us (27%)
  starting transfers between devices  25.6 us (21%)
  other arithmetic  12.8 us (10%)
  local copies, waits for them, and re-layouts  10.4 us (8%)
    ppermute x10, waiting for transfers between devices, moved(): return lax.ppermute(value, ('member', 'grid'), pairs)  21.3 us
    ppermute x10, starting transfers between devices, moved(): return lax.ppermute(value, ('member', 'grid'), pairs)  14.9 us
    dot_general x1, matrix products, body(): jnp.dot(latent_state, hidden_weight, preferred_element_type=f32)  10.1 us
    all_to_all x1, waiting for transfers between devices, body(): blocks = lax.all_to_all(blocks, 'member', 0, 0, tiled=True)  9.77 us
    all_to_all x1, waiting for transfers between devices, body(): low = lax.all_to_all(low, 'member', 0, 0, tiled=True)  9.58 us
    dot_general x1, matrix products, body(): lax.dot_general(grad_pre, hidden_weight, (((1,), (1,)), ((), ())), prefer...  8.29 us
    all_to_all x1, starting transfers between devices, body(): blocks = lax.all_to_all(blocks, 'member', 0, 0, tiled=True)  7.01 us
    dot_general x1, matrix products, body(): lax.dot_general(grad_low, output_weight, (((0,), (1,)), ((), ())), prefer...  5.78 us
  transfers between devices with their start and end apart: 12, of which 8 were waited for; matrix products, arithmetic and copies ran while one was open for 7% of the time, Pallas kernels for 0%

profile of v1, /device:TPU:0, one launch (start us, length us, event | category | flops | bytes accessed | tf_op | source)
XLA Modules:
  0.0 123.7 jit_solution(10535456743255476173)
XLA Ops:
  0.6 0.0 copy-start
  0.6 0.0 copy-start.3
  0.7 1.6 %copy-done = bf16[1024,1024]{1,0:T(8,128)(2,1)S(1)} copy-done((bf16[1024,1024]{1,0:T(8,128)(2,1)S(1)}, bf16[1024,1024]{1,0:T(8,128)(2,1)}, u32[]{:S(2)}) %copy-start) | copy-done | bytes 2097176
  2.2 10.1 %multiply_convert_fusion.1 = (bf16[2048,1024]{1,0:T(8,128)(2,1)S(1)}, f32[2048,1024]{1,0:T(8,128)}) fusion(bf16[1024,1024]{1,0:T(8,128)(2,1)S(1)} %copy-done, bf16[1,2048,1024]{2,1,0:T(8,128)(2,1)} %param.5), kind=kOutput, calls=%fused_computation.1 | convolution fusion | flops 4305453056 | bytes 18874368 | tf_op jit(solution)/shard_map/dot_general | solution.py:67
  12.3 0.0 copy-done.3
  12.3 1.4 %fusion.5 = f16[2048,100]{0,1:T(8,128)(2,1)S(1)} fusion(bf16[2048,1024]{1,0:T(8,128)(2,1)S(1)} %get-tuple-element.8, bf16[1024,100]{0,1:T(8,128)(2,1)S(1)} %copy-done.3), kind=kOutput, calls=%fused_computation.11 | convolution fusion | flops 419840000 | bytes 4808704 | tf_op jit(solution)/shard_map/dot_general | solution.py:70
  13.8 0.1 copy.14
  13.9 0.1 slice.40
  14.0 0.9 copy.17
  14.9 0.0 copy-done.1
  14.9 7.0 %all-to-all-start = ((f16[8,100,256]{2,1,0:T(8,128)(2,1)}), f16[8,100,256]{2,1,0:T(8,128)(2,1)S(1)}, u32[]{:S(2)}, u32[]{:S(2)}) async-start(f16[8,100,256]{2,1,0:T(8,128)(2,1)} %bitcast.340), calls=%async_computation | async-start | bytes 851968 | tf_op jit(solution)/shard_map/all_to_all | solution.py:76
  21.9 0.8 dynamic_slice.33
  22.7 9.8 %all-to-all-done = f16[8,100,256]{2,1,0:T(8,128)(2,1)S(1)} async-done(((f16[8,100,256]{2,1,0:T(8,128)(2,1)}), f16[8,100,256]{2,1,0:T(8,128)(2,1)S(1)}, u32[]{:S(2)}, u32[]{:S(2)}) %all-to-all-start) | async-done | bytes 409632 | tf_op jit(solution)/shard_map/all_to_all | solution.py:76
  32.5 0.1 convert_multiply_fusion
  32.5 0.0 copy-done.2
  32.6 0.8 bitcast_dynamic-update-slice_fusion.7
  33.4 0.8 bitcast_dynamic-update-slice_fusion.6
  34.2 0.8 bitcast_dynamic-update-slice_fusion.5
  35.0 0.8 bitcast_dynamic-update-slice_fusion.4
  35.8 0.8 bitcast_dynamic-update-slice_fusion.3
  36.6 0.8 bitcast_dynamic-update-slice_fusion.2
  37.4 0.8 bitcast_dynamic-update-slice_fusion.1
  38.2 0.8 bitcast_dynamic-update-slice_fusion
  39.0 3.6 %all-to-all-start.1 = ((bf16[8,100,256]{2,1,0:T(8,128)(2,1)}), bf16[8,100,256]{2,1,0:T(8,128)(2,1)S(1)}, u32[]{:S(2)}, u32[]{:S(2)}) async-start(bf16[8,100,256]{2,1,0:T(8,128)(2,1)} %bitcast_dynamic-update-slice_fusion), calls=%async_computation.1 | async-start | bytes 851968 | tf_op jit(solution)/shard_map/all_to_all | solution.py:93
  42.6 9.6 %all-to-all-done.1 = bf16[8,100,256]{2,1,0:T(8,128)(2,1)S(1)} async-done(((bf16[8,100,256]{2,1,0:T(8,128)(2,1)}), bf16[8,100,256]{2,1,0:T(8,128)(2,1)S(1)}, u32[]{:S(2)}, u32[]{:S(2)}) %all-to-all-start.1) | async-done | bytes 409632 | tf_op jit(solution)/shard_map/all_to_all | solution.py:93
  52.2 0.1 copy.12
  52.3 0.1 copy.15
  52.4 2.9 %convolution_convert_fusion = bf16[1024,100]{0,1:T(8,128)(2,1)S(1)} fusion(bf16[2048,1024]{1,0:T(8,128)(2,1)} %copy-done.1, bf16[100,2048]{1,0:T(8,128)(2,1)S(1)} %bitcast.344), kind=kOutput, calls=%fused_computation.16 | convolution fusion | flops 419532800 | bytes 4808704 | tf_op jit(solution)/shard_map/dot_general | solution.py:101
  55.3 0.0 copy-done.4
  55.3 0.0 copy-start.5
  55.4 5.8 %multiply_convert_fusion = bf16[2048,1024]{1,0:T(8,128)(2,1)S(1)} fusion(f32[2048,1024]{1,0:T(8,128)} %get-tuple-element.9, bf16[100,2048]{1,0:T(8,128)(2,1)S(1)} %bitcast.345, bf16[1024,100]{0,1:T(8,128)(2,1)S(1)} %copy-done.4), kind=kOutput, calls=%fused_computation | convolution fusion | flops 438304768 | bytes 13197312 | tf_op jit(solution)/shard_map/dot_general | solution.py:95
  61.2 4.8 %convert_bitcast_fusion.1 = bf16[1024,1024]{0,1:T(8,128)(2,1)S(1)} fusion(bf16[2048,1024]{1,0:T(8,128)(2,1)S(1)} %multiply_convert_fusion, bf16[1,2048,1024]{2,1,0:T(8,128)(2,1)S(1)} %copy-done.5), kind=kOutput, calls=%fused_computation.15 | convolution fusion | flops 4296015872 | bytes 10485760 | tf_op jit(solution)/shard_map/dot_general | solution.py:104
  66.0 0.0 copy-done.6
  66.0 1.6 %fusion.6 = bf16[1024,1152]{0,1:T(8,128)(2,1)} fusion(bf16[1024,100]{0,1:T(8,128)(2,1)S(1)} %convolution_convert_fusion, bf16[1024,1024]{0,1:T(8,128)(2,1)S(1)} %convert_bitcast_fusion.1), kind=kLoop, calls=%fused_computation.12 | loop fusion | flops 7077888 | bytes 4661248 | tf_op jit(solution)/shard_map/concatenate | solution.py:107
  67.6 4.3 %copy.13 = bf16[1024,1152]{1,0:T(8,128)(2,1)} copy(bf16[1024,1152]{0,1:T(8,128)(2,1)} %fusion.6) | data formatting | bytes 4718592 | tf_op jit(solution)/shard_map/concatenate | solution.py:107
  71.9 1.4 %dynamic-slice_bitcast_fusion = bf16[2,4,64,1152]{3,2,1,0:T(8,128)(2,1)S(1)} fusion(bf16[2,4,2,64,1152]{4,3,2,1,0:T(8,128)(2,1)} %bitcast.341, s32[]{:T(128)S(6)} %select_n.64), kind=kLoop, calls=%fused_computation.17 | loop fusion | bytes 2359300 | tf_op jit(solution)/shard_map/jit(dynamic_index_in_dim)/squeeze | solution.py:42
  73.3 0.3 collective-permute-start
  73.7 2.9 %collective-permute-done = bf16[2,4,64,1152]{3,2,1,0:T(8,128)(2,1)} collective-permute-done((bf16[2,4,64,1152]{3,2,1,0:T(8,128)(2,1)S(1)}, bf16[2,4,64,1152]{3,2,1,0:T(8,128)(2,1)}, u32[]{:S(2)}, u32[]{:S(2)}) %collective-permute-start) | collective-permute-done | bytes 1179680 | tf_op jit(solution)/shard_map/ppermute | solution.py:25
  76.5 1.9 %fusion.7 = bf16[2,4,64,1152]{3,2,1,0:T(8,128)(2,1)S(1)} fusion(bf16[2,4,64,1152]{3,2,1,0:T(8,128)(2,1)} %collective-permute-done, bf16[2,4,2,64,1152]{4,3,2,1,0:T(8,128)(2,1)} %bitcast.342, s32[]{:T(128)S(6)} %select_n.63), kind=kLoop, calls=%fused_computation.14 | loop fusion | flops 2359296 | bytes 3538948 | tf_op jit(solution)/shard_map/convert_element_type | solution.py:45
  78.5 1.0 dynamic-slice_bitcast_fusion.3
  79.4 1.9 %collective-permute-start.1 = (bf16[2,64,1152]{2,1,0:T(8,128)(2,1)}, bf16[2,64,1152]{2,1,0:T(8,128)(2,1)}, u32[]{:S(2)}, u32[]{:S(2)}) collective-permute-start(bf16[2,64,1152]{2,1,0:T(8,128)(2,1)} %get-tuple-element.3), channel_id=1, source_target_pairs={{0,2},{1,3},{2,4},{3,5},{4,6},{5,7},{6,0},{7,1},{8,10},{9,11},{10,... | collective-permute-start | bytes 884744 | tf_op jit(solution)/shard_map/ppermute | solution.py:25
  81.3 3.6 %collective-permute-start.2 = (bf16[2,64,1152]{2,1,0:T(8,128)(2,1)}, bf16[2,64,1152]{2,1,0:T(8,128)(2,1)}, u32[]{:S(2)}, u32[]{:S(2)}) collective-permute-start(bf16[2,64,1152]{2,1,0:T(8,128)(2,1)} %get-tuple-element.5), channel_id=1, source_target_pairs={{0,4},{1,5},{2,6},{3,7},{4,0},{5,1},{6,2},{7,3},{8,12},{9,13},{10,... | collective-permute-start | bytes 884744 | tf_op jit(solution)/shard_map/ppermute | solution.py:25
  84.9 1.0 collective-permute-start.3
  85.9 5.2 %collective-permute-done.1 = bf16[2,64,1152]{2,1,0:T(8,128)(2,1)} collective-permute-done((bf16[2,64,1152]{2,1,0:T(8,128)(2,1)}, bf16[2,64,1152]{2,1,0:T(8,128)(2,1)}, u32[]{:S(2)}, u32[]{:S(2)}) %collective-permute-start.1) | collective-permute-done | bytes 294944 | tf_op jit(solution)/shard_map/ppermute | solution.py:25
  91.1 7.5 %collective-permute-done.2 = bf16[2,64,1152]{2,1,0:T(8,128)(2,1)} collective-permute-done((bf16[2,64,1152]{2,1,0:T(8,128)(2,1)}, bf16[2,64,1152]{2,1,0:T(8,128)(2,1)}, u32[]{:S(2)}, u32[]{:S(2)}) %collective-permute-start.2) | collective-permute-done | bytes 294944 | tf_op jit(solution)/shard_map/ppermute | solution.py:25
  98.6 0.0 collective-permute-done.3
  98.6 1.3 %fusion.12 = bf16[2,64,1152]{2,1,0:T(8,128)(2,1)S(1)} fusion(bf16[2,64,1152]{2,1,0:T(8,128)(2,1)} %collective-permute-done.3, bf16[2,64,1152]{2,1,0:T(8,128)(2,1)} %collective-permute-done.2, bf16[2,64,1152]{2,1,0:T(8,128)(2,1)} %collective-permute-done.1, bf16[2,4,64,1152]{3,2,1,0:T(8,128)(2,1)S(1)} %fusion.7, s32[]{:T(128)S(6)} %select_n.67), kind=kLoop, calls=%fused_computation.22 | loop fusion | flops 1179648 | bytes 1474564 | tf_op jit(solution)/shard_map/convert_element_type | solution.py:50
  99.9 0.7 collective-permute-start.4
  100.6 1.4 %collective-permute-start.5 = (bf16[64,1152]{1,0:T(8,128)(2,1)S(1)}, bf16[64,1152]{1,0:T(8,128)(2,1)S(1)}, u32[]{:S(2)}, u32[]{:S(2)}) collective-permute-start(bf16[64,1152]{1,0:T(8,128)(2,1)S(1)} %get-tuple-element.6), channel_id=1, source_target_pairs={{0,16},{1,17},{2,18},{3,19},{4,20},{5,21},{6,22},{7,23},{8,24},{9,... | collective-permute-start | bytes 442376 | tf_op jit(solution)/shard_map/ppermute | solution.py:25
  102.0 2.7 %collective-permute-start.6 = (bf16[64,1152]{1,0:T(8,128)(2,1)S(1)}, bf16[64,1152]{1,0:T(8,128)(2,1)S(1)}, u32[]{:S(2)}, u32[]{:S(2)}) collective-permute-start(bf16[64,1152]{1,0:T(8,128)(2,1)S(1)} %get-tuple-element.7), channel_id=1, source_target_pairs={{0,24},{1,25},{2,26},{3,27},{4,28},{5,29},{6,30},{7,31},{8,16},{9,... | collective-permute-start | bytes 442376 | tf_op jit(solution)/shard_map/ppermute | solution.py:25
  104.7 1.9 %collective-permute-done.4 = bf16[64,1152]{1,0:T(8,128)(2,1)S(1)} collective-permute-done((bf16[64,1152]{1,0:T(8,128)(2,1)S(1)}, bf16[64,1152]{1,0:T(8,128)(2,1)S(1)}, u32[]{:S(2)}, u32[]{:S(2)}) %collective-permute-start.4) | collective-permute-done | bytes 147488 | tf_op jit(solution)/shard_map/ppermute | solution.py:25
  106.6 1.8 %collective-permute-done.5 = bf16[64,1152]{1,0:T(8,128)(2,1)S(1)} collective-permute-done((bf16[64,1152]{1,0:T(8,128)(2,1)S(1)}, bf16[64,1152]{1,0:T(8,128)(2,1)S(1)}, u32[]{:S(2)}, u32[]{:S(2)}) %collective-permute-start.5) | collective-permute-done | bytes 147488 | tf_op jit(solution)/shard_map/ppermute | solution.py:25
  108.4 2.1 %collective-permute-done.6 = bf16[64,1152]{1,0:T(8,128)(2,1)S(1)} collective-permute-done((bf16[64,1152]{1,0:T(8,128)(2,1)S(1)}, bf16[64,1152]{1,0:T(8,128)(2,1)S(1)}, u32[]{:S(2)}, u32[]{:S(2)}) %collective-permute-start.6) | collective-permute-done | bytes 147488 | tf_op jit(solution)/shard_map/ppermute | solution.py:25
  110.5 0.1 add_convert_fusion
  110.5 0.5 collective-permute-start.7
  111.0 2.0 %collective-permute-start.8 = (bf16[64,1152]{1,0:T(8,128)(2,1)S(1)}, bf16[64,1152]{1,0:T(8,128)(2,1)S(1)}, u32[]{:S(2)}, u32[]{:S(2)}) collective-permute-start(bf16[64,1152]{1,0:T(8,128)(2,1)S(1)} %add_convert_fusion), channel_id=1, source_target_pairs={{0,64},{1,65},{2,66},{3,67},{4,68},{5,69},{6,70},{7,71},{8,72},{9,... | collective-permute-start | bytes 442376 | tf_op jit(solution)/shard_map/ppermute | solution.py:25
  113.0 0.9 collective-permute-start.9
  113.9 8.3 %convert_bitcast_fusion = bf16[1,2048,1024]{2,1,0:T(8,128)(2,1)} fusion(bf16[2048,1024]{1,0:T(8,128)(2,1)} %copy-done.6, bf16[1024,1024]{1,0:T(8,128)(2,1)S(1)} %copy-done), kind=kOutput, calls=%fused_computation.9 | convolution fusion | flops 4297064448 | bytes 10485760 | tf_op jit(solution)/shard_map/dot_general | solution.py:111
  122.2 0.0 collective-permute-done.7
  122.2 0.0 collective-permute-done.8
  122.2 0.0 collective-permute-done.9
  122.2 0.1 convert_add_fusion.2
  122.3 0.7 slice_multiply_fusion
  123.0 0.6 slice_multiply_fusion.1
  (7 shorter events, 0.1 us)
Async XLA Ops:
  0.6 1.6 %copy-start = (bf16[1024,1024]{1,0:T(8,128)(2,1)S(1)}, bf16[1024,1024]{1,0:T(8,128)(2,1)}, u32[]{:S(2)}) copy-start(bf16[1024,1024]{1,0:T(8,128)(2,1)} %param.6) | copy-start | bytes 6291460
  0.6 11.7 %copy-start.3 = (bf16[1024,100]{0,1:T(8,128)(2,1)S(1)}, bf16[1024,100]{0,1:T(8,128)(2,1)}, u32[]{:S(2)}) copy-start(bf16[1024,100]{0,1:T(8,128)(2,1)} %param.7) | copy-start | bytes 614404
  12.3 2.6 %copy-start.1 = (bf16[2048,1024]{1,0:T(8,128)(2,1)}, bf16[2048,1024]{1,0:T(8,128)(2,1)S(1)}, u32[]{:S(2)}) copy-start(bf16[2048,1024]{1,0:T(8,128)(2,1)S(1)} %get-tuple-element.8) | copy-start | bytes 12582916
  12.3 20.2 %copy-start.2 = (f32[100,2048]{1,0:T(8,128)S(1)}, f32[100,2048]{1,0:T(8,128)}, u32[]{:S(2)}) copy-start(f32[100,2048]{1,0:T(8,128)} %param.8) | copy-start | bytes 2457604
  14.9 17.5 %all-to-all-start = ((f16[8,100,256]{2,1,0:T(8,128)(2,1)}), f16[8,100,256]{2,1,0:T(8,128)(2,1)S(1)}, u32[]{:S(2)}, u32[]{:S(2)}) async-start(f16[8,100,256]{2,1,0:T(8,128)(2,1)} %bitcast.340), calls=%async_computation | async-start | bytes 851968 | tf_op jit(solution)/shard_map/all_to_all | solution.py:76
  39.0 16.4 %copy-start.4 = (bf16[1024,100]{0,1:T(8,128)(2,1)S(1)}, bf16[1024,100]{0,1:T(8,128)(2,1)}, u32[]{:S(2)}) copy-start(bf16[1024,100]{0,1:T(8,128)(2,1)} %param.7) | copy-start | bytes 614404
  39.0 13.2 %all-to-all-start.1 = ((bf16[8,100,256]{2,1,0:T(8,128)(2,1)}), bf16[8,100,256]{2,1,0:T(8,128)(2,1)S(1)}, u32[]{:S(2)}, u32[]{:S(2)}) async-start(bf16[8,100,256]{2,1,0:T(8,128)(2,1)} %bitcast_dynamic-update-slice_fusion), calls=%async_computation.1 | async-start | bytes 851968 | tf_op jit(solution)/shard_map/all_to_all | solution.py:93
  55.3 5.8 %copy-start.5 = (bf16[1,2048,1024]{2,1,0:T(8,128)(2,1)S(1)}, bf16[1,2048,1024]{2,1,0:T(8,128)(2,1)}, u32[]{:S(2)}) copy-start(bf16[1,2048,1024]{2,1,0:T(8,128)(2,1)} %param.5) | copy-start | bytes 12582916
  61.2 4.8 %copy-start.6 = (bf16[2048,1024]{1,0:T(8,128)(2,1)}, bf16[2048,1024]{1,0:T(8,128)(2,1)S(1)}, u32[]{:S(2)}) copy-start(bf16[2048,1024]{1,0:T(8,128)(2,1)S(1)} %multiply_convert_fusion) | copy-start | bytes 12582916
  73.3 3.2 %collective-permute-start = (bf16[2,4,64,1152]{3,2,1,0:T(8,128)(2,1)S(1)}, bf16[2,4,64,1152]{3,2,1,0:T(8,128)(2,1)}, u32[]{:S(2)}, u32[]{:S(2)}) collective-permute-start(bf16[2,4,64,1152]{3,2,1,0:T(8,128)(2,1)S(1)} %dynamic-slice_bitcast_fusion), channel_id=1, source_target_pairs={{0,1},{1,0},{2,3},{3,2},{4,5},{5,4},{6,7},{7,6},{8,9},{9,8},{10,11... | collective-permute-start | bytes 3538952 | tf_op jit(solution)/shard_map/ppermute | solution.py:25
  79.4 11.7 %collective-permute-start.1 = (bf16[2,64,1152]{2,1,0:T(8,128)(2,1)}, bf16[2,64,1152]{2,1,0:T(8,128)(2,1)}, u32[]{:S(2)}, u32[]{:S(2)}) collective-permute-start(bf16[2,64,1152]{2,1,0:T(8,128)(2,1)} %get-tuple-element.3), channel_id=1, source_target_pairs={{0,2},{1,3},{2,4},{3,5},{4,6},{5,7},{6,0},{7,1},{8,10},{9,11},{10,... | collective-permute-start | bytes 884744 | tf_op jit(solution)/shard_map/ppermute | solution.py:25
  81.3 17.2 %collective-permute-start.2 = (bf16[2,64,1152]{2,1,0:T(8,128)(2,1)}, bf16[2,64,1152]{2,1,0:T(8,128)(2,1)}, u32[]{:S(2)}, u32[]{:S(2)}) collective-permute-start(bf16[2,64,1152]{2,1,0:T(8,128)(2,1)} %get-tuple-element.5), channel_id=1, source_target_pairs={{0,4},{1,5},{2,6},{3,7},{4,0},{5,1},{6,2},{7,3},{8,12},{9,13},{10,... | collective-permute-start | bytes 884744 | tf_op jit(solution)/shard_map/ppermute | solution.py:25
  84.9 13.7 %collective-permute-start.3 = (bf16[2,64,1152]{2,1,0:T(8,128)(2,1)}, bf16[2,64,1152]{2,1,0:T(8,128)(2,1)}, u32[]{:S(2)}, u32[]{:S(2)}) collective-permute-start(bf16[2,64,1152]{2,1,0:T(8,128)(2,1)} %get-tuple-element.4), channel_id=1, source_target_pairs={{0,6},{1,7},{2,0},{3,1},{4,2},{5,3},{6,4},{7,5},{8,14},{9,15},{10,... | collective-permute-start | bytes 884744 | tf_op jit(solution)/shard_map/ppermute | solution.py:25
  99.9 6.7 %collective-permute-start.4 = (bf16[64,1152]{1,0:T(8,128)(2,1)S(1)}, bf16[64,1152]{1,0:T(8,128)(2,1)S(1)}, u32[]{:S(2)}, u32[]{:S(2)}) collective-permute-start(bf16[64,1152]{1,0:T(8,128)(2,1)S(1)} %get-tuple-element.7), channel_id=1, source_target_pairs={{0,8},{1,9},{2,10},{3,11},{4,12},{5,13},{6,14},{7,15},{8,0},{9,1},... | collective-permute-start | bytes 442376 | tf_op jit(solution)/shard_map/ppermute | solution.py:25
  100.6 7.8 %collective-permute-start.5 = (bf16[64,1152]{1,0:T(8,128)(2,1)S(1)}, bf16[64,1152]{1,0:T(8,128)(2,1)S(1)}, u32[]{:S(2)}, u32[]{:S(2)}) collective-permute-start(bf16[64,1152]{1,0:T(8,128)(2,1)S(1)} %get-tuple-element.6), channel_id=1, source_target_pairs={{0,16},{1,17},{2,18},{3,19},{4,20},{5,21},{6,22},{7,23},{8,24},{9,... | collective-permute-start | bytes 442376 | tf_op jit(solution)/shard_map/ppermute | solution.py:25
  102.0 8.4 %collective-permute-start.6 = (bf16[64,1152]{1,0:T(8,128)(2,1)S(1)}, bf16[64,1152]{1,0:T(8,128)(2,1)S(1)}, u32[]{:S(2)}, u32[]{:S(2)}) collective-permute-start(bf16[64,1152]{1,0:T(8,128)(2,1)S(1)} %get-tuple-element.7), channel_id=1, source_target_pairs={{0,24},{1,25},{2,26},{3,27},{4,28},{5,29},{6,30},{7,31},{8,16},{9,... | collective-permute-start | bytes 442376 | tf_op jit(solution)/shard_map/ppermute | solution.py:25
  110.5 11.7 %collective-permute-start.7 = (bf16[64,1152]{1,0:T(8,128)(2,1)S(1)}, bf16[64,1152]{1,0:T(8,128)(2,1)S(1)}, u32[]{:S(2)}, u32[]{:S(2)}) collective-permute-start(bf16[64,1152]{1,0:T(8,128)(2,1)S(1)} %add_convert_fusion), channel_id=1, source_target_pairs={{0,32},{1,33},{2,34},{3,35},{4,36},{5,37},{6,38},{7,39},{8,40},{9,... | collective-permute-start | bytes 442376 | tf_op jit(solution)/shard_map/ppermute | solution.py:25
  111.0 11.2 %collective-permute-start.8 = (bf16[64,1152]{1,0:T(8,128)(2,1)S(1)}, bf16[64,1152]{1,0:T(8,128)(2,1)S(1)}, u32[]{:S(2)}, u32[]{:S(2)}) collective-permute-start(bf16[64,1152]{1,0:T(8,128)(2,1)S(1)} %add_convert_fusion), channel_id=1, source_target_pairs={{0,64},{1,65},{2,66},{3,67},{4,68},{5,69},{6,70},{7,71},{8,72},{9,... | collective-permute-start | bytes 442376 | tf_op jit(solution)/shard_map/ppermute | solution.py:25
  113.0 9.2 %collective-permute-start.9 = (bf16[64,1152]{1,0:T(8,128)(2,1)S(1)}, bf16[64,1152]{1,0:T(8,128)(2,1)S(1)}, u32[]{:S(2)}, u32[]{:S(2)}) collective-permute-start(bf16[64,1152]{1,0:T(8,128)(2,1)S(1)} %add_convert_fusion), channel_id=1, source_target_pairs={{0,96},{1,97},{2,98},{3,99},{4,100},{5,101},{6,102},{7,103},{8,104... | collective-permute-start | bytes 442376 | tf_op jit(solution)/shard_map/ppermute | solution.py:25

commit v2 on v0

v2 whole, which is shorter than its diff:
```python
import functools
import math

import jax
import jax.numpy as jnp
from jax import lax
from jax.experimental import pallas as pl
from jax.experimental.pallas import tpu as pltpu
from jax.sharding import PartitionSpec as P

smooth_sq = 0.0025
bf16 = jnp.bfloat16
f16 = jnp.float16
f32 = jnp.float32

NT = (((1,), (1,)), ((), ()))
WIDE = 128
TALL = 112
SHARE = 256


def params(mib):
    return pltpu.CompilerParams(vmem_limit_bytes=mib * 1024 * 1024)


def cost(flops, nbytes, trans=0):
    return pl.CostEstimate(flops=flops, bytes_accessed=nbytes, transcendentals=trans)


def forward_kernel(latent_ref, weight_ref, out_weight_ref, forecast_ref, hidden_ref, slope_ref, padded_ref):
    rows, width = latent_ref.shape
    variables = out_weight_ref.shape[1]

    @pl.when(pl.program_id(0) == 0)
    def _():
        padded_ref[...] = jnp.concatenate(
            [out_weight_ref[...], jnp.zeros((width, WIDE - variables), bf16)], axis=1
        )

    for start in range(0, width, 256):
        columns = slice(start, start + 256)
        pre = jnp.dot(latent_ref[...], weight_ref[:, columns], preferred_element_type=f32)
        sig = 1.0 / (1.0 + jnp.exp(-pre))
        hidden_ref[:, columns] = (pre * sig).astype(bf16)
        slope_ref[:, columns] = (sig * (1.0 + pre * (1.0 - sig))).astype(bf16)
    for share in range(rows // SHARE):
        forecast = jnp.dot(
            hidden_ref[share * SHARE : (share + 1) * SHARE, :], padded_ref[...], preferred_element_type=f32
        )
        forecast_ref[share] = forecast.T[:TALL].astype(forecast_ref.dtype)


def forward(latent, weight, out_weight):
    nodes, width = latent.shape
    variables = out_weight.shape[1]
    rows = 512
    return pl.pallas_call(
        forward_kernel,
        grid=(nodes // rows,),
        in_specs=[
            pl.BlockSpec((rows, width), lambda i: (i, 0)),
            pl.BlockSpec((width, width), lambda i: (0, 0)),
            pl.BlockSpec((width, variables), lambda i: (0, 0)),
        ],
        out_specs=[
            pl.BlockSpec((rows // SHARE, TALL, SHARE), lambda i: (i, 0, 0)),
            pl.BlockSpec((rows, width), lambda i: (i, 0)),
            pl.BlockSpec((rows, width), lambda i: (i, 0)),
            pl.BlockSpec((width, WIDE), lambda i: (0, 0)),
        ],
        out_shape=[
            jax.ShapeDtypeStruct((nodes // SHARE, TALL, SHARE), f32),
            jax.ShapeDtypeStruct((nodes, width), bf16),
            jax.ShapeDtypeStruct((nodes, width), bf16),
            jax.ShapeDtypeStruct((width, WIDE), bf16),
        ],
        compiler_params=params(32),
        cost_estimate=cost(2 * nodes * width * (width + WIDE), 20 << 20),
        name="forward",
    )(latent, weight, out_weight)


def slope_function(diff):
    return diff * lax.rsqrt(diff * diff + smooth_sq)


def pair_kernel(place_ref, blocks_ref, observed_ref, area_ref, low_ref):
    members = blocks_ref.shape[0]
    variables = observed_ref.shape[0]
    for start in range(0, TALL, 16):
        rows = slice(start, start + 16)
        real = min(16, variables - start)
        observed = observed_ref[start : start + real, :]
        if real < 16:
            observed = jnp.concatenate([observed, jnp.zeros((16 - real, SHARE), f32)], axis=0)
        values = [blocks_ref[a, rows, :] for a in range(members)]
        totals = [0.0] * members
        for a in range(members):
            for b in range(a + 1, members):
                slope = slope_function(values[a] - values[b])
                totals[a] = totals[a] + slope
                totals[b] = totals[b] - slope
        for a in range(members):
            field = area_ref[...] * (slope_function(values[a] - observed) - totals[a] * (1.0 / (members - 1)))
            low_ref[a, rows, :] = field.astype(bf16)


def pairs(place, blocks, observed, area):
    members = blocks.shape[0]
    variables = observed.shape[0]
    return pl.pallas_call(
        pair_kernel,
        grid_spec=pltpu.PrefetchScalarGridSpec(
            num_scalar_prefetch=1,
            grid=(1,),
            in_specs=[
                pl.BlockSpec((members, TALL, SHARE), lambda i, place: (0, 0, 0)),
                pl.BlockSpec((variables, SHARE), lambda i, place: (0, place[0])),
                pl.BlockSpec((1, SHARE), lambda i, place: (0, place[0])),
            ],
            out_specs=pl.BlockSpec((members, TALL, SHARE), lambda i, place: (0, 0, 0)),
        ),
        out_shape=jax.ShapeDtypeStruct((members, TALL, SHARE), bf16),
        compiler_params=params(16),
        cost_estimate=cost(4 << 20, 2 << 20),
        name="pairs",
    )(place, blocks, observed, area)


def place_rows(order_ref, group, block, store):
    core = order_ref[8]
    at = order_ref[group] * 64
    store(pl.multiple_of(core * 512 + at, 64), block[:64])
    store(pl.multiple_of((1 - core) * 512 + at, 64), block[64:])


def turn_kernel(order_ref, latent_ref, turned_ref):
    def store(at, value):
        turned_ref[pl.ds(at, 64), :] = value

    for group in range(8):
        block = latent_ref[:, group * 128 : (group + 1) * 128].T
        place_rows(order_ref, group, block, store)


def turned(order, latent):
    nodes, width = latent.shape
    rows = 512
    return pl.pallas_call(
        turn_kernel,
        grid_spec=pltpu.PrefetchScalarGridSpec(
            num_scalar_prefetch=1,
            grid=(nodes // rows,),
            in_specs=[pl.BlockSpec((rows, width), lambda i, order: (i, 0))],
            out_specs=pl.BlockSpec((width, rows), lambda i, order: (0, i)),
        ),
        out_shape=jax.ShapeDtypeStruct((width, nodes), bf16),
        compiler_params=params(16),
        cost_estimate=cost(0, 8 << 20),
        name="turned",
    )(order, latent)


def backward_kernel(
    order_ref, low_ref, turned_ref, slope_ref, hidden_ref, padded_ref, pre_ref, send_ref, keep_ref, turn_ref, flat_ref, second_ref
):
    step = pl.program_id(0)
    steps = pl.num_programs(0)
    nodes = turn_ref.shape[0]
    width = turned_ref.shape[0]
    shares = low_ref.shape[0]
    half = width // 2

    @pl.when(step == 0)
    def _():
        for share in range(shares):
            columns = slice(share * SHARE, (share + 1) * SHARE)
            low = jnp.concatenate([low_ref[share], jnp.zeros((WIDE - TALL, SHARE), bf16)], axis=0)
            flat_ref[:, columns] = low
            turn_ref[columns, :] = low.T

    for start in range(0, nodes, 512):
        rows = slice(start, start + 512)
        grad_hidden = lax.dot_general(turn_ref[rows, :], padded_ref[...], NT, preferred_element_type=f32)
        pre_ref[rows, :] = (grad_hidden * slope_ref[rows, :].astype(f32)).astype(bf16)
    for out_ref, base in ((send_ref, 0), (keep_ref, half)):
        for start in range(0, half, 256):
            rows = slice(start, start + 256)
            part = jnp.dot(turned_ref[base + start : base + start + 256, :], pre_ref[...], preferred_element_type=f32)
            out_ref[rows, pl.ds(pl.multiple_of(step * 256, 256), 256)] = part.astype(bf16)
    second_ref[step] = jnp.dot(flat_ref[...], hidden_ref[...], preferred_element_type=f32).T

    @pl.when(step == steps - 1)
    def _():
        for group in range(8):
            block = second_ref[group // 2, (group % 2) * 128 : (group % 2 + 1) * 128, :].astype(bf16)
            at = pl.multiple_of(order_ref[group] * 64, 64)
            first_core = order_ref[8] == 1
            mine = jnp.where(first_core, block[:64], block[64:])
            other = jnp.where(first_core, block[64:], block[:64])
            keep_ref[pl.ds(at, 64), width : width + WIDE] = mine
            send_ref[pl.ds(at, 64), width : width + WIDE] = other


def backward(order, low, turned_latent, slope, hidden, padded):
    nodes, width = slope.shape
    half = width // 2
    total = width + WIDE
    return pl.pallas_call(
        backward_kernel,
        grid_spec=pltpu.PrefetchScalarGridSpec(
            num_scalar_prefetch=1,
            grid=(width // 256,),
            in_specs=[
                pl.BlockSpec(low.shape, lambda i, order: (0, 0, 0)),
                pl.BlockSpec((width, nodes), lambda i, order: (0, 0)),
                pl.BlockSpec((nodes, 256), lambda i, order: (0, i)),
                pl.BlockSpec((nodes, 256), lambda i, order: (0, i)),
                pl.BlockSpec((256, WIDE), lambda i, order: (i, 0)),
            ],
            out_specs=[
                pl.BlockSpec((nodes, 256), lambda i, order: (0, i)),
                pl.BlockSpec((half, total), lambda i, order: (0, 0)),
                pl.BlockSpec((half, total), lambda i, order: (0, 0)),
            ],
            scratch_shapes=[
                pltpu.VMEM((nodes, WIDE), bf16),
                pltpu.VMEM((WIDE, nodes), bf16),
                pltpu.VMEM((width // 256, 256, WIDE), f32),
            ],
        ),
        out_shape=[
            jax.ShapeDtypeStruct((nodes, width), bf16),
            jax.ShapeDtypeStruct((half, total), bf16),
            jax.ShapeDtypeStruct((half, total), bf16),
        ],
        compiler_params=params(36),
        cost_estimate=cost(2 * nodes * width * (width + 2 * WIDE), 20 << 20),
        name="backward",
    )(order, low, turned_latent, slope, hidden, padded)


def latent_kernel(pre_ref, weight_ref, out_ref):
    rows, width = pre_ref.shape
    for start in range(0, width, 256):
        columns = slice(start, start + 256)
        out_ref[:, columns] = lax.dot_general(
            pre_ref[...], weight_ref[columns, :], NT, preferred_element_type=f32
        ).astype(bf16)


def latent_gradient(grad_pre, weight):
    nodes, width = grad_pre.shape
    rows = 512
    return pl.pallas_call(
        latent_kernel,
        grid=(nodes // rows,),
        in_specs=[
            pl.BlockSpec((rows, width), lambda i: (i, 0)),
            pl.BlockSpec((width, width), lambda i: (0, 0)),
        ],
        out_specs=pl.BlockSpec((rows, width), lambda i: (i, 0)),
        out_shape=jax.ShapeDtypeStruct((nodes, width), bf16),
        compiler_params=params(24),
        cost_estimate=cost(2 * nodes * width * width, 10 << 20),
        name="latent_gradient",
    )(grad_pre, weight)


def moved(value, move):
    moves = []
    for member in range(8):
        for grid in range(16):
            y, x_hi, x_lo, z, core = member // 2, member % 2, grid // 8, (grid // 2) % 4, grid % 2
            y, x, z, core = move(y, x_hi * 2 + x_lo, z, core)
            target = (y * 2 + x // 2) * 16 + ((x % 2) * 4 + z) * 2 + core
            moves.append((member * 16 + grid, target))
    return lax.ppermute(value, ("member", "grid"), moves)


def summed(own, others):
    total = own.astype(f32)
    for other in others:
        total = total + other.astype(f32)
    return total


def reduced(send, keep):
    columns = send.shape[1]
    got = moved(send, lambda y, x, z, c: (y, x, z, 1 - c))
    blocks = summed(keep, [got]).astype(bf16).reshape(4, 2, 64, columns)
    got = [moved(blocks[k], lambda y, x, z, c, k=k: (y, x, (z + k) % 4, c)) for k in (1, 3, 2)]
    blocks = summed(blocks[0], got).astype(bf16)
    got = [
        moved(blocks[0] if k == 2 else blocks[1], lambda y, x, z, c, k=k: (y, x ^ k, z, c))
        for k in (1, 3, 2)
    ]
    block = summed(blocks[0], got).astype(bf16)
    got = [moved(block, lambda y, x, z, c, k=k: ((y + k) % 4, x, z, c)) for k in (1, 3, 2)]
    return summed(block, got)


def body(latents, hidden_weight, output_weight, observed, node_area_weight):
    latent = latents[0]
    members = lax.axis_size("member")
    groups = lax.axis_size("grid")
    nodes, width = latent.shape
    variables = output_weight.shape[1]
    member = lax.axis_index("member")
    grid = lax.axis_index("grid")
    x_lo, z, core = grid // 8, (grid // 2) % 4, grid % 2
    order = jnp.stack(
        [((g % 4 - z) % 4) * 2 + jnp.abs(g // 4 - x_lo) for g in range(8)] + [1 - core]
    ).astype(jnp.int32)
    place = member.astype(jnp.int32).reshape(1)

    forecast, hidden, slope, padded = forward(latent, hidden_weight, output_weight)
    blocks = lax.all_to_all((0.25 * forecast).astype(f16), "member", 0, 0, tiled=True)
    low = pairs(place, 4.0 * blocks.astype(f32), observed, node_area_weight.reshape(1, nodes))
    low = lax.all_to_all(low, "member", 0, 0, tiled=True)
    turned_latent = turned(order, latent)
    grad_pre, send, keep = backward(order, low, turned_latent, slope, hidden, padded)
    total = reduced(send, keep)
    grad_latent = latent_gradient(grad_pre, hidden_weight)
    factor = 1.0 / math.sqrt(members * nodes * groups)
    return (grad_latent[None], total[:, :width] * factor, total[:, width : width + variables] * factor)


def solution(mesh):
    in_specs = (P("member", "grid", None), P(), P(), P(None, "grid"), P("grid"))
    out_specs = (P("member", "grid", None), P("grid", None), P("grid", None))
    return jax.shard_map(body, mesh=mesh, in_specs=in_specs, out_specs=out_specs, check_vma=False)
```

time: 351 us -> 112 us (0.32)
  waiting for transfers between devices: 239 us -> 35.5 us
  blocking collectives: 41.5 us -> 0 us
  matrix products: 39.1 us -> 0 us
  Pallas kernels: 0 us -> 29.9 us
  starting transfers between devices: 0.34 us -> 24.3 us
  between operations: 13.8 us -> 0.9 us
  local copies, waits for them, and re-layouts: 10.1 us -> 17.7 us
  other arithmetic: 6.57 us -> 2.88 us
    all_gather x1 -> x0, waiting for transfers between devices: 95.7 us -> none  [body(): lax.all_gather(single_prediction[None], 'member', axis=0, tiled=True)]
    psum x1 -> x0, waiting for transfers between devices: 83.6 us -> none  [body(): lax.psum(row_sums[0].astype(jnp.bfloat16), 'member').astype(jnp.float32)]
    psum x1 -> x0, blocking collectives: 41.5 us -> none  [body(): lax.psum(row_sums[1].astype(jnp.bfloat16), 'member').astype(jnp.float32)]
    dot_general x6 -> x0, matrix products: 39.1 us -> none  [the longest x1 10.1 us: body(): jnp.dot(latent_state, hidden_weight, preferred_element_type=jnp.float32)]
    reduce_scatter x1 -> x0, waiting for transfers between devices: 36.4 us -> none  [body(): lax.psum_scatter(part_second.astype(jnp.bfloat16), 'grid', scatter_dimens...]
    pallas_call x0 -> x5, Pallas kernels: none -> 29.9 us  [the longest x1 10.4 us: backward(): pl.pallas_call(backward_kernel, grid_spec=pltpu.PrefetchScalarGridSpec(nu...]
    unnamed x5 -> x0, waiting for transfers between devices: 23.3 us -> none
    ppermute x0 -> x10, waiting for transfers between devices: none -> 21.4 us  [moved(): return lax.ppermute(value, ('member', 'grid'), moves)]
  transfers between devices with their start and end apart: 4 -> 12, of which waited for: 4 -> 9; matrix products, arithmetic and copies ran while one was open for 6% -> 0% of each run, Pallas kernels for 0% -> 8%
where the time goes in v2:
time: 112 us; the launch traced here: 111 us
  waiting for transfers between devices  35.5 us (32%)
  Pallas kernels  29.9 us (27%)
  starting transfers between devices  24.3 us (22%)
  local copies, waits for them, and re-layouts  17.7 us (16%)
  other arithmetic  2.88 us (3%)
    ppermute x10, waiting for transfers between devices, moved(): return lax.ppermute(value, ('member', 'grid'), moves)  21.4 us
    unnamed x23, local copies, waits for them, and re-layouts  17.4 us
    ppermute x10, starting transfers between devices, moved(): return lax.ppermute(value, ('member', 'grid'), moves)  13.8 us
    all_to_all x1, waiting for transfers between devices, body(): lax.all_to_all((0.25 * forecast).astype(f16), 'member', 0, 0, tiled=True)  10.9 us
    pallas_call x1, Pallas kernels, backward(): pl.pallas_call(backward_kernel, grid_spec=pltpu.PrefetchScalarGridSpec(nu...  10.4 us
    pallas_call x1, Pallas kernels, forward(): pl.pallas_call(forward_kernel, grid=(nodes // rows,), in_specs=[pl.BlockS...  9.2 us
    all_to_all x1, starting transfers between devices, body(): lax.all_to_all((0.25 * forecast).astype(f16), 'member', 0, 0, tiled=True)  7.02 us
    pallas_call x1, Pallas kernels, latent_gradient(): pl.pallas_call(latent_kernel, grid=(nodes // rows,), in_specs=[pl.BlockSp...  6.18 us
  transfers between devices with their start and end apart: 12, of which 9 were waited for; matrix products, arithmetic and copies ran while one was open for 0% of the time, Pallas kernels for 8%

profile of v2, /device:TPU:0, one launch (start us, length us, event | category | flops | bytes accessed | tf_op | source)
XLA Modules:
  0.0 111.1 jit_solution(440191644068427042)
XLA Ops:
  0.6 1.1 copy.8.out_weight_ref
  1.7 0.0 copy-start
  1.8 2.2 %copy-done = bf16[1,2048,1024]{2,1,0:T(8,128)(2,1)S(1)} copy-done((bf16[1,2048,1024]{2,1,0:T(8,128)(2,1)S(1)}, bf16[1,2048,1024]{2,1,0:T(8,128)(2,1)}, u32[]{:S(2)}) %copy-start) | copy-done | bytes 4194328
  3.9 0.0 copy-start.6
  3.9 1.6 %copy-done.6 = bf16[1024,1024]{1,0:T(8,128)(2,1)S(1)} copy-done((bf16[1024,1024]{1,0:T(8,128)(2,1)S(1)}, bf16[1024,1024]{1,0:T(8,128)(2,1)}, u32[]{:S(2)}) %copy-start.6) | copy-done | bytes 2097176
  5.5 9.2 %forward.1 = (f32[8,112,256]{2,1,0:T(8,128)S(1)}, bf16[2048,1024]{1,0:T(8,128)(2,1)S(1)}, bf16[2048,1024]{1,0:T(8,128)(2,1)S(1)}, bf16[1024,128]{1,0:T(8,128)(2,1)S(1)}) custom-call(bf16[2048,1024]{1,0:T(8,128)(2,1)S(1)} %bitcast.24, bf16[1024,1024]{1,0:T(8,128)(2,1)S(1)} %copy-done.6, bf16[1024,100]{1,0:T(8,128)(2,1)S(1)} %copy.8.out_weight_ref), custom_call_target="tpu_custom_call" | custom-call | flops 4831838208 | bytes 20971520 | tf_op jit(solution)/shard_map/forward/pallas_call | solution.py:57
  14.7 0.0 copy-start.8
  14.7 1.9 %copy-done.8 = bf16[2048,1024]{1,0:T(8,128)(2,1)} copy-done((bf16[2048,1024]{1,0:T(8,128)(2,1)}, bf16[2048,1024]{1,0:T(8,128)(2,1)S(1)}, u32[]{:S(2)}) %copy-start.8) | copy-done | bytes 4194328
  16.7 0.0 copy-start.9
  16.7 2.0 %copy-done.9 = bf16[2048,1024]{1,0:T(8,128)(2,1)} copy-done((bf16[2048,1024]{1,0:T(8,128)(2,1)}, bf16[2048,1024]{1,0:T(8,128)(2,1)S(1)}, u32[]{:S(2)}) %copy-start.9) | copy-done | bytes 4194328
  18.7 0.0 copy-start.4
  18.7 0.0 copy-start.5
  18.7 0.9 multiply_convert_fusion
  19.6 7.0 %all-to-all-start = ((f16[8,112,256]{2,1,0:T(8,128)(2,1)}), f16[8,112,256]{2,1,0:T(8,128)(2,1)S(1)}, u32[]{:S(2)}, u32[]{:S(2)}) async-start(f16[8,112,256]{2,1,0:T(8,128)(2,1)} %multiply_convert_fusion), calls=%async_computation | async-start | bytes 917504 | tf_op jit(solution)/shard_map/all_to_all | solution.py:318
  26.6 10.9 %all-to-all-done = f16[8,112,256]{2,1,0:T(8,128)(2,1)S(1)} async-done(((f16[8,112,256]{2,1,0:T(8,128)(2,1)}), f16[8,112,256]{2,1,0:T(8,128)(2,1)S(1)}, u32[]{:S(2)}, u32[]{:S(2)}) %all-to-all-start) | async-done | bytes 458784 | tf_op jit(solution)/shard_map/all_to_all | solution.py:318
  37.5 0.1 convert_multiply_fusion.blocks_ref
  37.6 0.0 copy-done.4
  37.6 0.0 copy-done.5
  37.6 1.9 %pairs.1 = bf16[8,112,256]{2,1,0:T(8,128)(2,1)} custom-call(s32[1]{0:T(128)} %bitcast.9.place_ref, f32[8,112,256]{2,1,0:T(8,128)S(1)} %convert_multiply_fusion.blocks_ref, f32[100,2048]{1,0:T(8,128)S(1)} %copy-done.4, f32[1,2048]{1,0:T(1,128)S(1)} %bitcast.26), custom_call_target="tpu_custom_call" | custom-call | flops 4194304 | bytes 2097152 | tf_op jit(solution)/shard_map/pairs/pallas_call | solution.py:111
  39.5 3.5 %all-to-all-start.1 = ((bf16[8,112,256]{2,1,0:T(8,128)(2,1)}), bf16[8,112,256]{2,1,0:T(8,128)(2,1)S(1)}, u32[]{:S(2)}, u32[]{:S(2)}) async-start(bf16[8,112,256]{2,1,0:T(8,128)(2,1)} %pairs.1), calls=%async_computation.1 | async-start | bytes 917504 | tf_op jit(solution)/shard_map/all_to_all | solution.py:320
  43.1 0.1 stack.39.order_ref
  43.2 0.0 copy-start.1
  43.2 2.2 %copy-done.1 = bf16[1,2048,1024]{2,1,0:T(8,128)(2,1)S(1)} copy-done((bf16[1,2048,1024]{2,1,0:T(8,128)(2,1)S(1)}, bf16[1,2048,1024]{2,1,0:T(8,128)(2,1)}, u32[]{:S(2)}) %copy-start.1) | copy-done | bytes 4194328
  45.4 2.2 %turned.1.turned_ref = bf16[1024,2048]{1,0:T(8,128)(2,1)S(1)} custom-call(s32[9]{0:T(128)S(1)} %stack.39.order_ref, bf16[2048,1024]{1,0:T(8,128)(2,1)S(1)} %bitcast.25), custom_call_target="tpu_custom_call" | custom-call | bytes 8388608 | tf_op jit(solution)/shard_map/turned/pallas_call | solution.py:149
  47.6 0.0 copy-start.2
  47.6 2.0 %copy-done.2 = bf16[1024,2048]{1,0:T(8,128)(2,1)} copy-done((bf16[1024,2048]{1,0:T(8,128)(2,1)}, bf16[1024,2048]{1,0:T(8,128)(2,1)S(1)}, u32[]{:S(2)}) %copy-start.2) | copy-done | bytes 4194328
  49.6 3.2 %all-to-all-done.1.low_ref = bf16[8,112,256]{2,1,0:T(8,128)(2,1)S(1)} async-done(((bf16[8,112,256]{2,1,0:T(8,128)(2,1)}), bf16[8,112,256]{2,1,0:T(8,128)(2,1)S(1)}, u32[]{:S(2)}, u32[]{:S(2)}) %all-to-all-start.1) | async-done | bytes 458784 | tf_op jit(solution)/shard_map/all_to_all | solution.py:320
  52.9 0.0 copy-start.3
  52.9 2.2 %copy-done.3 = bf16[1024,2048]{1,0:T(8,128)(2,1)S(1)} copy-done((bf16[1024,2048]{1,0:T(8,128)(2,1)S(1)}, bf16[1024,2048]{1,0:T(8,128)(2,1)}, u32[]{:S(2)}) %copy-start.3) | copy-done | bytes 4194328
  55.0 0.0 copy-start.10
  55.1 2.2 %copy-done.10 = bf16[2048,1024]{1,0:T(8,128)(2,1)S(1)} copy-done((bf16[2048,1024]{1,0:T(8,128)(2,1)S(1)}, bf16[2048,1024]{1,0:T(8,128)(2,1)}, u32[]{:S(2)}) %copy-start.10) | copy-done | bytes 4194328
  57.2 10.4 %backward.1 = (bf16[2048,1024]{1,0:T(8,128)(2,1)S(1)}, bf16[512,1152]{1,0:T(8,128)(2,1)S(1)}, bf16[512,1152]{1,0:T(8,128)(2,1)S(1)}) custom-call(s32[9]{0:T(128)S(1)} %stack.39.order_ref, bf16[8,112,256]{2,1,0:T(8,128)(2,1)S(1)} %all-to-all-done.1.low_ref, bf16[1024,2048]{1,0:T(8,128)(2,1)S(1)} %copy-done.3, bf16[2048,1024]{1,0:T(8,128)(2,1)S(1)} %copy-done.10, ...), custom_call_target="tpu_custom_call" | custom-call | flops 5368709120 | bytes 20971520 | tf_op jit(solution)/shard_map/backward/pallas_call | solution.py:209
  67.6 0.1 collective-permute-start
  67.7 2.8 %collective-permute-done = bf16[512,1152]{1,0:T(8,128)(2,1)S(1)} collective-permute-done((bf16[512,1152]{1,0:T(8,128)(2,1)S(1)}, bf16[512,1152]{1,0:T(8,128)(2,1)S(1)}, u32[]{:S(2)}, u32[]{:S(2)}) %collective-permute-start) | collective-permute-done | bytes 1179680 | tf_op jit(solution)/shard_map/ppermute | solution.py:278
  70.5 0.3 add_convert_fusion
  70.8 0.0 copy-start.7
  70.8 0.1 fusion.3
  71.0 4.0 %collective-permute-start.3 = (bf16[2,64,1152]{2,1,0:T(8,128)(2,1)S(1)}, bf16[2,64,1152]{2,1,0:T(8,128)(2,1)S(1)}, u32[]{:S(2)}, u32[]{:S(2)}) collective-permute-start(bf16[2,64,1152]{2,1,0:T(8,128)(2,1)S(1)} %bitcast.30), channel_id=1, source_target_pairs={{0,4},{1,5},{2,6},{3,7},{4,0},{5,1},{6,2},{7,3},{8,12},{9,13},{10,... | collective-permute-start | bytes 884744 | tf_op jit(solution)/shard_map/ppermute | solution.py:278
  74.9 1.1 collective-permute-start.1
  76.0 2.1 %collective-permute-start.2 = (bf16[2,64,1152]{2,1,0:T(8,128)(2,1)S(1)}, bf16[2,64,1152]{2,1,0:T(8,128)(2,1)S(1)}, u32[]{:S(2)}, u32[]{:S(2)}) collective-permute-start(bf16[2,64,1152]{2,1,0:T(8,128)(2,1)S(1)} %bitcast.28), channel_id=1, source_target_pairs={{0,6},{1,7},{2,0},{3,1},{4,2},{5,3},{6,4},{7,5},{8,14},{9,15},{10,... | collective-permute-start | bytes 884744 | tf_op jit(solution)/shard_map/ppermute | solution.py:278
  78.1 4.6 %collective-permute-done.3 = bf16[2,64,1152]{2,1,0:T(8,128)(2,1)S(1)} collective-permute-done((bf16[2,64,1152]{2,1,0:T(8,128)(2,1)S(1)}, bf16[2,64,1152]{2,1,0:T(8,128)(2,1)S(1)}, u32[]{:S(2)}, u32[]{:S(2)}) %collective-permute-start.3) | collective-permute-done | bytes 294944 | tf_op jit(solution)/shard_map/ppermute | solution.py:278
  82.7 5.8 %collective-permute-done.1 = bf16[2,64,1152]{2,1,0:T(8,128)(2,1)S(1)} collective-permute-done((bf16[2,64,1152]{2,1,0:T(8,128)(2,1)S(1)}, bf16[2,64,1152]{2,1,0:T(8,128)(2,1)S(1)}, u32[]{:S(2)}, u32[]{:S(2)}) %collective-permute-start.1) | collective-permute-done | bytes 294944 | tf_op jit(solution)/shard_map/ppermute | solution.py:278
  88.5 0.8 collective-permute-done.2
  89.4 0.2 fusion.2
  89.6 0.9 collective-permute-start.6
  90.5 2.4 %collective-permute-start.5 = (bf16[64,1152]{1,0:T(8,128)(2,1)S(1)}, bf16[64,1152]{1,0:T(8,128)(2,1)S(1)}, u32[]{:S(2)}, u32[]{:S(2)}) collective-permute-start(bf16[64,1152]{1,0:T(8,128)(2,1)S(1)} %get-tuple-element.21), channel_id=1, source_target_pairs={{0,24},{1,25},{2,26},{3,27},{4,28},{5,29},{6,30},{7,31},{8,16},{9,... | collective-permute-start | bytes 442376 | tf_op jit(solution)/shard_map/ppermute | solution.py:278
  92.9 0.2 collective-permute-start.4
  93.1 4.7 %collective-permute-done.6 = bf16[64,1152]{1,0:T(8,128)(2,1)S(1)} collective-permute-done((bf16[64,1152]{1,0:T(8,128)(2,1)S(1)}, bf16[64,1152]{1,0:T(8,128)(2,1)S(1)}, u32[]{:S(2)}, u32[]{:S(2)}) %collective-permute-start.6) | collective-permute-done | bytes 147488 | tf_op jit(solution)/shard_map/ppermute | solution.py:278
  97.8 1.6 %collective-permute-done.5 = bf16[64,1152]{1,0:T(8,128)(2,1)S(1)} collective-permute-done((bf16[64,1152]{1,0:T(8,128)(2,1)S(1)}, bf16[64,1152]{1,0:T(8,128)(2,1)S(1)}, u32[]{:S(2)}, u32[]{:S(2)}) %collective-permute-start.5) | collective-permute-done | bytes 147488 | tf_op jit(solution)/shard_map/ppermute | solution.py:278
  99.4 0.0 collective-permute-done.4
  99.4 0.1 add_convert_fusion.1
  99.5 1.0 collective-permute-start.9
  100.4 2.0 %collective-permute-start.8 = (bf16[64,1152]{1,0:T(8,128)(2,1)S(1)}, bf16[64,1152]{1,0:T(8,128)(2,1)S(1)}, u32[]{:S(2)}, u32[]{:S(2)}) collective-permute-start(bf16[64,1152]{1,0:T(8,128)(2,1)S(1)} %add_convert_fusion.1), channel_id=1, source_target_pairs={{0,96},{1,97},{2,98},{3,99},{4,100},{5,101},{6,102},{7,103},{8,104... | collective-permute-start | bytes 442376 | tf_op jit(solution)/shard_map/ppermute | solution.py:278
  102.5 0.0 collective-permute-start.7
  102.5 0.0 copy-done.7
  102.5 6.2 %latent_gradient.1 = bf16[2048,1024]{1,0:T(8,128)(2,1)} custom-call(bf16[2048,1024]{1,0:T(8,128)(2,1)S(1)} %get-tuple-element.14.pre_ref, bf16[1024,1024]{1,0:T(8,128)(2,1)S(1)} %copy-done.7), custom_call_target="tpu_custom_call" | custom-call | flops 4294967296 | bytes 10485760 | tf_op jit(solution)/shard_map/latent_gradient/pallas_call | solution.py:255
  108.6 0.0 collective-permute-done.9
  108.6 0.0 collective-permute-done.8
  108.6 1.1 collective-permute-done.7
  109.7 0.1 convert_add_fusion.1
  109.8 0.6 slice_multiply_fusion.1
  110.4 0.7 slice_multiply_fusion
  (1 shorter events, 0.0 us)
Async XLA Ops:
  1.7 2.2 %copy-start = (bf16[1,2048,1024]{2,1,0:T(8,128)(2,1)S(1)}, bf16[1,2048,1024]{2,1,0:T(8,128)(2,1)}, u32[]{:S(2)}) copy-start(bf16[1,2048,1024]{2,1,0:T(8,128)(2,1)} %param.5) | copy-start | bytes 12582916
  3.9 1.6 %copy-start.6 = (bf16[1024,1024]{1,0:T(8,128)(2,1)S(1)}, bf16[1024,1024]{1,0:T(8,128)(2,1)}, u32[]{:S(2)}) copy-start(bf16[1024,1024]{1,0:T(8,128)(2,1)} %weight_ref.3) | copy-start | bytes 6291460
  14.7 1.9 %copy-start.8 = (bf16[2048,1024]{1,0:T(8,128)(2,1)}, bf16[2048,1024]{1,0:T(8,128)(2,1)S(1)}, u32[]{:S(2)}) copy-start(bf16[2048,1024]{1,0:T(8,128)(2,1)S(1)} %get-tuple-element.12.hidden_ref) | copy-start | bytes 12582916
  16.7 2.0 %copy-start.9 = (bf16[2048,1024]{1,0:T(8,128)(2,1)}, bf16[2048,1024]{1,0:T(8,128)(2,1)S(1)}, u32[]{:S(2)}) copy-start(bf16[2048,1024]{1,0:T(8,128)(2,1)S(1)} %get-tuple-element.11.slope_ref) | copy-start | bytes 12582916
  18.7 18.9 %copy-start.4 = (f32[100,2048]{1,0:T(8,128)S(1)}, f32[100,2048]{1,0:T(8,128)}, u32[]{:S(2)}) copy-start(f32[100,2048]{1,0:T(8,128)} %observed_ref.1) | copy-start | bytes 2457604
  18.7 18.9 %copy-start.5 = (f32[2048]{0:T(1024)S(1)}, f32[2048]{0:T(1024)}, u32[]{:S(2)}) copy-start(f32[2048]{0:T(1024)} %param.9) | copy-start | bytes 24580
  19.6 17.9 %all-to-all-start = ((f16[8,112,256]{2,1,0:T(8,128)(2,1)}), f16[8,112,256]{2,1,0:T(8,128)(2,1)S(1)}, u32[]{:S(2)}, u32[]{:S(2)}) async-start(f16[8,112,256]{2,1,0:T(8,128)(2,1)} %multiply_convert_fusion), calls=%async_computation | async-start | bytes 917504 | tf_op jit(solution)/shard_map/all_to_all | solution.py:318
  39.5 13.4 %all-to-all-start.1 = ((bf16[8,112,256]{2,1,0:T(8,128)(2,1)}), bf16[8,112,256]{2,1,0:T(8,128)(2,1)S(1)}, u32[]{:S(2)}, u32[]{:S(2)}) async-start(bf16[8,112,256]{2,1,0:T(8,128)(2,1)} %pairs.1), calls=%async_computation.1 | async-start | bytes 917504 | tf_op jit(solution)/shard_map/all_to_all | solution.py:320
  43.2 2.2 %copy-start.1 = (bf16[1,2048,1024]{2,1,0:T(8,128)(2,1)S(1)}, bf16[1,2048,1024]{2,1,0:T(8,128)(2,1)}, u32[]{:S(2)}) copy-start(bf16[1,2048,1024]{2,1,0:T(8,128)(2,1)} %param.5) | copy-start | bytes 12582916
  47.6 2.0 %copy-start.2 = (bf16[1024,2048]{1,0:T(8,128)(2,1)}, bf16[1024,2048]{1,0:T(8,128)(2,1)S(1)}, u32[]{:S(2)}) copy-start(bf16[1024,2048]{1,0:T(8,128)(2,1)S(1)} %turned.1.turned_ref) | copy-start | bytes 12582916
  52.9 2.2 %copy-start.3 = (bf16[1024,2048]{1,0:T(8,128)(2,1)S(1)}, bf16[1024,2048]{1,0:T(8,128)(2,1)}, u32[]{:S(2)}) copy-start(bf16[1024,2048]{1,0:T(8,128)(2,1)} %copy-done.2) | copy-start | bytes 12582916
  55.0 2.2 %copy-start.10 = (bf16[2048,1024]{1,0:T(8,128)(2,1)S(1)}, bf16[2048,1024]{1,0:T(8,128)(2,1)}, u32[]{:S(2)}) copy-start(bf16[2048,1024]{1,0:T(8,128)(2,1)} %copy-done.9) | copy-start | bytes 12582916
  67.6 2.9 %collective-permute-start = (bf16[512,1152]{1,0:T(8,128)(2,1)S(1)}, bf16[512,1152]{1,0:T(8,128)(2,1)S(1)}, u32[]{:S(2)}, u32[]{:S(2)}) collective-permute-start(bf16[512,1152]{1,0:T(8,128)(2,1)S(1)} %get-tuple-element.16), channel_id=1, source_target_pairs={{0,1},{1,0},{2,3},{3,2},{4,5},{5,4},{6,7},{7,6},{8,9},{9,8},{10,11... | collective-permute-start | bytes 3538952 | tf_op jit(solution)/shard_map/ppermute | solution.py:278
  70.8 31.6 %copy-start.7 = (bf16[1024,1024]{1,0:T(8,128)(2,1)S(1)}, bf16[1024,1024]{1,0:T(8,128)(2,1)}, u32[]{:S(2)}) copy-start(bf16[1024,1024]{1,0:T(8,128)(2,1)} %weight_ref.3) | copy-start | bytes 6291460
  71.0 11.8 %collective-permute-start.3 = (bf16[2,64,1152]{2,1,0:T(8,128)(2,1)S(1)}, bf16[2,64,1152]{2,1,0:T(8,128)(2,1)S(1)}, u32[]{:S(2)}, u32[]{:S(2)}) collective-permute-start(bf16[2,64,1152]{2,1,0:T(8,128)(2,1)S(1)} %bitcast.30), channel_id=1, source_target_pairs={{0,4},{1,5},{2,6},{3,7},{4,0},{5,1},{6,2},{7,3},{8,12},{9,13},{10,... | collective-permute-start | bytes 884744 | tf_op jit(solution)/shard_map/ppermute | solution.py:278
  74.9 13.6 %collective-permute-start.1 = (bf16[2,64,1152]{2,1,0:T(8,128)(2,1)S(1)}, bf16[2,64,1152]{2,1,0:T(8,128)(2,1)S(1)}, u32[]{:S(2)}, u32[]{:S(2)}) collective-permute-start(bf16[2,64,1152]{2,1,0:T(8,128)(2,1)S(1)} %bitcast.29), channel_id=1, source_target_pairs={{0,2},{1,3},{2,4},{3,5},{4,6},{5,7},{6,0},{7,1},{8,10},{9,11},{10,... | collective-permute-start | bytes 884744 | tf_op jit(solution)/shard_map/ppermute | solution.py:278
  76.0 13.4 %collective-permute-start.2 = (bf16[2,64,1152]{2,1,0:T(8,128)(2,1)S(1)}, bf16[2,64,1152]{2,1,0:T(8,128)(2,1)S(1)}, u32[]{:S(2)}, u32[]{:S(2)}) collective-permute-start(bf16[2,64,1152]{2,1,0:T(8,128)(2,1)S(1)} %bitcast.28), channel_id=1, source_target_pairs={{0,6},{1,7},{2,0},{3,1},{4,2},{5,3},{6,4},{7,5},{8,14},{9,15},{10,... | collective-permute-start | bytes 884744 | tf_op jit(solution)/shard_map/ppermute | solution.py:278
  89.6 8.2 %collective-permute-start.6 = (bf16[64,1152]{1,0:T(8,128)(2,1)S(1)}, bf16[64,1152]{1,0:T(8,128)(2,1)S(1)}, u32[]{:S(2)}, u32[]{:S(2)}) collective-permute-start(bf16[64,1152]{1,0:T(8,128)(2,1)S(1)} %get-tuple-element.22), channel_id=1, source_target_pairs={{0,16},{1,17},{2,18},{3,19},{4,20},{5,21},{6,22},{7,23},{8,24},{9,... | collective-permute-start | bytes 442376 | tf_op jit(solution)/shard_map/ppermute | solution.py:278
  90.5 8.9 %collective-permute-start.5 = (bf16[64,1152]{1,0:T(8,128)(2,1)S(1)}, bf16[64,1152]{1,0:T(8,128)(2,1)S(1)}, u32[]{:S(2)}, u32[]{:S(2)}) collective-permute-start(bf16[64,1152]{1,0:T(8,128)(2,1)S(1)} %get-tuple-element.21), channel_id=1, source_target_pairs={{0,24},{1,25},{2,26},{3,27},{4,28},{5,29},{6,30},{7,31},{8,16},{9,... | collective-permute-start | bytes 442376 | tf_op jit(solution)/shard_map/ppermute | solution.py:278
  92.9 6.5 %collective-permute-start.4 = (bf16[64,1152]{1,0:T(8,128)(2,1)S(1)}, bf16[64,1152]{1,0:T(8,128)(2,1)S(1)}, u32[]{:S(2)}, u32[]{:S(2)}) collective-permute-start(bf16[64,1152]{1,0:T(8,128)(2,1)S(1)} %get-tuple-element.21), channel_id=1, source_target_pairs={{0,8},{1,9},{2,10},{3,11},{4,12},{5,13},{6,14},{7,15},{8,0},{9,1},... | collective-permute-start | bytes 442376 | tf_op jit(solution)/shard_map/ppermute | solution.py:278
  99.5 9.2 %collective-permute-start.9 = (bf16[64,1152]{1,0:T(8,128)(2,1)S(1)}, bf16[64,1152]{1,0:T(8,128)(2,1)S(1)}, u32[]{:S(2)}, u32[]{:S(2)}) collective-permute-start(bf16[64,1152]{1,0:T(8,128)(2,1)S(1)} %add_convert_fusion.1), channel_id=1, source_target_pairs={{0,64},{1,65},{2,66},{3,67},{4,68},{5,69},{6,70},{7,71},{8,72},{9,... | collective-permute-start | bytes 442376 | tf_op jit(solution)/shard_map/ppermute | solution.py:278
  100.4 8.2 %collective-permute-start.8 = (bf16[64,1152]{1,0:T(8,128)(2,1)S(1)}, bf16[64,1152]{1,0:T(8,128)(2,1)S(1)}, u32[]{:S(2)}, u32[]{:S(2)}) collective-permute-start(bf16[64,1152]{1,0:T(8,128)(2,1)S(1)} %add_convert_fusion.1), channel_id=1, source_target_pairs={{0,96},{1,97},{2,98},{3,99},{4,100},{5,101},{6,102},{7,103},{8,104... | collective-permute-start | bytes 442376 | tf_op jit(solution)/shard_map/ppermute | solution.py:278
  102.5 7.3 %collective-permute-start.7 = (bf16[64,1152]{1,0:T(8,128)(2,1)S(1)}, bf16[64,1152]{1,0:T(8,128)(2,1)S(1)}, u32[]{:S(2)}, u32[]{:S(2)}) collective-permute-start(bf16[64,1152]{1,0:T(8,128)(2,1)S(1)} %add_convert_fusion.1), channel_id=1, source_target_pairs={{0,32},{1,33},{2,34},{3,35},{4,36},{5,37},{6,38},{7,39},{8,40},{9,... | collective-permute-start | bytes 442376 | tf_op jit(solution)/shard_map/ppermute | solution.py:278

commit v3 on v2

v3 whole, which is shorter than its diff:
```python
import functools
import math

import jax
import jax.numpy as jnp
from jax import lax
from jax.experimental import pallas as pl
from jax.experimental.pallas import tpu as pltpu
from jax.sharding import PartitionSpec as P

smooth_sq = 0.0025
bf16 = jnp.bfloat16
f16 = jnp.float16
f32 = jnp.float32

NT = (((1,), (1,)), ((), ()))
WIDE = 128
TALL = 112
SHARE = 256
ROWS = 512
COLS = 256

vmem = pl.BlockSpec(memory_space=pltpu.VMEM)
smem = pl.BlockSpec(memory_space=pltpu.SMEM)
anywhere = pl.BlockSpec(memory_space=pltpu.HBM)


def params(mib):
    return pltpu.CompilerParams(vmem_limit_bytes=mib * 1024 * 1024)


def cost(flops, nbytes, trans=0):
    return pl.CostEstimate(flops=flops, bytes_accessed=nbytes, transcendentals=trans)


CHUNKS = (512, 512, 1024)
FCOLS = 512


def forward_kernel(
    latent_ref, weight_ref, out_weight_ref, forecast_ref, hidden_ref, slope_ref, latent_copy, weight_copy, padded_ref, out_weight_copy, latent_sems, weight_sems, out_weight_sem
):
    nodes, width = latent_ref.shape
    variables = out_weight_ref.shape[0]
    out_weight_load = pltpu.make_async_copy(out_weight_ref, out_weight_copy, out_weight_sem)
    spans = []
    for size in CHUNKS:
        begin = spans[-1].stop if spans else 0
        spans.append(slice(begin, begin + size))
    weight_loads = [
        pltpu.make_async_copy(
            weight_ref.at[:, pl.ds(start, FCOLS)], weight_copy.at[:, pl.ds(start, FCOLS)], weight_sems.at[start // FCOLS]
        )
        for start in range(0, width, FCOLS)
    ]
    latent_loads = [
        pltpu.make_async_copy(
            latent_ref.at[pl.ds(rows.start, rows.stop - rows.start)],
            latent_copy.at[pl.ds(rows.start, rows.stop - rows.start)],
            latent_sems.at[index],
        )
        for index, rows in enumerate(spans)
    ]
    weight_loads[0].start()
    latent_loads[0].start()
    for load in weight_loads[1:] + latent_loads[1:]:
        load.start()
    out_weight_load.start()
    out_weight_load.wait()
    turned_weight = jnp.concatenate(
        [out_weight_copy[...], jnp.zeros((WIDE - variables, width), bf16)], axis=0
    )
    padded_ref[...] = turned_weight.T

    for index, rows in enumerate(spans):
        latent_loads[index].wait()
        for start in range(0, width, FCOLS):
            columns = slice(start, start + FCOLS)
            if index == 0:
                weight_loads[start // FCOLS].wait()
            pre = jnp.dot(latent_copy[rows, :], weight_copy[:, columns], preferred_element_type=f32)
            sig = 0.5 * jnp.tanh(0.5 * pre) + 0.5
            hidden = pre * sig
            hidden_ref[rows, columns] = hidden.astype(bf16)
            slope_ref[rows, columns] = (sig + hidden * (1.0 - sig)).astype(bf16)
        for share in range(rows.start // SHARE, rows.stop // SHARE):
            forecast_ref[share] = lax.dot_general(
                turned_weight[:TALL],
                hidden_ref[share * SHARE : (share + 1) * SHARE, :],
                NT,
                preferred_element_type=f32,
            )


def forward(latent, weight, out_weight):
    nodes, width = latent.shape
    latent = pltpu.with_memory_space_constraint(latent, pltpu.HBM)
    weight = pltpu.with_memory_space_constraint(weight, pltpu.HBM)
    out_weight = pltpu.with_memory_space_constraint(out_weight, pltpu.HBM)
    return pl.pallas_call(
        forward_kernel,
        in_specs=[anywhere] * 3,
        out_specs=[vmem] * 6,
        out_shape=[
            jax.ShapeDtypeStruct((nodes // SHARE, TALL, SHARE), f32),
            jax.ShapeDtypeStruct((nodes, width), bf16),
            jax.ShapeDtypeStruct((nodes, width), bf16),
            jax.ShapeDtypeStruct((nodes, width), bf16),
            jax.ShapeDtypeStruct((width, width), bf16),
            jax.ShapeDtypeStruct((width, WIDE), bf16),
        ],
        scratch_shapes=[
            pltpu.VMEM(out_weight.shape, bf16),
            pltpu.SemaphoreType.DMA((len(CHUNKS),)),
            pltpu.SemaphoreType.DMA((width // FCOLS,)),
            pltpu.SemaphoreType.DMA,
        ],
        compiler_params=params(12),
        cost_estimate=cost(2 * nodes * width * (width + WIDE), 20 << 20),
        name="forward",
    )(latent, weight, out_weight)


def slope_function(diff):
    return diff * lax.rsqrt(diff * diff + smooth_sq)


def pair_kernel(place_ref, blocks_ref, observed_ref, area_ref, low_ref, here_ref, weight_ref, sems):
    members = blocks_ref.shape[0]
    variables = observed_ref.shape[0]
    at = pl.multiple_of(place_ref[0] * SHARE, SHARE)
    loads = [
        pltpu.make_async_copy(observed_ref.at[:, pl.ds(at, SHARE)], here_ref, sems.at[0]),
        pltpu.make_async_copy(area_ref.at[:, pl.ds(at, SHARE)], weight_ref, sems.at[1]),
    ]
    for load in loads:
        load.start()
    for load in loads:
        load.wait()
    area = weight_ref[...]
    for start in range(0, TALL, 16):
        rows = slice(start, start + 16)
        real = min(16, variables - start)
        observed = here_ref[start : start + real, :]
        if real < 16:
            observed = jnp.concatenate([observed, jnp.zeros((16 - real, SHARE), f32)], axis=0)
        values = [blocks_ref[a, rows, :] for a in range(members)]
        totals = [0.0] * members
        for a in range(members):
            for b in range(a + 1, members):
                slope = slope_function(values[a] - values[b])
                totals[a] = totals[a] + slope
                totals[b] = totals[b] - slope
        for a in range(members):
            field = area * (slope_function(values[a] - observed) - totals[a] * (1.0 / (members - 1)))
            low_ref[a, rows, :] = field.astype(bf16)


def pairs(place, blocks, observed, area):
    members = blocks.shape[0]
    variables = observed.shape[0]
    return pl.pallas_call(
        pair_kernel,
        in_specs=[smem, vmem, anywhere, anywhere],
        out_specs=vmem,
        out_shape=jax.ShapeDtypeStruct((members, TALL, SHARE), bf16),
        scratch_shapes=[
            pltpu.VMEM((variables, SHARE), f32),
            pltpu.VMEM((1, SHARE), f32),
            pltpu.SemaphoreType.DMA((2,)),
        ],
        compiler_params=params(8),
        cost_estimate=cost(4 << 20, 2 << 20),
        name="pairs",
    )(place, blocks, observed, area)


def turn_kernel(order_ref, latent_ref, turned_ref):
    nodes, width = latent_ref.shape
    half = width // 2
    core = order_ref[8]
    for group in range(8):
        at = order_ref[group] * 64
        first = pl.multiple_of(core * half + at, 64)
        second = pl.multiple_of((1 - core) * half + at, 64)
        for row in range(0, nodes, ROWS):
            columns = slice(row, row + ROWS)
            block = latent_ref[columns, group * 128 : (group + 1) * 128].T
            turned_ref[pl.ds(first, 64), columns] = block[:64]
            turned_ref[pl.ds(second, 64), columns] = block[64:]


def turned(order, latent):
    nodes, width = latent.shape
    return pl.pallas_call(
        turn_kernel,
        in_specs=[smem, vmem],
        out_specs=vmem,
        out_shape=jax.ShapeDtypeStruct((width, nodes), bf16),
        compiler_params=params(8),
        cost_estimate=cost(0, 8 << 20),
        name="turned",
    )(order, latent)


def first_product(turned_ref, slope_ref, padded_ref, turn_ref, pre_ref, send_ref, keep_ref, begin):
    nodes, span = pre_ref.shape
    half = turned_ref.shape[0] // 2
    for column in range(0, span, COLS):
        columns = slice(column, column + COLS)
        source = slice(begin + column, begin + column + COLS)
        for start in range(0, nodes, ROWS):
            rows = slice(start, start + ROWS)
            grad_hidden = lax.dot_general(turn_ref[rows, :], padded_ref[source, :], NT, preferred_element_type=f32)
            pre_ref[rows, columns] = (grad_hidden * slope_ref[rows, source].astype(f32)).astype(bf16)
        for out_ref, base in ((send_ref, 0), (keep_ref, half)):
            part = jnp.dot(turned_ref[base : base + half, :], pre_ref[:, columns], preferred_element_type=f32)
            out_ref[:, columns] = part.astype(bf16)


def backward_a_kernel(low_ref, turned_ref, slope_ref, padded_ref, pre_ref, send_ref, keep_ref, turn_ref, flat_ref):
    for share in range(low_ref.shape[0]):
        columns = slice(share * SHARE, (share + 1) * SHARE)
        low = jnp.concatenate([low_ref[share], jnp.zeros((WIDE - TALL, SHARE), bf16)], axis=0)
        flat_ref[:, columns] = low
        turn_ref[columns, :] = low.T
    first_product(turned_ref, slope_ref, padded_ref, turn_ref, pre_ref, send_ref, keep_ref, 0)


def backward_b_kernel(
    order_ref, turned_ref, slope_ref, hidden_ref, padded_ref, turn_ref, flat_ref, pre_ref, send_ref, keep_ref, second_ref
):
    width = hidden_ref.shape[1]
    span = pre_ref.shape[1]
    first_product(turned_ref, slope_ref, padded_ref, turn_ref, pre_ref, send_ref, keep_ref, width - span)
    for column in range(0, width, COLS):
        columns = slice(column, column + COLS)
        second_ref[columns, :] = jnp.dot(flat_ref[...], hidden_ref[:, columns], preferred_element_type=f32).T.astype(bf16)
    core = order_ref[8]
    for group in range(8):
        at = pl.multiple_of(order_ref[group] * 64, 64)
        mine = pl.multiple_of(group * 128 + 64 * (1 - core), 64)
        other = pl.multiple_of(group * 128 + 64 * core, 64)
        keep_ref[pl.ds(at, 64), span:] = second_ref[pl.ds(mine, 64), :]
        send_ref[pl.ds(at, 64), span:] = second_ref[pl.ds(other, 64), :]


def backward_a(low, turned_latent, slope, padded):
    nodes, width = slope.shape
    half = width // 2
    return pl.pallas_call(
        backward_a_kernel,
        in_specs=[vmem] * 4,
        out_specs=[vmem] * 5,
        out_shape=[
            jax.ShapeDtypeStruct((nodes, half), bf16),
            jax.ShapeDtypeStruct((half, half), bf16),
            jax.ShapeDtypeStruct((half, half), bf16),
            jax.ShapeDtypeStruct((nodes, WIDE), bf16),
            jax.ShapeDtypeStruct((WIDE, nodes), bf16),
        ],
        compiler_params=params(12),
        cost_estimate=cost(nodes * width * (width + WIDE), 8 << 20),
        name="backward_a",
    )(low, turned_latent, slope, padded)


def backward_b(order, turned_latent, slope, hidden, padded, turn, flat):
    nodes, width = slope.shape
    half = width // 2
    return pl.pallas_call(
        backward_b_kernel,
        in_specs=[smem] + [vmem] * 6,
        out_specs=[vmem] * 3,
        out_shape=[
            jax.ShapeDtypeStruct((nodes, half), bf16),
            jax.ShapeDtypeStruct((half, half + WIDE), bf16),
            jax.ShapeDtypeStruct((half, half + WIDE), bf16),
        ],
        scratch_shapes=[pltpu.VMEM((width, WIDE), bf16)],
        compiler_params=params(12),
        cost_estimate=cost(nodes * width * (width + 3 * WIDE), 8 << 20),
        name="backward_b",
    )(order, turned_latent, slope, hidden, padded, turn, flat)


def latent_kernel(left_ref, right_ref, weight_ref, out_ref, result_ref, sems):
    nodes, half = left_ref.shape
    width = weight_ref.shape[1]
    stores = []
    for row in range(0, nodes, ROWS):
        rows = slice(row, row + ROWS)
        for start in range(0, width, COLS):
            columns = slice(start, start + COLS)
            left = lax.dot_general(left_ref[rows, :], weight_ref[columns, :half], NT, preferred_element_type=f32)
            right = lax.dot_general(right_ref[rows, :], weight_ref[columns, half:], NT, preferred_element_type=f32)
            result_ref[rows, columns] = (left + right).astype(bf16)
        store = pltpu.make_async_copy(
            result_ref.at[pl.ds(row, ROWS)], out_ref.at[pl.ds(row, ROWS)], sems.at[row // ROWS]
        )
        store.start()
        stores.append(store)
    for store in stores:
        store.wait()


def latent_gradient(left, right, weight):
    nodes = left.shape[0]
    width = weight.shape[1]
    return pl.pallas_call(
        latent_kernel,
        in_specs=[vmem] * 3,
        out_specs=anywhere,
        out_shape=jax.ShapeDtypeStruct((nodes, width), bf16),
        scratch_shapes=[pltpu.VMEM((nodes, width), bf16), pltpu.SemaphoreType.DMA((nodes // ROWS,))],
        compiler_params=params(12),
        cost_estimate=cost(2 * nodes * width * width, 10 << 20),
        name="latent_gradient",
    )(left, right, weight)


def moved(value, move):
    moves = []
    for member in range(8):
        for grid in range(16):
            y, x_hi, x_lo, z, core = member // 2, member % 2, grid // 8, (grid // 2) % 4, grid % 2
            y, x, z, core = move(y, x_hi * 2 + x_lo, z, core)
            target = (y * 2 + x // 2) * 16 + ((x % 2) * 4 + z) * 2 + core
            moves.append((member * 16 + grid, target))
    return lax.ppermute(value, ("member", "grid"), moves)


def summed(own, others):
    total = own.astype(f32)
    for other in others:
        total = total + other.astype(f32)
    return total


def reduced(send, keep):
    columns = send.shape[1]
    got = moved(send, lambda y, x, z, c: (y, x, z, 1 - c))
    blocks = summed(keep, [got]).astype(bf16).reshape(4, 2, 64, columns)
    got = [moved(blocks[k], lambda y, x, z, c, k=k: (y, x, (z + k) % 4, c)) for k in (1, 3, 2)]
    blocks = summed(blocks[0], got).astype(bf16)
    got = [
        moved(blocks[0] if k == 2 else blocks[1], lambda y, x, z, c, k=k: (y, x ^ k, z, c))
        for k in (1, 3, 2)
    ]
    block = summed(blocks[0], got).astype(bf16)
    got = [moved(block, lambda y, x, z, c, k=k: ((y + k) % 4, x, z, c)) for k in (1, 3, 2)]
    return summed(block, got)


def body(latents, hidden_weight, output_weight, observed, node_area_weight):
    latent = latents[0]
    members = lax.axis_size("member")
    groups = lax.axis_size("grid")
    nodes, width = latent.shape
    variables = output_weight.shape[1]
    member = lax.axis_index("member")
    grid = lax.axis_index("grid")
    x_lo, z, core = grid // 8, (grid // 2) % 4, grid % 2
    order = jnp.stack(
        [((g % 4 - z) % 4) * 2 + jnp.abs(g // 4 - x_lo) for g in range(8)] + [1 - core]
    ).astype(jnp.int32)
    place = member.astype(jnp.int32).reshape(1)

    forecast, hidden, slope, latent_copy, weight_copy, padded = forward(latent, hidden_weight, output_weight.T)
    blocks = lax.all_to_all((0.25 * forecast).astype(f16), "member", 0, 0, tiled=True)
    low = pairs(place, 4.0 * blocks.astype(f32), observed, node_area_weight.reshape(1, nodes))
    low = lax.all_to_all(low, "member", 0, 0, tiled=True)
    turned_latent = turned(order, latent_copy)
    pre_a, send_a, keep_a, turn, flat = backward_a(low, turned_latent, slope, padded)
    pre_b, send_b, keep_b = backward_b(order, turned_latent, slope, hidden, padded, turn, flat)
    total_a = reduced(send_a, keep_a)
    total_b = reduced(send_b, keep_b)
    grad_latent = latent_gradient(pre_a, pre_b, weight_copy)
    factor = 1.0 / math.sqrt(members * nodes * groups)
    half = width // 2
    first = jnp.concatenate([total_a, total_b[:, :half]], axis=1)
    return (grad_latent[None], first * factor, total_b[:, half : half + variables] * factor)


def solution(mesh):
    in_specs = (P("member", "grid", None), P(), P(), P(None, "grid"), P("grid"))
    out_specs = (P("member", "grid", None), P("grid", None), P("grid", None))
    return jax.shard_map(body, mesh=mesh, in_specs=in_specs, out_specs=out_specs, check_vma=False)
```

time: 112 us -> 111 us (level)
  starting transfers between devices: 24.3 us -> 36.8 us
  waiting for transfers between devices: 35.5 us -> 24.5 us
  Pallas kernels: 29.9 us -> 26.9 us
    ppermute x10 -> x20, starting transfers between devices: 13.8 us -> 26.3 us  [moved(): return lax.ppermute(value, ('member', 'grid'), moves)]
    ppermute x10 -> x20, waiting for transfers between devices: 21.4 us -> 9.81 us  [moved(): return lax.ppermute(value, ('member', 'grid'), moves)]
    pallas_call x5 -> x6, Pallas kernels: 29.9 us -> 26.9 us  [the longest x1 10.7 us: forward(): pl.pallas_call(forward_kernel, in_specs=[anywhere] * 3, out_specs=[vmem]...]
    unnamed x23 -> x28, local copies, waits for them, and re-layouts: 17.4 us -> 18.3 us
  transfers between devices with their start and end apart: 12 -> 22, of which waited for: 9 -> 10; matrix products, arithmetic and copies ran while one was open for 0% -> 1% of each run, Pallas kernels for 8% -> 10%
where the time goes in v3:
time: 111 us
  starting transfers between devices  36.8 us (33%)
  Pallas kernels  26.9 us (24%)
  waiting for transfers between devices  24.5 us (22%)
  local copies, waits for them, and re-layouts  18.5 us (17%)
  other arithmetic  2.9 us (3%)
    ppermute x20, starting transfers between devices, moved(): return lax.ppermute(value, ('member', 'grid'), moves)  26.3 us
    unnamed x28, local copies, waits for them, and re-layouts  18.3 us
    all_to_all x1, waiting for transfers between devices, body(): lax.all_to_all((0.25 * forecast).astype(f16), 'member', 0, 0, tiled=True)  10.9 us
    pallas_call x1, Pallas kernels, forward(): pl.pallas_call(forward_kernel, in_specs=[anywhere] * 3, out_specs=[vmem]...  10.7 us
    ppermute x20, waiting for transfers between devices, moved(): return lax.ppermute(value, ('member', 'grid'), moves)  9.81 us
    all_to_all x1, starting transfers between devices, body(): lax.all_to_all((0.25 * forecast).astype(f16), 'member', 0, 0, tiled=True)  7.01 us
    pallas_call x1, Pallas kernels, latent_gradient(): pl.pallas_call(latent_kernel, in_specs=[vmem] * 3, out_specs=anywhere, ou...  5.65 us
    pallas_call x1, Pallas kernels, backward_b(): pl.pallas_call(backward_b_kernel, in_specs=[smem] + [vmem] * 6, out_specs...  4.07 us
  transfers between devices with their start and end apart: 22, of which 10 were waited for; matrix products, arithmetic and copies ran while one was open for 1% of the time, Pallas kernels for 10%

profile of v3, /device:TPU:0, one launch (start us, length us, event | category | flops | bytes accessed | tf_op | source)
XLA Modules:
  0.0 110.6 jit_solution(7190510155969251689)
XLA Ops:
  0.6 10.7 %forward.1 = (f32[8,112,256]{2,1,0:T(8,128)S(1)}, bf16[2048,1024]{1,0:T(8,128)(2,1)S(1)}, bf16[2048,1024]{1,0:T(8,128)(2,1)S(1)}, bf16[2048,1024]{1,0:T(8,128)(2...) custom-call(bf16[2048,1024]{1,0:T(8,128)(2,1)} %bitcast.45, bf16[1024,1024]{1,0:T(8,128)(2,1)} %weight_ref.1, ...), custom_call_target="tpu_custom_call" | custom-call | flops 4831838208 | bytes 20971520 | tf_op jit(solution)/shard_map/forward/pallas_call | solution.py:100
  11.4 2.0 %copy-done.3 = bf16[2048,1024]{1,0:T(8,128)(2,1)} copy-done((bf16[2048,1024]{1,0:T(8,128)(2,1)}, bf16[2048,1024]{1,0:T(8,128)(2,1)S(1)}, u32[]{:S(2)}) %copy-start.3) | copy-done | bytes 4194328
  13.3 2.0 %copy-done.6 = bf16[2048,1024]{1,0:T(8,128)(2,1)} copy-done((bf16[2048,1024]{1,0:T(8,128)(2,1)}, bf16[2048,1024]{1,0:T(8,128)(2,1)S(1)}, u32[]{:S(2)}) %copy-start.6) | copy-done | bytes 4194328
  15.3 2.0 %copy-done.8 = bf16[2048,1024]{1,0:T(8,128)(2,1)} copy-done((bf16[2048,1024]{1,0:T(8,128)(2,1)}, bf16[2048,1024]{1,0:T(8,128)(2,1)S(1)}, u32[]{:S(2)}) %copy-start.8) | copy-done | bytes 4194328
  17.4 1.3 %copy-done.12 = bf16[1024,1024]{1,0:T(8,128)(2,1)} copy-done((bf16[1024,1024]{1,0:T(8,128)(2,1)}, bf16[1024,1024]{1,0:T(8,128)(2,1)S(1)}, u32[]{:S(2)}) %copy-start.12) | copy-done | bytes 2097176
  18.7 0.9 multiply_convert_fusion
  19.6 7.0 %all-to-all-start = ((f16[8,112,256]{2,1,0:T(8,128)(2,1)}), f16[8,112,256]{2,1,0:T(8,128)(2,1)S(1)}, u32[]{:S(2)}, u32[]{:S(2)}) async-start(f16[8,112,256]{2,1,0:T(8,128)(2,1)} %multiply_convert_fusion), calls=%async_computation | async-start | bytes 917504 | tf_op jit(solution)/shard_map/all_to_all | solution.py:370
  26.6 10.9 %all-to-all-done = f16[8,112,256]{2,1,0:T(8,128)(2,1)S(1)} async-done(((f16[8,112,256]{2,1,0:T(8,128)(2,1)}), f16[8,112,256]{2,1,0:T(8,128)(2,1)S(1)}, u32[]{:S(2)}, u32[]{:S(2)}) %all-to-all-start) | async-done | bytes 458784 | tf_op jit(solution)/shard_map/all_to_all | solution.py:370
  37.5 0.1 convert_multiply_fusion.blocks_ref
  37.6 1.8 %pairs.1 = bf16[8,112,256]{2,1,0:T(8,128)(2,1)} custom-call(s32[1]{0:T(128)} %bitcast.place_ref, f32[8,112,256]{2,1,0:T(8,128)S(1)} %convert_multiply_fusion.blocks_ref, f32[100,2048]{1,0:T(8,128)S(1)} %copy-done.10, f32[1,2048]{1,0:T(1,128)S(1)} %bitcast.36), custom_call_target="tpu_custom_call" | custom-call | flops 4194304 | bytes 2097152 | tf_op jit(solution)/shard_map/pairs/pallas_call | solution.py:162
  39.4 3.5 %all-to-all-start.1 = ((bf16[8,112,256]{2,1,0:T(8,128)(2,1)}), bf16[8,112,256]{2,1,0:T(8,128)(2,1)S(1)}, u32[]{:S(2)}, u32[]{:S(2)}) async-start(bf16[8,112,256]{2,1,0:T(8,128)(2,1)} %pairs.1), calls=%async_computation.1 | async-start | bytes 917504 | tf_op jit(solution)/shard_map/all_to_all | solution.py:372
  43.0 0.1 stack.39.order_ref
  43.1 2.2 %copy-done.7 = bf16[2048,1024]{1,0:T(8,128)(2,1)S(1)} copy-done((bf16[2048,1024]{1,0:T(8,128)(2,1)S(1)}, bf16[2048,1024]{1,0:T(8,128)(2,1)}, u32[]{:S(2)}) %copy-start.7) | copy-done | bytes 4194328
  45.3 1.7 %turned.1.turned_ref = bf16[1024,2048]{1,0:T(8,128)(2,1)S(1)} custom-call(s32[9]{0:T(128)S(1)} %stack.39.order_ref, bf16[2048,1024]{1,0:T(8,128)(2,1)S(1)} %copy-done.7), custom_call_target="tpu_custom_call" | custom-call | bytes 8388608 | tf_op jit(solution)/shard_map/turned/pallas_call | solution.py:195
  46.9 0.0 copy-start
  47.0 2.0 %copy-done = bf16[1024,2048]{1,0:T(8,128)(2,1)} copy-done((bf16[1024,2048]{1,0:T(8,128)(2,1)}, bf16[1024,2048]{1,0:T(8,128)(2,1)S(1)}, u32[]{:S(2)}) %copy-start) | copy-done | bytes 4194328
  49.0 3.8 %all-to-all-done.1.low_ref = bf16[8,112,256]{2,1,0:T(8,128)(2,1)S(1)} async-done(((bf16[8,112,256]{2,1,0:T(8,128)(2,1)}), bf16[8,112,256]{2,1,0:T(8,128)(2,1)S(1)}, u32[]{:S(2)}, u32[]{:S(2)}) %all-to-all-start.1) | async-done | bytes 458784 | tf_op jit(solution)/shard_map/all_to_all | solution.py:372
  52.8 2.2 %copy-done.1 = bf16[1024,2048]{1,0:T(8,128)(2,1)S(1)} copy-done((bf16[1024,2048]{1,0:T(8,128)(2,1)S(1)}, bf16[1024,2048]{1,0:T(8,128)(2,1)}, u32[]{:S(2)}) %copy-start.1) | copy-done | bytes 4194328
  55.0 2.2 %copy-done.4 = bf16[2048,1024]{1,0:T(8,128)(2,1)S(1)} copy-done((bf16[2048,1024]{1,0:T(8,128)(2,1)S(1)}, bf16[2048,1024]{1,0:T(8,128)(2,1)}, u32[]{:S(2)}) %copy-start.4) | copy-done | bytes 4194328
  57.1 3.0 %backward_a.1 = (bf16[2048,512]{1,0:T(8,128)(2,1)S(1)}, bf16[512,512]{1,0:T(8,128)(2,1)S(1)}, bf16[512,512]{1,0:T(8,128)(2,1)S(1)}, bf16[2048,128]{1,0:T(8,128)(2,1)S(1)}, bf16[128,2048]{1,0:T(8,128)(2,1)S(1)}) custom-call(bf16[8,112,256]{2,1,0:T(8,128)(2,1)S(1)} %all-to-all-done.1.low_ref, bf16[1024,2048]{1,0:T(8,128)(2,1)S(1)} %copy-done.1, ...), custom_call_target="tpu_custom_call" | custom-call | flops 2415919104 | bytes 8388608 | tf_op jit(solution)/shard_map/backward_a/pallas_call | solution.py:251
  60.1 0.3 collective-permute-start
  60.4 0.2 copy-done.5
  60.6 2.2 %copy-done.9 = bf16[2048,1024]{1,0:T(8,128)(2,1)S(1)} copy-done((bf16[2048,1024]{1,0:T(8,128)(2,1)S(1)}, bf16[2048,1024]{1,0:T(8,128)(2,1)}, u32[]{:S(2)}) %copy-start.9) | copy-done | bytes 4194328
  62.8 4.1 %backward_b.1 = (bf16[2048,512]{1,0:T(8,128)(2,1)S(1)}, bf16[512,640]{1,0:T(8,128)(2,1)S(1)}, bf16[512,640]{1,0:T(8,128)(2,1)S(1)}) custom-call(s32[9]{0:T(128)S(1)} %stack.39.order_ref, bf16[1024,2048]{1,0:T(8,128)(2,1)S(1)} %copy-done.2, bf16[2048,1024]{1,0:T(8,128)(2,1)S(1)} %copy-done.5, bf16[2048,1024]{1,0:T(8,128)(2,1)S(1)} %copy-done.9, ...), custom_call_target="tpu_custom_call" | custom-call | flops 2952790016 | bytes 8388608 | tf_op jit(solution)/shard_map/backward_b/pallas_call | solution.py:271
  66.9 0.4 collective-permute-start.10
  67.2 5.7 %latent_gradient.1 = bf16[2048,1024]{1,0:T(8,128)(2,1)} custom-call(bf16[2048,512]{1,0:T(8,128)(2,1)S(1)} %get-tuple-element.21.left_ref, bf16[2048,512]{1,0:T(8,128)(2,1)S(1)} %get-tuple-element.25.right_ref, bf16[1024,1024]{1,0:T(8,128)(2,1)S(1)} %copy-done.13), custom_call_target="tpu_custom_call" | custom-call | flops 4294967296 | bytes 10485760 | tf_op jit(solution)/shard_map/latent_gradient/pallas_call | solution.py:310
  72.9 0.0 collective-permute-done
  72.9 0.1 add_convert_fusion.1
  73.1 2.0 %collective-permute-start.1 = (bf16[2,64,512]{2,1,0:T(8,128)(2,1)S(1)}, bf16[2,64,512]{2,1,0:T(8,128)(2,1)S(1)}, u32[]{:S(2)}, u32[]{:S(2)}) collective-permute-start(bf16[2,64,512]{2,1,0:T(8,128)(2,1)S(1)} %bitcast.44), channel_id=1, source_target_pairs={{0,2},{1,3},{2,4},{3,5},{4,6},{5,7},{6,0},{7,1},{8,10},{9,11},{10,... | collective-permute-start | bytes 393224 | tf_op jit(solution)/shard_map/ppermute | solution.py:330
  75.1 2.2 %collective-permute-start.2 = (bf16[2,64,512]{2,1,0:T(8,128)(2,1)S(1)}, bf16[2,64,512]{2,1,0:T(8,128)(2,1)S(1)}, u32[]{:S(2)}, u32[]{:S(2)}) collective-permute-start(bf16[2,64,512]{2,1,0:T(8,128)(2,1)S(1)} %bitcast.43), channel_id=1, source_target_pairs={{0,6},{1,7},{2,0},{3,1},{4,2},{5,3},{6,4},{7,5},{8,14},{9,15},{10,... | collective-permute-start | bytes 393224 | tf_op jit(solution)/shard_map/ppermute | solution.py:330
  77.3 1.8 %collective-permute-start.3 = (bf16[2,64,512]{2,1,0:T(8,128)(2,1)S(1)}, bf16[2,64,512]{2,1,0:T(8,128)(2,1)S(1)}, u32[]{:S(2)}, u32[]{:S(2)}) collective-permute-start(bf16[2,64,512]{2,1,0:T(8,128)(2,1)S(1)} %bitcast.42), channel_id=1, source_target_pairs={{0,4},{1,5},{2,6},{3,7},{4,0},{5,1},{6,2},{7,3},{8,12},{9,13},{10,... | collective-permute-start | bytes 393224 | tf_op jit(solution)/shard_map/ppermute | solution.py:330
  79.1 0.0 collective-permute-done.10
  79.1 0.2 add_convert_fusion
  79.2 0.1 fusion.6
  79.3 1.1 collective-permute-start.11
  80.4 2.2 %collective-permute-start.12 = (bf16[2,64,640]{2,1,0:T(8,128)(2,1)S(1)}, bf16[2,64,640]{2,1,0:T(8,128)(2,1)S(1)}, u32[]{:S(2)}, u32[]{:S(2)}) collective-permute-start(bf16[2,64,640]{2,1,0:T(8,128)(2,1)S(1)} %bitcast.40), channel_id=1, source_target_pairs={{0,6},{1,7},{2,0},{3,1},{4,2},{5,3},{6,4},{7,5},{8,14},{9,15},{10,... | collective-permute-start | bytes 491528 | tf_op jit(solution)/shard_map/ppermute | solution.py:330
  82.6 0.0 collective-permute-done.1
  82.6 0.5 collective-permute-start.13
  83.2 0.4 collective-permute-done.2
  83.6 2.3 %collective-permute-done.3 = bf16[2,64,512]{2,1,0:T(8,128)(2,1)S(1)} collective-permute-done((bf16[2,64,512]{2,1,0:T(8,128)(2,1)S(1)}, bf16[2,64,512]{2,1,0:T(8,128)(2,1)S(1)}, u32[]{:S(2)}, u32[]{:S(2)}) %collective-permute-start.3) | collective-permute-done | bytes 131104 | tf_op jit(solution)/shard_map/ppermute | solution.py:330
  85.8 0.1 fusion.5
  85.9 0.7 collective-permute-start.4
  86.6 0.8 collective-permute-start.5
  87.4 1.4 %collective-permute-done.11 = bf16[2,64,640]{2,1,0:T(8,128)(2,1)S(1)} collective-permute-done((bf16[2,64,640]{2,1,0:T(8,128)(2,1)S(1)}, bf16[2,64,640]{2,1,0:T(8,128)(2,1)S(1)}, u32[]{:S(2)}, u32[]{:S(2)}) %collective-permute-start.11) | collective-permute-done | bytes 163872 | tf_op jit(solution)/shard_map/ppermute | solution.py:330
  88.9 1.2 %collective-permute-start.6 = (bf16[64,512]{1,0:T(8,128)(2,1)S(1)}, bf16[64,512]{1,0:T(8,128)(2,1)S(1)}, u32[]{:S(2)}, u32[]{:S(2)}) collective-permute-start(bf16[64,512]{1,0:T(8,128)(2,1)S(1)} %get-tuple-element.42), channel_id=1, source_target_pairs={{0,16},{1,17},{2,18},{3,19},{4,20},{5,21},{6,22},{7,23},{8,24},{9,... | collective-permute-start | bytes 196616 | tf_op jit(solution)/shard_map/ppermute | solution.py:330
  90.1 0.2 collective-permute-done.12
  90.3 1.8 %collective-permute-done.13 = bf16[2,64,640]{2,1,0:T(8,128)(2,1)S(1)} collective-permute-done((bf16[2,64,640]{2,1,0:T(8,128)(2,1)S(1)}, bf16[2,64,640]{2,1,0:T(8,128)(2,1)S(1)}, u32[]{:S(2)}, u32[]{:S(2)}) %collective-permute-start.13) | collective-permute-done | bytes 163872 | tf_op jit(solution)/shard_map/ppermute | solution.py:330
  92.2 0.1 fusion.2
  92.3 0.7 collective-permute-start.14
  93.0 0.8 collective-permute-start.15
  93.8 0.0 collective-permute-done.4
  93.8 2.7 %collective-permute-start.16 = (bf16[64,640]{1,0:T(8,128)(2,1)S(1)}, bf16[64,640]{1,0:T(8,128)(2,1)S(1)}, u32[]{:S(2)}, u32[]{:S(2)}) collective-permute-start(bf16[64,640]{1,0:T(8,128)(2,1)S(1)} %get-tuple-element.40), channel_id=1, source_target_pairs={{0,16},{1,17},{2,18},{3,19},{4,20},{5,21},{6,22},{7,23},{8,24},{9,... | collective-permute-start | bytes 245768 | tf_op jit(solution)/shard_map/ppermute | solution.py:330
  96.5 0.0 collective-permute-done.5
  96.5 0.0 collective-permute-done.6
  96.5 0.3 collective-permute-start.7
  96.8 3.0 %collective-permute-start.8 = (bf16[64,512]{1,0:T(8,128)(2,1)S(1)}, bf16[64,512]{1,0:T(8,128)(2,1)S(1)}, u32[]{:S(2)}, u32[]{:S(2)}) collective-permute-start(bf16[64,512]{1,0:T(8,128)(2,1)S(1)} %add_convert_fusion.3), channel_id=1, source_target_pairs={{0,96},{1,97},{2,98},{3,99},{4,100},{5,101},{6,102},{7,103},{8,104... | collective-permute-start | bytes 196616 | tf_op jit(solution)/shard_map/ppermute | solution.py:330
  99.9 0.9 collective-permute-start.17
  100.8 2.4 %collective-permute-start.18 = (bf16[64,640]{1,0:T(8,128)(2,1)S(1)}, bf16[64,640]{1,0:T(8,128)(2,1)S(1)}, u32[]{:S(2)}, u32[]{:S(2)}) collective-permute-start(bf16[64,640]{1,0:T(8,128)(2,1)S(1)} %add_convert_fusion.2), channel_id=1, source_target_pairs={{0,96},{1,97},{2,98},{3,99},{4,100},{5,101},{6,102},{7,103},{8,104... | collective-permute-start | bytes 245768 | tf_op jit(solution)/shard_map/ppermute | solution.py:330
  103.2 2.3 %collective-permute-start.19 = (bf16[64,640]{1,0:T(8,128)(2,1)S(1)}, bf16[64,640]{1,0:T(8,128)(2,1)S(1)}, u32[]{:S(2)}, u32[]{:S(2)}) collective-permute-start(bf16[64,640]{1,0:T(8,128)(2,1)S(1)} %add_convert_fusion.2), channel_id=1, source_target_pairs={{0,64},{1,65},{2,66},{3,67},{4,68},{5,69},{6,70},{7,71},{8,72},{9,... | collective-permute-start | bytes 245768 | tf_op jit(solution)/shard_map/ppermute | solution.py:330
  105.5 0.9 collective-permute-done.9
  106.4 0.8 collective-permute-done.17
  107.2 2.0 %collective-permute-done.19 = bf16[64,640]{1,0:T(8,128)(2,1)S(1)} collective-permute-done((bf16[64,640]{1,0:T(8,128)(2,1)S(1)}, bf16[64,640]{1,0:T(8,128)(2,1)S(1)}, u32[]{:S(2)}, u32[]{:S(2)}) %collective-permute-start.19) | collective-permute-done | bytes 81952 | tf_op jit(solution)/shard_map/ppermute | solution.py:330
  109.2 0.6 slice_multiply_fusion
  109.8 0.7 maximum_multiply_fusion
  (32 shorter events, 0.3 us)
Async XLA Ops:
  11.4 2.0 %copy-start.3 = (bf16[2048,1024]{1,0:T(8,128)(2,1)}, bf16[2048,1024]{1,0:T(8,128)(2,1)S(1)}, u32[]{:S(2)}) copy-start(bf16[2048,1024]{1,0:T(8,128)(2,1)S(1)} %get-tuple-element.19.slope_ref) | copy-start | bytes 12582916
  13.3 2.0 %copy-start.6 = (bf16[2048,1024]{1,0:T(8,128)(2,1)}, bf16[2048,1024]{1,0:T(8,128)(2,1)S(1)}, u32[]{:S(2)}) copy-start(bf16[2048,1024]{1,0:T(8,128)(2,1)S(1)} %get-tuple-element.18.latent_ref) | copy-start | bytes 12582916
  15.3 2.0 %copy-start.8 = (bf16[2048,1024]{1,0:T(8,128)(2,1)}, bf16[2048,1024]{1,0:T(8,128)(2,1)S(1)}, u32[]{:S(2)}) copy-start(bf16[2048,1024]{1,0:T(8,128)(2,1)S(1)} %get-tuple-element.22.hidden_ref) | copy-start | bytes 12582916
  17.4 1.3 %copy-start.12 = (bf16[1024,1024]{1,0:T(8,128)(2,1)}, bf16[1024,1024]{1,0:T(8,128)(2,1)S(1)}, u32[]{:S(2)}) copy-start(bf16[1024,1024]{1,0:T(8,128)(2,1)S(1)} %get-tuple-element.26.weight_ref) | copy-start | bytes 6291460
  18.7 18.8 %copy-start.10 = (f32[100,2048]{1,0:T(8,128)S(1)}, f32[100,2048]{1,0:T(8,128)}, u32[]{:S(2)}) copy-start(f32[100,2048]{1,0:T(8,128)} %observed_ref.1) | copy-start | bytes 2457604
  18.7 18.8 %copy-start.11 = (f32[2048]{0:T(1024)S(1)}, f32[2048]{0:T(1024)}, u32[]{:S(2)}) copy-start(f32[2048]{0:T(1024)} %param.9) | copy-start | bytes 24580
  19.6 17.9 %all-to-all-start = ((f16[8,112,256]{2,1,0:T(8,128)(2,1)}), f16[8,112,256]{2,1,0:T(8,128)(2,1)S(1)}, u32[]{:S(2)}, u32[]{:S(2)}) async-start(f16[8,112,256]{2,1,0:T(8,128)(2,1)} %multiply_convert_fusion), calls=%async_computation | async-start | bytes 917504 | tf_op jit(solution)/shard_map/all_to_all | solution.py:370
  39.4 13.4 %all-to-all-start.1 = ((bf16[8,112,256]{2,1,0:T(8,128)(2,1)}), bf16[8,112,256]{2,1,0:T(8,128)(2,1)S(1)}, u32[]{:S(2)}, u32[]{:S(2)}) async-start(bf16[8,112,256]{2,1,0:T(8,128)(2,1)} %pairs.1), calls=%async_computation.1 | async-start | bytes 917504 | tf_op jit(solution)/shard_map/all_to_all | solution.py:372
  43.1 2.2 %copy-start.7 = (bf16[2048,1024]{1,0:T(8,128)(2,1)S(1)}, bf16[2048,1024]{1,0:T(8,128)(2,1)}, u32[]{:S(2)}) copy-start(bf16[2048,1024]{1,0:T(8,128)(2,1)} %copy-done.6) | copy-start | bytes 12582916
  46.9 2.0 %copy-start = (bf16[1024,2048]{1,0:T(8,128)(2,1)}, bf16[1024,2048]{1,0:T(8,128)(2,1)S(1)}, u32[]{:S(2)}) copy-start(bf16[1024,2048]{1,0:T(8,128)(2,1)S(1)} %turned.1.turned_ref) | copy-start | bytes 12582916
  52.8 2.2 %copy-start.1 = (bf16[1024,2048]{1,0:T(8,128)(2,1)S(1)}, bf16[1024,2048]{1,0:T(8,128)(2,1)}, u32[]{:S(2)}) copy-start(bf16[1024,2048]{1,0:T(8,128)(2,1)} %copy-done) | copy-start | bytes 12582916
  55.0 2.2 %copy-start.4 = (bf16[2048,1024]{1,0:T(8,128)(2,1)S(1)}, bf16[2048,1024]{1,0:T(8,128)(2,1)}, u32[]{:S(2)}) copy-start(bf16[2048,1024]{1,0:T(8,128)(2,1)} %copy-done.3) | copy-start | bytes 12582916
  57.1 3.2 %copy-start.2 = (bf16[1024,2048]{1,0:T(8,128)(2,1)S(1)}, bf16[1024,2048]{1,0:T(8,128)(2,1)}, u32[]{:S(2)}) copy-start(bf16[1024,2048]{1,0:T(8,128)(2,1)} %copy-done) | copy-start | bytes 12582916
  57.1 3.5 %copy-start.5 = (bf16[2048,1024]{1,0:T(8,128)(2,1)S(1)}, bf16[2048,1024]{1,0:T(8,128)(2,1)}, u32[]{:S(2)}) copy-start(bf16[2048,1024]{1,0:T(8,128)(2,1)} %copy-done.3) | copy-start | bytes 12582916
  60.1 12.8 %collective-permute-start = (bf16[512,512]{1,0:T(8,128)(2,1)S(1)}, bf16[512,512]{1,0:T(8,128)(2,1)S(1)}, u32[]{:S(2)}, u32[]{:S(2)}) collective-permute-start(bf16[512,512]{1,0:T(8,128)(2,1)S(1)} %get-tuple-element.28), channel_id=1, source_target_pairs={{0,1},{1,0},{2,3},{3,2},{4,5},{5,4},{6,7},{7,6},{8,9},{9,8},{10,11... | collective-permute-start | bytes 1572872 | tf_op jit(solution)/shard_map/ppermute | solution.py:330
  60.6 2.2 %copy-start.9 = (bf16[2048,1024]{1,0:T(8,128)(2,1)S(1)}, bf16[2048,1024]{1,0:T(8,128)(2,1)}, u32[]{:S(2)}) copy-start(bf16[2048,1024]{1,0:T(8,128)(2,1)} %copy-done.8) | copy-start | bytes 12582916
  62.8 4.4 %copy-start.13 = (bf16[1024,1024]{1,0:T(8,128)(2,1)S(1)}, bf16[1024,1024]{1,0:T(8,128)(2,1)}, u32[]{:S(2)}) copy-start(bf16[1024,1024]{1,0:T(8,128)(2,1)} %copy-done.12) | copy-start | bytes 6291460
  66.9 12.2 %collective-permute-start.10 = (bf16[512,640]{1,0:T(8,128)(2,1)S(1)}, bf16[512,640]{1,0:T(8,128)(2,1)S(1)}, u32[]{:S(2)}, u32[]{:S(2)}) collective-permute-start(bf16[512,640]{1,0:T(8,128)(2,1)S(1)} %get-tuple-element.30), channel_id=1, source_target_pairs={{0,1},{1,0},{2,3},{3,2},{4,5},{5,4},{6,7},{7,6},{8,9},{9,8},{10,11... | collective-permute-start | bytes 1966088 | tf_op jit(solution)/shard_map/ppermute | solution.py:330
  73.1 9.5 %collective-permute-start.1 = (bf16[2,64,512]{2,1,0:T(8,128)(2,1)S(1)}, bf16[2,64,512]{2,1,0:T(8,128)(2,1)S(1)}, u32[]{:S(2)}, u32[]{:S(2)}) collective-permute-start(bf16[2,64,512]{2,1,0:T(8,128)(2,1)S(1)} %bitcast.44), channel_id=1, source_target_pairs={{0,2},{1,3},{2,4},{3,5},{4,6},{5,7},{6,0},{7,1},{8,10},{9,11},{10,... | collective-permute-start | bytes 393224 | tf_op jit(solution)/shard_map/ppermute | solution.py:330
  75.1 8.5 %collective-permute-start.2 = (bf16[2,64,512]{2,1,0:T(8,128)(2,1)S(1)}, bf16[2,64,512]{2,1,0:T(8,128)(2,1)S(1)}, u32[]{:S(2)}, u32[]{:S(2)}) collective-permute-start(bf16[2,64,512]{2,1,0:T(8,128)(2,1)S(1)} %bitcast.43), channel_id=1, source_target_pairs={{0,6},{1,7},{2,0},{3,1},{4,2},{5,3},{6,4},{7,5},{8,14},{9,15},{10,... | collective-permute-start | bytes 393224 | tf_op jit(solution)/shard_map/ppermute | solution.py:330
  77.3 8.5 %collective-permute-start.3 = (bf16[2,64,512]{2,1,0:T(8,128)(2,1)S(1)}, bf16[2,64,512]{2,1,0:T(8,128)(2,1)S(1)}, u32[]{:S(2)}, u32[]{:S(2)}) collective-permute-start(bf16[2,64,512]{2,1,0:T(8,128)(2,1)S(1)} %bitcast.42), channel_id=1, source_target_pairs={{0,4},{1,5},{2,6},{3,7},{4,0},{5,1},{6,2},{7,3},{8,12},{9,13},{10,... | collective-permute-start | bytes 393224 | tf_op jit(solution)/shard_map/ppermute | solution.py:330
  79.3 9.5 %collective-permute-start.11 = (bf16[2,64,640]{2,1,0:T(8,128)(2,1)S(1)}, bf16[2,64,640]{2,1,0:T(8,128)(2,1)S(1)}, u32[]{:S(2)}, u32[]{:S(2)}) collective-permute-start(bf16[2,64,640]{2,1,0:T(8,128)(2,1)S(1)} %bitcast.41), channel_id=1, source_target_pairs={{0,2},{1,3},{2,4},{3,5},{4,6},{5,7},{6,0},{7,1},{8,10},{9,11},{10,... | collective-permute-start | bytes 491528 | tf_op jit(solution)/shard_map/ppermute | solution.py:330
  80.4 9.9 %collective-permute-start.12 = (bf16[2,64,640]{2,1,0:T(8,128)(2,1)S(1)}, bf16[2,64,640]{2,1,0:T(8,128)(2,1)S(1)}, u32[]{:S(2)}, u32[]{:S(2)}) collective-permute-start(bf16[2,64,640]{2,1,0:T(8,128)(2,1)S(1)} %bitcast.40), channel_id=1, source_target_pairs={{0,6},{1,7},{2,0},{3,1},{4,2},{5,3},{6,4},{7,5},{8,14},{9,15},{10,... | collective-permute-start | bytes 491528 | tf_op jit(solution)/shard_map/ppermute | solution.py:330
  82.6 9.6 %collective-permute-start.13 = (bf16[2,64,640]{2,1,0:T(8,128)(2,1)S(1)}, bf16[2,64,640]{2,1,0:T(8,128)(2,1)S(1)}, u32[]{:S(2)}, u32[]{:S(2)}) collective-permute-start(bf16[2,64,640]{2,1,0:T(8,128)(2,1)S(1)} %bitcast.39), channel_id=1, source_target_pairs={{0,4},{1,5},{2,6},{3,7},{4,0},{5,1},{6,2},{7,3},{8,12},{9,13},{10,... | collective-permute-start | bytes 491528 | tf_op jit(solution)/shard_map/ppermute | solution.py:330
  85.9 7.9 %collective-permute-start.4 = (bf16[64,512]{1,0:T(8,128)(2,1)S(1)}, bf16[64,512]{1,0:T(8,128)(2,1)S(1)}, u32[]{:S(2)}, u32[]{:S(2)}) collective-permute-start(bf16[64,512]{1,0:T(8,128)(2,1)S(1)} %get-tuple-element.41), channel_id=1, source_target_pairs={{0,8},{1,9},{2,10},{3,11},{4,12},{5,13},{6,14},{7,15},{8,0},{9,1},... | collective-permute-start | bytes 196616 | tf_op jit(solution)/shard_map/ppermute | solution.py:330
  86.6 9.8 %collective-permute-start.5 = (bf16[64,512]{1,0:T(8,128)(2,1)S(1)}, bf16[64,512]{1,0:T(8,128)(2,1)S(1)}, u32[]{:S(2)}, u32[]{:S(2)}) collective-permute-start(bf16[64,512]{1,0:T(8,128)(2,1)S(1)} %get-tuple-element.41), channel_id=1, source_target_pairs={{0,24},{1,25},{2,26},{3,27},{4,28},{5,29},{6,30},{7,31},{8,16},{9,... | collective-permute-start | bytes 196616 | tf_op jit(solution)/shard_map/ppermute | solution.py:330
  88.9 7.6 %collective-permute-start.6 = (bf16[64,512]{1,0:T(8,128)(2,1)S(1)}, bf16[64,512]{1,0:T(8,128)(2,1)S(1)}, u32[]{:S(2)}, u32[]{:S(2)}) collective-permute-start(bf16[64,512]{1,0:T(8,128)(2,1)S(1)} %get-tuple-element.42), channel_id=1, source_target_pairs={{0,16},{1,17},{2,18},{3,19},{4,20},{5,21},{6,22},{7,23},{8,24},{9,... | collective-permute-start | bytes 196616 | tf_op jit(solution)/shard_map/ppermute | solution.py:330
  92.3 7.5 %collective-permute-start.14 = (bf16[64,640]{1,0:T(8,128)(2,1)S(1)}, bf16[64,640]{1,0:T(8,128)(2,1)S(1)}, u32[]{:S(2)}, u32[]{:S(2)}) collective-permute-start(bf16[64,640]{1,0:T(8,128)(2,1)S(1)} %get-tuple-element.39), channel_id=1, source_target_pairs={{0,8},{1,9},{2,10},{3,11},{4,12},{5,13},{6,14},{7,15},{8,0},{9,1},... | collective-permute-start | bytes 245768 | tf_op jit(solution)/shard_map/ppermute | solution.py:330
  93.0 6.8 %collective-permute-start.15 = (bf16[64,640]{1,0:T(8,128)(2,1)S(1)}, bf16[64,640]{1,0:T(8,128)(2,1)S(1)}, u32[]{:S(2)}, u32[]{:S(2)}) collective-permute-start(bf16[64,640]{1,0:T(8,128)(2,1)S(1)} %get-tuple-element.39), channel_id=1, source_target_pairs={{0,24},{1,25},{2,26},{3,27},{4,28},{5,29},{6,30},{7,31},{8,16},{9,... | collective-permute-start | bytes 245768 | tf_op jit(solution)/shard_map/ppermute | solution.py:330
  93.8 6.0 %collective-permute-start.16 = (bf16[64,640]{1,0:T(8,128)(2,1)S(1)}, bf16[64,640]{1,0:T(8,128)(2,1)S(1)}, u32[]{:S(2)}, u32[]{:S(2)}) collective-permute-start(bf16[64,640]{1,0:T(8,128)(2,1)S(1)} %get-tuple-element.40), channel_id=1, source_target_pairs={{0,16},{1,17},{2,18},{3,19},{4,20},{5,21},{6,22},{7,23},{8,24},{9,... | collective-permute-start | bytes 245768 | tf_op jit(solution)/shard_map/ppermute | solution.py:330
  96.5 6.7 %collective-permute-start.7 = (bf16[64,512]{1,0:T(8,128)(2,1)S(1)}, bf16[64,512]{1,0:T(8,128)(2,1)S(1)}, u32[]{:S(2)}, u32[]{:S(2)}) collective-permute-start(bf16[64,512]{1,0:T(8,128)(2,1)S(1)} %add_convert_fusion.3), channel_id=1, source_target_pairs={{0,32},{1,33},{2,34},{3,35},{4,36},{5,37},{6,38},{7,39},{8,40},{9,... | collective-permute-start | bytes 196616 | tf_op jit(solution)/shard_map/ppermute | solution.py:330
  96.8 8.7 %collective-permute-start.8 = (bf16[64,512]{1,0:T(8,128)(2,1)S(1)}, bf16[64,512]{1,0:T(8,128)(2,1)S(1)}, u32[]{:S(2)}, u32[]{:S(2)}) collective-permute-start(bf16[64,512]{1,0:T(8,128)(2,1)S(1)} %add_convert_fusion.3), channel_id=1, source_target_pairs={{0,96},{1,97},{2,98},{3,99},{4,100},{5,101},{6,102},{7,103},{8,104... | collective-permute-start | bytes 196616 | tf_op jit(solution)/shard_map/ppermute | solution.py:330
  99.8 6.6 %collective-permute-start.9 = (bf16[64,512]{1,0:T(8,128)(2,1)S(1)}, bf16[64,512]{1,0:T(8,128)(2,1)S(1)}, u32[]{:S(2)}, u32[]{:S(2)}) collective-permute-start(bf16[64,512]{1,0:T(8,128)(2,1)S(1)} %add_convert_fusion.3), channel_id=1, source_target_pairs={{0,64},{1,65},{2,66},{3,67},{4,68},{5,69},{6,70},{7,71},{8,72},{9,... | collective-permute-start | bytes 196616 | tf_op jit(solution)/shard_map/ppermute | solution.py:330
  99.9 7.3 %collective-permute-start.17 = (bf16[64,640]{1,0:T(8,128)(2,1)S(1)}, bf16[64,640]{1,0:T(8,128)(2,1)S(1)}, u32[]{:S(2)}, u32[]{:S(2)}) collective-permute-start(bf16[64,640]{1,0:T(8,128)(2,1)S(1)} %add_convert_fusion.2), channel_id=1, source_target_pairs={{0,32},{1,33},{2,34},{3,35},{4,36},{5,37},{6,38},{7,39},{8,40},{9,... | collective-permute-start | bytes 245768 | tf_op jit(solution)/shard_map/ppermute | solution.py:330
  100.8 6.4 %collective-permute-start.18 = (bf16[64,640]{1,0:T(8,128)(2,1)S(1)}, bf16[64,640]{1,0:T(8,128)(2,1)S(1)}, u32[]{:S(2)}, u32[]{:S(2)}) collective-permute-start(bf16[64,640]{1,0:T(8,128)(2,1)S(1)} %add_convert_fusion.2), channel_id=1, source_target_pairs={{0,96},{1,97},{2,98},{3,99},{4,100},{5,101},{6,102},{7,103},{8,104... | collective-permute-start | bytes 245768 | tf_op jit(solution)/shard_map/ppermute | solution.py:330
  103.2 5.9 %collective-permute-start.19 = (bf16[64,640]{1,0:T(8,128)(2,1)S(1)}, bf16[64,640]{1,0:T(8,128)(2,1)S(1)}, u32[]{:S(2)}, u32[]{:S(2)}) collective-permute-start(bf16[64,640]{1,0:T(8,128)(2,1)S(1)} %add_convert_fusion.2), channel_id=1, source_target_pairs={{0,64},{1,65},{2,66},{3,67},{4,68},{5,69},{6,70},{7,71},{8,72},{9,... | collective-permute-start | bytes 245768 | tf_op jit(solution)/shard_map/ppermute | solution.py:330

commit v4 on v3

--- a/solution.py
+++ b/solution.py
@@ -33,12 +33,28 @@
     return pl.CostEstimate(flops=flops, bytes_accessed=nbytes, transcendentals=trans)
 
 
-CHUNKS = (512, 512, 1024)
+CHUNKS = (512, 512, 512, 512)
 FCOLS = 512
 
 
 def forward_kernel(
-    latent_ref, weight_ref, out_weight_ref, forecast_ref, hidden_ref, slope_ref, latent_copy, weight_copy, padded_ref, out_weight_copy, latent_sems, weight_sems, out_weight_sem
+    latent_ref,
+    weight_ref,
+    out_weight_ref,
+    forecast_ref,
+    hidden_out,
+    slope_out,
+    padded_ref,
+    hidden_ref,
+    slope_ref,
+    latent_copy,
+    weight_copy,
+    out_weight_copy,
+    latent_sems,
+    weight_sems,
+    out_weight_sem,
+    hidden_sems,
+    slope_sems,
 ):
     nodes, width = latent_ref.shape
     variables = out_weight_ref.shape[0]
@@ -53,12 +69,12 @@
         )
         for start in range(0, width, FCOLS)
     ]
+
+    def chunk(ref, rows):
+        return ref.at[pl.ds(rows.start, rows.stop - rows.start)]
+
     latent_loads = [
-        pltpu.make_async_copy(
-            latent_ref.at[pl.ds(rows.start, rows.stop - rows.start)],
-            latent_copy.at[pl.ds(rows.start, rows.stop - rows.start)],
-            latent_sems.at[index],
-        )
+        pltpu.make_async_copy(chunk(latent_ref, rows), chunk(latent_copy, rows), latent_sems.at[index])
         for index, rows in enumerate(spans)
     ]
     weight_loads[0].start()
@@ -71,7 +87,7 @@
         [out_weight_copy[...], jnp.zeros((WIDE - variables, width), bf16)], axis=0
     )
     padded_ref[...] = turned_weight.T
-
+    stores = []
     for index, rows in enumerate(spans):
         latent_loads[index].wait()
         for start in range(0, width, FCOLS):
@@ -83,6 +99,10 @@
             hidden = pre * sig
             hidden_ref[rows, columns] = hidden.astype(bf16)
             slope_ref[rows, columns] = (sig + hidden * (1.0 - sig)).astype(bf16)
+        for made, out, sems in ((hidden_ref, hidden_out, hidden_sems), (slope_ref, slope_out, slope_sems)):
+            store = pltpu.make_async_copy(chunk(made, rows), chunk(out, rows), sems.at[index])
+            store.start()
+            stores.append(store)
         for share in range(rows.start // SHARE, rows.stop // SHARE):
             forecast_ref[share] = lax.dot_general(
                 turned_weight[:TALL],
@@ -90,35 +110,42 @@
                 NT,
                 preferred_element_type=f32,
             )
+    for store in stores:
+        store.wait()
+
+
+def pinned(value):
+    return pltpu.with_memory_space_constraint(value, pltpu.HBM)
 
 
 def forward(latent, weight, out_weight):
     nodes, width = latent.shape
-    latent = pltpu.with_memory_space_constraint(latent, pltpu.HBM)
-    weight = pltpu.with_memory_space_constraint(weight, pltpu.HBM)
-    out_weight = pltpu.with_memory_space_constraint(out_weight, pltpu.HBM)
     return pl.pallas_call(
         forward_kernel,
         in_specs=[anywhere] * 3,
-        out_specs=[vmem] * 6,
+        out_specs=[vmem, anywhere, anywhere, vmem],
         out_shape=[
             jax.ShapeDtypeStruct((nodes // SHARE, TALL, SHARE), f32),
-            jax.ShapeDtypeStruct((nodes, width), bf16),
-            jax.ShapeDtypeStruct((nodes, width), bf16),
-            jax.ShapeDtypeStruct((nodes, width), bf16),
-            jax.ShapeDtypeStruct((width, width), bf16),
+            pltpu.HBM((nodes, width), bf16),
+            pltpu.HBM((nodes, width), bf16),
             jax.ShapeDtypeStruct((width, WIDE), bf16),
         ],
         scratch_shapes=[
+            pltpu.VMEM((nodes, width), bf16),
+            pltpu.VMEM((nodes, width), bf16),
+            pltpu.VMEM((nodes, width), bf16),
+            pltpu.VMEM((width, width), bf16),
             pltpu.VMEM(out_weight.shape, bf16),
             pltpu.SemaphoreType.DMA((len(CHUNKS),)),
             pltpu.SemaphoreType.DMA((width // FCOLS,)),
             pltpu.SemaphoreType.DMA,
-        ],
-        compiler_params=params(12),
+            pltpu.SemaphoreType.DMA((len(CHUNKS),)),
+            pltpu.SemaphoreType.DMA((len(CHUNKS),)),
+        ],
+        compiler_params=params(32),
         cost_estimate=cost(2 * nodes * width * (width + WIDE), 20 << 20),
         name="forward",
-    )(latent, weight, out_weight)
+    )(pinned(latent), pinned(weight), pinned(out_weight))
 
 
 def slope_function(diff):
@@ -175,14 +202,23 @@
     )(place, blocks, observed, area)
 
 
-def turn_kernel(order_ref, latent_ref, turned_ref):
+def position(grid_ref):
+    grid = grid_ref[0]
+    return grid >> 3, (grid >> 1) & 3, grid & 1
+
+
+def slot(group, x_lo, z):
+    return (((group - z) & 3) * 2 + ((group >> 2) ^ x_lo)) * 64
+
+
+def turn_kernel(grid_ref, latent_ref, turned_ref):
     nodes, width = latent_ref.shape
     half = width // 2
-    core = order_ref[8]
+    x_lo, z, core = position(grid_ref)
     for group in range(8):
-        at = order_ref[group] * 64
-        first = pl.multiple_of(core * half + at, 64)
-        second = pl.multiple_of((1 - core) * half + at, 64)
+        at = slot(group, x_lo, z)
+        first = pl.multiple_of((1 - core) * half + at, 64)
+        second = pl.multiple_of(core * half + at, 64)
         for row in range(0, nodes, ROWS):
             columns = slice(row, row + ROWS)
             block = latent_ref[columns, group * 128 : (group + 1) * 128].T
@@ -190,7 +226,7 @@
             turned_ref[pl.ds(second, 64), columns] = block[64:]
 
 
-def turned(order, latent):
+def turned(grid, latent):
     nodes, width = latent.shape
     return pl.pallas_call(
         turn_kernel,
@@ -200,10 +236,10 @@
         compiler_params=params(8),
         cost_estimate=cost(0, 8 << 20),
         name="turned",
-    )(order, latent)
-
-
-def first_product(turned_ref, slope_ref, padded_ref, turn_ref, pre_ref, send_ref, keep_ref, begin):
+    )(grid, latent)
+
+
+def first_product(turned_ref, slope_ref, padded_ref, turn_ref, pre_ref, send_ref, keep_ref, begin, ready):
     nodes, span = pre_ref.shape
     half = turned_ref.shape[0] // 2
     for column in range(0, span, COLS):
@@ -212,35 +248,82 @@
         for start in range(0, nodes, ROWS):
             rows = slice(start, start + ROWS)
             grad_hidden = lax.dot_general(turn_ref[rows, :], padded_ref[source, :], NT, preferred_element_type=f32)
-            pre_ref[rows, columns] = (grad_hidden * slope_ref[rows, source].astype(f32)).astype(bf16)
+            pre_ref[rows, columns] = (grad_hidden * slope_ref[rows, columns].astype(f32)).astype(bf16)
+    ready()
+    for column in range(0, span, COLS):
+        columns = slice(column, column + COLS)
         for out_ref, base in ((send_ref, 0), (keep_ref, half)):
             part = jnp.dot(turned_ref[base : base + half, :], pre_ref[:, columns], preferred_element_type=f32)
             out_ref[:, columns] = part.astype(bf16)
 
 
-def backward_a_kernel(low_ref, turned_ref, slope_ref, padded_ref, pre_ref, send_ref, keep_ref, turn_ref, flat_ref):
+def backward_a_kernel(
+    low_ref,
+    turned_hbm,
+    slope_hbm,
+    padded_ref,
+    pre_ref,
+    send_ref,
+    keep_ref,
+    turn_ref,
+    flat_ref,
+    turned_ref,
+    slope_ref,
+    turned_sem,
+    slope_sem,
+):
+    span = pre_ref.shape[1]
+    slope_load = pltpu.make_async_copy(slope_hbm.at[:, pl.ds(0, span)], slope_ref, slope_sem)
+    turned_load = pltpu.make_async_copy(turned_hbm, turned_ref, turned_sem)
+    slope_load.start()
+    turned_load.start()
     for share in range(low_ref.shape[0]):
         columns = slice(share * SHARE, (share + 1) * SHARE)
         low = jnp.concatenate([low_ref[share], jnp.zeros((WIDE - TALL, SHARE), bf16)], axis=0)
         flat_ref[:, columns] = low
         turn_ref[columns, :] = low.T
-    first_product(turned_ref, slope_ref, padded_ref, turn_ref, pre_ref, send_ref, keep_ref, 0)
+    slope_load.wait()
+    first_product(
+        turned_ref, slope_ref, padded_ref, turn_ref, pre_ref, send_ref, keep_ref, 0, turned_load.wait
+    )
 
 
 def backward_b_kernel(
-    order_ref, turned_ref, slope_ref, hidden_ref, padded_ref, turn_ref, flat_ref, pre_ref, send_ref, keep_ref, second_ref
+    grid_ref,
+    turned_ref,
+    slope_hbm,
+    hidden_hbm,
+    padded_ref,
+    turn_ref,
+    flat_ref,
+    pre_ref,
+    send_ref,
+    keep_ref,
+    second_ref,
+    slope_ref,
+    hidden_ref,
+    slope_sem,
+    hidden_sem,
 ):
     width = hidden_ref.shape[1]
     span = pre_ref.shape[1]
-    first_product(turned_ref, slope_ref, padded_ref, turn_ref, pre_ref, send_ref, keep_ref, width - span)
+    slope_load = pltpu.make_async_copy(slope_hbm.at[:, pl.ds(width - span, span)], slope_ref, slope_sem)
+    hidden_load = pltpu.make_async_copy(hidden_hbm, hidden_ref, hidden_sem)
+    slope_load.start()
+    hidden_load.start()
+    slope_load.wait()
+    first_product(
+        turned_ref, slope_ref, padded_ref, turn_ref, pre_ref, send_ref, keep_ref, width - span, lambda: None
+    )
+    hidden_load.wait()
     for column in range(0, width, COLS):
         columns = slice(column, column + COLS)
         second_ref[columns, :] = jnp.dot(flat_ref[...], hidden_ref[:, columns], preferred_element_type=f32).T.astype(bf16)
-    core = order_ref[8]
+    x_lo, z, core = position(grid_ref)
     for group in range(8):
-        at = pl.multiple_of(order_ref[group] * 64, 64)
-        mine = pl.multiple_of(group * 128 + 64 * (1 - core), 64)
-        other = pl.multiple_of(group * 128 + 64 * core, 64)
+        at = pl.multiple_of(slot(group, x_lo, z), 64)
+        mine = pl.multiple_of(group * 128 + 64 * core, 64)
+        other = pl.multiple_of(group * 128 + 64 * (1 - core), 64)
         keep_ref[pl.ds(at, 64), span:] = second_ref[pl.ds(mine, 64), :]
         send_ref[pl.ds(at, 64), span:] = second_ref[pl.ds(other, 64), :]
 
@@ -250,53 +333,69 @@
     half = width // 2
     return pl.pallas_call(
         backward_a_kernel,
-        in_specs=[vmem] * 4,
-        out_specs=[vmem] * 5,
+        in_specs=[vmem, anywhere, anywhere, vmem],
+        out_specs=[vmem] * 6,
         out_shape=[
             jax.ShapeDtypeStruct((nodes, half), bf16),
             jax.ShapeDtypeStruct((half, half), bf16),
             jax.ShapeDtypeStruct((half, half), bf16),
             jax.ShapeDtypeStruct((nodes, WIDE), bf16),
             jax.ShapeDtypeStruct((WIDE, nodes), bf16),
-        ],
-        compiler_params=params(12),
+            jax.ShapeDtypeStruct((width, nodes), bf16),
+        ],
+        scratch_shapes=[
+            pltpu.VMEM((nodes, half), bf16),
+            pltpu.SemaphoreType.DMA,
+            pltpu.SemaphoreType.DMA,
+        ],
+        compiler_params=params(16),
         cost_estimate=cost(nodes * width * (width + WIDE), 8 << 20),
         name="backward_a",
-    )(low, turned_latent, slope, padded)
-
-
-def backward_b(order, turned_latent, slope, hidden, padded, turn, flat):
+    )(low, pinned(turned_latent), pinned(slope), padded)
+
+
+def backward_b(grid, turned_latent, slope, hidden, padded, turn, flat):
     nodes, width = slope.shape
     half = width // 2
     return pl.pallas_call(
         backward_b_kernel,
-        in_specs=[smem] + [vmem] * 6,
+        in_specs=[smem, vmem, anywhere, anywhere] + [vmem] * 3,
         out_specs=[vmem] * 3,
         out_shape=[
             jax.ShapeDtypeStruct((nodes, half), bf16),
             jax.ShapeDtypeStruct((half, half + WIDE), bf16),
             jax.ShapeDtypeStruct((half, half + WIDE), bf16),
         ],
-        scratch_shapes=[pltpu.VMEM((width, WIDE), bf16)],
-        compiler_params=params(12),
+        scratch_shapes=[
+            pltpu.VMEM((width, WIDE), bf16),
+            pltpu.VMEM((nodes, half), bf16),
+            pltpu.VMEM((nodes, width), bf16),
+            pltpu.SemaphoreType.DMA,
+            pltpu.SemaphoreType.DMA,
+        ],
+        compiler_params=params(16),
         cost_estimate=cost(nodes * width * (width + 3 * WIDE), 8 << 20),
         name="backward_b",
-    )(order, turned_latent, slope, hidden, padded, turn, flat)
-
-
-def latent_kernel(left_ref, right_ref, weight_ref, out_ref, result_ref, sems):
+    )(grid, turned_latent, pinned(slope), pinned(hidden), padded, turn, flat)
+
+
+def latent_kernel(left_ref, right_ref, weight_hbm, *refs, begin):
+    out_ref, weight_ref, result_ref, weight_sem, sems = refs[-5:]
     nodes, half = left_ref.shape
     width = weight_ref.shape[1]
+    load = pltpu.make_async_copy(weight_hbm, weight_ref, weight_sem)
+    load.start()
+    load.wait()
     stores = []
-    for row in range(0, nodes, ROWS):
-        rows = slice(row, row + ROWS)
+    for row in range(0, nodes // 2, ROWS):
+        rows = slice(begin + row, begin + row + ROWS)
         for start in range(0, width, COLS):
             columns = slice(start, start + COLS)
             left = lax.dot_general(left_ref[rows, :], weight_ref[columns, :half], NT, preferred_element_type=f32)
             right = lax.dot_general(right_ref[rows, :], weight_ref[columns, half:], NT, preferred_element_type=f32)
-            result_ref[rows, columns] = (left + right).astype(bf16)
+            result_ref[row : row + ROWS, columns] = (left + right).astype(bf16)
         store = pltpu.make_async_copy(
-            result_ref.at[pl.ds(row, ROWS)], out_ref.at[pl.ds(row, ROWS)], sems.at[row // ROWS]
+            result_ref.at[pl.ds(row, ROWS)], out_ref.at[pl.ds(begin + row, ROWS)], sems.at[row // ROWS]
         )
         store.start()
         stores.append(store)
@@ -304,19 +403,26 @@
         store.wait()
 
 
-def latent_gradient(left, right, weight):
+def latent_gradient(left, right, weight, begin, so_far=None):
     nodes = left.shape[0]
     width = weight.shape[1]
-    return pl.pallas_call(
-        latent_kernel,
-        in_specs=[vmem] * 3,
+    more = [] if so_far is None else [so_far]
+    return pl.pallas_call(
+        functools.partial(latent_kernel, begin=begin),
+        in_specs=[vmem, vmem, anywhere] + [anywhere] * len(more),
         out_specs=anywhere,
-        out_shape=jax.ShapeDtypeStruct((nodes, width), bf16),
-        scratch_shapes=[pltpu.VMEM((nodes, width), bf16), pltpu.SemaphoreType.DMA((nodes // ROWS,))],
+        out_shape=pltpu.HBM((nodes, width), bf16),
+        input_output_aliases={3: 0} if more else {},
+        scratch_shapes=[
+            pltpu.VMEM((width, width), bf16),
+            pltpu.VMEM((nodes // 2, width), bf16),
+            pltpu.SemaphoreType.DMA,
+            pltpu.SemaphoreType.DMA((nodes // 2 // ROWS,)),
+        ],
         compiler_params=params(12),
-        cost_estimate=cost(2 * nodes * width * width, 10 << 20),
+        cost_estimate=cost(nodes * width * width, 5 << 20),
         name="latent_gradient",
-    )(left, right, weight)
+    )(left, right, pinned(weight), *more)
 
 
 def moved(value, move):
@@ -337,10 +443,13 @@
     return total
 
 
-def reduced(send, keep):
-    columns = send.shape[1]
+def over_core(send, keep):
     got = moved(send, lambda y, x, z, c: (y, x, z, 1 - c))
-    blocks = summed(keep, [got]).astype(bf16).reshape(4, 2, 64, columns)
+    return summed(keep, [got]).astype(bf16)
+
+
+def over_chips(rows):
+    blocks = rows.reshape(4, 2, 64, rows.shape[1])
     got = [moved(blocks[k], lambda y, x, z, c, k=k: (y, x, (z + k) % 4, c)) for k in (1, 3, 2)]
     blocks = summed(blocks[0], got).astype(bf16)
     got = [
@@ -358,24 +467,23 @@
     groups = lax.axis_size("grid")
     nodes, width = latent.shape
     variables = output_weight.shape[1]
-    member = lax.axis_index("member")
-    grid = lax.axis_index("grid")
-    x_lo, z, core = grid // 8, (grid // 2) % 4, grid % 2
-    order = jnp.stack(
-        [((g % 4 - z) % 4) * 2 + jnp.abs(g // 4 - x_lo) for g in range(8)] + [1 - core]
-    ).astype(jnp.int32)
-    place = member.astype(jnp.int32).reshape(1)
-
-    forecast, hidden, slope, latent_copy, weight_copy, padded = forward(latent, hidden_weight, output_weight.T)
-    blocks = lax.all_to_all((0.25 * forecast).astype(f16), "member", 0, 0, tiled=True)
+    place = lax.axis_index("member").astype(jnp.int32).reshape(1)
+    grid = lax.axis_index("grid").astype(jnp.int32).reshape(1)
+
+    forecast, hidden, slope, padded = forward(latent, hidden_weight, output_weight.T)
+    blocks, late_grid = lax.optimization_barrier(((0.25 * forecast).astype(f16), grid))
+    blocks = lax.all_to_all(blocks, "member", 0, 0, tiled=True)
+    turned_latent = turned(late_grid, latent)
     low = pairs(place, 4.0 * blocks.astype(f32), observed, node_area_weight.reshape(1, nodes))
     low = lax.all_to_all(low, "member", 0, 0, tiled=True)
-    turned_latent = turned(order, latent_copy)
-    pre_a, send_a, keep_a, turn, flat = backward_a(low, turned_latent, slope, padded)
-    pre_b, send_b, keep_b = backward_b(order, turned_latent, slope, hidden, padded, turn, flat)
-    total_a = reduced(send_a, keep_a)
-    total_b = reduced(send_b, keep_b)
-    grad_latent = latent_gradient(pre_a, pre_b, weight_copy)
+    pre_a, send_a, keep_a, turn, flat, turned_latent = backward_a(low, turned_latent, slope, padded)
+    pre_b, send_b, keep_b = backward_b(grid, turned_latent, slope, hidden, padded, turn, flat)
+    rows_a, pre_a = lax.optimization_barrier((over_core(send_a, keep_a), pre_a))
+    grad_latent = latent_gradient(pre_a, pre_b, hidden_weight, 0)
+    rows_b, pre_b = lax.optimization_barrier((over_core(send_b, keep_b), pre_b))
+    grad_latent = latent_gradient(pre_a, pre_b, hidden_weight, nodes // 2, grad_latent)
+    total_a = over_chips(rows_a)
+    total_b = over_chips(rows_b)
     factor = 1.0 / math.sqrt(members * nodes * groups)
     half = width // 2
     first = jnp.concatenate([total_a, total_b[:, :half]], axis=1)

time: 111 us -> 105 us (0.946)
  local copies, waits for them, and re-layouts: 18.5 us -> 4.34 us
  Pallas kernels: 26.9 us -> 35.6 us
  waiting for transfers between devices: 24.5 us -> 21.4 us
  starting transfers between devices: 36.8 us -> 39.6 us
    unnamed x28 -> x8, local copies, waits for them, and re-layouts: 18.3 us -> 4.21 us
    pallas_call x4 -> x5, Pallas kernels: 23.4 us -> 32.6 us  [the longest x1 12 us: forward(): pl.pallas_call(forward_kernel, in_specs=[anywhere] * 3, out_specs=[vmem,...]
    ppermute x20, waiting for transfers between devices: 9.81 us -> 5.96 us  [moved(): return lax.ppermute(value, ('member', 'grid'), moves)]
    ppermute x20, starting transfers between devices: 26.3 us -> 29.1 us  [moved(): return lax.ppermute(value, ('member', 'grid'), moves)]
  transfers between devices with their start and end apart: 22 -> 22, of which waited for: 10 -> 6; matrix products, arithmetic and copies ran while one was open for 1% -> 1% of each run, Pallas kernels for 10% -> 16%
where the time goes in v4:
time: 105 us
  starting transfers between devices  39.6 us (38%)
  Pallas kernels  35.6 us (34%)
  waiting for transfers between devices  21.4 us (20%)
  local copies, waits for them, and re-layouts  4.34 us (4%)
  other arithmetic  2.94 us (3%)
    ppermute x20, starting transfers between devices, moved(): return lax.ppermute(value, ('member', 'grid'), moves)  29.1 us
    pallas_call x1, Pallas kernels, forward(): pl.pallas_call(forward_kernel, in_specs=[anywhere] * 3, out_specs=[vmem,...  12 us
    all_to_all x1, waiting for transfers between devices, body(): blocks = lax.all_to_all(blocks, 'member', 0, 0, tiled=True)  10.9 us
    pallas_call x2, Pallas kernels, latent_gradient(): pl.pallas_call(functools.partial(latent_kernel, begin=begin), in_specs=[v...  10 us
    all_to_all x1, starting transfers between devices, body(): blocks = lax.all_to_all(blocks, 'member', 0, 0, tiled=True)  7.01 us
    ppermute x20, waiting for transfers between devices, moved(): return lax.ppermute(value, ('member', 'grid'), moves)  5.96 us
    pallas_call x1, Pallas kernels, backward_b(): pl.pallas_call(backward_b_kernel, in_specs=[smem, vmem, anywhere, anywher...  5.35 us
    pallas_call x1, Pallas kernels, backward_a(): pl.pallas_call(backward_a_kernel, in_specs=[vmem, anywhere, anywhere, vme...  5.21 us
  transfers between devices with their start and end apart: 22, of which 6 were waited for; matrix products, arithmetic and copies ran while one was open for 1% of the time, Pallas kernels for 16%

profile of v4, /device:TPU:0, one launch (start us, length us, event | category | flops | bytes accessed | tf_op | source)
XLA Modules:
  0.0 104.7 jit_solution(7548839326574264507)
XLA Ops:
  0.6 12.0 %forward.1 = (f32[8,112,256]{2,1,0:T(8,128)S(1)}, bf16[2048,1024]{1,0:T(8,128)(2,1)}, bf16[2048,1024]{1,0:T(8,128)(2,1)}, bf16[1024,128]{1,0:T(8,128)(2,1)S(1)}) custom-call(bf16[2048,1024]{1,0:T(8,128)(2,1)} %bitcast.28, bf16[1024,1024]{1,0:T(8,128)(2,1)} %weight_hbm.3, bf16[100,1024]{1,0:T(8,128)(2,1)} %bitcast.40), custom_call_target="tpu_custom_call" | custom-call | flops 4831838208 | bytes 20971520 | tf_op jit(solution)/shard_map/forward/pallas_call | solution.py:123
  12.7 0.0 copy-start.2
  12.7 0.9 multiply_convert_fusion
  13.6 7.0 %all-to-all-start = ((f16[8,112,256]{2,1,0:T(8,128)(2,1)}), f16[8,112,256]{2,1,0:T(8,128)(2,1)S(1)}, u32[]{:S(2)}, u32[]{:S(2)}) async-start(f16[8,112,256]{2,1,0:T(8,128)(2,1)} %multiply_convert_fusion), calls=%async_computation | async-start | bytes 917504 | tf_op jit(solution)/shard_map/all_to_all | solution.py:475
  20.6 10.9 %all-to-all-done = f16[8,112,256]{2,1,0:T(8,128)(2,1)S(1)} async-done(((f16[8,112,256]{2,1,0:T(8,128)(2,1)}), f16[8,112,256]{2,1,0:T(8,128)(2,1)S(1)}, u32[]{:S(2)}, u32[]{:S(2)}) %all-to-all-start) | async-done | bytes 458784 | tf_op jit(solution)/shard_map/all_to_all | solution.py:475
  31.5 0.1 convert_multiply_fusion.blocks_ref
  31.6 1.9 %pairs.1 = bf16[8,112,256]{2,1,0:T(8,128)(2,1)} custom-call(s32[1]{0:T(128)} %bitcast.place_ref, f32[8,112,256]{2,1,0:T(8,128)S(1)} %convert_multiply_fusion.blocks_ref, f32[100,2048]{1,0:T(8,128)S(1)} %copy-done.2, f32[1,2048]{1,0:T(1,128)S(1)} %bitcast.30), custom_call_target="tpu_custom_call" | custom-call | flops 4194304 | bytes 2097152 | tf_op jit(solution)/shard_map/pairs/pallas_call | solution.py:189
  33.5 3.5 %all-to-all-start.1 = ((bf16[8,112,256]{2,1,0:T(8,128)(2,1)}), bf16[8,112,256]{2,1,0:T(8,128)(2,1)S(1)}, u32[]{:S(2)}, u32[]{:S(2)}) async-start(bf16[8,112,256]{2,1,0:T(8,128)(2,1)} %pairs.1), calls=%async_computation.1 | async-start | bytes 917504 | tf_op jit(solution)/shard_map/all_to_all | solution.py:478
  36.9 0.0 copy-start.1
  37.0 2.2 %copy-done.1 = bf16[1,2048,1024]{2,1,0:T(8,128)(2,1)S(1)} copy-done((bf16[1,2048,1024]{2,1,0:T(8,128)(2,1)S(1)}, bf16[1,2048,1024]{2,1,0:T(8,128)(2,1)}, u32[]{:S(2)}) %copy-start.1) | copy-done | bytes 4194328
  39.1 1.1 %turned.1.turned_hbm = bf16[1024,2048]{1,0:T(8,128)(2,1)S(1)} custom-call(s32[1]{0:T(128)} %bitcast.3.grid_ref, bf16[2048,1024]{1,0:T(8,128)(2,1)S(1)} %bitcast.29), custom_call_target="tpu_custom_call" | custom-call | bytes 8388608 | tf_op jit(solution)/shard_map/turned/pallas_call | solution.py:231
  40.3 2.0 %copy-done = bf16[1024,2048]{1,0:T(8,128)(2,1)} copy-done((bf16[1024,2048]{1,0:T(8,128)(2,1)}, bf16[1024,2048]{1,0:T(8,128)(2,1)S(1)}, u32[]{:S(2)}) %copy-start) | copy-done | bytes 4194328
  42.3 4.6 %all-to-all-done.1.low_ref = bf16[8,112,256]{2,1,0:T(8,128)(2,1)S(1)} async-done(((bf16[8,112,256]{2,1,0:T(8,128)(2,1)}), bf16[8,112,256]{2,1,0:T(8,128)(2,1)S(1)}, u32[]{:S(2)}, u32[]{:S(2)}) %all-to-all-start.1) | async-done | bytes 458784 | tf_op jit(solution)/shard_map/all_to_all | solution.py:478
  46.9 5.2 %backward_a.1 = (bf16[2048,512]{1,0:T(8,128)(2,1)S(1)}, bf16[512,512]{1,0:T(8,128)(2,1)S(1)}, bf16[512,512]{1,0:T(8,128)(2,1)S(1)}, bf16[2048,128]{1,0:T(8,128)(...) custom-call(bf16[8,112,256]{2,1,0:T(8,128)(2,1)S(1)} %all-to-all-done.1.low_ref, ...), custom_call_target="tpu_custom_call" | custom-call | flops 2415919104 | bytes 8388608 | tf_op jit(solution)/shard_map/backward_a/pallas_call | solution.py:334
  52.1 0.3 collective-permute-start
  52.4 5.3 %backward_b.1 = (bf16[2048,512]{1,0:T(8,128)(2,1)S(1)}, bf16[512,640]{1,0:T(8,128)(2,1)S(1)}, bf16[512,640]{1,0:T(8,128)(2,1)S(1)}) custom-call(s32[1]{0:T(128)} %bitcast.3.grid_ref, bf16[1024,2048]{1,0:T(8,128)(2,1)S(1)} %get-tuple-element.31.turned_ref, bf16[2048,1024]{1,0:T(8,128)(2,1)} %get-tuple-element.25.slope_hbm, ...), custom_call_target="tpu_custom_call" | custom-call | flops 2952790016 | bytes 8388608 | tf_op jit(solution)/shard_map/backward_b/pallas_call | solution.py:360
  57.7 0.6 collective-permute-start.1
  58.3 0.0 collective-permute-done
  58.3 0.1 add_convert_fusion.1
  58.5 4.0 %collective-permute-start.4 = (bf16[2,64,512]{2,1,0:T(8,128)(2,1)S(1)}, bf16[2,64,512]{2,1,0:T(8,128)(2,1)S(1)}, u32[]{:S(2)}, u32[]{:S(2)}) collective-permute-start(bf16[2,64,512]{2,1,0:T(8,128)(2,1)S(1)} %bitcast.39), channel_id=1, source_target_pairs={{0,4},{1,5},{2,6},{3,7},{4,0},{5,1},{6,2},{7,3},{8,12},{9,13},{10,... | collective-permute-start | bytes 393224 | tf_op jit(solution)/shard_map/ppermute | solution.py:436
  62.5 1.0 collective-permute-start.2
  63.4 2.3 %collective-permute-start.3 = (bf16[2,64,512]{2,1,0:T(8,128)(2,1)S(1)}, bf16[2,64,512]{2,1,0:T(8,128)(2,1)S(1)}, u32[]{:S(2)}, u32[]{:S(2)}) collective-permute-start(bf16[2,64,512]{2,1,0:T(8,128)(2,1)S(1)} %bitcast.37), channel_id=1, source_target_pairs={{0,6},{1,7},{2,0},{3,1},{4,2},{5,3},{6,4},{7,5},{8,14},{9,15},{10,... | collective-permute-start | bytes 393224 | tf_op jit(solution)/shard_map/ppermute | solution.py:436
  65.7 5.0 %latent_gradient.2.refs_0_ = bf16[2048,1024]{1,0:T(8,128)(2,1)} custom-call(bf16[2048,512]{1,0:T(8,128)(2,1)S(1)} %get-tuple-element.30.left_ref, bf16[2048,512]{1,0:T(8,128)(2,1)S(1)} %get-tuple-element.38.right_ref, bf16[1024,1024]{1,0:T(8,128)(2,1)} %weight_hbm.3), custom_call_target="tpu_custom_call" | custom-call | flops 2147483648 | bytes 5242880 | tf_op jit(solution)/shard_map/latent_gradient/pallas_call | solution.py:410
  70.7 0.0 collective-permute-done.4
  70.7 0.0 collective-permute-done.2
  70.7 0.0 collective-permute-done.3
  70.7 0.1 fusion.5
  70.8 0.6 collective-permute-start.6
  71.5 0.3 collective-permute-start.5
  71.7 0.0 collective-permute-done.1
  71.7 0.2 add_convert_fusion
  71.9 0.1 fusion.6
  72.0 1.1 %collective-permute-start.13 = (bf16[2,64,640]{2,1,0:T(8,128)(2,1)S(1)}, bf16[2,64,640]{2,1,0:T(8,128)(2,1)S(1)}, u32[]{:S(2)}, u32[]{:S(2)}) collective-permute-start(bf16[2,64,640]{2,1,0:T(8,128)(2,1)S(1)} %bitcast.36), channel_id=1, source_target_pairs={{0,4},{1,5},{2,6},{3,7},{4,0},{5,1},{6,2},{7,3},{8,12},{9,13},{10,... | collective-permute-start | bytes 491528 | tf_op jit(solution)/shard_map/ppermute | solution.py:436
  73.0 1.7 %collective-permute-start.11 = (bf16[2,64,640]{2,1,0:T(8,128)(2,1)S(1)}, bf16[2,64,640]{2,1,0:T(8,128)(2,1)S(1)}, u32[]{:S(2)}, u32[]{:S(2)}) collective-permute-start(bf16[2,64,640]{2,1,0:T(8,128)(2,1)S(1)} %bitcast.35), channel_id=1, source_target_pairs={{0,2},{1,3},{2,4},{3,5},{4,6},{5,7},{6,0},{7,1},{8,10},{9,11},{10,... | collective-permute-start | bytes 491528 | tf_op jit(solution)/shard_map/ppermute | solution.py:436
  74.7 1.6 %collective-permute-start.12 = (bf16[2,64,640]{2,1,0:T(8,128)(2,1)S(1)}, bf16[2,64,640]{2,1,0:T(8,128)(2,1)S(1)}, u32[]{:S(2)}, u32[]{:S(2)}) collective-permute-start(bf16[2,64,640]{2,1,0:T(8,128)(2,1)S(1)} %bitcast.34), channel_id=1, source_target_pairs={{0,6},{1,7},{2,0},{3,1},{4,2},{5,3},{6,4},{7,5},{8,14},{9,15},{10,... | collective-permute-start | bytes 491528 | tf_op jit(solution)/shard_map/ppermute | solution.py:436
  76.2 5.0 %latent_gradient.3 = bf16[2048,1024]{1,0:T(8,128)(2,1)} custom-call(bf16[2048,512]{1,0:T(8,128)(2,1)S(1)} %get-tuple-element.30.left_ref, bf16[2048,512]{1,0:T(8,128)(2,1)S(1)} %get-tuple-element.38.right_ref, bf16[1024,1024]{1,0:T(8,128)(2,1)} %weight_hbm.3, bf16[2048,1024]{1,0:T(8,128)(2,1)} %latent_gradient.2.refs_0_), custom_call_target="tpu_custom_call", output_to_operand_aliasing={{}: (3, {})} | custom-call | flops 2147483648 | bytes 5242880 | tf_op jit(solution)/shard_map/latent_gradient/pallas_call | solution.py:410
  81.3 0.0 collective-permute-done.13
  81.3 4.0 %collective-permute-start.7 = (bf16[64,512]{1,0:T(8,128)(2,1)S(1)}, bf16[64,512]{1,0:T(8,128)(2,1)S(1)}, u32[]{:S(2)}, u32[]{:S(2)}) collective-permute-start(bf16[64,512]{1,0:T(8,128)(2,1)S(1)} %get-tuple-element.52), channel_id=1, source_target_pairs={{0,16},{1,17},{2,18},{3,19},{4,20},{5,21},{6,22},{7,23},{8,24},{9,... | collective-permute-start | bytes 196616 | tf_op jit(solution)/shard_map/ppermute | solution.py:436
  85.3 0.0 collective-permute-done.11
  85.3 0.0 collective-permute-done.12
  85.3 0.1 fusion.2
  85.4 0.7 collective-permute-start.15
  86.0 0.0 collective-permute-start.14
  86.0 1.5 %collective-permute-done.7 = bf16[64,512]{1,0:T(8,128)(2,1)S(1)} collective-permute-done((bf16[64,512]{1,0:T(8,128)(2,1)S(1)}, bf16[64,512]{1,0:T(8,128)(2,1)S(1)}, u32[]{:S(2)}, u32[]{:S(2)}) %collective-permute-start.7) | collective-permute-done | bytes 65568 | tf_op jit(solution)/shard_map/ppermute | solution.py:436
  87.5 3.5 %collective-permute-start.16 = (bf16[64,640]{1,0:T(8,128)(2,1)S(1)}, bf16[64,640]{1,0:T(8,128)(2,1)S(1)}, u32[]{:S(2)}, u32[]{:S(2)}) collective-permute-start(bf16[64,640]{1,0:T(8,128)(2,1)S(1)} %get-tuple-element.50), channel_id=1, source_target_pairs={{0,16},{1,17},{2,18},{3,19},{4,20},{5,21},{6,22},{7,23},{8,24},{9,... | collective-permute-start | bytes 245768 | tf_op jit(solution)/shard_map/ppermute | solution.py:436
  91.0 0.0 collective-permute-done.6
  91.0 0.0 collective-permute-done.5
  91.1 0.9 collective-permute-start.10
  92.0 2.1 %collective-permute-start.9 = (bf16[64,512]{1,0:T(8,128)(2,1)S(1)}, bf16[64,512]{1,0:T(8,128)(2,1)S(1)}, u32[]{:S(2)}, u32[]{:S(2)}) collective-permute-start(bf16[64,512]{1,0:T(8,128)(2,1)S(1)} %add_convert_fusion.3), channel_id=1, source_target_pairs={{0,96},{1,97},{2,98},{3,99},{4,100},{5,101},{6,102},{7,103},{8,104... | collective-permute-start | bytes 196616 | tf_op jit(solution)/shard_map/ppermute | solution.py:436
  94.1 0.0 collective-permute-done.16
  94.1 0.0 collective-permute-start.8
  94.1 0.0 collective-permute-done.15
  94.1 0.0 collective-permute-done.14
  94.1 2.7 %collective-permute-start.19 = (bf16[64,640]{1,0:T(8,128)(2,1)S(1)}, bf16[64,640]{1,0:T(8,128)(2,1)S(1)}, u32[]{:S(2)}, u32[]{:S(2)}) collective-permute-start(bf16[64,640]{1,0:T(8,128)(2,1)S(1)} %add_convert_fusion.2), channel_id=1, source_target_pairs={{0,64},{1,65},{2,66},{3,67},{4,68},{5,69},{6,70},{7,71},{8,72},{9,... | collective-permute-start | bytes 245768 | tf_op jit(solution)/shard_map/ppermute | solution.py:436
  96.8 0.8 collective-permute-start.18
  97.7 0.0 collective-permute-done.10
  97.7 1.2 %collective-permute-start.17 = (bf16[64,640]{1,0:T(8,128)(2,1)S(1)}, bf16[64,640]{1,0:T(8,128)(2,1)S(1)}, u32[]{:S(2)}, u32[]{:S(2)}) collective-permute-start(bf16[64,640]{1,0:T(8,128)(2,1)S(1)} %add_convert_fusion.2), channel_id=1, source_target_pairs={{0,32},{1,33},{2,34},{3,35},{4,36},{5,37},{6,38},{7,39},{8,40},{9,... | collective-permute-start | bytes 245768 | tf_op jit(solution)/shard_map/ppermute | solution.py:436
  98.9 0.0 collective-permute-done.9
  98.9 1.5 %collective-permute-done.8 = bf16[64,512]{1,0:T(8,128)(2,1)S(1)} collective-permute-done((bf16[64,512]{1,0:T(8,128)(2,1)S(1)}, bf16[64,512]{1,0:T(8,128)(2,1)S(1)}, u32[]{:S(2)}, u32[]{:S(2)}) %collective-permute-start.8) | collective-permute-done | bytes 65568 | tf_op jit(solution)/shard_map/ppermute | solution.py:436
  100.5 0.0 collective-permute-done.19
  100.5 1.1 %collective-permute-done.18 = bf16[64,640]{1,0:T(8,128)(2,1)S(1)} collective-permute-done((bf16[64,640]{1,0:T(8,128)(2,1)S(1)}, bf16[64,640]{1,0:T(8,128)(2,1)S(1)}, u32[]{:S(2)}, u32[]{:S(2)}) %collective-permute-start.18) | collective-permute-done | bytes 81952 | tf_op jit(solution)/shard_map/ppermute | solution.py:436
  101.6 1.8 %collective-permute-done.17 = bf16[64,640]{1,0:T(8,128)(2,1)S(1)} collective-permute-done((bf16[64,640]{1,0:T(8,128)(2,1)S(1)}, bf16[64,640]{1,0:T(8,128)(2,1)S(1)}, u32[]{:S(2)}, u32[]{:S(2)}) %collective-permute-start.17) | collective-permute-done | bytes 81952 | tf_op jit(solution)/shard_map/ppermute | solution.py:436
  103.4 0.6 slice_multiply_fusion
  104.0 0.7 maximum_multiply_fusion
  (12 shorter events, 0.2 us)
Async XLA Ops:
  0.6 30.9 %copy-start.3 = (f32[2048]{0:T(1024)S(1)}, f32[2048]{0:T(1024)}, u32[]{:S(2)}) copy-start(f32[2048]{0:T(1024)} %param.9) | copy-start | bytes 24580
  12.7 18.9 %copy-start.2 = (f32[100,2048]{1,0:T(8,128)S(1)}, f32[100,2048]{1,0:T(8,128)}, u32[]{:S(2)}) copy-start(f32[100,2048]{1,0:T(8,128)} %observed_ref.1) | copy-start | bytes 2457604
  13.6 17.9 %all-to-all-start = ((f16[8,112,256]{2,1,0:T(8,128)(2,1)}), f16[8,112,256]{2,1,0:T(8,128)(2,1)S(1)}, u32[]{:S(2)}, u32[]{:S(2)}) async-start(f16[8,112,256]{2,1,0:T(8,128)(2,1)} %multiply_convert_fusion), calls=%async_computation | async-start | bytes 917504 | tf_op jit(solution)/shard_map/all_to_all | solution.py:475
  33.5 13.4 %all-to-all-start.1 = ((bf16[8,112,256]{2,1,0:T(8,128)(2,1)}), bf16[8,112,256]{2,1,0:T(8,128)(2,1)S(1)}, u32[]{:S(2)}, u32[]{:S(2)}) async-start(bf16[8,112,256]{2,1,0:T(8,128)(2,1)} %pairs.1), calls=%async_computation.1 | async-start | bytes 917504 | tf_op jit(solution)/shard_map/all_to_all | solution.py:478
  36.9 2.2 %copy-start.1 = (bf16[1,2048,1024]{2,1,0:T(8,128)(2,1)S(1)}, bf16[1,2048,1024]{2,1,0:T(8,128)(2,1)}, u32[]{:S(2)}) copy-start(bf16[1,2048,1024]{2,1,0:T(8,128)(2,1)} %param.5) | copy-start | bytes 12582916
  40.3 2.0 %copy-start = (bf16[1024,2048]{1,0:T(8,128)(2,1)}, bf16[1024,2048]{1,0:T(8,128)(2,1)S(1)}, u32[]{:S(2)}) copy-start(bf16[1024,2048]{1,0:T(8,128)(2,1)S(1)} %turned.1.turned_hbm) | copy-start | bytes 12582916
  52.1 6.2 %collective-permute-start = (bf16[512,512]{1,0:T(8,128)(2,1)S(1)}, bf16[512,512]{1,0:T(8,128)(2,1)S(1)}, u32[]{:S(2)}, u32[]{:S(2)}) collective-permute-start(bf16[512,512]{1,0:T(8,128)(2,1)S(1)} %get-tuple-element.28), channel_id=1, source_target_pairs={{0,1},{1,0},{2,3},{3,2},{4,5},{5,4},{6,7},{7,6},{8,9},{9,8},{10,11... | collective-permute-start | bytes 1572872 | tf_op jit(solution)/shard_map/ppermute | solution.py:436
  57.7 14.0 %collective-permute-start.1 = (bf16[512,640]{1,0:T(8,128)(2,1)S(1)}, bf16[512,640]{1,0:T(8,128)(2,1)S(1)}, u32[]{:S(2)}, u32[]{:S(2)}) collective-permute-start(bf16[512,640]{1,0:T(8,128)(2,1)S(1)} %get-tuple-element.36), channel_id=1, source_target_pairs={{0,1},{1,0},{2,3},{3,2},{4,5},{5,4},{6,7},{7,6},{8,9},{9,8},{10,11... | collective-permute-start | bytes 1966088 | tf_op jit(solution)/shard_map/ppermute | solution.py:436
  58.5 12.2 %collective-permute-start.4 = (bf16[2,64,512]{2,1,0:T(8,128)(2,1)S(1)}, bf16[2,64,512]{2,1,0:T(8,128)(2,1)S(1)}, u32[]{:S(2)}, u32[]{:S(2)}) collective-permute-start(bf16[2,64,512]{2,1,0:T(8,128)(2,1)S(1)} %bitcast.39), channel_id=1, source_target_pairs={{0,4},{1,5},{2,6},{3,7},{4,0},{5,1},{6,2},{7,3},{8,12},{9,13},{10,... | collective-permute-start | bytes 393224 | tf_op jit(solution)/shard_map/ppermute | solution.py:436
  62.5 8.3 %collective-permute-start.2 = (bf16[2,64,512]{2,1,0:T(8,128)(2,1)S(1)}, bf16[2,64,512]{2,1,0:T(8,128)(2,1)S(1)}, u32[]{:S(2)}, u32[]{:S(2)}) collective-permute-start(bf16[2,64,512]{2,1,0:T(8,128)(2,1)S(1)} %bitcast.38), channel_id=1, source_target_pairs={{0,2},{1,3},{2,4},{3,5},{4,6},{5,7},{6,0},{7,1},{8,10},{9,11},{10,... | collective-permute-start | bytes 393224 | tf_op jit(solution)/shard_map/ppermute | solution.py:436
  63.4 7.3 %collective-permute-start.3 = (bf16[2,64,512]{2,1,0:T(8,128)(2,1)S(1)}, bf16[2,64,512]{2,1,0:T(8,128)(2,1)S(1)}, u32[]{:S(2)}, u32[]{:S(2)}) collective-permute-start(bf16[2,64,512]{2,1,0:T(8,128)(2,1)S(1)} %bitcast.37), channel_id=1, source_target_pairs={{0,6},{1,7},{2,0},{3,1},{4,2},{5,3},{6,4},{7,5},{8,14},{9,15},{10,... | collective-permute-start | bytes 393224 | tf_op jit(solution)/shard_map/ppermute | solution.py:436
  70.8 20.2 %collective-permute-start.6 = (bf16[64,512]{1,0:T(8,128)(2,1)S(1)}, bf16[64,512]{1,0:T(8,128)(2,1)S(1)}, u32[]{:S(2)}, u32[]{:S(2)}) collective-permute-start(bf16[64,512]{1,0:T(8,128)(2,1)S(1)} %get-tuple-element.51), channel_id=1, source_target_pairs={{0,24},{1,25},{2,26},{3,27},{4,28},{5,29},{6,30},{7,31},{8,16},{9,... | collective-permute-start | bytes 196616 | tf_op jit(solution)/shard_map/ppermute | solution.py:436
  71.5 19.6 %collective-permute-start.5 = (bf16[64,512]{1,0:T(8,128)(2,1)S(1)}, bf16[64,512]{1,0:T(8,128)(2,1)S(1)}, u32[]{:S(2)}, u32[]{:S(2)}) collective-permute-start(bf16[64,512]{1,0:T(8,128)(2,1)S(1)} %get-tuple-element.51), channel_id=1, source_target_pairs={{0,8},{1,9},{2,10},{3,11},{4,12},{5,13},{6,14},{7,15},{8,0},{9,1},... | collective-permute-start | bytes 196616 | tf_op jit(solution)/shard_map/ppermute | solution.py:436
  72.0 9.3 %collective-permute-start.13 = (bf16[2,64,640]{2,1,0:T(8,128)(2,1)S(1)}, bf16[2,64,640]{2,1,0:T(8,128)(2,1)S(1)}, u32[]{:S(2)}, u32[]{:S(2)}) collective-permute-start(bf16[2,64,640]{2,1,0:T(8,128)(2,1)S(1)} %bitcast.36), channel_id=1, source_target_pairs={{0,4},{1,5},{2,6},{3,7},{4,0},{5,1},{6,2},{7,3},{8,12},{9,13},{10,... | collective-permute-start | bytes 491528 | tf_op jit(solution)/shard_map/ppermute | solution.py:436
  73.0 12.2 %collective-permute-start.11 = (bf16[2,64,640]{2,1,0:T(8,128)(2,1)S(1)}, bf16[2,64,640]{2,1,0:T(8,128)(2,1)S(1)}, u32[]{:S(2)}, u32[]{:S(2)}) collective-permute-start(bf16[2,64,640]{2,1,0:T(8,128)(2,1)S(1)} %bitcast.35), channel_id=1, source_target_pairs={{0,2},{1,3},{2,4},{3,5},{4,6},{5,7},{6,0},{7,1},{8,10},{9,11},{10,... | collective-permute-start | bytes 491528 | tf_op jit(solution)/shard_map/ppermute | solution.py:436
  74.7 10.6 %collective-permute-start.12 = (bf16[2,64,640]{2,1,0:T(8,128)(2,1)S(1)}, bf16[2,64,640]{2,1,0:T(8,128)(2,1)S(1)}, u32[]{:S(2)}, u32[]{:S(2)}) collective-permute-start(bf16[2,64,640]{2,1,0:T(8,128)(2,1)S(1)} %bitcast.34), channel_id=1, source_target_pairs={{0,6},{1,7},{2,0},{3,1},{4,2},{5,3},{6,4},{7,5},{8,14},{9,15},{10,... | collective-permute-start | bytes 491528 | tf_op jit(solution)/shard_map/ppermute | solution.py:436
  81.3 6.3 %collective-permute-start.7 = (bf16[64,512]{1,0:T(8,128)(2,1)S(1)}, bf16[64,512]{1,0:T(8,128)(2,1)S(1)}, u32[]{:S(2)}, u32[]{:S(2)}) collective-permute-start(bf16[64,512]{1,0:T(8,128)(2,1)S(1)} %get-tuple-element.52), channel_id=1, source_target_pairs={{0,16},{1,17},{2,18},{3,19},{4,20},{5,21},{6,22},{7,23},{8,24},{9,... | collective-permute-start | bytes 196616 | tf_op jit(solution)/shard_map/ppermute | solution.py:436
  85.4 8.7 %collective-permute-start.15 = (bf16[64,640]{1,0:T(8,128)(2,1)S(1)}, bf16[64,640]{1,0:T(8,128)(2,1)S(1)}, u32[]{:S(2)}, u32[]{:S(2)}) collective-permute-start(bf16[64,640]{1,0:T(8,128)(2,1)S(1)} %get-tuple-element.49), channel_id=1, source_target_pairs={{0,24},{1,25},{2,26},{3,27},{4,28},{5,29},{6,30},{7,31},{8,16},{9,... | collective-permute-start | bytes 245768 | tf_op jit(solution)/shard_map/ppermute | solution.py:436
  86.0 8.0 %collective-permute-start.14 = (bf16[64,640]{1,0:T(8,128)(2,1)S(1)}, bf16[64,640]{1,0:T(8,128)(2,1)S(1)}, u32[]{:S(2)}, u32[]{:S(2)}) collective-permute-start(bf16[64,640]{1,0:T(8,128)(2,1)S(1)} %get-tuple-element.49), channel_id=1, source_target_pairs={{0,8},{1,9},{2,10},{3,11},{4,12},{5,13},{6,14},{7,15},{8,0},{9,1},... | collective-permute-start | bytes 245768 | tf_op jit(solution)/shard_map/ppermute | solution.py:436
  87.5 6.5 %collective-permute-start.16 = (bf16[64,640]{1,0:T(8,128)(2,1)S(1)}, bf16[64,640]{1,0:T(8,128)(2,1)S(1)}, u32[]{:S(2)}, u32[]{:S(2)}) collective-permute-start(bf16[64,640]{1,0:T(8,128)(2,1)S(1)} %get-tuple-element.50), channel_id=1, source_target_pairs={{0,16},{1,17},{2,18},{3,19},{4,20},{5,21},{6,22},{7,23},{8,24},{9,... | collective-permute-start | bytes 245768 | tf_op jit(solution)/shard_map/ppermute | solution.py:436
  91.1 6.6 %collective-permute-start.10 = (bf16[64,512]{1,0:T(8,128)(2,1)S(1)}, bf16[64,512]{1,0:T(8,128)(2,1)S(1)}, u32[]{:S(2)}, u32[]{:S(2)}) collective-permute-start(bf16[64,512]{1,0:T(8,128)(2,1)S(1)} %add_convert_fusion.3), channel_id=1, source_target_pairs={{0,64},{1,65},{2,66},{3,67},{4,68},{5,69},{6,70},{7,71},{8,72},{9,... | collective-permute-start | bytes 196616 | tf_op jit(solution)/shard_map/ppermute | solution.py:436
  92.0 6.9 %collective-permute-start.9 = (bf16[64,512]{1,0:T(8,128)(2,1)S(1)}, bf16[64,512]{1,0:T(8,128)(2,1)S(1)}, u32[]{:S(2)}, u32[]{:S(2)}) collective-permute-start(bf16[64,512]{1,0:T(8,128)(2,1)S(1)} %add_convert_fusion.3), channel_id=1, source_target_pairs={{0,96},{1,97},{2,98},{3,99},{4,100},{5,101},{6,102},{7,103},{8,104... | collective-permute-start | bytes 196616 | tf_op jit(solution)/shard_map/ppermute | solution.py:436
  94.1 6.4 %collective-permute-start.8 = (bf16[64,512]{1,0:T(8,128)(2,1)S(1)}, bf16[64,512]{1,0:T(8,128)(2,1)S(1)}, u32[]{:S(2)}, u32[]{:S(2)}) collective-permute-start(bf16[64,512]{1,0:T(8,128)(2,1)S(1)} %add_convert_fusion.3), channel_id=1, source_target_pairs={{0,32},{1,33},{2,34},{3,35},{4,36},{5,37},{6,38},{7,39},{8,40},{9,... | collective-permute-start | bytes 196616 | tf_op jit(solution)/shard_map/ppermute | solution.py:436
  94.1 6.3 %collective-permute-start.19 = (bf16[64,640]{1,0:T(8,128)(2,1)S(1)}, bf16[64,640]{1,0:T(8,128)(2,1)S(1)}, u32[]{:S(2)}, u32[]{:S(2)}) collective-permute-start(bf16[64,640]{1,0:T(8,128)(2,1)S(1)} %add_convert_fusion.2), channel_id=1, source_target_pairs={{0,64},{1,65},{2,66},{3,67},{4,68},{5,69},{6,70},{7,71},{8,72},{9,... | collective-permute-start | bytes 245768 | tf_op jit(solution)/shard_map/ppermute | solution.py:436
  96.8 4.7 %collective-permute-start.18 = (bf16[64,640]{1,0:T(8,128)(2,1)S(1)}, bf16[64,640]{1,0:T(8,128)(2,1)S(1)}, u32[]{:S(2)}, u32[]{:S(2)}) collective-permute-start(bf16[64,640]{1,0:T(8,128)(2,1)S(1)} %add_convert_fusion.2), channel_id=1, source_target_pairs={{0,96},{1,97},{2,98},{3,99},{4,100},{5,101},{6,102},{7,103},{8,104... | collective-permute-start | bytes 245768 | tf_op jit(solution)/shard_map/ppermute | solution.py:436
  97.7 5.7 %collective-permute-start.17 = (bf16[64,640]{1,0:T(8,128)(2,1)S(1)}, bf16[64,640]{1,0:T(8,128)(2,1)S(1)}, u32[]{:S(2)}, u32[]{:S(2)}) collective-permute-start(bf16[64,640]{1,0:T(8,128)(2,1)S(1)} %add_convert_fusion.2), channel_id=1, source_target_pairs={{0,32},{1,33},{2,34},{3,35},{4,36},{5,37},{6,38},{7,39},{8,40},{9,... | collective-permute-start | bytes 245768 | tf_op jit(solution)/shard_map/ppermute | solution.py:436

commit v5 on v4

--- a/solution.py
+++ b/solution.py
@@ -33,7 +33,7 @@
     return pl.CostEstimate(flops=flops, bytes_accessed=nbytes, transcendentals=trans)
 
 
-CHUNKS = (512, 512, 512, 512)
+CHUNKS = (512, 512, 512, 256, 256)
 FCOLS = 512
 
 
@@ -239,22 +239,21 @@
     )(grid, latent)
 
 
-def first_product(turned_ref, slope_ref, padded_ref, turn_ref, pre_ref, send_ref, keep_ref, begin, ready):
-    nodes, span = pre_ref.shape
+def gradient_of_pre(slope_ref, padded_ref, turn_ref, pre_ref, columns, begin):
+    for start in range(0, pre_ref.shape[0], ROWS):
+        rows = slice(start, start + ROWS)
+        grad_hidden = lax.dot_general(turn_ref[rows, :], padded_ref[columns, :], NT, preferred_element_type=f32)
+        grad_pre = (grad_hidden * slope_ref[rows, columns].astype(f32)).astype(bf16)
+        pre_ref[rows, columns.start - begin : columns.stop - begin] = grad_pre
+
+
+def first_product(turned_ref, pre_ref, send_ref, keep_ref, rows):
+    span = pre_ref.shape[1]
     half = turned_ref.shape[0] // 2
-    for column in range(0, span, COLS):
-        columns = slice(column, column + COLS)
-        source = slice(begin + column, begin + column + COLS)
-        for start in range(0, nodes, ROWS):
-            rows = slice(start, start + ROWS)
-            grad_hidden = lax.dot_general(turn_ref[rows, :], padded_ref[source, :], NT, preferred_element_type=f32)
-            pre_ref[rows, columns] = (grad_hidden * slope_ref[rows, columns].astype(f32)).astype(bf16)
-    ready()
-    for column in range(0, span, COLS):
-        columns = slice(column, column + COLS)
-        for out_ref, base in ((send_ref, 0), (keep_ref, half)):
-            part = jnp.dot(turned_ref[base : base + half, :], pre_ref[:, columns], preferred_element_type=f32)
-            out_ref[:, columns] = part.astype(bf16)
+    out_ref = send_ref if rows.start < half else keep_ref
+    at = rows.start % half
+    part = jnp.dot(turned_ref[rows, :], pre_ref[...], preferred_element_type=f32)
+    out_ref[at : at + rows.stop - rows.start, :span] = part.astype(bf16)
 
 
 def backward_a_kernel(
@@ -269,52 +268,71 @@
     flat_ref,
     turned_ref,
     slope_ref,
-    turned_sem,
-    slope_sem,
+    turned_sems,
+    slope_sems,
 ):
     span = pre_ref.shape[1]
-    slope_load = pltpu.make_async_copy(slope_hbm.at[:, pl.ds(0, span)], slope_ref, slope_sem)
-    turned_load = pltpu.make_async_copy(turned_hbm, turned_ref, turned_sem)
-    slope_load.start()
-    turned_load.start()
+    width = slope_ref.shape[1]
+    column_parts = [slice(start, start + COLS) for start in range(0, width, COLS)]
+    row_parts = [slice(start, start + 256) for start in range(0, width, 256)]
+    slope_loads = [
+        pltpu.make_async_copy(
+            slope_hbm.at[:, pl.ds(part.start, COLS)], slope_ref.at[:, pl.ds(part.start, COLS)], slope_sems.at[index]
+        )
+        for index, part in enumerate(column_parts)
+    ]
+    turned_loads = [
+        pltpu.make_async_copy(
+            turned_hbm.at[pl.ds(part.start, 256)], turned_ref.at[pl.ds(part.start, 256)], turned_sems.at[index]
+        )
+        for index, part in enumerate(row_parts)
+    ]
+    now = span // COLS
+    for load in slope_loads[:now] + turned_loads + slope_loads[now:]:
+        load.start()
     for share in range(low_ref.shape[0]):
         columns = slice(share * SHARE, (share + 1) * SHARE)
         low = jnp.concatenate([low_ref[share], jnp.zeros((WIDE - TALL, SHARE), bf16)], axis=0)
         flat_ref[:, columns] = low
         turn_ref[columns, :] = low.T
-    slope_load.wait()
-    first_product(
-        turned_ref, slope_ref, padded_ref, turn_ref, pre_ref, send_ref, keep_ref, 0, turned_load.wait
-    )
+    for load, columns in zip(slope_loads[:now], column_parts):
+        load.wait()
+        gradient_of_pre(slope_ref, padded_ref, turn_ref, pre_ref, columns, 0)
+    for load, rows in zip(turned_loads, row_parts):
+        load.wait()
+        first_product(turned_ref, pre_ref, send_ref, keep_ref, rows)
+    for load in slope_loads[now:]:
+        load.wait()
 
 
 def backward_b_kernel(
     grid_ref,
     turned_ref,
-    slope_hbm,
+    slope_ref,
     hidden_hbm,
+    weight_hbm,
     padded_ref,
     turn_ref,
     flat_ref,
     pre_ref,
     send_ref,
     keep_ref,
+    weight_ref,
     second_ref,
-    slope_ref,
     hidden_ref,
-    slope_sem,
     hidden_sem,
+    weight_sem,
 ):
     width = hidden_ref.shape[1]
     span = pre_ref.shape[1]
-    slope_load = pltpu.make_async_copy(slope_hbm.at[:, pl.ds(width - span, span)], slope_ref, slope_sem)
     hidden_load = pltpu.make_async_copy(hidden_hbm, hidden_ref, hidden_sem)
-    slope_load.start()
+    weight_load = pltpu.make_async_copy(weight_hbm, weight_ref, weight_sem)
     hidden_load.start()
-    slope_load.wait()
-    first_product(
-        turned_ref, slope_ref, padded_ref, turn_ref, pre_ref, send_ref, keep_ref, width - span, lambda: None
-    )
+    weight_load.start()
+    for start in range(width - span, width, COLS):
+        gradient_of_pre(slope_ref, padded_ref, turn_ref, pre_ref, slice(start, start + COLS), width - span)
+    for start in range(0, width, 512):
+        first_product(turned_ref, pre_ref, send_ref, keep_ref, slice(start, start + 512))
     hidden_load.wait()
     for column in range(0, width, COLS):
         columns = slice(column, column + COLS)
@@ -326,6 +344,7 @@
         other = pl.multiple_of(group * 128 + 64 * (1 - core), 64)
         keep_ref[pl.ds(at, 64), span:] = second_ref[pl.ds(mine, 64), :]
         send_ref[pl.ds(at, 64), span:] = second_ref[pl.ds(other, 64), :]
+    weight_load.wait()
 
 
 def backward_a(low, turned_latent, slope, padded):
@@ -334,7 +353,7 @@
     return pl.pallas_call(
         backward_a_kernel,
         in_specs=[vmem, anywhere, anywhere, vmem],
-        out_specs=[vmem] * 6,
+        out_specs=[vmem] * 7,
         out_shape=[
             jax.ShapeDtypeStruct((nodes, half), bf16),
             jax.ShapeDtypeStruct((half, half), bf16),
@@ -342,11 +361,11 @@
             jax.ShapeDtypeStruct((nodes, WIDE), bf16),
             jax.ShapeDtypeStruct((WIDE, nodes), bf16),
             jax.ShapeDtypeStruct((width, nodes), bf16),
+            jax.ShapeDtypeStruct((nodes, width), bf16),
         ],
         scratch_shapes=[
-            pltpu.VMEM((nodes, half), bf16),
-            pltpu.SemaphoreType.DMA,
-            pltpu.SemaphoreType.DMA,
+            pltpu.SemaphoreType.DMA((width // 256,)),
+            pltpu.SemaphoreType.DMA((width // COLS,)),
         ],
         compiler_params=params(16),
         cost_estimate=cost(nodes * width * (width + WIDE), 8 << 20),
@@ -354,21 +373,21 @@
     )(low, pinned(turned_latent), pinned(slope), padded)
 
 
-def backward_b(grid, turned_latent, slope, hidden, padded, turn, flat):
+def backward_b(grid, turned_latent, slope, hidden, weight, padded, turn, flat):
     nodes, width = slope.shape
     half = width // 2
     return pl.pallas_call(
         backward_b_kernel,
-        in_specs=[smem, vmem, anywhere, anywhere] + [vmem] * 3,
-        out_specs=[vmem] * 3,
+        in_specs=[smem, vmem, vmem, anywhere, anywhere] + [vmem] * 3,
+        out_specs=[vmem] * 4,
         out_shape=[
             jax.ShapeDtypeStruct((nodes, half), bf16),
             jax.ShapeDtypeStruct((half, half + WIDE), bf16),
             jax.ShapeDtypeStruct((half, half + WIDE), bf16),
+            jax.ShapeDtypeStruct((width, width), bf16),
         ],
         scratch_shapes=[
             pltpu.VMEM((width, WIDE), bf16),
-            pltpu.VMEM((nodes, half), bf16),
             pltpu.VMEM((nodes, width), bf16),
             pltpu.SemaphoreType.DMA,
             pltpu.SemaphoreType.DMA,
@@ -376,26 +395,22 @@
         compiler_params=params(16),
         cost_estimate=cost(nodes * width * (width + 3 * WIDE), 8 << 20),
         name="backward_b",
-    )(grid, turned_latent, pinned(slope), pinned(hidden), padded, turn, flat)
-
-
-def latent_kernel(left_ref, right_ref, weight_hbm, *refs, begin):
-    out_ref, weight_ref, result_ref, weight_sem, sems = refs[-5:]
+    )(grid, turned_latent, slope, pinned(hidden), pinned(weight), padded, turn, flat)
+
+
+def latent_kernel(left_ref, right_ref, weight_ref, out_ref, result_ref, sems):
     nodes, half = left_ref.shape
     width = weight_ref.shape[1]
-    load = pltpu.make_async_copy(weight_hbm, weight_ref, weight_sem)
-    load.start()
-    load.wait()
     stores = []
-    for row in range(0, nodes // 2, ROWS):
-        rows = slice(begin + row, begin + row + ROWS)
+    for row in range(0, nodes, ROWS):
+        rows = slice(row, row + ROWS)
         for start in range(0, width, COLS):
             columns = slice(start, start + COLS)
             left = lax.dot_general(left_ref[rows, :], weight_ref[columns, :half], NT, preferred_element_type=f32)
             right = lax.dot_general(right_ref[rows, :], weight_ref[columns, half:], NT, preferred_element_type=f32)
-            result_ref[row : row + ROWS, columns] = (left + right).astype(bf16)
+            result_ref[rows, columns] = (left + right).astype(bf16)
         store = pltpu.make_async_copy(
-            result_ref.at[pl.ds(row, ROWS)], out_ref.at[pl.ds(begin + row, ROWS)], sems.at[row // ROWS]
+            result_ref.at[pl.ds(row, ROWS)], out_ref.at[pl.ds(row, ROWS)], sems.at[row // ROWS]
         )
         store.start()
         stores.append(store)
@@ -403,26 +418,19 @@
         store.wait()
 
 
-def latent_gradient(left, right, weight, begin, so_far=None):
+def latent_gradient(left, right, weight):
     nodes = left.shape[0]
     width = weight.shape[1]
-    more = [] if so_far is None else [so_far]
     return pl.pallas_call(
-        functools.partial(latent_kernel, begin=begin),
-        in_specs=[vmem, vmem, anywhere] + [anywhere] * len(more),
+        latent_kernel,
+        in_specs=[vmem] * 3,
         out_specs=anywhere,
         out_shape=pltpu.HBM((nodes, width), bf16),
-        input_output_aliases={3: 0} if more else {},
-        scratch_shapes=[
-            pltpu.VMEM((width, width), bf16),
-            pltpu.VMEM((nodes // 2, width), bf16),
-            pltpu.SemaphoreType.DMA,
-            pltpu.SemaphoreType.DMA((nodes // 2 // ROWS,)),
-        ],
+        scratch_shapes=[pltpu.VMEM((nodes, width), bf16), pltpu.SemaphoreType.DMA((nodes // ROWS,))],
         compiler_params=params(12),
-        cost_estimate=cost(nodes * width * width, 5 << 20),
+        cost_estimate=cost(2 * nodes * width * width, 10 << 20),
         name="latent_gradient",
-    )(left, right, pinned(weight), *more)
+    )(left, right, weight)
 
 
 def moved(value, move):
@@ -448,16 +456,19 @@
     return summed(keep, [got]).astype(bf16)
 
 
-def over_chips(rows):
+def over_z(rows):
     blocks = rows.reshape(4, 2, 64, rows.shape[1])
     got = [moved(blocks[k], lambda y, x, z, c, k=k: (y, x, (z + k) % 4, c)) for k in (1, 3, 2)]
-    blocks = summed(blocks[0], got).astype(bf16)
+    return summed(blocks[0], got).astype(bf16)
+
+
+def over_x_and_y(blocks):
     got = [
         moved(blocks[0] if k == 2 else blocks[1], lambda y, x, z, c, k=k: (y, x ^ k, z, c))
         for k in (1, 3, 2)
     ]
     block = summed(blocks[0], got).astype(bf16)
-    got = [moved(block, lambda y, x, z, c, k=k: ((y + k) % 4, x, z, c)) for k in (1, 3, 2)]
+    got = [moved(block, lambda y, x, z, c, k=k: (y ^ k, x, z, c)) for k in (1, 3, 2)]
     return summed(block, got)
 
 
@@ -476,18 +487,18 @@
     turned_latent = turned(late_grid, latent)
     low = pairs(place, 4.0 * blocks.astype(f32), observed, node_area_weight.reshape(1, nodes))
     low = lax.all_to_all(low, "member", 0, 0, tiled=True)
-    pre_a, send_a, keep_a, turn, flat, turned_latent = backward_a(low, turned_latent, slope, padded)
-    pre_b, send_b, keep_b = backward_b(grid, turned_latent, slope, hidden, padded, turn, flat)
-    rows_a, pre_a = lax.optimization_barrier((over_core(send_a, keep_a), pre_a))
-    grad_latent = latent_gradient(pre_a, pre_b, hidden_weight, 0)
+    pre_a, send_a, keep_a, turn, flat, turned_latent, slope = backward_a(low, turned_latent, slope, padded)
+    pre_b, send_b, keep_b, weight_copy = backward_b(
+        grid, turned_latent, slope, hidden, hidden_weight, padded, turn, flat
+    )
+    rows_a = over_core(send_a, keep_a)
     rows_b, pre_b = lax.optimization_barrier((over_core(send_b, keep_b), pre_b))
-    grad_latent = latent_gradient(pre_a, pre_b, hidden_weight, nodes // 2, grad_latent)
-    total_a = over_chips(rows_a)
-    total_b = over_chips(rows_b)
+    grad_latent = latent_gradient(pre_a, pre_b, weight_copy)
+    blocks = jnp.concatenate([over_z(rows_a), over_z(rows_b)], axis=2)
+    blocks, grad_latent = lax.optimization_barrier((blocks, grad_latent))
+    total = over_x_and_y(blocks)
     factor = 1.0 / math.sqrt(members * nodes * groups)
-    half = width // 2
-    first = jnp.concatenate([total_a, total_b[:, :half]], axis=1)
-    return (grad_latent[None], first * factor, total_b[:, half : half + variables] * factor)
+    return (grad_latent[None], total[:, :width] * factor, total[:, width : width + variables] * factor)
 
 
 def solution(mesh):

time: 105 us -> 96.2 us (0.916)
  starting transfers between devices: 39.6 us -> 29.1 us
  waiting for transfers between devices: 21.4 us -> 28.5 us
  Pallas kernels: 35.6 us -> 30.1 us
    ppermute x20 -> x14, starting transfers between devices: 29.1 us -> 18.6 us  [moved(): return lax.ppermute(value, ('member', 'grid'), moves)]
    ppermute x20 -> x14, waiting for transfers between devices: 5.96 us -> 13.1 us  [moved(): return lax.ppermute(value, ('member', 'grid'), moves)]
    pallas_call x3 -> x2, Pallas kernels: 15.4 us -> 9.43 us  [the longest x1 5.65 us: latent_gradient(): pl.pallas_call(latent_kernel, in_specs=[vmem] * 3, out_specs=anywhere, ou...]
  transfers between devices with their start and end apart: 22 -> 16, of which waited for: 6 -> 9; matrix products, arithmetic and copies ran while one was open for 1% -> 0% of each run, Pallas kernels for 16% -> 11%
where the time goes in v5:
time: 96.2 us; the launch traced here: 95.9 us
  Pallas kernels  30.1 us (31%)
  starting transfers between devices  29.1 us (30%)
  waiting for transfers between devices  28.5 us (30%)
  local copies, waits for them, and re-layouts  4.33 us (5%)
  other arithmetic  2.93 us (3%)
    ppermute x14, starting transfers between devices, moved(): return lax.ppermute(value, ('member', 'grid'), moves)  18.6 us
    ppermute x14, waiting for transfers between devices, moved(): return lax.ppermute(value, ('member', 'grid'), moves)  13.1 us
    pallas_call x1, Pallas kernels, forward(): pl.pallas_call(forward_kernel, in_specs=[anywhere] * 3, out_specs=[vmem,...  12.1 us
    all_to_all x1, waiting for transfers between devices, body(): blocks = lax.all_to_all(blocks, 'member', 0, 0, tiled=True)  10.9 us
    all_to_all x1, starting transfers between devices, body(): blocks = lax.all_to_all(blocks, 'member', 0, 0, tiled=True)  7.01 us
    pallas_call x1, Pallas kernels, backward_a(): pl.pallas_call(backward_a_kernel, in_specs=[vmem, anywhere, anywhere, vme...  5.65 us
    pallas_call x1, Pallas kernels, latent_gradient(): pl.pallas_call(latent_kernel, in_specs=[vmem] * 3, out_specs=anywhere, ou...  5.65 us
    all_to_all x1, waiting for transfers between devices, body(): low = lax.all_to_all(low, 'member', 0, 0, tiled=True)  4.56 us
  transfers between devices with their start and end apart: 16, of which 9 were waited for; matrix products, arithmetic and copies ran while one was open for 0% of the time, Pallas kernels for 11%

profile of v5, /device:TPU:0, one launch (start us, length us, event | category | flops | bytes accessed | tf_op | source)
XLA Modules:
  0.0 95.9 jit_solution(15735382022296428945)
XLA Ops:
  0.6 0.0 copy-start.3
  0.6 12.1 %forward.1 = (f32[8,112,256]{2,1,0:T(8,128)S(1)}, bf16[2048,1024]{1,0:T(8,128)(2,1)}, bf16[2048,1024]{1,0:T(8,128)(2,1)}, bf16[1024,128]{1,0:T(8,128)(2,1)S(1)}) custom-call(bf16[2048,1024]{1,0:T(8,128)(2,1)} %bitcast.22, bf16[1024,1024]{1,0:T(8,128)(2,1)} %weight_hbm.1, bf16[100,1024]{1,0:T(8,128)(2,1)} %bitcast.33), custom_call_target="tpu_custom_call" | custom-call | flops 4831838208 | bytes 20971520 | tf_op jit(solution)/shard_map/forward/pallas_call | solution.py:123
  12.7 0.0 copy-start.2
  12.7 0.9 multiply_convert_fusion
  13.6 7.0 %all-to-all-start = ((f16[8,112,256]{2,1,0:T(8,128)(2,1)}), f16[8,112,256]{2,1,0:T(8,128)(2,1)S(1)}, u32[]{:S(2)}, u32[]{:S(2)}) async-start(f16[8,112,256]{2,1,0:T(8,128)(2,1)} %multiply_convert_fusion), calls=%async_computation | async-start | bytes 917504 | tf_op jit(solution)/shard_map/all_to_all | solution.py:486
  20.6 10.9 %all-to-all-done = f16[8,112,256]{2,1,0:T(8,128)(2,1)S(1)} async-done(((f16[8,112,256]{2,1,0:T(8,128)(2,1)}), f16[8,112,256]{2,1,0:T(8,128)(2,1)S(1)}, u32[]{:S(2)}, u32[]{:S(2)}) %all-to-all-start) | async-done | bytes 458784 | tf_op jit(solution)/shard_map/all_to_all | solution.py:486
  31.5 0.1 convert_multiply_fusion.blocks_ref
  31.6 0.0 copy-done.3
  31.6 0.0 copy-done.2
  31.6 1.9 %pairs.1 = bf16[8,112,256]{2,1,0:T(8,128)(2,1)} custom-call(s32[1]{0:T(128)} %bitcast.place_ref, f32[8,112,256]{2,1,0:T(8,128)S(1)} %convert_multiply_fusion.blocks_ref, f32[100,2048]{1,0:T(8,128)S(1)} %copy-done.2, f32[1,2048]{1,0:T(1,128)S(1)} %bitcast.24), custom_call_target="tpu_custom_call" | custom-call | flops 4194304 | bytes 2097152 | tf_op jit(solution)/shard_map/pairs/pallas_call | solution.py:189
  33.5 3.5 %all-to-all-start.1 = ((bf16[8,112,256]{2,1,0:T(8,128)(2,1)}), bf16[8,112,256]{2,1,0:T(8,128)(2,1)S(1)}, u32[]{:S(2)}, u32[]{:S(2)}) async-start(bf16[8,112,256]{2,1,0:T(8,128)(2,1)} %pairs.1), calls=%async_computation.1 | async-start | bytes 917504 | tf_op jit(solution)/shard_map/all_to_all | solution.py:489
  37.0 0.0 copy-start.1
  37.0 2.2 %copy-done.1 = bf16[1,2048,1024]{2,1,0:T(8,128)(2,1)S(1)} copy-done((bf16[1,2048,1024]{2,1,0:T(8,128)(2,1)S(1)}, bf16[1,2048,1024]{2,1,0:T(8,128)(2,1)}, u32[]{:S(2)}) %copy-start.1) | copy-done | bytes 4194328
  39.2 1.1 %turned.1.turned_hbm = bf16[1024,2048]{1,0:T(8,128)(2,1)S(1)} custom-call(s32[1]{0:T(128)} %bitcast.3.grid_ref, bf16[2048,1024]{1,0:T(8,128)(2,1)S(1)} %bitcast.23), custom_call_target="tpu_custom_call" | custom-call | bytes 8388608 | tf_op jit(solution)/shard_map/turned/pallas_call | solution.py:231
  40.3 0.0 copy-start
  40.3 2.0 %copy-done = bf16[1024,2048]{1,0:T(8,128)(2,1)} copy-done((bf16[1024,2048]{1,0:T(8,128)(2,1)}, bf16[1024,2048]{1,0:T(8,128)(2,1)S(1)}, u32[]{:S(2)}) %copy-start) | copy-done | bytes 4194328
  42.3 4.6 %all-to-all-done.1.low_ref = bf16[8,112,256]{2,1,0:T(8,128)(2,1)S(1)} async-done(((bf16[8,112,256]{2,1,0:T(8,128)(2,1)}), bf16[8,112,256]{2,1,0:T(8,128)(2,1)S(1)}, u32[]{:S(2)}, u32[]{:S(2)}) %all-to-all-start.1) | async-done | bytes 458784 | tf_op jit(solution)/shard_map/all_to_all | solution.py:489
  46.9 5.6 %backward_a.1 = (bf16[2048,512]{1,0:T(8,128)(2,1)S(1)}, bf16[512,512]{1,0:T(8,128)(2,1)S(1)}, bf16[512,512]{1,0:T(8,128)(2,1)S(1)}, bf16[2048,128]{1,0:T(8,128)(...) custom-call(bf16[8,112,256]{2,1,0:T(8,128)(2,1)S(1)} %all-to-all-done.1.low_, ...), custom_call_target="tpu_custom_call" | custom-call | flops 2415919104 | bytes 8388608 | tf_op jit(solution)/shard_map/backward_a/pallas_call | solution.py:353
  52.6 0.3 collective-permute-start
  52.8 3.8 %backward_b.1 = (bf16[2048,512]{1,0:T(8,128)(2,1)S(1)}, bf16[512,640]{1,0:T(8,128)(2,1)S(1)}, bf16[512,640]{1,0:T(8,128)(2,1)S(1)}, bf16[1024,1024]{1,0:T(8,128)(2,1)S(1)}) custom-call(s32[1]{0:T(128)} %bitcast.3.grid_ref, bf16[1024,2048]{1,0:T(8,128)(2,1)S(1)} %get-tuple-element.31.turned_ref, bf16[2048,1024]{1,0:T(8,128)(2,1)S(1)} %get-tuple-element.32.slope_ref, ...), custom_call_target="tpu_custom_call" | custom-call | flops 2952790016 | bytes 8388608 | tf_op jit(solution)/shard_map/backward_b/pallas_call | solution.py:379
  56.6 0.6 collective-permute-start.4
  57.2 0.0 collective-permute-done
  57.2 0.1 add_convert_fusion.1
  57.4 4.0 %collective-permute-start.3 = (bf16[2,64,512]{2,1,0:T(8,128)(2,1)S(1)}, bf16[2,64,512]{2,1,0:T(8,128)(2,1)S(1)}, u32[]{:S(2)}, u32[]{:S(2)}) collective-permute-start(bf16[2,64,512]{2,1,0:T(8,128)(2,1)S(1)} %bitcast.32), channel_id=1, source_target_pairs={{0,4},{1,5},{2,6},{3,7},{4,0},{5,1},{6,2},{7,3},{8,12},{9,13},{10,... | collective-permute-start | bytes 393224 | tf_op jit(solution)/shard_map/ppermute | solution.py:444
  61.3 1.0 %collective-permute-start.1 = (bf16[2,64,512]{2,1,0:T(8,128)(2,1)S(1)}, bf16[2,64,512]{2,1,0:T(8,128)(2,1)S(1)}, u32[]{:S(2)}, u32[]{:S(2)}) collective-permute-start(bf16[2,64,512]{2,1,0:T(8,128)(2,1)S(1)} %bitcast.31), channel_id=1, source_target_pairs={{0,2},{1,3},{2,4},{3,5},{4,6},{5,7},{6,0},{7,1},{8,10},{9,11},{10,... | collective-permute-start | bytes 393224 | tf_op jit(solution)/shard_map/ppermute | solution.py:444
  62.3 2.2 %collective-permute-start.2 = (bf16[2,64,512]{2,1,0:T(8,128)(2,1)S(1)}, bf16[2,64,512]{2,1,0:T(8,128)(2,1)S(1)}, u32[]{:S(2)}, u32[]{:S(2)}) collective-permute-start(bf16[2,64,512]{2,1,0:T(8,128)(2,1)S(1)} %bitcast.30), channel_id=1, source_target_pairs={{0,6},{1,7},{2,0},{3,1},{4,2},{5,3},{6,4},{7,5},{8,14},{9,15},{10,... | collective-permute-start | bytes 393224 | tf_op jit(solution)/shard_map/ppermute | solution.py:444
  64.6 0.0 collective-permute-done.4
  64.6 0.2 add_convert_fusion
  64.7 0.1 fusion.6
  64.8 0.1 collective-permute-start.7
  64.9 0.8 collective-permute-start.5
  65.8 5.6 %latent_gradient.1 = bf16[2048,1024]{1,0:T(8,128)(2,1)} custom-call(bf16[2048,512]{1,0:T(8,128)(2,1)S(1)} %get-tuple-element.40.left_ref, bf16[2048,512]{1,0:T(8,128)(2,1)S(1)} %get-tuple-element.41.right_ref, bf16[1024,1024]{1,0:T(8,128)(2,1)S(1)} %get-tuple-element.42.weight_ref), custom_call_target="tpu_custom_call" | custom-call | flops 4294967296 | bytes 10485760 | tf_op jit(solution)/shard_map/latent_gradient/pallas_call | solution.py:424
  71.4 0.0 collective-permute-done.3
  71.4 2.5 %collective-permute-start.6 = (bf16[2,64,640]{2,1,0:T(8,128)(2,1)S(1)}, bf16[2,64,640]{2,1,0:T(8,128)(2,1)S(1)}, u32[]{:S(2)}, u32[]{:S(2)}) collective-permute-start(bf16[2,64,640]{2,1,0:T(8,128)(2,1)S(1)} %bitcast.27), channel_id=1, source_target_pairs={{0,6},{1,7},{2,0},{3,1},{4,2},{5,3},{6,4},{7,5},{8,14},{9,15},{10,... | collective-permute-start | bytes 491528 | tf_op jit(solution)/shard_map/ppermute | solution.py:444
  73.9 0.0 collective-permute-done.1
  73.9 0.0 collective-permute-done.2
  73.9 0.1 fusion.5
  74.0 0.0 collective-permute-done.7
  74.0 1.1 %collective-permute-done.5 = bf16[2,64,640]{2,1,0:T(8,128)(2,1)S(1)} collective-permute-done((bf16[2,64,640]{2,1,0:T(8,128)(2,1)S(1)}, bf16[2,64,640]{2,1,0:T(8,128)(2,1)S(1)}, u32[]{:S(2)}, u32[]{:S(2)}) %collective-permute-start.5) | collective-permute-done | bytes 163872 | tf_op jit(solution)/shard_map/ppermute | solution.py:444
  75.1 2.3 %collective-permute-done.6 = bf16[2,64,640]{2,1,0:T(8,128)(2,1)S(1)} collective-permute-done((bf16[2,64,640]{2,1,0:T(8,128)(2,1)S(1)}, bf16[2,64,640]{2,1,0:T(8,128)(2,1)S(1)}, u32[]{:S(2)}, u32[]{:S(2)}) %collective-permute-start.6) | collective-permute-done | bytes 163872 | tf_op jit(solution)/shard_map/ppermute | solution.py:444
  77.4 0.1 fusion.2
  77.6 0.9 collective-permute-start.10
  78.5 2.4 %collective-permute-start.9 = (bf16[64,1152]{1,0:T(8,128)(2,1)S(1)}, bf16[64,1152]{1,0:T(8,128)(2,1)S(1)}, u32[]{:S(2)}, u32[]{:S(2)}) collective-permute-start(bf16[64,1152]{1,0:T(8,128)(2,1)S(1)} %get-tuple-element.53), channel_id=1, source_target_pairs={{0,24},{1,25},{2,26},{3,27},{4,28},{5,29},{6,30},{7,31},{8,16},{9,... | collective-permute-start | bytes 442376 | tf_op jit(solution)/shard_map/ppermute | solution.py:444
  80.9 0.2 collective-permute-start.8
  81.1 3.3 %collective-permute-done.10 = bf16[64,1152]{1,0:T(8,128)(2,1)S(1)} collective-permute-done((bf16[64,1152]{1,0:T(8,128)(2,1)S(1)}, bf16[64,1152]{1,0:T(8,128)(2,1)S(1)}, u32[]{:S(2)}, u32[]{:S(2)}) %collective-permute-start.10) | collective-permute-done | bytes 147488 | tf_op jit(solution)/shard_map/ppermute | solution.py:444
  84.4 1.5 %collective-permute-done.9 = bf16[64,1152]{1,0:T(8,128)(2,1)S(1)} collective-permute-done((bf16[64,1152]{1,0:T(8,128)(2,1)S(1)}, bf16[64,1152]{1,0:T(8,128)(2,1)S(1)}, u32[]{:S(2)}, u32[]{:S(2)}) %collective-permute-start.9) | collective-permute-done | bytes 147488 | tf_op jit(solution)/shard_map/ppermute | solution.py:444
  85.9 0.2 collective-permute-done.8
  86.1 0.1 add_convert_fusion.2
  86.2 0.9 collective-permute-start.13
  87.1 2.1 %collective-permute-start.12 = (bf16[64,1152]{1,0:T(8,128)(2,1)S(1)}, bf16[64,1152]{1,0:T(8,128)(2,1)S(1)}, u32[]{:S(2)}, u32[]{:S(2)}) collective-permute-start(bf16[64,1152]{1,0:T(8,128)(2,1)S(1)} %add_convert_fusion.2), channel_id=1, source_target_pairs={{0,96},{1,97},{2,98},{3,99},{4,100},{5,101},{6,102},{7,103},{8,104... | collective-permute-start | bytes 442376 | tf_op jit(solution)/shard_map/ppermute | solution.py:444
  89.1 0.6 collective-permute-start.11
  89.7 3.3 %collective-permute-done.13 = bf16[64,1152]{1,0:T(8,128)(2,1)S(1)} collective-permute-done((bf16[64,1152]{1,0:T(8,128)(2,1)S(1)}, bf16[64,1152]{1,0:T(8,128)(2,1)S(1)}, u32[]{:S(2)}, u32[]{:S(2)}) %collective-permute-start.13) | collective-permute-done | bytes 147488 | tf_op jit(solution)/shard_map/ppermute | solution.py:444
  93.0 1.5 %collective-permute-done.12 = bf16[64,1152]{1,0:T(8,128)(2,1)S(1)} collective-permute-done((bf16[64,1152]{1,0:T(8,128)(2,1)S(1)}, bf16[64,1152]{1,0:T(8,128)(2,1)S(1)}, u32[]{:S(2)}, u32[]{:S(2)}) %collective-permute-start.12) | collective-permute-done | bytes 147488 | tf_op jit(solution)/shard_map/ppermute | solution.py:444
  94.5 0.0 collective-permute-done.11
  94.5 0.1 convert_add_fusion.1
  94.5 0.6 slice_multiply_fusion.1
  95.2 0.7 slice_multiply_fusion
  (3 shorter events, 0.1 us)
Async XLA Ops:
  0.6 31.0 %copy-start.3 = (f32[2048]{0:T(1024)S(1)}, f32[2048]{0:T(1024)}, u32[]{:S(2)}) copy-start(f32[2048]{0:T(1024)} %param.9) | copy-start | bytes 24580
  12.7 18.9 %copy-start.2 = (f32[100,2048]{1,0:T(8,128)S(1)}, f32[100,2048]{1,0:T(8,128)}, u32[]{:S(2)}) copy-start(f32[100,2048]{1,0:T(8,128)} %observed_ref.1) | copy-start | bytes 2457604
  13.6 17.9 %all-to-all-start = ((f16[8,112,256]{2,1,0:T(8,128)(2,1)}), f16[8,112,256]{2,1,0:T(8,128)(2,1)S(1)}, u32[]{:S(2)}, u32[]{:S(2)}) async-start(f16[8,112,256]{2,1,0:T(8,128)(2,1)} %multiply_convert_fusion), calls=%async_computation | async-start | bytes 917504 | tf_op jit(solution)/shard_map/all_to_all | solution.py:486
  33.5 13.4 %all-to-all-start.1 = ((bf16[8,112,256]{2,1,0:T(8,128)(2,1)}), bf16[8,112,256]{2,1,0:T(8,128)(2,1)S(1)}, u32[]{:S(2)}, u32[]{:S(2)}) async-start(bf16[8,112,256]{2,1,0:T(8,128)(2,1)} %pairs.1), calls=%async_computation.1 | async-start | bytes 917504 | tf_op jit(solution)/shard_map/all_to_all | solution.py:489
  37.0 2.2 %copy-start.1 = (bf16[1,2048,1024]{2,1,0:T(8,128)(2,1)S(1)}, bf16[1,2048,1024]{2,1,0:T(8,128)(2,1)}, u32[]{:S(2)}) copy-start(bf16[1,2048,1024]{2,1,0:T(8,128)(2,1)} %param.5) | copy-start | bytes 12582916
  40.3 2.0 %copy-start = (bf16[1024,2048]{1,0:T(8,128)(2,1)}, bf16[1024,2048]{1,0:T(8,128)(2,1)S(1)}, u32[]{:S(2)}) copy-start(bf16[1024,2048]{1,0:T(8,128)(2,1)S(1)} %turned.1.turned_hbm) | copy-start | bytes 12582916
  52.6 4.6 %collective-permute-start = (bf16[512,512]{1,0:T(8,128)(2,1)S(1)}, bf16[512,512]{1,0:T(8,128)(2,1)S(1)}, u32[]{:S(2)}, u32[]{:S(2)}) collective-permute-start(bf16[512,512]{1,0:T(8,128)(2,1)S(1)} %get-tuple-element.30), channel_id=1, source_target_pairs={{0,1},{1,0},{2,3},{3,2},{4,5},{5,4},{6,7},{7,6},{8,9},{9,8},{10,11... | collective-permute-start | bytes 1572872 | tf_op jit(solution)/shard_map/ppermute | solution.py:444
  56.6 8.0 %collective-permute-start.4 = (bf16[512,640]{1,0:T(8,128)(2,1)S(1)}, bf16[512,640]{1,0:T(8,128)(2,1)S(1)}, u32[]{:S(2)}, u32[]{:S(2)}) collective-permute-start(bf16[512,640]{1,0:T(8,128)(2,1)S(1)} %get-tuple-element.37), channel_id=1, source_target_pairs={{0,1},{1,0},{2,3},{3,2},{4,5},{5,4},{6,7},{7,6},{8,9},{9,8},{10,11... | collective-permute-start | bytes 1966088 | tf_op jit(solution)/shard_map/ppermute | solution.py:444
  57.4 14.0 %collective-permute-start.3 = (bf16[2,64,512]{2,1,0:T(8,128)(2,1)S(1)}, bf16[2,64,512]{2,1,0:T(8,128)(2,1)S(1)}, u32[]{:S(2)}, u32[]{:S(2)}) collective-permute-start(bf16[2,64,512]{2,1,0:T(8,128)(2,1)S(1)} %bitcast.32), channel_id=1, source_target_pairs={{0,4},{1,5},{2,6},{3,7},{4,0},{5,1},{6,2},{7,3},{8,12},{9,13},{10,... | collective-permute-start | bytes 393224 | tf_op jit(solution)/shard_map/ppermute | solution.py:444
  61.3 12.6 %collective-permute-start.1 = (bf16[2,64,512]{2,1,0:T(8,128)(2,1)S(1)}, bf16[2,64,512]{2,1,0:T(8,128)(2,1)S(1)}, u32[]{:S(2)}, u32[]{:S(2)}) collective-permute-start(bf16[2,64,512]{2,1,0:T(8,128)(2,1)S(1)} %bitcast.31), channel_id=1, source_target_pairs={{0,2},{1,3},{2,4},{3,5},{4,6},{5,7},{6,0},{7,1},{8,10},{9,11},{10,... | collective-permute-start | bytes 393224 | tf_op jit(solution)/shard_map/ppermute | solution.py:444
  62.3 11.6 %collective-permute-start.2 = (bf16[2,64,512]{2,1,0:T(8,128)(2,1)S(1)}, bf16[2,64,512]{2,1,0:T(8,128)(2,1)S(1)}, u32[]{:S(2)}, u32[]{:S(2)}) collective-permute-start(bf16[2,64,512]{2,1,0:T(8,128)(2,1)S(1)} %bitcast.30), channel_id=1, source_target_pairs={{0,6},{1,7},{2,0},{3,1},{4,2},{5,3},{6,4},{7,5},{8,14},{9,15},{10,... | collective-permute-start | bytes 393224 | tf_op jit(solution)/shard_map/ppermute | solution.py:444
  64.8 9.2 %collective-permute-start.7 = (bf16[2,64,640]{2,1,0:T(8,128)(2,1)S(1)}, bf16[2,64,640]{2,1,0:T(8,128)(2,1)S(1)}, u32[]{:S(2)}, u32[]{:S(2)}) collective-permute-start(bf16[2,64,640]{2,1,0:T(8,128)(2,1)S(1)} %bitcast.29), channel_id=1, source_target_pairs={{0,4},{1,5},{2,6},{3,7},{4,0},{5,1},{6,2},{7,3},{8,12},{9,13},{10,... | collective-permute-start | bytes 491528 | tf_op jit(solution)/shard_map/ppermute | solution.py:444
  64.9 10.2 %collective-permute-start.5 = (bf16[2,64,640]{2,1,0:T(8,128)(2,1)S(1)}, bf16[2,64,640]{2,1,0:T(8,128)(2,1)S(1)}, u32[]{:S(2)}, u32[]{:S(2)}) collective-permute-start(bf16[2,64,640]{2,1,0:T(8,128)(2,1)S(1)} %bitcast.28), channel_id=1, source_target_pairs={{0,2},{1,3},{2,4},{3,5},{4,6},{5,7},{6,0},{7,1},{8,10},{9,11},{10,... | collective-permute-start | bytes 491528 | tf_op jit(solution)/shard_map/ppermute | solution.py:444
  71.4 6.0 %collective-permute-start.6 = (bf16[2,64,640]{2,1,0:T(8,128)(2,1)S(1)}, bf16[2,64,640]{2,1,0:T(8,128)(2,1)S(1)}, u32[]{:S(2)}, u32[]{:S(2)}) collective-permute-start(bf16[2,64,640]{2,1,0:T(8,128)(2,1)S(1)} %bitcast.27), channel_id=1, source_target_pairs={{0,6},{1,7},{2,0},{3,1},{4,2},{5,3},{6,4},{7,5},{8,14},{9,15},{10,... | collective-permute-start | bytes 491528 | tf_op jit(solution)/shard_map/ppermute | solution.py:444
  77.6 6.8 %collective-permute-start.10 = (bf16[64,1152]{1,0:T(8,128)(2,1)S(1)}, bf16[64,1152]{1,0:T(8,128)(2,1)S(1)}, u32[]{:S(2)}, u32[]{:S(2)}) collective-permute-start(bf16[64,1152]{1,0:T(8,128)(2,1)S(1)} %get-tuple-element.54), channel_id=1, source_target_pairs={{0,16},{1,17},{2,18},{3,19},{4,20},{5,21},{6,22},{7,23},{8,24},{9,... | collective-permute-start | bytes 442376 | tf_op jit(solution)/shard_map/ppermute | solution.py:444
  78.5 7.4 %collective-permute-start.9 = (bf16[64,1152]{1,0:T(8,128)(2,1)S(1)}, bf16[64,1152]{1,0:T(8,128)(2,1)S(1)}, u32[]{:S(2)}, u32[]{:S(2)}) collective-permute-start(bf16[64,1152]{1,0:T(8,128)(2,1)S(1)} %get-tuple-element.53), channel_id=1, source_target_pairs={{0,24},{1,25},{2,26},{3,27},{4,28},{5,29},{6,30},{7,31},{8,16},{9,... | collective-permute-start | bytes 442376 | tf_op jit(solution)/shard_map/ppermute | solution.py:444
  80.9 5.1 %collective-permute-start.8 = (bf16[64,1152]{1,0:T(8,128)(2,1)S(1)}, bf16[64,1152]{1,0:T(8,128)(2,1)S(1)}, u32[]{:S(2)}, u32[]{:S(2)}) collective-permute-start(bf16[64,1152]{1,0:T(8,128)(2,1)S(1)} %get-tuple-element.53), channel_id=1, source_target_pairs={{0,8},{1,9},{2,10},{3,11},{4,12},{5,13},{6,14},{7,15},{8,0},{9,1},... | collective-permute-start | bytes 442376 | tf_op jit(solution)/shard_map/ppermute | solution.py:444
  86.2 6.8 %collective-permute-start.13 = (bf16[64,1152]{1,0:T(8,128)(2,1)S(1)}, bf16[64,1152]{1,0:T(8,128)(2,1)S(1)}, u32[]{:S(2)}, u32[]{:S(2)}) collective-permute-start(bf16[64,1152]{1,0:T(8,128)(2,1)S(1)} %add_convert_fusion.2), channel_id=1, source_target_pairs={{0,64},{1,65},{2,66},{3,67},{4,68},{5,69},{6,70},{7,71},{8,72},{9,... | collective-permute-start | bytes 442376 | tf_op jit(solution)/shard_map/ppermute | solution.py:444
  87.1 7.4 %collective-permute-start.12 = (bf16[64,1152]{1,0:T(8,128)(2,1)S(1)}, bf16[64,1152]{1,0:T(8,128)(2,1)S(1)}, u32[]{:S(2)}, u32[]{:S(2)}) collective-permute-start(bf16[64,1152]{1,0:T(8,128)(2,1)S(1)} %add_convert_fusion.2), channel_id=1, source_target_pairs={{0,96},{1,97},{2,98},{3,99},{4,100},{5,101},{6,102},{7,103},{8,104... | collective-permute-start | bytes 442376 | tf_op jit(solution)/shard_map/ppermute | solution.py:444
  89.1 5.3 %collective-permute-start.11 = (bf16[64,1152]{1,0:T(8,128)(2,1)S(1)}, bf16[64,1152]{1,0:T(8,128)(2,1)S(1)}, u32[]{:S(2)}, u32[]{:S(2)}) collective-permute-start(bf16[64,1152]{1,0:T(8,128)(2,1)S(1)} %add_convert_fusion.2), channel_id=1, source_target_pairs={{0,32},{1,33},{2,34},{3,35},{4,36},{5,37},{6,38},{7,39},{8,40},{9,... | collective-permute-start | bytes 442376 | tf_op jit(solution)/shard_map/ppermute | solution.py:444

commit v6 on v5

v6 whole, which is shorter than its diff:
```python
import functools
import math

import jax
import jax.numpy as jnp
from jax import lax
from jax.experimental import pallas as pl
from jax.experimental.pallas import tpu as pltpu
from jax.sharding import PartitionSpec as P

smooth_sq = 0.0025
bf16 = jnp.bfloat16
f16 = jnp.float16
f32 = jnp.float32

NT = (((1,), (1,)), ((), ()))
WIDE = 128
TALL = 112
SHARE = 256
ROWS = 512
COLS = 256

vmem = pl.BlockSpec(memory_space=pltpu.VMEM)
smem = pl.BlockSpec(memory_space=pltpu.SMEM)
anywhere = pl.BlockSpec(memory_space=pltpu.HBM)


def params(mib):
    return pltpu.CompilerParams(vmem_limit_bytes=mib * 1024 * 1024)


def cost(flops, nbytes, trans=0):
    return pl.CostEstimate(flops=flops, bytes_accessed=nbytes, transcendentals=trans)


CHUNKS = (512, 512, 512, 256, 256)
FCOLS = 512


def forward_kernel(
    latent_ref,
    weight_ref,
    out_weight_ref,
    forecast_ref,
    hidden_out,
    slope_out,
    padded_ref,
    hidden_ref,
    slope_ref,
    latent_copy,
    weight_copy,
    out_weight_copy,
    latent_sems,
    weight_sems,
    out_weight_sem,
    hidden_sems,
    slope_sems,
):
    nodes, width = latent_ref.shape
    variables = out_weight_ref.shape[0]
    out_weight_load = pltpu.make_async_copy(out_weight_ref, out_weight_copy, out_weight_sem)
    spans = []
    for size in CHUNKS:
        begin = spans[-1].stop if spans else 0
        spans.append(slice(begin, begin + size))
    weight_loads = [
        pltpu.make_async_copy(
            weight_ref.at[:, pl.ds(start, FCOLS)], weight_copy.at[:, pl.ds(start, FCOLS)], weight_sems.at[start // FCOLS]
        )
        for start in range(0, width, FCOLS)
    ]

    def chunk(ref, rows):
        return ref.at[pl.ds(rows.start, rows.stop - rows.start)]

    latent_loads = [
        pltpu.make_async_copy(chunk(latent_ref, rows), chunk(latent_copy, rows), latent_sems.at[index])
        for index, rows in enumerate(spans)
    ]
    weight_loads[0].start()
    latent_loads[0].start()
    for load in weight_loads[1:] + latent_loads[1:]:
        load.start()
    out_weight_load.start()
    out_weight_load.wait()
    turned_weight = jnp.concatenate(
        [out_weight_copy[...], jnp.zeros((WIDE - variables, width), bf16)], axis=0
    )
    padded_ref[...] = turned_weight.T
    stores = []
    for index, rows in enumerate(spans):
        latent_loads[index].wait()
        for start in range(0, width, FCOLS):
            columns = slice(start, start + FCOLS)
            if index == 0:
                weight_loads[start // FCOLS].wait()
            pre = jnp.dot(latent_copy[rows, :], weight_copy[:, columns], preferred_element_type=f32)
            sig = 0.5 * jnp.tanh(0.5 * pre) + 0.5
            hidden = pre * sig
            hidden_ref[rows, columns] = hidden.astype(bf16)
            slope_ref[rows, columns] = (sig + hidden * (1.0 - sig)).astype(bf16)
        for made, out, sems in ((hidden_ref, hidden_out, hidden_sems), (slope_ref, slope_out, slope_sems)):
            store = pltpu.make_async_copy(chunk(made, rows), chunk(out, rows), sems.at[index])
            store.start()
            stores.append(store)
        for share in range(rows.start // SHARE, rows.stop // SHARE):
            forecast_ref[share] = lax.dot_general(
                turned_weight[:TALL],
                hidden_ref[share * SHARE : (share + 1) * SHARE, :],
                NT,
                preferred_element_type=f32,
            )
    for store in stores:
        store.wait()


def pinned(value):
    return pltpu.with_memory_space_constraint(value, pltpu.HBM)


def forward(latent, weight, out_weight):
    nodes, width = latent.shape
    return pl.pallas_call(
        forward_kernel,
        in_specs=[anywhere] * 3,
        out_specs=[vmem, anywhere, anywhere, vmem],
        out_shape=[
            jax.ShapeDtypeStruct((nodes // SHARE, TALL, SHARE), f32),
            pltpu.HBM((nodes, width), bf16),
            pltpu.HBM((nodes, width), bf16),
            jax.ShapeDtypeStruct((width, WIDE), bf16),
        ],
        scratch_shapes=[
            pltpu.VMEM((nodes, width), bf16),
            pltpu.VMEM((nodes, width), bf16),
            pltpu.VMEM((nodes, width), bf16),
            pltpu.VMEM((width, width), bf16),
            pltpu.VMEM(out_weight.shape, bf16),
            pltpu.SemaphoreType.DMA((len(CHUNKS),)),
            pltpu.SemaphoreType.DMA((width // FCOLS,)),
            pltpu.SemaphoreType.DMA,
            pltpu.SemaphoreType.DMA((len(CHUNKS),)),
            pltpu.SemaphoreType.DMA((len(CHUNKS),)),
        ],
        compiler_params=params(32),
        cost_estimate=cost(2 * nodes * width * (width + WIDE), 20 << 20),
        name="forward",
    )(pinned(latent), pinned(weight), pinned(out_weight))


def slope_function(diff):
    return diff * lax.rsqrt(diff * diff + smooth_sq)


def pair_kernel(place_ref, blocks_ref, observed_ref, area_ref, low_ref, here_ref, weight_ref, sems):
    members = blocks_ref.shape[0]
    variables = observed_ref.shape[0]
    at = pl.multiple_of(place_ref[0] * SHARE, SHARE)
    loads = [
        pltpu.make_async_copy(observed_ref.at[:, pl.ds(at, SHARE)], here_ref, sems.at[0]),
        pltpu.make_async_copy(area_ref.at[:, pl.ds(at, SHARE)], weight_ref, sems.at[1]),
    ]
    for load in loads:
        load.start()
    for start in range(0, TALL, 16):
        rows = slice(start, start + 16)
        values = [blocks_ref[a, rows, :] for a in range(members)]
        totals = [0.0] * members
        for a in range(members):
            for b in range(a + 1, members):
                slope = slope_function(values[a] - values[b])
                totals[a] = totals[a] + slope
                totals[b] = totals[b] - slope
        if start == 0:
            for load in loads:
                load.wait()
        area = weight_ref[...]
        real = min(16, variables - start)
        observed = here_ref[start : start + real, :]
        if real < 16:
            observed = jnp.concatenate([observed, jnp.zeros((16 - real, SHARE), f32)], axis=0)
        for a in range(members):
            field = area * (slope_function(values[a] - observed) - totals[a] * (1.0 / (members - 1)))
            low_ref[a, rows, :] = field.astype(bf16)


def pairs(place, blocks, observed, area):
    members = blocks.shape[0]
    variables = observed.shape[0]
    return pl.pallas_call(
        pair_kernel,
        in_specs=[smem, vmem, anywhere, anywhere],
        out_specs=vmem,
        out_shape=jax.ShapeDtypeStruct((members, TALL, SHARE), bf16),
        scratch_shapes=[
            pltpu.VMEM((variables, SHARE), f32),
            pltpu.VMEM((1, SHARE), f32),
            pltpu.SemaphoreType.DMA((2,)),
        ],
        compiler_params=params(8),
        cost_estimate=cost(4 << 20, 2 << 20),
        name="pairs",
    )(place, blocks, observed, area)


def position(grid_ref):
    grid = grid_ref[0]
    return grid >> 3, (grid >> 1) & 3, grid & 1


STEPS = ((1, 3), (2, 0))


def owner(block, steps, x_lo, z):
    return ((block & 1) ^ x_lo) * 4 + ((z + steps[block >> 1]) & 3)


def turn_kernel(grid_ref, latent_ref, turned_ref):
    nodes, width = latent_ref.shape
    x_lo, z, core = position(grid_ref)
    for group in range(8):
        step = (group - z) & 3
        odd = step & 1
        place = odd * (step >> 1) + (1 - odd) * (3 - (step >> 1))
        at = (place >> 1) * 512 + (place & 1) * 128 + ((group >> 2) ^ x_lo) * 64
        first = pl.multiple_of(at + (1 - core) * 256, 64)
        second = pl.multiple_of(at + core * 256, 64)
        for row in range(0, nodes, ROWS):
            columns = slice(row, row + ROWS)
            block = latent_ref[columns, group * 128 : (group + 1) * 128].T
            turned_ref[pl.ds(first, 64), columns] = block[:64]
            turned_ref[pl.ds(second, 64), columns] = block[64:]


def turned(grid, latent):
    nodes, width = latent.shape
    return pl.pallas_call(
        turn_kernel,
        in_specs=[smem, vmem],
        out_specs=vmem,
        out_shape=jax.ShapeDtypeStruct((width, nodes), bf16),
        compiler_params=params(8),
        cost_estimate=cost(0, 8 << 20),
        name="turned",
    )(grid, latent)


class PartLoads:
    def __init__(self, part, grid_ref, turned_hbm, hidden_hbm, turned_ref, hidden_ref, turned_sems, hidden_sems):
        x_lo, z, self.core = position(grid_ref)
        self.turned_ref, self.hidden_ref = turned_ref, hidden_ref
        self.turned = [
            pltpu.make_async_copy(
                turned_hbm.at[pl.ds(part * 512 + start, 256)], turned_ref.at[pl.ds(start, 256)], turned_sems.at[start // 256]
            )
            for start in (0, 256)
        ]
        self.hidden = [
            pltpu.make_async_copy(
                hidden_hbm.at[:, pl.ds(pl.multiple_of(owner(block, STEPS[part], x_lo, z) * 128, 128), 128)],
                hidden_ref.at[:, pl.ds(block * 128, 128)],
                hidden_sems.at[block],
            )
            for block in range(4)
        ]

    def start(self):
        for load in self.turned + self.hidden:
            load.start()

    def products(self, pre_ref, flat_ref, send_ref, keep_ref, second_ref):
        width = pre_ref.shape[1]
        for load, out_ref, start in zip(self.turned, (send_ref, keep_ref), (0, 256)):
            load.wait()
            for column in range(0, width, 512):
                columns = slice(column, column + 512)
                part = jnp.dot(self.turned_ref[start : start + 256, :], pre_ref[:, columns], preferred_element_type=f32)
                out_ref[:, columns] = part.astype(bf16)
        for load in self.hidden:
            load.wait()
        for start in (0, 256):
            rows = slice(start, start + 256)
            second = jnp.dot(flat_ref[...], self.hidden_ref[:, rows], preferred_element_type=f32)
            second_ref[rows, :] = second.T.astype(bf16)
        for block in range(4):
            rows = slice(block * 64, (block + 1) * 64)
            mine = pl.multiple_of(block * 128 + self.core * 64, 64)
            other = pl.multiple_of(block * 128 + (1 - self.core) * 64, 64)
            keep_ref[rows, width:] = second_ref[pl.ds(mine, 64), :]
            send_ref[rows, width:] = second_ref[pl.ds(other, 64), :]


def backward_a_kernel(
    grid_ref,
    low_ref,
    turned_hbm,
    slope_hbm,
    hidden_hbm,
    padded_ref,
    pre_ref,
    send_ref,
    keep_ref,
    flat_ref,
    turn_ref,
    turned_ref,
    hidden_ref,
    second_ref,
    slope_ref,
    turned_sems,
    hidden_sems,
    slope_sems,
):
    nodes, width = pre_ref.shape
    loads = PartLoads(0, grid_ref, turned_hbm, hidden_hbm, turned_ref, hidden_ref, turned_sems, hidden_sems)
    slope_loads = [
        pltpu.make_async_copy(
            slope_hbm.at[:, pl.ds(start, COLS)], slope_ref.at[:, pl.ds(start, COLS)], slope_sems.at[start // COLS]
        )
        for start in range(0, width, COLS)
    ]
    for load in slope_loads:
        load.start()
    loads.start()
    for share in range(low_ref.shape[0]):
        columns = slice(share * SHARE, (share + 1) * SHARE)
        low = jnp.concatenate([low_ref[share], jnp.zeros((WIDE - TALL, SHARE), bf16)], axis=0)
        flat_ref[:, columns] = low
        turn_ref[columns, :] = low.T
    for column in range(0, width, COLS):
        columns = slice(column, column + COLS)
        slope_loads[column // COLS].wait()
        for start in range(0, nodes, ROWS):
            rows = slice(start, start + ROWS)
            grad_hidden = lax.dot_general(turn_ref[rows, :], padded_ref[columns, :], NT, preferred_element_type=f32)
            pre_ref[rows, columns] = (grad_hidden * slope_ref[rows, columns].astype(f32)).astype(bf16)
    loads.products(pre_ref, flat_ref, send_ref, keep_ref, second_ref)


def backward_b_kernel(
    grid_ref,
    turned_hbm,
    hidden_hbm,
    pre_ref,
    flat_ref,
    send_ref,
    keep_ref,
    turned_ref,
    hidden_ref,
    second_ref,
    turned_sems,
    hidden_sems,
):
    loads = PartLoads(1, grid_ref, turned_hbm, hidden_hbm, turned_ref, hidden_ref, turned_sems, hidden_sems)
    loads.start()
    loads.products(pre_ref, flat_ref, send_ref, keep_ref, second_ref)


def part_shapes(nodes, width):
    out = [jax.ShapeDtypeStruct((256, width + WIDE), bf16)] * 2
    scratch = [
        pltpu.VMEM((512, nodes), bf16),
        pltpu.VMEM((nodes, 512), bf16),
        pltpu.VMEM((512, WIDE), bf16),
    ]
    sems = [pltpu.SemaphoreType.DMA((2,)), pltpu.SemaphoreType.DMA((4,))]
    return out, scratch, sems


def backward_a(grid, low, turned_latent, slope, hidden, padded):
    nodes, width = slope.shape
    out, scratch, sems = part_shapes(nodes, width)
    return pl.pallas_call(
        backward_a_kernel,
        in_specs=[smem, vmem, anywhere, anywhere, anywhere, vmem],
        out_specs=[vmem] * 4,
        out_shape=[jax.ShapeDtypeStruct((nodes, width), bf16)] + out + [jax.ShapeDtypeStruct((WIDE, nodes), bf16)],
        scratch_shapes=[pltpu.VMEM((nodes, WIDE), bf16)]
        + scratch
        + [pltpu.VMEM((nodes, width), bf16)]
        + sems
        + [pltpu.SemaphoreType.DMA((width // COLS,))],
        compiler_params=params(20),
        cost_estimate=cost(nodes * width * (width + 3 * WIDE), 8 << 20),
        name="backward_a",
    )(grid, low, pinned(turned_latent), pinned(slope), pinned(hidden), padded)


def backward_b(grid, turned_latent, hidden, grad_pre, flat):
    nodes, width = hidden.shape
    out, scratch, sems = part_shapes(nodes, width)
    return pl.pallas_call(
        backward_b_kernel,
        in_specs=[smem, anywhere, anywhere, vmem, vmem],
        out_specs=[vmem] * 2,
        out_shape=out,
        scratch_shapes=scratch + sems,
        compiler_params=params(16),
        cost_estimate=cost(nodes * width * (width + WIDE), 4 << 20),
        name="backward_b",
    )(grid, pinned(turned_latent), pinned(hidden), grad_pre, flat)


def latent_kernel(pre_ref, weight_hbm, out_ref, weight_ref, result_ref, weight_sems, sems):
    nodes, width = pre_ref.shape
    loads = [
        pltpu.make_async_copy(
            weight_hbm.at[pl.ds(start, COLS)], weight_ref.at[pl.ds(start, COLS)], weight_sems.at[start // COLS]
        )
        for start in range(0, width, COLS)
    ]
    for load in loads:
        load.start()
    stores = []
    for row in range(0, nodes, ROWS):
        rows = slice(row, row + ROWS)
        for start in range(0, width, COLS):
            if row == 0:
                loads[start // COLS].wait()
            columns = slice(start, start + COLS)
            result_ref[rows, columns] = lax.dot_general(
                pre_ref[rows, :], weight_ref[columns, :], NT, preferred_element_type=f32
            ).astype(bf16)
        store = pltpu.make_async_copy(
            result_ref.at[pl.ds(row, ROWS)], out_ref.at[pl.ds(row, ROWS)], sems.at[row // ROWS]
        )
        store.start()
        stores.append(store)
    for store in stores:
        store.wait()


def latent_gradient(grad_pre, weight):
    nodes, width = grad_pre.shape
    return pl.pallas_call(
        latent_kernel,
        in_specs=[vmem, anywhere],
        out_specs=anywhere,
        out_shape=pltpu.HBM((nodes, width), bf16),
        scratch_shapes=[
            pltpu.VMEM((width, width), bf16),
            pltpu.VMEM((nodes, width), bf16),
            pltpu.SemaphoreType.DMA((width // COLS,)),
            pltpu.SemaphoreType.DMA((nodes // ROWS,)),
        ],
        compiler_params=params(12),
        cost_estimate=cost(2 * nodes * width * width, 10 << 20),
        name="latent_gradient",
    )(grad_pre, pinned(weight))


def finish_kernel(own_ref, *refs, factor):
    *others, first_ref, second_ref = refs
    width, variables = first_ref.shape[1], second_ref.shape[1]
    total = own_ref[...].astype(f32)
    for other in others:
        total = total + other[...].astype(f32)
    total = total * factor
    first_ref[...] = total[:, :width]
    second_ref[...] = total[:, width : width + variables]


def finish(own, others, width, variables, factor):
    rows = own.shape[0]
    return pl.pallas_call(
        functools.partial(finish_kernel, factor=factor),
        in_specs=[vmem] * (1 + len(others)),
        out_specs=[vmem] * 2,
        out_shape=[jax.ShapeDtypeStruct((rows, width), f32), jax.ShapeDtypeStruct((rows, variables), f32)],
        compiler_params=params(8),
        cost_estimate=cost(0, 1 << 20),
        name="finish",
    )(own, *others)


def moved(value, move):
    moves = []
    for member in range(8):
        for grid in range(16):
            y, x_hi, x_lo, z, core = member // 2, member % 2, grid // 8, (grid // 2) % 4, grid % 2
            y, x, z, core = move(y, x_hi * 2 + x_lo, z, core)
            target = (y * 2 + x // 2) * 16 + ((x % 2) * 4 + z) * 2 + core
            moves.append((member * 16 + grid, target))
    return lax.ppermute(value, ("member", "grid"), moves)


def summed(own, others):
    total = own.astype(f32)
    for other in others:
        total = total + other.astype(f32)
    return total


def over_core(send, keep):
    got = moved(send, lambda y, x, z, c: (y, x, z, 1 - c))
    return summed(keep, [got]).astype(bf16)


def over_z(part, rows):
    blocks = rows.reshape(2, 2, 64, rows.shape[1])
    return [
        moved(block, lambda y, x, z, c, k=k: (y, x, (z + k) % 4, c)) if k else block
        for k, block in zip(STEPS[part], blocks)
    ]


def over_x(blocks):
    got = [
        moved(blocks[0] if k == 2 else blocks[1], lambda y, x, z, c, k=k: (y, x ^ k, z, c))
        for k in (1, 3, 2)
    ]
    return summed(blocks[0], got).astype(bf16)


def over_y(block):
    return [moved(block, lambda y, x, z, c, k=k: (y ^ k, x, z, c)) for k in (1, 3, 2)]


def body(latents, hidden_weight, output_weight, observed, node_area_weight):
    latent = latents[0]
    members = lax.axis_size("member")
    groups = lax.axis_size("grid")
    nodes, width = latent.shape
    variables = output_weight.shape[1]
    place = lax.axis_index("member").astype(jnp.int32).reshape(1)
    grid = lax.axis_index("grid").astype(jnp.int32).reshape(1)

    forecast, hidden, slope, padded = forward(latent, hidden_weight, output_weight.T)
    blocks, late_grid = lax.optimization_barrier(((0.25 * forecast).astype(f16), grid))
    blocks = lax.all_to_all(blocks, "member", 0, 0, tiled=True)
    turned_latent = turned(late_grid, latent)
    low = pairs(place, 4.0 * blocks.astype(f32), observed, node_area_weight.reshape(1, nodes))
    low = lax.all_to_all(low, "member", 0, 0, tiled=True)
    grad_pre, send_a, keep_a, flat = backward_a(grid, low, turned_latent, slope, hidden, padded)
    send_b, keep_b = backward_b(grid, turned_latent, hidden, grad_pre, flat)
    rows_a, send_b = lax.optimization_barrier((over_core(send_a, keep_a), send_b))
    rows_b, grad_pre = lax.optimization_barrier((over_core(send_b, keep_b), grad_pre))
    grad_latent = latent_gradient(grad_pre, hidden_weight)
    plus, minus = over_z(0, rows_a)
    across, own = over_z(1, rows_b)
    blocks = summed(own, [plus, minus, across]).astype(bf16)
    blocks, grad_latent = lax.optimization_barrier((blocks, grad_latent))
    block = over_x(blocks)
    factor = 1.0 / math.sqrt(members * nodes * groups)
    first, second = finish(block, over_y(block), width, variables, factor)
    return grad_latent[None], first, second


def solution(mesh):
    in_specs = (P("member", "grid", None), P(), P(), P(None, "grid"), P("grid"))
    out_specs = (P("member", "grid", None), P("grid", None), P("grid", None))
    return jax.shard_map(body, mesh=mesh, in_specs=in_specs, out_specs=out_specs, check_vma=False)
```

time: 96.2 us -> 98.3 us (1.022)
  Pallas kernels: 30.1 us -> 35.8 us
  starting transfers between devices: 29.1 us -> 24.8 us
  waiting for transfers between devices: 28.5 us -> 30.4 us
  other arithmetic: 2.93 us -> 1.48 us
    pallas_call x3 -> x4, Pallas kernels: 15.1 us -> 20.7 us  [the longest x1 8.39 us: latent_gradient(): pl.pallas_call(latent_kernel, in_specs=[vmem, anywhere], out_specs=anywhe...]
    ppermute x14 -> x11, starting transfers between devices: 18.6 us -> 14.1 us  [moved(): return lax.ppermute(value, ('member', 'grid'), moves)]
    ppermute x14 -> x11, waiting for transfers between devices: 13.1 us -> 15.2 us  [moved(): return lax.ppermute(value, ('member', 'grid'), moves)]
    mul x2 -> x0, other arithmetic: 1.34 us -> none  [the longest x1 0.72 us: body(): total[:, :width] * factor]
  transfers between devices with their start and end apart: 16 -> 13, of which waited for: 9 -> 8; matrix products, arithmetic and copies ran while one was open for 0% -> 0% of each run, Pallas kernels for 11% -> 15%
where the time goes in v6:
time: 98.3 us; the launch traced here: 97.6 us
  Pallas kernels  35.8 us (36%)
  waiting for transfers between devices  30.4 us (31%)
  starting transfers between devices  24.8 us (25%)
  local copies, waits for them, and re-layouts  4.32 us (4%)
  other arithmetic  1.48 us (2%)
    ppermute x11, waiting for transfers between devices, moved(): return lax.ppermute(value, ('member', 'grid'), moves)  15.2 us
    ppermute x11, starting transfers between devices, moved(): return lax.ppermute(value, ('member', 'grid'), moves)  14.1 us
    pallas_call x1, Pallas kernels, forward(): pl.pallas_call(forward_kernel, in_specs=[anywhere] * 3, out_specs=[vmem,...  12.1 us
    all_to_all x1, waiting for transfers between devices, body(): blocks = lax.all_to_all(blocks, 'member', 0, 0, tiled=True)  10.9 us
    pallas_call x1, Pallas kernels, latent_gradient(): pl.pallas_call(latent_kernel, in_specs=[vmem, anywhere], out_specs=anywhe...  8.39 us
    all_to_all x1, starting transfers between devices, body(): blocks = lax.all_to_all(blocks, 'member', 0, 0, tiled=True)  7.01 us
    pallas_call x1, Pallas kernels, backward_a(): pl.pallas_call(backward_a_kernel, in_specs=[smem, vmem, anywhere, anywher...  6.75 us
    pallas_call x1, Pallas kernels, backward_b(): pl.pallas_call(backward_b_kernel, in_specs=[smem, anywhere, anywhere, vme...  4.78 us
  transfers between devices with their start and end apart: 13, of which 8 were waited for; matrix products, arithmetic and copies ran while one was open for 0% of the time, Pallas kernels for 15%

profile of v6, /device:TPU:0, one launch (start us, length us, event | category | flops | bytes accessed | tf_op | source)
XLA Modules:
  0.0 97.6 jit_solution(4461244047961992074)
XLA Ops:
  0.6 12.1 %forward.1 = (f32[8,112,256]{2,1,0:T(8,128)S(1)}, bf16[2048,1024]{1,0:T(8,128)(2,1)}, bf16[2048,1024]{1,0:T(8,128)(2,1)}, bf16[1024,128]{1,0:T(8,128)(2,1)S(1)}) custom-call(bf16[2048,1024]{1,0:T(8,128)(2,1)} %bitcast.17, bf16[1024,1024]{1,0:T(8,128)(2,1)} %weight_hbm.1, bf16[100,1024]{1,0:T(8,128)(2,1)} %bitcast.24), custom_call_target="tpu_custom_call" | custom-call | flops 4831838208 | bytes 20971520 | tf_op jit(solution)/shard_map/forward/pallas_call | solution.py:123
  12.7 0.0 copy-start.2
  12.7 0.0 copy-start.3
  12.7 0.9 multiply_convert_fusion
  13.6 7.0 %all-to-all-start = ((f16[8,112,256]{2,1,0:T(8,128)(2,1)}), f16[8,112,256]{2,1,0:T(8,128)(2,1)S(1)}, u32[]{:S(2)}, u32[]{:S(2)}) async-start(f16[8,112,256]{2,1,0:T(8,128)(2,1)} %multiply_convert_fusion), calls=%async_computation | async-start | bytes 917504 | tf_op jit(solution)/shard_map/all_to_all | solution.py:529
  20.6 10.9 %all-to-all-done = f16[8,112,256]{2,1,0:T(8,128)(2,1)S(1)} async-done(((f16[8,112,256]{2,1,0:T(8,128)(2,1)}), f16[8,112,256]{2,1,0:T(8,128)(2,1)S(1)}, u32[]{:S(2)}, u32[]{:S(2)}) %all-to-all-start) | async-done | bytes 458784 | tf_op jit(solution)/shard_map/all_to_all | solution.py:529
  31.5 0.1 convert_multiply_fusion.blocks_ref
  31.6 0.0 copy-done.2
  31.6 0.0 copy-done.3
  31.6 1.9 %pairs.1 = bf16[8,112,256]{2,1,0:T(8,128)(2,1)} custom-call(s32[1]{0:T(128)} %bitcast.3.place_ref, f32[8,112,256]{2,1,0:T(8,128)S(1)} %convert_multiply_fusion.blocks_ref, f32[100,2048]{1,0:T(8,128)S(1)} %copy-done.2, f32[1,2048]{1,0:T(1,128)S(1)} %bitcast.19), custom_call_target="tpu_custom_call" | custom-call | flops 4194304 | bytes 2097152 | tf_op jit(solution)/shard_map/pairs/pallas_call | solution.py:190
  33.5 3.7 %all-to-all-start.1 = ((bf16[8,112,256]{2,1,0:T(8,128)(2,1)}), bf16[8,112,256]{2,1,0:T(8,128)(2,1)S(1)}, u32[]{:S(2)}, u32[]{:S(2)}) async-start(bf16[8,112,256]{2,1,0:T(8,128)(2,1)} %pairs.1), calls=%async_computation.1 | async-start | bytes 917504 | tf_op jit(solution)/shard_map/all_to_all | solution.py:532
  37.2 0.0 copy-start.1
  37.2 2.2 %copy-done.1 = bf16[1,2048,1024]{2,1,0:T(8,128)(2,1)S(1)} copy-done((bf16[1,2048,1024]{2,1,0:T(8,128)(2,1)S(1)}, bf16[1,2048,1024]{2,1,0:T(8,128)(2,1)}, u32[]{:S(2)}) %copy-start.1) | copy-done | bytes 4194328
  39.4 1.1 %turned.1.turned_hbm = bf16[1024,2048]{1,0:T(8,128)(2,1)S(1)} custom-call(s32[1]{0:T(128)} %bitcast.grid_ref, bf16[2048,1024]{1,0:T(8,128)(2,1)S(1)} %bitcast.18), custom_call_target="tpu_custom_call" | custom-call | bytes 8388608 | tf_op jit(solution)/shard_map/turned/pallas_call | solution.py:237
  40.5 0.0 copy-start
  40.5 2.0 %copy-done = bf16[1024,2048]{1,0:T(8,128)(2,1)} copy-done((bf16[1024,2048]{1,0:T(8,128)(2,1)}, bf16[1024,2048]{1,0:T(8,128)(2,1)S(1)}, u32[]{:S(2)}) %copy-start) | copy-done | bytes 4194328
  42.5 4.4 %all-to-all-done.1.low_ref = bf16[8,112,256]{2,1,0:T(8,128)(2,1)S(1)} async-done(((bf16[8,112,256]{2,1,0:T(8,128)(2,1)}), bf16[8,112,256]{2,1,0:T(8,128)(2,1)S(1)}, u32[]{:S(2)}, u32[]{:S(2)}) %all-to-all-start.1) | async-done | bytes 458784 | tf_op jit(solution)/shard_map/all_to_all | solution.py:532
  46.9 6.8 %backward_a.1 = (bf16[2048,1024]{1,0:T(8,128)(2,1)S(1)}, bf16[256,1152]{1,0:T(8,128)(2,1)S(1)}, bf16[256,1152]{1,0:T(8,128)(2,1)S(1)}, bf16[128,2048]{1,0:T(8,128)(2,1)S(1)}) custom-call(s32[1]{0:T(128)} %bitcast.grid_ref, bf16[8,112,256]{2,1,0:T(8,128)(2,1)S(1)} %all-to-all-done.1.low_ref, bf16[1024,2048]{1,0:T(8,128)(2,1)} %copy-done, ...), custom_call_target="tpu_custom_call" | custom-call | flops 2952790016 | bytes 8388608 | tf_op jit(solution)/shard_map/backward_a/pallas_call | solution.py:372
  53.7 0.1 collective-permute-start
  53.7 4.8 %backward_b.1 = (bf16[256,1152]{1,0:T(8,128)(2,1)S(1)}, bf16[256,1152]{1,0:T(8,128)(2,1)S(1)}) custom-call(s32[1]{0:T(128)} %bitcast.grid_ref, bf16[1024,2048]{1,0:T(8,128)(2,1)} %copy-done, bf16[2048,1024]{1,0:T(8,128)(2,1)} %get-tuple-element.25.hidden_hbm, bf16[2048,1024]{1,0:T(8,128)(2,1)S(1)} %get-tuple-element.38.pre_ref, ...), custom_call_target="tpu_custom_call" | custom-call | flops 2415919104 | bytes 4194304 | tf_op jit(solution)/shard_map/backward_b/pallas_call | solution.py:391
  58.5 0.0 collective-permute-done
  58.5 0.1 add_convert_fusion.1
  58.7 0.6 collective-permute-start.1
  59.3 4.1 %collective-permute-start.3 = (bf16[2,64,1152]{2,1,0:T(8,128)(2,1)S(1)}, bf16[2,64,1152]{2,1,0:T(8,128)(2,1)S(1)}, u32[]{:S(2)}, u32[]{:S(2)}) collective-permute-start(bf16[2,64,1152]{2,1,0:T(8,128)(2,1)S(1)} %bitcast.22), channel_id=1, source_target_pairs={{0,6},{1,7},{2,0},{3,1},{4,2},{5,3},{6,4},{7,5},{8,14},{9,15},{10,... | collective-permute-start | bytes 884744 | tf_op jit(solution)/shard_map/ppermute | solution.py:483
  63.4 0.0 collective-permute-start.2
  63.4 0.0 collective-permute-done.1
  63.4 0.1 add_convert_fusion
  63.6 2.2 %collective-permute-start.4 = (bf16[2,64,1152]{2,1,0:T(8,128)(2,1)S(1)}, bf16[2,64,1152]{2,1,0:T(8,128)(2,1)S(1)}, u32[]{:S(2)}, u32[]{:S(2)}) collective-permute-start(bf16[2,64,1152]{2,1,0:T(8,128)(2,1)S(1)} %bitcast.23), channel_id=1, source_target_pairs={{0,4},{1,5},{2,6},{3,7},{4,0},{5,1},{6,2},{7,3},{8,12},{9,13},{10,... | collective-permute-start | bytes 884744 | tf_op jit(solution)/shard_map/ppermute | solution.py:483
  65.8 8.4 %latent_gradient.1 = bf16[2048,1024]{1,0:T(8,128)(2,1)} custom-call(bf16[2048,1024]{1,0:T(8,128)(2,1)S(1)} %get-tuple-element.38.pre_ref, bf16[1024,1024]{1,0:T(8,128)(2,1)} %weight_hbm.1), custom_call_target="tpu_custom_call" | custom-call | flops 4294967296 | bytes 10485760 | tf_op jit(solution)/shard_map/latent_gradient/pallas_call | solution.py:434
  74.2 2.0 %collective-permute-done.3 = bf16[2,64,1152]{2,1,0:T(8,128)(2,1)S(1)} collective-permute-done((bf16[2,64,1152]{2,1,0:T(8,128)(2,1)S(1)}, bf16[2,64,1152]{2,1,0:T(8,128)(2,1)S(1)}, u32[]{:S(2)}, u32[]{:S(2)}) %collective-permute-start.3) | collective-permute-done | bytes 294944 | tf_op jit(solution)/shard_map/ppermute | solution.py:483
  76.2 3.4 %collective-permute-done.2 = bf16[2,64,1152]{2,1,0:T(8,128)(2,1)S(1)} collective-permute-done((bf16[2,64,1152]{2,1,0:T(8,128)(2,1)S(1)}, bf16[2,64,1152]{2,1,0:T(8,128)(2,1)S(1)}, u32[]{:S(2)}, u32[]{:S(2)}) %collective-permute-start.2) | collective-permute-done | bytes 294944 | tf_op jit(solution)/shard_map/ppermute | solution.py:483
  79.6 0.0 collective-permute-done.4
  79.6 0.2 fusion.2
  79.8 0.9 collective-permute-start.7
  80.7 2.5 %collective-permute-start.6 = (bf16[64,1152]{1,0:T(8,128)(2,1)S(1)}, bf16[64,1152]{1,0:T(8,128)(2,1)S(1)}, u32[]{:S(2)}, u32[]{:S(2)}) collective-permute-start(bf16[64,1152]{1,0:T(8,128)(2,1)S(1)} %get-tuple-element.47), channel_id=1, source_target_pairs={{0,24},{1,25},{2,26},{3,27},{4,28},{5,29},{6,30},{7,31},{8,16},{9,... | collective-permute-start | bytes 442376 | tf_op jit(solution)/shard_map/ppermute | solution.py:483
  83.2 0.2 collective-permute-start.5
  83.4 3.7 %collective-permute-done.7 = bf16[64,1152]{1,0:T(8,128)(2,1)S(1)} collective-permute-done((bf16[64,1152]{1,0:T(8,128)(2,1)S(1)}, bf16[64,1152]{1,0:T(8,128)(2,1)S(1)}, u32[]{:S(2)}, u32[]{:S(2)}) %collective-permute-start.7) | collective-permute-done | bytes 147488 | tf_op jit(solution)/shard_map/ppermute | solution.py:483
  87.1 1.3 %collective-permute-done.6 = bf16[64,1152]{1,0:T(8,128)(2,1)S(1)} collective-permute-done((bf16[64,1152]{1,0:T(8,128)(2,1)S(1)}, bf16[64,1152]{1,0:T(8,128)(2,1)S(1)}, u32[]{:S(2)}, u32[]{:S(2)}) %collective-permute-start.6) | collective-permute-done | bytes 147488 | tf_op jit(solution)/shard_map/ppermute | solution.py:483
  88.4 0.0 collective-permute-done.5
  88.4 0.1 add_convert_fusion.2.own_ref
  88.5 1.0 %collective-permute-start.10 = (bf16[64,1152]{1,0:T(8,128)(2,1)S(1)}, bf16[64,1152]{1,0:T(8,128)(2,1)S(1)}, u32[]{:S(2)}, u32[]{:S(2)}) collective-permute-start(bf16[64,1152]{1,0:T(8,128)(2,1)S(1)} %add_convert_fusion.2.own_ref), channel_id=1, source_target_pairs={{0,64},{1,65},{2,66},{3,67},{4,68},{5,69},{6,70},{7,71},{8,72},{9,... | collective-permute-start | bytes 442376 | tf_op jit(solution)/shard_map/ppermute | solution.py:483
  89.5 2.1 %collective-permute-start.9 = (bf16[64,1152]{1,0:T(8,128)(2,1)S(1)}, bf16[64,1152]{1,0:T(8,128)(2,1)S(1)}, u32[]{:S(2)}, u32[]{:S(2)}) collective-permute-start(bf16[64,1152]{1,0:T(8,128)(2,1)S(1)} %add_convert_fusion.2.own_ref), channel_id=1, source_target_pairs={{0,96},{1,97},{2,98},{3,99},{4,100},{5,101},{6,102},{7,103},{8,104... | collective-permute-start | bytes 442376 | tf_op jit(solution)/shard_map/ppermute | solution.py:483
  91.6 0.5 collective-permute-start.8
  92.0 3.3 %collective-permute-done.10.refs_2_ = bf16[64,1152]{1,0:T(8,128)(2,1)S(1)} collective-permute-done((bf16[64,1152]{1,0:T(8,128)(2,1)S(1)}, bf16[64,1152]{1,0:T(8,128)(2,1)S(1)}, u32[]{:S(2)}, u32[]{:S(2)}) %collective-permute-start.10) | collective-permute-done | bytes 147488 | tf_op jit(solution)/shard_map/ppermute | solution.py:483
  95.3 1.5 %collective-permute-done.9.refs_1_ = bf16[64,1152]{1,0:T(8,128)(2,1)S(1)} collective-permute-done((bf16[64,1152]{1,0:T(8,128)(2,1)S(1)}, bf16[64,1152]{1,0:T(8,128)(2,1)S(1)}, u32[]{:S(2)}, u32[]{:S(2)}) %collective-permute-start.9) | collective-permute-done | bytes 147488 | tf_op jit(solution)/shard_map/ppermute | solution.py:483
  96.8 0.0 collective-permute-done.8.refs_0_
  96.8 0.8 finish.1
  (3 shorter events, 0.1 us)
Async XLA Ops:
  12.7 18.9 %copy-start.2 = (f32[100,2048]{1,0:T(8,128)S(1)}, f32[100,2048]{1,0:T(8,128)}, u32[]{:S(2)}) copy-start(f32[100,2048]{1,0:T(8,128)} %observed_ref.1) | copy-start | bytes 2457604
  12.7 18.9 %copy-start.3 = (f32[2048]{0:T(1024)S(1)}, f32[2048]{0:T(1024)}, u32[]{:S(2)}) copy-start(f32[2048]{0:T(1024)} %param.9) | copy-start | bytes 24580
  13.6 17.9 %all-to-all-start = ((f16[8,112,256]{2,1,0:T(8,128)(2,1)}), f16[8,112,256]{2,1,0:T(8,128)(2,1)S(1)}, u32[]{:S(2)}, u32[]{:S(2)}) async-start(f16[8,112,256]{2,1,0:T(8,128)(2,1)} %multiply_convert_fusion), calls=%async_computation | async-start | bytes 917504 | tf_op jit(solution)/shard_map/all_to_all | solution.py:529
  33.5 13.4 %all-to-all-start.1 = ((bf16[8,112,256]{2,1,0:T(8,128)(2,1)}), bf16[8,112,256]{2,1,0:T(8,128)(2,1)S(1)}, u32[]{:S(2)}, u32[]{:S(2)}) async-start(bf16[8,112,256]{2,1,0:T(8,128)(2,1)} %pairs.1), calls=%async_computation.1 | async-start | bytes 917504 | tf_op jit(solution)/shard_map/all_to_all | solution.py:532
  37.2 2.2 %copy-start.1 = (bf16[1,2048,1024]{2,1,0:T(8,128)(2,1)S(1)}, bf16[1,2048,1024]{2,1,0:T(8,128)(2,1)}, u32[]{:S(2)}) copy-start(bf16[1,2048,1024]{2,1,0:T(8,128)(2,1)} %param.5) | copy-start | bytes 12582916
  40.5 2.0 %copy-start = (bf16[1024,2048]{1,0:T(8,128)(2,1)}, bf16[1024,2048]{1,0:T(8,128)(2,1)S(1)}, u32[]{:S(2)}) copy-start(bf16[1024,2048]{1,0:T(8,128)(2,1)S(1)} %turned.1.turned_hbm) | copy-start | bytes 12582916
  53.7 4.9 %collective-permute-start = (bf16[256,1152]{1,0:T(8,128)(2,1)S(1)}, bf16[256,1152]{1,0:T(8,128)(2,1)S(1)}, u32[]{:S(2)}, u32[]{:S(2)}) collective-permute-start(bf16[256,1152]{1,0:T(8,128)(2,1)S(1)} %get-tuple-element.33), channel_id=1, source_target_pairs={{0,1},{1,0},{2,3},{3,2},{4,5},{5,4},{6,7},{7,6},{8,9},{9,8},{10,11... | collective-permute-start | bytes 1769480 | tf_op jit(solution)/shard_map/ppermute | solution.py:483
  58.7 4.7 %collective-permute-start.1 = (bf16[256,1152]{1,0:T(8,128)(2,1)S(1)}, bf16[256,1152]{1,0:T(8,128)(2,1)S(1)}, u32[]{:S(2)}, u32[]{:S(2)}) collective-permute-start(bf16[256,1152]{1,0:T(8,128)(2,1)S(1)} %get-tuple-element.35), channel_id=1, source_target_pairs={{0,1},{1,0},{2,3},{3,2},{4,5},{5,4},{6,7},{7,6},{8,9},{9,8},{10,11... | collective-permute-start | bytes 1769480 | tf_op jit(solution)/shard_map/ppermute | solution.py:483
  59.3 16.9 %collective-permute-start.3 = (bf16[2,64,1152]{2,1,0:T(8,128)(2,1)S(1)}, bf16[2,64,1152]{2,1,0:T(8,128)(2,1)S(1)}, u32[]{:S(2)}, u32[]{:S(2)}) collective-permute-start(bf16[2,64,1152]{2,1,0:T(8,128)(2,1)S(1)} %bitcast.22), channel_id=1, source_target_pairs={{0,6},{1,7},{2,0},{3,1},{4,2},{5,3},{6,4},{7,5},{8,14},{9,15},{10,... | collective-permute-start | bytes 884744 | tf_op jit(solution)/shard_map/ppermute | solution.py:483
  63.4 16.2 %collective-permute-start.2 = (bf16[2,64,1152]{2,1,0:T(8,128)(2,1)S(1)}, bf16[2,64,1152]{2,1,0:T(8,128)(2,1)S(1)}, u32[]{:S(2)}, u32[]{:S(2)}) collective-permute-start(bf16[2,64,1152]{2,1,0:T(8,128)(2,1)S(1)} %bitcast.21), channel_id=1, source_target_pairs={{0,2},{1,3},{2,4},{3,5},{4,6},{5,7},{6,0},{7,1},{8,10},{9,11},{10,... | collective-permute-start | bytes 884744 | tf_op jit(solution)/shard_map/ppermute | solution.py:483
  63.6 16.0 %collective-permute-start.4 = (bf16[2,64,1152]{2,1,0:T(8,128)(2,1)S(1)}, bf16[2,64,1152]{2,1,0:T(8,128)(2,1)S(1)}, u32[]{:S(2)}, u32[]{:S(2)}) collective-permute-start(bf16[2,64,1152]{2,1,0:T(8,128)(2,1)S(1)} %bitcast.23), channel_id=1, source_target_pairs={{0,4},{1,5},{2,6},{3,7},{4,0},{5,1},{6,2},{7,3},{8,12},{9,13},{10,... | collective-permute-start | bytes 884744 | tf_op jit(solution)/shard_map/ppermute | solution.py:483
  79.8 7.3 %collective-permute-start.7 = (bf16[64,1152]{1,0:T(8,128)(2,1)S(1)}, bf16[64,1152]{1,0:T(8,128)(2,1)S(1)}, u32[]{:S(2)}, u32[]{:S(2)}) collective-permute-start(bf16[64,1152]{1,0:T(8,128)(2,1)S(1)} %get-tuple-element.48), channel_id=1, source_target_pairs={{0,16},{1,17},{2,18},{3,19},{4,20},{5,21},{6,22},{7,23},{8,24},{9,... | collective-permute-start | bytes 442376 | tf_op jit(solution)/shard_map/ppermute | solution.py:483
  80.7 7.7 %collective-permute-start.6 = (bf16[64,1152]{1,0:T(8,128)(2,1)S(1)}, bf16[64,1152]{1,0:T(8,128)(2,1)S(1)}, u32[]{:S(2)}, u32[]{:S(2)}) collective-permute-start(bf16[64,1152]{1,0:T(8,128)(2,1)S(1)} %get-tuple-element.47), channel_id=1, source_target_pairs={{0,24},{1,25},{2,26},{3,27},{4,28},{5,29},{6,30},{7,31},{8,16},{9,... | collective-permute-start | bytes 442376 | tf_op jit(solution)/shard_map/ppermute | solution.py:483
  83.2 5.2 %collective-permute-start.5 = (bf16[64,1152]{1,0:T(8,128)(2,1)S(1)}, bf16[64,1152]{1,0:T(8,128)(2,1)S(1)}, u32[]{:S(2)}, u32[]{:S(2)}) collective-permute-start(bf16[64,1152]{1,0:T(8,128)(2,1)S(1)} %get-tuple-element.47), channel_id=1, source_target_pairs={{0,8},{1,9},{2,10},{3,11},{4,12},{5,13},{6,14},{7,15},{8,0},{9,1},... | collective-permute-start | bytes 442376 | tf_op jit(solution)/shard_map/ppermute | solution.py:483
  88.5 6.8 %collective-permute-start.10 = (bf16[64,1152]{1,0:T(8,128)(2,1)S(1)}, bf16[64,1152]{1,0:T(8,128)(2,1)S(1)}, u32[]{:S(2)}, u32[]{:S(2)}) collective-permute-start(bf16[64,1152]{1,0:T(8,128)(2,1)S(1)} %add_convert_fusion.2.own_ref), channel_id=1, source_target_pairs={{0,64},{1,65},{2,66},{3,67},{4,68},{5,69},{6,70},{7,71},{8,72},{9,... | collective-permute-start | bytes 442376 | tf_op jit(solution)/shard_map/ppermute | solution.py:483
  89.5 7.3 %collective-permute-start.9 = (bf16[64,1152]{1,0:T(8,128)(2,1)S(1)}, bf16[64,1152]{1,0:T(8,128)(2,1)S(1)}, u32[]{:S(2)}, u32[]{:S(2)}) collective-permute-start(bf16[64,1152]{1,0:T(8,128)(2,1)S(1)} %add_convert_fusion.2.own_ref), channel_id=1, source_target_pairs={{0,96},{1,97},{2,98},{3,99},{4,100},{5,101},{6,102},{7,103},{8,104... | collective-permute-start | bytes 442376 | tf_op jit(solution)/shard_map/ppermute | solution.py:483
  91.6 5.2 %collective-permute-start.8 = (bf16[64,1152]{1,0:T(8,128)(2,1)S(1)}, bf16[64,1152]{1,0:T(8,128)(2,1)S(1)}, u32[]{:S(2)}, u32[]{:S(2)}) collective-permute-start(bf16[64,1152]{1,0:T(8,128)(2,1)S(1)} %add_convert_fusion.2.own_ref), channel_id=1, source_target_pairs={{0,32},{1,33},{2,34},{3,35},{4,36},{5,37},{6,38},{7,39},{8,40},{9,... | collective-permute-start | bytes 442376 | tf_op jit(solution)/shard_map/ppermute | solution.py:483

commit v7 on v6

--- a/solution.py
+++ b/solution.py
@@ -245,52 +245,46 @@
     )(grid, latent)
 
 
-class PartLoads:
-    def __init__(self, part, grid_ref, turned_hbm, hidden_hbm, turned_ref, hidden_ref, turned_sems, hidden_sems):
-        x_lo, z, self.core = position(grid_ref)
-        self.turned_ref, self.hidden_ref = turned_ref, hidden_ref
-        self.turned = [
-            pltpu.make_async_copy(
-                turned_hbm.at[pl.ds(part * 512 + start, 256)], turned_ref.at[pl.ds(start, 256)], turned_sems.at[start // 256]
-            )
-            for start in (0, 256)
-        ]
-        self.hidden = [
-            pltpu.make_async_copy(
-                hidden_hbm.at[:, pl.ds(pl.multiple_of(owner(block, STEPS[part], x_lo, z) * 128, 128), 128)],
-                hidden_ref.at[:, pl.ds(block * 128, 128)],
-                hidden_sems.at[block],
-            )
-            for block in range(4)
-        ]
-
-    def start(self):
-        for load in self.turned + self.hidden:
-            load.start()
-
-    def products(self, pre_ref, flat_ref, send_ref, keep_ref, second_ref):
-        width = pre_ref.shape[1]
-        for load, out_ref, start in zip(self.turned, (send_ref, keep_ref), (0, 256)):
-            load.wait()
-            for column in range(0, width, 512):
-                columns = slice(column, column + 512)
-                part = jnp.dot(self.turned_ref[start : start + 256, :], pre_ref[:, columns], preferred_element_type=f32)
-                out_ref[:, columns] = part.astype(bf16)
-        for load in self.hidden:
-            load.wait()
-        for start in (0, 256):
-            rows = slice(start, start + 256)
-            second = jnp.dot(flat_ref[...], self.hidden_ref[:, rows], preferred_element_type=f32)
-            second_ref[rows, :] = second.T.astype(bf16)
-        for block in range(4):
-            rows = slice(block * 64, (block + 1) * 64)
-            mine = pl.multiple_of(block * 128 + self.core * 64, 64)
-            other = pl.multiple_of(block * 128 + (1 - self.core) * 64, 64)
-            keep_ref[rows, width:] = second_ref[pl.ds(mine, 64), :]
-            send_ref[rows, width:] = second_ref[pl.ds(other, 64), :]
-
-
-def backward_a_kernel(
+def turned_load(turned_hbm, start, turned_ref, sem):
+    return pltpu.make_async_copy(turned_hbm.at[pl.ds(start, 256)], turned_ref, sem)
+
+
+def hidden_loads(part, grid_ref, hidden_hbm, hidden_ref, sems):
+    x_lo, z, core = position(grid_ref)
+    return [
+        pltpu.make_async_copy(
+            hidden_hbm.at[:, pl.ds(pl.multiple_of(owner(block, STEPS[part], x_lo, z) * 128, 128), 128)],
+            hidden_ref.at[:, pl.ds(block * 128, 128)],
+            sems.at[block],
+        )
+        for block in range(4)
+    ]
+
+
+def first_product(turned_ref, pre_ref, out_ref):
+    width = pre_ref.shape[1]
+    for column in range(0, width, 512):
+        columns = slice(column, column + 512)
+        part = jnp.dot(turned_ref[...], pre_ref[:, columns], preferred_element_type=f32)
+        out_ref[:, columns] = part.astype(bf16)
+
+
+def second_product(grid_ref, flat_ref, hidden_ref, send_ref, second_ref, scratch_ref):
+    width = send_ref.shape[1] - WIDE
+    core = position(grid_ref)[2]
+    for start in (0, 256):
+        rows = slice(start, start + 256)
+        second = jnp.dot(flat_ref[...], hidden_ref[:, rows], preferred_element_type=f32)
+        scratch_ref[rows, :] = second.T.astype(bf16)
+    for block in range(4):
+        rows = slice(block * 64, (block + 1) * 64)
+        mine = pl.multiple_of(block * 128 + core * 64, 64)
+        other = pl.multiple_of(block * 128 + (1 - core) * 64, 64)
+        second_ref[rows, :] = scratch_ref[pl.ds(mine, 64), :]
+        send_ref[rows, width:] = scratch_ref[pl.ds(other, 64), :]
+
+
+def send_a_kernel(
     grid_ref,
     low_ref,
     turned_hbm,
@@ -299,28 +293,30 @@
     padded_ref,
     pre_ref,
     send_ref,
-    keep_ref,
+    second_ref,
     flat_ref,
+    next_turned_ref,
     turn_ref,
     turned_ref,
     hidden_ref,
-    second_ref,
+    scratch_ref,
     slope_ref,
     turned_sems,
     hidden_sems,
     slope_sems,
 ):
     nodes, width = pre_ref.shape
-    loads = PartLoads(0, grid_ref, turned_hbm, hidden_hbm, turned_ref, hidden_ref, turned_sems, hidden_sems)
     slope_loads = [
         pltpu.make_async_copy(
             slope_hbm.at[:, pl.ds(start, COLS)], slope_ref.at[:, pl.ds(start, COLS)], slope_sems.at[start // COLS]
         )
         for start in range(0, width, COLS)
     ]
-    for load in slope_loads:
+    turned_now = turned_load(turned_hbm, 0, turned_ref, turned_sems.at[0])
+    turned_next = turned_load(turned_hbm, 256, next_turned_ref, turned_sems.at[1])
+    hidden_now = hidden_loads(0, grid_ref, hidden_hbm, hidden_ref, hidden_sems)
+    for load in slope_loads + [turned_now] + hidden_now + [turned_next]:
         load.start()
-    loads.start()
     for share in range(low_ref.shape[0]):
         columns = slice(share * SHARE, (share + 1) * SHARE)
         low = jnp.concatenate([low_ref[share], jnp.zeros((WIDE - TALL, SHARE), bf16)], axis=0)
@@ -333,89 +329,146 @@
             rows = slice(start, start + ROWS)
             grad_hidden = lax.dot_general(turn_ref[rows, :], padded_ref[columns, :], NT, preferred_element_type=f32)
             pre_ref[rows, columns] = (grad_hidden * slope_ref[rows, columns].astype(f32)).astype(bf16)
-    loads.products(pre_ref, flat_ref, send_ref, keep_ref, second_ref)
-
-
-def backward_b_kernel(
+    turned_now.wait()
+    first_product(turned_ref, pre_ref, send_ref)
+    for load in hidden_now:
+        load.wait()
+    second_product(grid_ref, flat_ref, hidden_ref, send_ref, second_ref, scratch_ref)
+    turned_next.wait()
+
+
+def keep_a_kernel(
     grid_ref,
     turned_hbm,
     hidden_hbm,
     pre_ref,
+    turned_ref,
+    second_ref,
+    keep_ref,
+    next_turned_ref,
+    next_hidden_ref,
+    turned_sem,
+    hidden_sems,
+):
+    loads = [turned_load(turned_hbm, 512, next_turned_ref, turned_sem)]
+    loads += hidden_loads(1, grid_ref, hidden_hbm, next_hidden_ref, hidden_sems)
+    for load in loads:
+        load.start()
+    first_product(turned_ref, pre_ref, keep_ref)
+    keep_ref[:, pre_ref.shape[1] :] = second_ref[...]
+    for load in loads:
+        load.wait()
+
+
+def send_b_kernel(
+    grid_ref,
+    turned_hbm,
+    pre_ref,
     flat_ref,
-    send_ref,
-    keep_ref,
     turned_ref,
     hidden_ref,
+    send_ref,
     second_ref,
-    turned_sems,
-    hidden_sems,
+    next_turned_ref,
+    scratch_ref,
+    turned_sem,
 ):
-    loads = PartLoads(1, grid_ref, turned_hbm, hidden_hbm, turned_ref, hidden_ref, turned_sems, hidden_sems)
-    loads.start()
-    loads.products(pre_ref, flat_ref, send_ref, keep_ref, second_ref)
-
-
-def part_shapes(nodes, width):
-    out = [jax.ShapeDtypeStruct((256, width + WIDE), bf16)] * 2
-    scratch = [
-        pltpu.VMEM((512, nodes), bf16),
-        pltpu.VMEM((nodes, 512), bf16),
-        pltpu.VMEM((512, WIDE), bf16),
-    ]
-    sems = [pltpu.SemaphoreType.DMA((2,)), pltpu.SemaphoreType.DMA((4,))]
-    return out, scratch, sems
-
-
-def backward_a(grid, low, turned_latent, slope, hidden, padded):
+    load = turned_load(turned_hbm, 768, next_turned_ref, turned_sem)
+    load.start()
+    first_product(turned_ref, pre_ref, send_ref)
+    second_product(grid_ref, flat_ref, hidden_ref, send_ref, second_ref, scratch_ref)
+    load.wait()
+
+
+def keep_b_kernel(weight_hbm, pre_ref, turned_ref, second_ref, keep_ref, weight_ref, weight_sem):
+    load = pltpu.make_async_copy(weight_hbm, weight_ref, weight_sem)
+    load.start()
+    first_product(turned_ref, pre_ref, keep_ref)
+    keep_ref[:, pre_ref.shape[1] :] = second_ref[...]
+    load.wait()
+
+
+def shape(*dims):
+    return jax.ShapeDtypeStruct(dims, bf16)
+
+
+def send_a(grid, low, turned_latent, slope, hidden, padded):
     nodes, width = slope.shape
-    out, scratch, sems = part_shapes(nodes, width)
-    return pl.pallas_call(
-        backward_a_kernel,
+    return pl.pallas_call(
+        send_a_kernel,
         in_specs=[smem, vmem, anywhere, anywhere, anywhere, vmem],
-        out_specs=[vmem] * 4,
-        out_shape=[jax.ShapeDtypeStruct((nodes, width), bf16)] + out + [jax.ShapeDtypeStruct((WIDE, nodes), bf16)],
-        scratch_shapes=[pltpu.VMEM((nodes, WIDE), bf16)]
-        + scratch
-        + [pltpu.VMEM((nodes, width), bf16)]
-        + sems
-        + [pltpu.SemaphoreType.DMA((width // COLS,))],
+        out_specs=[vmem] * 5,
+        out_shape=[
+            shape(nodes, width),
+            shape(256, width + WIDE),
+            shape(256, WIDE),
+            shape(WIDE, nodes),
+            shape(256, nodes),
+        ],
+        scratch_shapes=[
+            pltpu.VMEM((nodes, WIDE), bf16),
+            pltpu.VMEM((256, nodes), bf16),
+            pltpu.VMEM((nodes, 512), bf16),
+            pltpu.VMEM((512, WIDE), bf16),
+            pltpu.VMEM((nodes, width), bf16),
+            pltpu.SemaphoreType.DMA((2,)),
+            pltpu.SemaphoreType.DMA((4,)),
+            pltpu.SemaphoreType.DMA((width // COLS,)),
+        ],
         compiler_params=params(20),
-        cost_estimate=cost(nodes * width * (width + 3 * WIDE), 8 << 20),
-        name="backward_a",
+        cost_estimate=cost(nodes * width * (width // 2 + 3 * WIDE), 8 << 20),
+        name="send_a",
     )(grid, low, pinned(turned_latent), pinned(slope), pinned(hidden), padded)
 
 
-def backward_b(grid, turned_latent, hidden, grad_pre, flat):
+def keep_a(grid, turned_latent, hidden, grad_pre, turned_now, second):
     nodes, width = hidden.shape
-    out, scratch, sems = part_shapes(nodes, width)
-    return pl.pallas_call(
-        backward_b_kernel,
-        in_specs=[smem, anywhere, anywhere, vmem, vmem],
+    return pl.pallas_call(
+        keep_a_kernel,
+        in_specs=[smem, anywhere, anywhere] + [vmem] * 3,
+        out_specs=[vmem] * 3,
+        out_shape=[shape(256, width + WIDE), shape(256, nodes), shape(nodes, 512)],
+        scratch_shapes=[pltpu.SemaphoreType.DMA, pltpu.SemaphoreType.DMA((4,))],
+        compiler_params=params(12),
+        cost_estimate=cost(nodes * width * width // 2, 4 << 20),
+        name="keep_a",
+    )(grid, pinned(turned_latent), pinned(hidden), grad_pre, turned_now, second)
+
+
+def send_b(grid, turned_latent, grad_pre, flat, turned_now, hidden_now):
+    nodes, width = grad_pre.shape
+    return pl.pallas_call(
+        send_b_kernel,
+        in_specs=[smem, anywhere] + [vmem] * 4,
+        out_specs=[vmem] * 3,
+        out_shape=[shape(256, width + WIDE), shape(256, WIDE), shape(256, nodes)],
+        scratch_shapes=[pltpu.VMEM((512, WIDE), bf16), pltpu.SemaphoreType.DMA],
+        compiler_params=params(12),
+        cost_estimate=cost(nodes * width * width // 2, 4 << 20),
+        name="send_b",
+    )(grid, pinned(turned_latent), grad_pre, flat, turned_now, hidden_now)
+
+
+def keep_b(weight, grad_pre, turned_now, second):
+    nodes, width = grad_pre.shape
+    return pl.pallas_call(
+        keep_b_kernel,
+        in_specs=[anywhere] + [vmem] * 3,
         out_specs=[vmem] * 2,
-        out_shape=out,
-        scratch_shapes=scratch + sems,
-        compiler_params=params(16),
-        cost_estimate=cost(nodes * width * (width + WIDE), 4 << 20),
-        name="backward_b",
-    )(grid, pinned(turned_latent), pinned(hidden), grad_pre, flat)
-
-
-def latent_kernel(pre_ref, weight_hbm, out_ref, weight_ref, result_ref, weight_sems, sems):
+        out_shape=[shape(256, width + WIDE), shape(width, width)],
+        scratch_shapes=[pltpu.SemaphoreType.DMA],
+        compiler_params=params(12),
+        cost_estimate=cost(nodes * width * width // 2, 4 << 20),
+        name="keep_b",
+    )(pinned(weight), grad_pre, turned_now, second)
+
+
+def latent_kernel(pre_ref, weight_ref, out_ref, result_ref, sems):
     nodes, width = pre_ref.shape
-    loads = [
-        pltpu.make_async_copy(
-            weight_hbm.at[pl.ds(start, COLS)], weight_ref.at[pl.ds(start, COLS)], weight_sems.at[start // COLS]
-        )
-        for start in range(0, width, COLS)
-    ]
-    for load in loads:
-        load.start()
     stores = []
     for row in range(0, nodes, ROWS):
         rows = slice(row, row + ROWS)
         for start in range(0, width, COLS):
-            if row == 0:
-                loads[start // COLS].wait()
             columns = slice(start, start + COLS)
             result_ref[rows, columns] = lax.dot_general(
                 pre_ref[rows, :], weight_ref[columns, :], NT, preferred_element_type=f32
@@ -433,19 +486,14 @@
     nodes, width = grad_pre.shape
     return pl.pallas_call(
         latent_kernel,
-        in_specs=[vmem, anywhere],
+        in_specs=[vmem, vmem],
         out_specs=anywhere,
         out_shape=pltpu.HBM((nodes, width), bf16),
-        scratch_shapes=[
-            pltpu.VMEM((width, width), bf16),
-            pltpu.VMEM((nodes, width), bf16),
-            pltpu.SemaphoreType.DMA((width // COLS,)),
-            pltpu.SemaphoreType.DMA((nodes // ROWS,)),
-        ],
+        scratch_shapes=[pltpu.VMEM((nodes, width), bf16), pltpu.SemaphoreType.DMA((nodes // ROWS,))],
         compiler_params=params(12),
         cost_estimate=cost(2 * nodes * width * width, 10 << 20),
         name="latent_gradient",
-    )(grad_pre, pinned(weight))
+    )(grad_pre, weight)
 
 
 def finish_kernel(own_ref, *refs, factor):
@@ -530,11 +578,13 @@
     turned_latent = turned(late_grid, latent)
     low = pairs(place, 4.0 * blocks.astype(f32), observed, node_area_weight.reshape(1, nodes))
     low = lax.all_to_all(low, "member", 0, 0, tiled=True)
-    grad_pre, send_a, keep_a, flat = backward_a(grid, low, turned_latent, slope, hidden, padded)
-    send_b, keep_b = backward_b(grid, turned_latent, hidden, grad_pre, flat)
-    rows_a, send_b = lax.optimization_barrier((over_core(send_a, keep_a), send_b))
-    rows_b, grad_pre = lax.optimization_barrier((over_core(send_b, keep_b), grad_pre))
-    grad_latent = latent_gradient(grad_pre, hidden_weight)
+    grad_pre, rows_a, second_a, flat, turned_now = send_a(grid, low, turned_latent, slope, hidden, padded)
+    kept_a, turned_now, hidden_now = keep_a(grid, turned_latent, hidden, grad_pre, turned_now, second_a)
+    rows_a, flat = lax.optimization_barrier((over_core(rows_a, kept_a), flat))
+    rows_b, second_b, turned_now = send_b(grid, turned_latent, grad_pre, flat, turned_now, hidden_now)
+    kept_b, weight_copy = keep_b(hidden_weight, grad_pre, turned_now, second_b)
+    rows_b, grad_pre = lax.optimization_barrier((over_core(rows_b, kept_b), grad_pre))
+    grad_latent = latent_gradient(grad_pre, weight_copy)
     plus, minus = over_z(0, rows_a)
     across, own = over_z(1, rows_b)
     blocks = summed(own, [plus, minus, across]).astype(bf16)

time: 98.3 us -> 97.9 us (level)
  Pallas kernels: 35.8 us -> 33.8 us
  waiting for transfers between devices: 30.4 us -> 32 us
    pallas_call x3 -> x5, Pallas kernels: 19.9 us -> 18 us  [the longest x1 5.59 us: latent_gradient(): pl.pallas_call(latent_kernel, in_specs=[vmem, vmem], out_specs=anywhere,...]
    ppermute x11, waiting for transfers between devices: 15.2 us -> 16.5 us  [moved(): return lax.ppermute(value, ('member', 'grid'), moves)]
  transfers between devices with their start and end apart: 13 -> 13, of which waited for: 8 -> 8; matrix products, arithmetic and copies ran while one was open for 0% -> 0% of each run, Pallas kernels for 15% -> 12%
where the time goes in v7:
time: 97.9 us; the launch traced here: 97 us
  Pallas kernels  33.8 us (35%)
  waiting for transfers between devices  32 us (33%)
  starting transfers between devices  24.6 us (25%)
  local copies, waits for them, and re-layouts  4.32 us (4%)
  other arithmetic  1.52 us (2%)
    ppermute x11, waiting for transfers between devices, moved(): return lax.ppermute(value, ('member', 'grid'), moves)  16.5 us
    ppermute x11, starting transfers between devices, moved(): return lax.ppermute(value, ('member', 'grid'), moves)  14.1 us
    pallas_call x1, Pallas kernels, forward(): pl.pallas_call(forward_kernel, in_specs=[anywhere] * 3, out_specs=[vmem,...  12.1 us
    all_to_all x1, waiting for transfers between devices, body(): blocks = lax.all_to_all(blocks, 'member', 0, 0, tiled=True)  10.9 us
    all_to_all x1, starting transfers between devices, body(): blocks = lax.all_to_all(blocks, 'member', 0, 0, tiled=True)  7.01 us
    pallas_call x1, Pallas kernels, latent_gradient(): pl.pallas_call(latent_kernel, in_specs=[vmem, vmem], out_specs=anywhere,...  5.59 us
    pallas_call x1, Pallas kernels, send_a(): pl.pallas_call(send_a_kernel, in_specs=[smem, vmem, anywhere, anywhere, a...  5.48 us
    all_to_all x1, waiting for transfers between devices, body(): low = lax.all_to_all(low, 'member', 0, 0, tiled=True)  4.56 us
  transfers between devices with their start and end apart: 13, of which 8 were waited for; matrix products, arithmetic and copies ran while one was open for 0% of the time, Pallas kernels for 12%

profile of v7, /device:TPU:0, one launch (start us, length us, event | category | flops | bytes accessed | tf_op | source)
XLA Modules:
  0.0 97.0 jit_solution(18387088725815808302)
XLA Ops:
  0.6 12.1 %forward.1 = (f32[8,112,256]{2,1,0:T(8,128)S(1)}, bf16[2048,1024]{1,0:T(8,128)(2,1)}, bf16[2048,1024]{1,0:T(8,128)(2,1)}, bf16[1024,128]{1,0:T(8,128)(2,1)S(1)}) custom-call(bf16[2048,1024]{1,0:T(8,128)(2,1)} %bitcast.17, bf16[1024,1024]{1,0:T(8,128)(2,1)} %weight_hbm.1, bf16[100,1024]{1,0:T(8,128)(2,1)} %bitcast.24), custom_call_target="tpu_custom_call" | custom-call | flops 4831838208 | bytes 20971520 | tf_op jit(solution)/shard_map/forward/pallas_call | solution.py:123
  12.7 0.0 copy-start.2
  12.7 0.0 copy-start.3
  12.7 0.9 multiply_convert_fusion
  13.6 7.0 %all-to-all-start = ((f16[8,112,256]{2,1,0:T(8,128)(2,1)}), f16[8,112,256]{2,1,0:T(8,128)(2,1)S(1)}, u32[]{:S(2)}, u32[]{:S(2)}) async-start(f16[8,112,256]{2,1,0:T(8,128)(2,1)} %multiply_convert_fusion), calls=%async_computation | async-start | bytes 917504 | tf_op jit(solution)/shard_map/all_to_all | solution.py:577
  20.6 10.9 %all-to-all-done = f16[8,112,256]{2,1,0:T(8,128)(2,1)S(1)} async-done(((f16[8,112,256]{2,1,0:T(8,128)(2,1)}), f16[8,112,256]{2,1,0:T(8,128)(2,1)S(1)}, u32[]{:S(2)}, u32[]{:S(2)}) %all-to-all-start) | async-done | bytes 458784 | tf_op jit(solution)/shard_map/all_to_all | solution.py:577
  31.5 0.1 convert_multiply_fusion.blocks_ref
  31.6 0.0 copy-done.2
  31.6 0.0 copy-done.3
  31.6 1.9 %pairs.1 = bf16[8,112,256]{2,1,0:T(8,128)(2,1)} custom-call(s32[1]{0:T(128)} %bitcast.1.place_ref, f32[8,112,256]{2,1,0:T(8,128)S(1)} %convert_multiply_fusion.blocks_ref, f32[100,2048]{1,0:T(8,128)S(1)} %copy-done.2, f32[1,2048]{1,0:T(1,128)S(1)} %bitcast.19), custom_call_target="tpu_custom_call" | custom-call | flops 4194304 | bytes 2097152 | tf_op jit(solution)/shard_map/pairs/pallas_call | solution.py:190
  33.5 3.5 %all-to-all-start.1 = ((bf16[8,112,256]{2,1,0:T(8,128)(2,1)}), bf16[8,112,256]{2,1,0:T(8,128)(2,1)S(1)}, u32[]{:S(2)}, u32[]{:S(2)}) async-start(bf16[8,112,256]{2,1,0:T(8,128)(2,1)} %pairs.1), calls=%async_computation.1 | async-start | bytes 917504 | tf_op jit(solution)/shard_map/all_to_all | solution.py:580
  37.0 0.0 copy-start.1
  37.0 2.2 %copy-done.1 = bf16[1,2048,1024]{2,1,0:T(8,128)(2,1)S(1)} copy-done((bf16[1,2048,1024]{2,1,0:T(8,128)(2,1)S(1)}, bf16[1,2048,1024]{2,1,0:T(8,128)(2,1)}, u32[]{:S(2)}) %copy-start.1) | copy-done | bytes 4194328
  39.2 1.1 %turned.1.turned_hbm = bf16[1024,2048]{1,0:T(8,128)(2,1)S(1)} custom-call(s32[1]{0:T(128)} %bitcast.grid_ref, bf16[2048,1024]{1,0:T(8,128)(2,1)S(1)} %bitcast.18), custom_call_target="tpu_custom_call" | custom-call | bytes 8388608 | tf_op jit(solution)/shard_map/turned/pallas_call | solution.py:237
  40.3 0.0 copy-start
  40.3 2.0 %copy-done = bf16[1024,2048]{1,0:T(8,128)(2,1)} copy-done((bf16[1024,2048]{1,0:T(8,128)(2,1)}, bf16[1024,2048]{1,0:T(8,128)(2,1)S(1)}, u32[]{:S(2)}) %copy-start) | copy-done | bytes 4194328
  42.4 4.6 %all-to-all-done.1.low_ref = bf16[8,112,256]{2,1,0:T(8,128)(2,1)S(1)} async-done(((bf16[8,112,256]{2,1,0:T(8,128)(2,1)}), bf16[8,112,256]{2,1,0:T(8,128)(2,1)S(1)}, u32[]{:S(2)}, u32[]{:S(2)}) %all-to-all-start.1) | async-done | bytes 458784 | tf_op jit(solution)/shard_map/all_to_all | solution.py:580
  46.9 5.5 %send_a.1 = (bf16[2048,1024]{1,0:T(8,128)(2,1)S(1)}, bf16[256,1152]{1,0:T(8,128)(2,1)S(1)}, bf16[256,128]{1,0:T(8,128)(2,1)S(1)}, bf16[128,2048]{1,0:T(8,128)(2,1)S(1)}, bf16[256,2048]{1,0:T(8,128)(2,1)S(1)}) custom-call(s32[1]{0:T(128)} %bitcast.grid_ref, bf16[8,112,256]{2,1,0:T(8,128)(2,1)S(1)} %all-to-all-done.1.low_ref, bf16[1024,2048]{1,0:T(8,128)(2,1)} %copy-done, ...), custom_call_target="tpu_custom_call" | custom-call | flops 1879048192 | bytes 8388608 | tf_op jit(solution)/shard_map/send_a/pallas_call | solution.py:397
  52.4 0.3 collective-permute-start
  52.7 3.0 %keep_a.1 = (bf16[256,1152]{1,0:T(8,128)(2,1)S(1)}, bf16[256,2048]{1,0:T(8,128)(2,1)S(1)}, bf16[2048,512]{1,0:T(8,128)(2,1)S(1)}) custom-call(s32[1]{0:T(128)} %bitcast.grid_ref, bf16[1024,2048]{1,0:T(8,128)(2,1)} %copy-done, bf16[2048,1024]{1,0:T(8,128)(2,1)} %get-tuple-element.34.hidden_hbm, bf16[2048,1024]{1,0:T(8,128)(2,1)S(1)} %get-tuple-element.51.pre_ref, ...), custom_call_target="tpu_custom_call" | custom-call | flops 1073741824 | bytes 4194304 | tf_op jit(solution)/shard_map/keep_a/pallas_call | solution.py:426
  55.6 0.0 collective-permute-done
  55.7 0.1 add_convert_fusion.1
  55.8 2.3 %send_b.1 = (bf16[256,1152]{1,0:T(8,128)(2,1)S(1)}, bf16[256,128]{1,0:T(8,128)(2,1)S(1)}, bf16[256,2048]{1,0:T(8,128)(2,1)S(1)}) custom-call(s32[1]{0:T(128)} %bitcast.grid_ref, bf16[1024,2048]{1,0:T(8,128)(2,1)} %copy-done, bf16[2048,1024]{1,0:T(8,128)(2,1)S(1)} %get-tuple-element.51.pre_ref, bf16[128,2048]{1,0:T(8,128)(2,1)S(1)} %get-tuple-element.42.flat_ref, ...), custom_call_target="tpu_custom_call" | custom-call | flops 1073741824 | bytes 4194304 | tf_op jit(solution)/shard_map/send_b/pallas_call | solution.py:440
  58.1 0.6 collective-permute-start.1
  58.8 4.1 %collective-permute-start.3 = (bf16[2,64,1152]{2,1,0:T(8,128)(2,1)S(1)}, bf16[2,64,1152]{2,1,0:T(8,128)(2,1)S(1)}, u32[]{:S(2)}, u32[]{:S(2)}) collective-permute-start(bf16[2,64,1152]{2,1,0:T(8,128)(2,1)S(1)} %bitcast.22), channel_id=1, source_target_pairs={{0,6},{1,7},{2,0},{3,1},{4,2},{5,3},{6,4},{7,5},{8,14},{9,15},{10,... | collective-permute-start | bytes 884744 | tf_op jit(solution)/shard_map/ppermute | solution.py:531
  62.9 0.0 collective-permute-start.2
  62.9 1.6 %keep_b.1 = (bf16[256,1152]{1,0:T(8,128)(2,1)S(1)}, bf16[1024,1024]{1,0:T(8,128)(2,1)S(1)}) custom-call(bf16[1024,1024]{1,0:T(8,128)(2,1)} %weight_hbm.1, bf16[2048,1024]{1,0:T(8,128)(2,1)S(1)} %get-tuple-element.51.pre_ref, bf16[256,2048]{1,0:T(8,128)(2,1)S(1)} %get-tuple-element.45.turned_ref, bf16[256,128]{1,0:T(8,128)(2,1)S(1)} %get-tuple-element.46.second_ref), custom_call_target="tpu_custom_call" | custom-call | flops 1073741824 | bytes 4194304 | tf_op jit(solution)/shard_map/keep_b/pallas_call | solution.py:454
  64.5 0.0 collective-permute-done.1
  64.5 0.2 add_convert_fusion
  64.7 2.0 %collective-permute-start.4 = (bf16[2,64,1152]{2,1,0:T(8,128)(2,1)S(1)}, bf16[2,64,1152]{2,1,0:T(8,128)(2,1)S(1)}, u32[]{:S(2)}, u32[]{:S(2)}) collective-permute-start(bf16[2,64,1152]{2,1,0:T(8,128)(2,1)S(1)} %bitcast.23), channel_id=1, source_target_pairs={{0,4},{1,5},{2,6},{3,7},{4,0},{5,1},{6,2},{7,3},{8,12},{9,13},{10,... | collective-permute-start | bytes 884744 | tf_op jit(solution)/shard_map/ppermute | solution.py:531
  66.7 5.6 %latent_gradient.1 = bf16[2048,1024]{1,0:T(8,128)(2,1)} custom-call(bf16[2048,1024]{1,0:T(8,128)(2,1)S(1)} %get-tuple-element.51.pre_ref, bf16[1024,1024]{1,0:T(8,128)(2,1)S(1)} %get-tuple-element.52.weight_ref), custom_call_target="tpu_custom_call" | custom-call | flops 4294967296 | bytes 10485760 | tf_op jit(solution)/shard_map/latent_gradient/pallas_call | solution.py:487
  72.3 3.3 %collective-permute-done.3 = bf16[2,64,1152]{2,1,0:T(8,128)(2,1)S(1)} collective-permute-done((bf16[2,64,1152]{2,1,0:T(8,128)(2,1)S(1)}, bf16[2,64,1152]{2,1,0:T(8,128)(2,1)S(1)}, u32[]{:S(2)}, u32[]{:S(2)}) %collective-permute-start.3) | collective-permute-done | bytes 294944 | tf_op jit(solution)/shard_map/ppermute | solution.py:531
  75.6 3.4 %collective-permute-done.2 = bf16[2,64,1152]{2,1,0:T(8,128)(2,1)S(1)} collective-permute-done((bf16[2,64,1152]{2,1,0:T(8,128)(2,1)S(1)}, bf16[2,64,1152]{2,1,0:T(8,128)(2,1)S(1)}, u32[]{:S(2)}, u32[]{:S(2)}) %collective-permute-start.2) | collective-permute-done | bytes 294944 | tf_op jit(solution)/shard_map/ppermute | solution.py:531
  79.0 0.0 collective-permute-done.4
  79.1 0.2 fusion.2
  79.3 0.9 collective-permute-start.7
  80.2 2.5 %collective-permute-start.6 = (bf16[64,1152]{1,0:T(8,128)(2,1)S(1)}, bf16[64,1152]{1,0:T(8,128)(2,1)S(1)}, u32[]{:S(2)}, u32[]{:S(2)}) collective-permute-start(bf16[64,1152]{1,0:T(8,128)(2,1)S(1)} %get-tuple-element.61), channel_id=1, source_target_pairs={{0,24},{1,25},{2,26},{3,27},{4,28},{5,29},{6,30},{7,31},{8,16},{9,... | collective-permute-start | bytes 442376 | tf_op jit(solution)/shard_map/ppermute | solution.py:531
  82.7 0.2 collective-permute-start.5
  82.8 3.7 %collective-permute-done.7 = bf16[64,1152]{1,0:T(8,128)(2,1)S(1)} collective-permute-done((bf16[64,1152]{1,0:T(8,128)(2,1)S(1)}, bf16[64,1152]{1,0:T(8,128)(2,1)S(1)}, u32[]{:S(2)}, u32[]{:S(2)}) %collective-permute-start.7) | collective-permute-done | bytes 147488 | tf_op jit(solution)/shard_map/ppermute | solution.py:531
  86.5 1.3 %collective-permute-done.6 = bf16[64,1152]{1,0:T(8,128)(2,1)S(1)} collective-permute-done((bf16[64,1152]{1,0:T(8,128)(2,1)S(1)}, bf16[64,1152]{1,0:T(8,128)(2,1)S(1)}, u32[]{:S(2)}, u32[]{:S(2)}) %collective-permute-start.6) | collective-permute-done | bytes 147488 | tf_op jit(solution)/shard_map/ppermute | solution.py:531
  87.8 0.0 collective-permute-done.5
  87.8 0.1 add_convert_fusion.2.own_ref
  87.9 1.0 %collective-permute-start.10 = (bf16[64,1152]{1,0:T(8,128)(2,1)S(1)}, bf16[64,1152]{1,0:T(8,128)(2,1)S(1)}, u32[]{:S(2)}, u32[]{:S(2)}) collective-permute-start(bf16[64,1152]{1,0:T(8,128)(2,1)S(1)} %add_convert_fusion.2.own_ref), channel_id=1, source_target_pairs={{0,64},{1,65},{2,66},{3,67},{4,68},{5,69},{6,70},{7,71},{8,72},{9,... | collective-permute-start | bytes 442376 | tf_op jit(solution)/shard_map/ppermute | solution.py:531
  88.9 2.1 %collective-permute-start.9 = (bf16[64,1152]{1,0:T(8,128)(2,1)S(1)}, bf16[64,1152]{1,0:T(8,128)(2,1)S(1)}, u32[]{:S(2)}, u32[]{:S(2)}) collective-permute-start(bf16[64,1152]{1,0:T(8,128)(2,1)S(1)} %add_convert_fusion.2.own_ref), channel_id=1, source_target_pairs={{0,96},{1,97},{2,98},{3,99},{4,100},{5,101},{6,102},{7,103},{8,104... | collective-permute-start | bytes 442376 | tf_op jit(solution)/shard_map/ppermute | solution.py:531
  91.0 0.5 collective-permute-start.8
  91.5 3.3 %collective-permute-done.10.refs_2_ = bf16[64,1152]{1,0:T(8,128)(2,1)S(1)} collective-permute-done((bf16[64,1152]{1,0:T(8,128)(2,1)S(1)}, bf16[64,1152]{1,0:T(8,128)(2,1)S(1)}, u32[]{:S(2)}, u32[]{:S(2)}) %collective-permute-start.10) | collective-permute-done | bytes 147488 | tf_op jit(solution)/shard_map/ppermute | solution.py:531
  94.8 1.5 %collective-permute-done.9.refs_1_ = bf16[64,1152]{1,0:T(8,128)(2,1)S(1)} collective-permute-done((bf16[64,1152]{1,0:T(8,128)(2,1)S(1)}, bf16[64,1152]{1,0:T(8,128)(2,1)S(1)}, u32[]{:S(2)}, u32[]{:S(2)}) %collective-permute-start.9) | collective-permute-done | bytes 147488 | tf_op jit(solution)/shard_map/ppermute | solution.py:531
  96.3 0.0 collective-permute-done.8.refs_0_
  96.3 0.8 finish.1
  (3 shorter events, 0.1 us)
Async XLA Ops:
  12.7 18.9 %copy-start.2 = (f32[100,2048]{1,0:T(8,128)S(1)}, f32[100,2048]{1,0:T(8,128)}, u32[]{:S(2)}) copy-start(f32[100,2048]{1,0:T(8,128)} %observed_ref.1) | copy-start | bytes 2457604
  12.7 18.9 %copy-start.3 = (f32[2048]{0:T(1024)S(1)}, f32[2048]{0:T(1024)}, u32[]{:S(2)}) copy-start(f32[2048]{0:T(1024)} %param.9) | copy-start | bytes 24580
  13.6 17.9 %all-to-all-start = ((f16[8,112,256]{2,1,0:T(8,128)(2,1)}), f16[8,112,256]{2,1,0:T(8,128)(2,1)S(1)}, u32[]{:S(2)}, u32[]{:S(2)}) async-start(f16[8,112,256]{2,1,0:T(8,128)(2,1)} %multiply_convert_fusion), calls=%async_computation | async-start | bytes 917504 | tf_op jit(solution)/shard_map/all_to_all | solution.py:577
  33.5 13.4 %all-to-all-start.1 = ((bf16[8,112,256]{2,1,0:T(8,128)(2,1)}), bf16[8,112,256]{2,1,0:T(8,128)(2,1)S(1)}, u32[]{:S(2)}, u32[]{:S(2)}) async-start(bf16[8,112,256]{2,1,0:T(8,128)(2,1)} %pairs.1), calls=%async_computation.1 | async-start | bytes 917504 | tf_op jit(solution)/shard_map/all_to_all | solution.py:580
  37.0 2.2 %copy-start.1 = (bf16[1,2048,1024]{2,1,0:T(8,128)(2,1)S(1)}, bf16[1,2048,1024]{2,1,0:T(8,128)(2,1)}, u32[]{:S(2)}) copy-start(bf16[1,2048,1024]{2,1,0:T(8,128)(2,1)} %param.5) | copy-start | bytes 12582916
  40.3 2.0 %copy-start = (bf16[1024,2048]{1,0:T(8,128)(2,1)}, bf16[1024,2048]{1,0:T(8,128)(2,1)S(1)}, u32[]{:S(2)}) copy-start(bf16[1024,2048]{1,0:T(8,128)(2,1)S(1)} %turned.1.turned_hbm) | copy-start | bytes 12582916
  52.4 3.2 %collective-permute-start = (bf16[256,1152]{1,0:T(8,128)(2,1)S(1)}, bf16[256,1152]{1,0:T(8,128)(2,1)S(1)}, u32[]{:S(2)}, u32[]{:S(2)}) collective-permute-start(bf16[256,1152]{1,0:T(8,128)(2,1)S(1)} %get-tuple-element.40), channel_id=1, source_target_pairs={{0,1},{1,0},{2,3},{3,2},{4,5},{5,4},{6,7},{7,6},{8,9},{9,8},{10,11... | collective-permute-start | bytes 1769480 | tf_op jit(solution)/shard_map/ppermute | solution.py:531
  58.1 6.3 %collective-permute-start.1 = (bf16[256,1152]{1,0:T(8,128)(2,1)S(1)}, bf16[256,1152]{1,0:T(8,128)(2,1)S(1)}, u32[]{:S(2)}, u32[]{:S(2)}) collective-permute-start(bf16[256,1152]{1,0:T(8,128)(2,1)S(1)} %get-tuple-element.48), channel_id=1, source_target_pairs={{0,1},{1,0},{2,3},{3,2},{4,5},{5,4},{6,7},{7,6},{8,9},{9,8},{10,11... | collective-permute-start | bytes 1769480 | tf_op jit(solution)/shard_map/ppermute | solution.py:531
  58.8 16.9 %collective-permute-start.3 = (bf16[2,64,1152]{2,1,0:T(8,128)(2,1)S(1)}, bf16[2,64,1152]{2,1,0:T(8,128)(2,1)S(1)}, u32[]{:S(2)}, u32[]{:S(2)}) collective-permute-start(bf16[2,64,1152]{2,1,0:T(8,128)(2,1)S(1)} %bitcast.22), channel_id=1, source_target_pairs={{0,6},{1,7},{2,0},{3,1},{4,2},{5,3},{6,4},{7,5},{8,14},{9,15},{10,... | collective-permute-start | bytes 884744 | tf_op jit(solution)/shard_map/ppermute | solution.py:531
  62.9 16.2 %collective-permute-start.2 = (bf16[2,64,1152]{2,1,0:T(8,128)(2,1)S(1)}, bf16[2,64,1152]{2,1,0:T(8,128)(2,1)S(1)}, u32[]{:S(2)}, u32[]{:S(2)}) collective-permute-start(bf16[2,64,1152]{2,1,0:T(8,128)(2,1)S(1)} %bitcast.21), channel_id=1, source_target_pairs={{0,2},{1,3},{2,4},{3,5},{4,6},{5,7},{6,0},{7,1},{8,10},{9,11},{10,... | collective-permute-start | bytes 884744 | tf_op jit(solution)/shard_map/ppermute | solution.py:531
  64.7 14.3 %collective-permute-start.4 = (bf16[2,64,1152]{2,1,0:T(8,128)(2,1)S(1)}, bf16[2,64,1152]{2,1,0:T(8,128)(2,1)S(1)}, u32[]{:S(2)}, u32[]{:S(2)}) collective-permute-start(bf16[2,64,1152]{2,1,0:T(8,128)(2,1)S(1)} %bitcast.23), channel_id=1, source_target_pairs={{0,4},{1,5},{2,6},{3,7},{4,0},{5,1},{6,2},{7,3},{8,12},{9,13},{10,... | collective-permute-start | bytes 884744 | tf_op jit(solution)/shard_map/ppermute | solution.py:531
  79.3 7.3 %collective-permute-start.7 = (bf16[64,1152]{1,0:T(8,128)(2,1)S(1)}, bf16[64,1152]{1,0:T(8,128)(2,1)S(1)}, u32[]{:S(2)}, u32[]{:S(2)}) collective-permute-start(bf16[64,1152]{1,0:T(8,128)(2,1)S(1)} %get-tuple-element.62), channel_id=1, source_target_pairs={{0,16},{1,17},{2,18},{3,19},{4,20},{5,21},{6,22},{7,23},{8,24},{9,... | collective-permute-start | bytes 442376 | tf_op jit(solution)/shard_map/ppermute | solution.py:531
  80.2 7.7 %collective-permute-start.6 = (bf16[64,1152]{1,0:T(8,128)(2,1)S(1)}, bf16[64,1152]{1,0:T(8,128)(2,1)S(1)}, u32[]{:S(2)}, u32[]{:S(2)}) collective-permute-start(bf16[64,1152]{1,0:T(8,128)(2,1)S(1)} %get-tuple-element.61), channel_id=1, source_target_pairs={{0,24},{1,25},{2,26},{3,27},{4,28},{5,29},{6,30},{7,31},{8,16},{9,... | collective-permute-start | bytes 442376 | tf_op jit(solution)/shard_map/ppermute | solution.py:531
  82.7 5.2 %collective-permute-start.5 = (bf16[64,1152]{1,0:T(8,128)(2,1)S(1)}, bf16[64,1152]{1,0:T(8,128)(2,1)S(1)}, u32[]{:S(2)}, u32[]{:S(2)}) collective-permute-start(bf16[64,1152]{1,0:T(8,128)(2,1)S(1)} %get-tuple-element.61), channel_id=1, source_target_pairs={{0,8},{1,9},{2,10},{3,11},{4,12},{5,13},{6,14},{7,15},{8,0},{9,1},... | collective-permute-start | bytes 442376 | tf_op jit(solution)/shard_map/ppermute | solution.py:531
  87.9 6.8 %collective-permute-start.10 = (bf16[64,1152]{1,0:T(8,128)(2,1)S(1)}, bf16[64,1152]{1,0:T(8,128)(2,1)S(1)}, u32[]{:S(2)}, u32[]{:S(2)}) collective-permute-start(bf16[64,1152]{1,0:T(8,128)(2,1)S(1)} %add_convert_fusion.2.own_ref), channel_id=1, source_target_pairs={{0,64},{1,65},{2,66},{3,67},{4,68},{5,69},{6,70},{7,71},{8,72},{9,... | collective-permute-start | bytes 442376 | tf_op jit(solution)/shard_map/ppermute | solution.py:531
  88.9 7.3 %collective-permute-start.9 = (bf16[64,1152]{1,0:T(8,128)(2,1)S(1)}, bf16[64,1152]{1,0:T(8,128)(2,1)S(1)}, u32[]{:S(2)}, u32[]{:S(2)}) collective-permute-start(bf16[64,1152]{1,0:T(8,128)(2,1)S(1)} %add_convert_fusion.2.own_ref), channel_id=1, source_target_pairs={{0,96},{1,97},{2,98},{3,99},{4,100},{5,101},{6,102},{7,103},{8,104... | collective-permute-start | bytes 442376 | tf_op jit(solution)/shard_map/ppermute | solution.py:531
  91.0 5.2 %collective-permute-start.8 = (bf16[64,1152]{1,0:T(8,128)(2,1)S(1)}, bf16[64,1152]{1,0:T(8,128)(2,1)S(1)}, u32[]{:S(2)}, u32[]{:S(2)}) collective-permute-start(bf16[64,1152]{1,0:T(8,128)(2,1)S(1)} %add_convert_fusion.2.own_ref), channel_id=1, source_target_pairs={{0,32},{1,33},{2,34},{3,35},{4,36},{5,37},{6,38},{7,39},{8,40},{9,... | collective-permute-start | bytes 442376 | tf_op jit(solution)/shard_map/ppermute | solution.py:531

commit v8 on v7

--- a/solution.py
+++ b/solution.py
@@ -208,7 +208,7 @@
     return grid >> 3, (grid >> 1) & 3, grid & 1
 
 
-STEPS = ((1, 3), (2, 0))
+STEPS = ((2, 0), (1, 3))
 
 
 def owner(block, steps, x_lo, z):
@@ -221,7 +221,7 @@
     for group in range(8):
         step = (group - z) & 3
         odd = step & 1
-        place = odd * (step >> 1) + (1 - odd) * (3 - (step >> 1))
+        place = odd * (2 + (step >> 1)) + (1 - odd) * (1 - (step >> 1))
         at = (place >> 1) * 512 + (place & 1) * 128 + ((group >> 2) ^ x_lo) * 64
         first = pl.multiple_of(at + (1 - core) * 256, 64)
         second = pl.multiple_of(at + core * 256, 64)
@@ -540,15 +540,15 @@
 
 def over_core(send, keep):
     got = moved(send, lambda y, x, z, c: (y, x, z, 1 - c))
-    return summed(keep, [got]).astype(bf16)
-
-
-def over_z(part, rows):
-    blocks = rows.reshape(2, 2, 64, rows.shape[1])
-    return [
-        moved(block, lambda y, x, z, c, k=k: (y, x, (z + k) % 4, c)) if k else block
-        for k, block in zip(STEPS[part], blocks)
-    ]
+    return summed(keep, [got]).reshape(2, 2, 64, send.shape[1])
+
+
+def up(value):
+    return moved(value, lambda y, x, z, c: (y, x, (z + 1) % 4, c))
+
+
+def down(value):
+    return moved(value, lambda y, x, z, c: (y, x, (z + 3) % 4, c))
 
 
 def over_x(blocks):
@@ -580,14 +580,17 @@
     low = lax.all_to_all(low, "member", 0, 0, tiled=True)
     grad_pre, rows_a, second_a, flat, turned_now = send_a(grid, low, turned_latent, slope, hidden, padded)
     kept_a, turned_now, hidden_now = keep_a(grid, turned_latent, hidden, grad_pre, turned_now, second_a)
-    rows_a, flat = lax.optimization_barrier((over_core(rows_a, kept_a), flat))
+    far, own = over_core(rows_a, kept_a).astype(bf16)
+    far, own, flat = lax.optimization_barrier((far, own, flat))
+    upward, downward = up(far[0]), down(far[1])
     rows_b, second_b, turned_now = send_b(grid, turned_latent, grad_pre, flat, turned_now, hidden_now)
     kept_b, weight_copy = keep_b(hidden_weight, grad_pre, turned_now, second_b)
-    rows_b, grad_pre = lax.optimization_barrier((over_core(rows_b, kept_b), grad_pre))
+    above, below = over_core(rows_b, kept_b)
+    above = jnp.stack([above[0] + upward.astype(f32), above[1]]).astype(bf16)
+    below = jnp.stack([below[0], below[1] + downward.astype(f32)]).astype(bf16)
+    above, below, grad_pre = lax.optimization_barrier((above, below, grad_pre))
     grad_latent = latent_gradient(grad_pre, weight_copy)
-    plus, minus = over_z(0, rows_a)
-    across, own = over_z(1, rows_b)
-    blocks = summed(own, [plus, minus, across]).astype(bf16)
+    blocks = summed(own, [up(above), down(below)]).astype(bf16)
     blocks, grad_latent = lax.optimization_barrier((blocks, grad_latent))
     block = over_x(blocks)
     factor = 1.0 / math.sqrt(members * nodes * groups)

time: 97.9 us -> 97.2 us (level)
  waiting for transfers between devices: 32 us -> 30.3 us
  starting transfers between devices: 24.6 us -> 25.9 us
    ppermute x11 -> x12, waiting for transfers between devices: 16.5 us -> 14.9 us  [moved(): return lax.ppermute(value, ('member', 'grid'), moves)]
    ppermute x11 -> x12, starting transfers between devices: 14.1 us -> 15.4 us  [moved(): return lax.ppermute(value, ('member', 'grid'), moves)]
  transfers between devices with their start and end apart: 13 -> 14, of which waited for: 8 -> 9; matrix products, arithmetic and copies ran while one was open for 0% -> 0% of each run, Pallas kernels for 12% -> 12%
where the time goes in v8:
time: 97.2 us; the launch traced here: 96.8 us
  Pallas kernels  33.8 us (35%)
  waiting for transfers between devices  30.3 us (31%)
  starting transfers between devices  25.9 us (27%)
  local copies, waits for them, and re-layouts  4.32 us (4%)
  other arithmetic  1.59 us (2%)
    ppermute x12, starting transfers between devices, moved(): return lax.ppermute(value, ('member', 'grid'), moves)  15.4 us
    ppermute x12, waiting for transfers between devices, moved(): return lax.ppermute(value, ('member', 'grid'), moves)  14.9 us
    pallas_call x1, Pallas kernels, forward(): pl.pallas_call(forward_kernel, in_specs=[anywhere] * 3, out_specs=[vmem,...  12.1 us
    all_to_all x1, waiting for transfers between devices, body(): blocks = lax.all_to_all(blocks, 'member', 0, 0, tiled=True)  10.9 us
    all_to_all x1, starting transfers between devices, body(): blocks = lax.all_to_all(blocks, 'member', 0, 0, tiled=True)  7.01 us
    pallas_call x1, Pallas kernels, latent_gradient(): pl.pallas_call(latent_kernel, in_specs=[vmem, vmem], out_specs=anywhere,...  5.58 us
    pallas_call x1, Pallas kernels, send_a(): pl.pallas_call(send_a_kernel, in_specs=[smem, vmem, anywhere, anywhere, a...  5.48 us
    all_to_all x1, waiting for transfers between devices, body(): low = lax.all_to_all(low, 'member', 0, 0, tiled=True)  4.57 us
  transfers between devices with their start and end apart: 14, of which 9 were waited for; matrix products, arithmetic and copies ran while one was open for 0% of the time, Pallas kernels for 12%

profile of v8, /device:TPU:0, one launch (start us, length us, event | category | flops | bytes accessed | tf_op | source)
XLA Modules:
  0.0 96.8 jit_solution(4265657593425242037)
XLA Ops:
  0.6 12.1 %forward.1 = (f32[8,112,256]{2,1,0:T(8,128)S(1)}, bf16[2048,1024]{1,0:T(8,128)(2,1)}, bf16[2048,1024]{1,0:T(8,128)(2,1)}, bf16[1024,128]{1,0:T(8,128)(2,1)S(1)}) custom-call(bf16[2048,1024]{1,0:T(8,128)(2,1)} %bitcast.26, bf16[1024,1024]{1,0:T(8,128)(2,1)} %weight_hbm.1, bf16[100,1024]{1,0:T(8,128)(2,1)} %bitcast.31), custom_call_target="tpu_custom_call" | custom-call | flops 4831838208 | bytes 20971520 | tf_op jit(solution)/shard_map/forward/pallas_call | solution.py:123
  12.7 0.0 copy-start.2
  12.7 0.0 copy-start.3
  12.7 0.9 multiply_convert_fusion
  13.6 7.0 %all-to-all-start = ((f16[8,112,256]{2,1,0:T(8,128)(2,1)}), f16[8,112,256]{2,1,0:T(8,128)(2,1)S(1)}, u32[]{:S(2)}, u32[]{:S(2)}) async-start(f16[8,112,256]{2,1,0:T(8,128)(2,1)} %multiply_convert_fusion), calls=%async_computation | async-start | bytes 917504 | tf_op jit(solution)/shard_map/all_to_all | solution.py:577
  20.6 10.9 %all-to-all-done = f16[8,112,256]{2,1,0:T(8,128)(2,1)S(1)} async-done(((f16[8,112,256]{2,1,0:T(8,128)(2,1)}), f16[8,112,256]{2,1,0:T(8,128)(2,1)S(1)}, u32[]{:S(2)}, u32[]{:S(2)}) %all-to-all-start) | async-done | bytes 458784 | tf_op jit(solution)/shard_map/all_to_all | solution.py:577
  31.5 0.1 convert_multiply_fusion.blocks_ref
  31.6 0.0 copy-done.2
  31.6 0.0 copy-done.3
  31.6 1.9 %pairs.1 = bf16[8,112,256]{2,1,0:T(8,128)(2,1)} custom-call(s32[1]{0:T(128)} %bitcast.3.place_ref, f32[8,112,256]{2,1,0:T(8,128)S(1)} %convert_multiply_fusion.blocks_ref, f32[100,2048]{1,0:T(8,128)S(1)} %copy-done.2, f32[1,2048]{1,0:T(1,128)S(1)} %bitcast.28), custom_call_target="tpu_custom_call" | custom-call | flops 4194304 | bytes 2097152 | tf_op jit(solution)/shard_map/pairs/pallas_call | solution.py:190
  33.5 3.5 %all-to-all-start.1 = ((bf16[8,112,256]{2,1,0:T(8,128)(2,1)}), bf16[8,112,256]{2,1,0:T(8,128)(2,1)S(1)}, u32[]{:S(2)}, u32[]{:S(2)}) async-start(bf16[8,112,256]{2,1,0:T(8,128)(2,1)} %pairs.1), calls=%async_computation.1 | async-start | bytes 917504 | tf_op jit(solution)/shard_map/all_to_all | solution.py:580
  37.0 0.0 copy-start.1
  37.0 2.2 %copy-done.1 = bf16[1,2048,1024]{2,1,0:T(8,128)(2,1)S(1)} copy-done((bf16[1,2048,1024]{2,1,0:T(8,128)(2,1)S(1)}, bf16[1,2048,1024]{2,1,0:T(8,128)(2,1)}, u32[]{:S(2)}) %copy-start.1) | copy-done | bytes 4194328
  39.2 1.1 %turned.1.turned_hbm = bf16[1024,2048]{1,0:T(8,128)(2,1)S(1)} custom-call(s32[1]{0:T(128)} %bitcast.grid_ref, bf16[2048,1024]{1,0:T(8,128)(2,1)S(1)} %bitcast.27), custom_call_target="tpu_custom_call" | custom-call | bytes 8388608 | tf_op jit(solution)/shard_map/turned/pallas_call | solution.py:237
  40.3 0.0 copy-start
  40.4 2.0 %copy-done = bf16[1024,2048]{1,0:T(8,128)(2,1)} copy-done((bf16[1024,2048]{1,0:T(8,128)(2,1)}, bf16[1024,2048]{1,0:T(8,128)(2,1)S(1)}, u32[]{:S(2)}) %copy-start) | copy-done | bytes 4194328
  42.4 4.6 %all-to-all-done.1.low_ref = bf16[8,112,256]{2,1,0:T(8,128)(2,1)S(1)} async-done(((bf16[8,112,256]{2,1,0:T(8,128)(2,1)}), bf16[8,112,256]{2,1,0:T(8,128)(2,1)S(1)}, u32[]{:S(2)}, u32[]{:S(2)}) %all-to-all-start.1) | async-done | bytes 458784 | tf_op jit(solution)/shard_map/all_to_all | solution.py:580
  46.9 5.5 %send_a.1 = (bf16[2048,1024]{1,0:T(8,128)(2,1)S(1)}, bf16[256,1152]{1,0:T(8,128)(2,1)S(1)}, bf16[256,128]{1,0:T(8,128)(2,1)S(1)}, bf16[128,2048]{1,0:T(8,128)(2,1)S(1)}, bf16[256,2048]{1,0:T(8,128)(2,1)S(1)}) custom-call(s32[1]{0:T(128)} %bitcast.grid_ref, bf16[8,112,256]{2,1,0:T(8,128)(2,1)S(1)} %all-to-all-done.1.low_ref, bf16[1024,2048]{1,0:T(8,128)(2,1)} %copy-done, ...), custom_call_target="tpu_custom_call" | custom-call | flops 1879048192 | bytes 8388608 | tf_op jit(solution)/shard_map/send_a/pallas_call | solution.py:397
  52.4 0.3 collective-permute-start
  52.7 3.0 %keep_a.1 = (bf16[256,1152]{1,0:T(8,128)(2,1)S(1)}, bf16[256,2048]{1,0:T(8,128)(2,1)S(1)}, bf16[2048,512]{1,0:T(8,128)(2,1)S(1)}) custom-call(s32[1]{0:T(128)} %bitcast.grid_ref, bf16[1024,2048]{1,0:T(8,128)(2,1)} %copy-done, bf16[2048,1024]{1,0:T(8,128)(2,1)} %get-tuple-element.34.hidden_hbm, bf16[2048,1024]{1,0:T(8,128)(2,1)S(1)} %get-tuple-element.55.pre_ref, ...), custom_call_target="tpu_custom_call" | custom-call | flops 1073741824 | bytes 4194304 | tf_op jit(solution)/shard_map/keep_a/pallas_call | solution.py:426
  55.7 0.0 collective-permute-done
  55.7 0.1 add_convert_fusion
  55.9 2.3 %send_b.1 = (bf16[256,1152]{1,0:T(8,128)(2,1)S(1)}, bf16[256,128]{1,0:T(8,128)(2,1)S(1)}, bf16[256,2048]{1,0:T(8,128)(2,1)S(1)}) custom-call(s32[1]{0:T(128)} %bitcast.grid_ref, bf16[1024,2048]{1,0:T(8,128)(2,1)} %copy-done, bf16[2048,1024]{1,0:T(8,128)(2,1)S(1)} %get-tuple-element.55.pre_ref, bf16[128,2048]{1,0:T(8,128)(2,1)S(1)} %get-tuple-element.45.flat_ref, ...), custom_call_target="tpu_custom_call" | custom-call | flops 1073741824 | bytes 4194304 | tf_op jit(solution)/shard_map/send_b/pallas_call | solution.py:440
  58.2 0.6 collective-permute-start.1
  58.8 4.1 %collective-permute-start.3 = (bf16[64,1152]{1,0:T(8,128)(2,1)S(1)}, bf16[64,1152]{1,0:T(8,128)(2,1)S(1)}, u32[]{:S(2)}, u32[]{:S(2)}) collective-permute-start(bf16[64,1152]{1,0:T(8,128)(2,1)S(1)} %get-tuple-element.71), channel_id=1, source_target_pairs={{0,6},{1,7},{2,0},{3,1},{4,2},{5,3},{6,4},{7,5},{8,14},{9,15},{10,... | collective-permute-start | bytes 442376 | tf_op jit(solution)/shard_map/ppermute | solution.py:531
  62.9 0.0 collective-permute-start.2
  62.9 1.6 %keep_b.1 = (bf16[256,1152]{1,0:T(8,128)(2,1)S(1)}, bf16[1024,1024]{1,0:T(8,128)(2,1)S(1)}) custom-call(bf16[1024,1024]{1,0:T(8,128)(2,1)} %weight_hbm.1, bf16[2048,1024]{1,0:T(8,128)(2,1)S(1)} %get-tuple-element.55.pre_ref, bf16[256,2048]{1,0:T(8,128)(2,1)S(1)} %get-tuple-element.48.turned_ref, bf16[256,128]{1,0:T(8,128)(2,1)S(1)} %get-tuple-element.49.second_ref), custom_call_target="tpu_custom_call" | custom-call | flops 1073741824 | bytes 4194304 | tf_op jit(solution)/shard_map/keep_b/pallas_call | solution.py:454
  64.5 0.0 collective-permute-done.1
  64.5 0.2 convert_add_fusion
  64.7 1.5 %collective-permute-done.3 = bf16[64,1152]{1,0:T(8,128)(2,1)S(1)} collective-permute-done((bf16[64,1152]{1,0:T(8,128)(2,1)S(1)}, bf16[64,1152]{1,0:T(8,128)(2,1)S(1)}, u32[]{:S(2)}, u32[]{:S(2)}) %collective-permute-start.3) | collective-permute-done | bytes 147488 | tf_op jit(solution)/shard_map/ppermute | solution.py:531
  66.2 3.4 %collective-permute-done.2 = bf16[64,1152]{1,0:T(8,128)(2,1)S(1)} collective-permute-done((bf16[64,1152]{1,0:T(8,128)(2,1)S(1)}, bf16[64,1152]{1,0:T(8,128)(2,1)S(1)}, u32[]{:S(2)}, u32[]{:S(2)}) %collective-permute-start.2) | collective-permute-done | bytes 147488 | tf_op jit(solution)/shard_map/ppermute | solution.py:531
  69.6 0.1 fusion.3
  69.7 0.1 pad_maximum_fusion
  69.7 0.1 collective-permute-start.4
  69.8 3.2 %collective-permute-start.5 = (bf16[2,64,1152]{2,1,0:T(8,128)(2,1)S(1)}, bf16[2,64,1152]{2,1,0:T(8,128)(2,1)S(1)}, u32[]{:S(2)}, u32[]{:S(2)}) collective-permute-start(bf16[2,64,1152]{2,1,0:T(8,128)(2,1)S(1)} %get-tuple-element.54), channel_id=1, source_target_pairs={{0,6},{1,7},{2,0},{3,1},{4,2},{5,3},{6,4},{7,5},{8,14},{9,15},{10,... | collective-permute-start | bytes 884744 | tf_op jit(solution)/shard_map/ppermute | solution.py:531
  73.1 5.6 %latent_gradient.1 = bf16[2048,1024]{1,0:T(8,128)(2,1)} custom-call(bf16[2048,1024]{1,0:T(8,128)(2,1)S(1)} %get-tuple-element.55.pre_ref, bf16[1024,1024]{1,0:T(8,128)(2,1)S(1)} %get-tuple-element.56.weight_ref), custom_call_target="tpu_custom_call" | custom-call | flops 4294967296 | bytes 10485760 | tf_op jit(solution)/shard_map/latent_gradient/pallas_call | solution.py:487
  78.6 0.1 collective-permute-done.4
  78.8 0.0 collective-permute-done.5
  78.8 0.1 add_convert_fusion.1
  78.9 0.9 collective-permute-start.8
  79.9 2.5 %collective-permute-start.7 = (bf16[64,1152]{1,0:T(8,128)(2,1)S(1)}, bf16[64,1152]{1,0:T(8,128)(2,1)S(1)}, u32[]{:S(2)}, u32[]{:S(2)}) collective-permute-start(bf16[64,1152]{1,0:T(8,128)(2,1)S(1)} %get-tuple-element.69), channel_id=1, source_target_pairs={{0,24},{1,25},{2,26},{3,27},{4,28},{5,29},{6,30},{7,31},{8,16},{9,... | collective-permute-start | bytes 442376 | tf_op jit(solution)/shard_map/ppermute | solution.py:531
  82.3 0.2 collective-permute-start.6
  82.5 3.6 %collective-permute-done.8 = bf16[64,1152]{1,0:T(8,128)(2,1)S(1)} collective-permute-done((bf16[64,1152]{1,0:T(8,128)(2,1)S(1)}, bf16[64,1152]{1,0:T(8,128)(2,1)S(1)}, u32[]{:S(2)}, u32[]{:S(2)}) %collective-permute-start.8) | collective-permute-done | bytes 147488 | tf_op jit(solution)/shard_map/ppermute | solution.py:531
  86.1 1.5 %collective-permute-done.7 = bf16[64,1152]{1,0:T(8,128)(2,1)S(1)} collective-permute-done((bf16[64,1152]{1,0:T(8,128)(2,1)S(1)}, bf16[64,1152]{1,0:T(8,128)(2,1)S(1)}, u32[]{:S(2)}, u32[]{:S(2)}) %collective-permute-start.7) | collective-permute-done | bytes 147488 | tf_op jit(solution)/shard_map/ppermute | solution.py:531
  87.6 0.0 collective-permute-done.6
  87.6 0.1 add_convert_fusion.2.own_ref
  87.7 0.9 collective-permute-start.11
  88.6 2.1 %collective-permute-start.10 = (bf16[64,1152]{1,0:T(8,128)(2,1)S(1)}, bf16[64,1152]{1,0:T(8,128)(2,1)S(1)}, u32[]{:S(2)}, u32[]{:S(2)}) collective-permute-start(bf16[64,1152]{1,0:T(8,128)(2,1)S(1)} %add_convert_fusion.2.own_ref), channel_id=1, source_target_pairs={{0,96},{1,97},{2,98},{3,99},{4,100},{5,101},{6,102},{7,103},{8,104... | collective-permute-start | bytes 442376 | tf_op jit(solution)/shard_map/ppermute | solution.py:531
  90.8 0.5 collective-permute-start.9
  91.3 3.3 %collective-permute-done.11.refs_2_ = bf16[64,1152]{1,0:T(8,128)(2,1)S(1)} collective-permute-done((bf16[64,1152]{1,0:T(8,128)(2,1)S(1)}, bf16[64,1152]{1,0:T(8,128)(2,1)S(1)}, u32[]{:S(2)}, u32[]{:S(2)}) %collective-permute-start.11) | collective-permute-done | bytes 147488 | tf_op jit(solution)/shard_map/ppermute | solution.py:531
  94.5 1.5 %collective-permute-done.10.refs_1_ = bf16[64,1152]{1,0:T(8,128)(2,1)S(1)} collective-permute-done((bf16[64,1152]{1,0:T(8,128)(2,1)S(1)}, bf16[64,1152]{1,0:T(8,128)(2,1)S(1)}, u32[]{:S(2)}, u32[]{:S(2)}) %collective-permute-start.10) | collective-permute-done | bytes 147488 | tf_op jit(solution)/shard_map/ppermute | solution.py:531
  96.0 0.0 collective-permute-done.9.refs_0_
  96.0 0.8 finish.1
  (4 shorter events, 0.1 us)
Async XLA Ops:
  12.7 18.9 %copy-start.2 = (f32[100,2048]{1,0:T(8,128)S(1)}, f32[100,2048]{1,0:T(8,128)}, u32[]{:S(2)}) copy-start(f32[100,2048]{1,0:T(8,128)} %observed_ref.1) | copy-start | bytes 2457604
  12.7 18.9 %copy-start.3 = (f32[2048]{0:T(1024)S(1)}, f32[2048]{0:T(1024)}, u32[]{:S(2)}) copy-start(f32[2048]{0:T(1024)} %param.9) | copy-start | bytes 24580
  13.6 17.9 %all-to-all-start = ((f16[8,112,256]{2,1,0:T(8,128)(2,1)}), f16[8,112,256]{2,1,0:T(8,128)(2,1)S(1)}, u32[]{:S(2)}, u32[]{:S(2)}) async-start(f16[8,112,256]{2,1,0:T(8,128)(2,1)} %multiply_convert_fusion), calls=%async_computation | async-start | bytes 917504 | tf_op jit(solution)/shard_map/all_to_all | solution.py:577
  33.5 13.4 %all-to-all-start.1 = ((bf16[8,112,256]{2,1,0:T(8,128)(2,1)}), bf16[8,112,256]{2,1,0:T(8,128)(2,1)S(1)}, u32[]{:S(2)}, u32[]{:S(2)}) async-start(bf16[8,112,256]{2,1,0:T(8,128)(2,1)} %pairs.1), calls=%async_computation.1 | async-start | bytes 917504 | tf_op jit(solution)/shard_map/all_to_all | solution.py:580
  37.0 2.2 %copy-start.1 = (bf16[1,2048,1024]{2,1,0:T(8,128)(2,1)S(1)}, bf16[1,2048,1024]{2,1,0:T(8,128)(2,1)}, u32[]{:S(2)}) copy-start(bf16[1,2048,1024]{2,1,0:T(8,128)(2,1)} %param.5) | copy-start | bytes 12582916
  40.3 2.0 %copy-start = (bf16[1024,2048]{1,0:T(8,128)(2,1)}, bf16[1024,2048]{1,0:T(8,128)(2,1)S(1)}, u32[]{:S(2)}) copy-start(bf16[1024,2048]{1,0:T(8,128)(2,1)S(1)} %turned.1.turned_hbm) | copy-start | bytes 12582916
  52.4 3.2 %collective-permute-start = (bf16[256,1152]{1,0:T(8,128)(2,1)S(1)}, bf16[256,1152]{1,0:T(8,128)(2,1)S(1)}, u32[]{:S(2)}, u32[]{:S(2)}) collective-permute-start(bf16[256,1152]{1,0:T(8,128)(2,1)S(1)} %get-tuple-element.42), channel_id=1, source_target_pairs={{0,1},{1,0},{2,3},{3,2},{4,5},{5,4},{6,7},{7,6},{8,9},{9,8},{10,11... | collective-permute-start | bytes 1769480 | tf_op jit(solution)/shard_map/ppermute | solution.py:531
  58.2 6.3 %collective-permute-start.1 = (bf16[256,1152]{1,0:T(8,128)(2,1)S(1)}, bf16[256,1152]{1,0:T(8,128)(2,1)S(1)}, u32[]{:S(2)}, u32[]{:S(2)}) collective-permute-start(bf16[256,1152]{1,0:T(8,128)(2,1)S(1)} %get-tuple-element.51), channel_id=1, source_target_pairs={{0,1},{1,0},{2,3},{3,2},{4,5},{5,4},{6,7},{7,6},{8,9},{9,8},{10,11... | collective-permute-start | bytes 1769480 | tf_op jit(solution)/shard_map/ppermute | solution.py:531
  58.8 7.4 %collective-permute-start.3 = (bf16[64,1152]{1,0:T(8,128)(2,1)S(1)}, bf16[64,1152]{1,0:T(8,128)(2,1)S(1)}, u32[]{:S(2)}, u32[]{:S(2)}) collective-permute-start(bf16[64,1152]{1,0:T(8,128)(2,1)S(1)} %get-tuple-element.71), channel_id=1, source_target_pairs={{0,6},{1,7},{2,0},{3,1},{4,2},{5,3},{6,4},{7,5},{8,14},{9,15},{10,... | collective-permute-start | bytes 442376 | tf_op jit(solution)/shard_map/ppermute | solution.py:531
  62.9 6.7 %collective-permute-start.2 = (bf16[64,1152]{1,0:T(8,128)(2,1)S(1)}, bf16[64,1152]{1,0:T(8,128)(2,1)S(1)}, u32[]{:S(2)}, u32[]{:S(2)}) collective-permute-start(bf16[64,1152]{1,0:T(8,128)(2,1)S(1)} %get-tuple-element.72), channel_id=1, source_target_pairs={{0,2},{1,3},{2,4},{3,5},{4,6},{5,7},{6,0},{7,1},{8,10},{9,11},{10,... | collective-permute-start | bytes 442376 | tf_op jit(solution)/shard_map/ppermute | solution.py:531
  69.7 9.0 %collective-permute-start.4 = (bf16[2,64,1152]{2,1,0:T(8,128)(2,1)S(1)}, bf16[2,64,1152]{2,1,0:T(8,128)(2,1)S(1)}, u32[]{:S(2)}, u32[]{:S(2)}) collective-permute-start(bf16[2,64,1152]{2,1,0:T(8,128)(2,1)S(1)} %get-tuple-element.53), channel_id=1, source_target_pairs={{0,2},{1,3},{2,4},{3,5},{4,6},{5,7},{6,0},{7,1},{8,10},{9,11},{10,... | collective-permute-start | bytes 884744 | tf_op jit(solution)/shard_map/ppermute | solution.py:531
  69.8 9.0 %collective-permute-start.5 = (bf16[2,64,1152]{2,1,0:T(8,128)(2,1)S(1)}, bf16[2,64,1152]{2,1,0:T(8,128)(2,1)S(1)}, u32[]{:S(2)}, u32[]{:S(2)}) collective-permute-start(bf16[2,64,1152]{2,1,0:T(8,128)(2,1)S(1)} %get-tuple-element.54), channel_id=1, source_target_pairs={{0,6},{1,7},{2,0},{3,1},{4,2},{5,3},{6,4},{7,5},{8,14},{9,15},{10,... | collective-permute-start | bytes 884744 | tf_op jit(solution)/shard_map/ppermute | solution.py:531
  78.9 7.2 %collective-permute-start.8 = (bf16[64,1152]{1,0:T(8,128)(2,1)S(1)}, bf16[64,1152]{1,0:T(8,128)(2,1)S(1)}, u32[]{:S(2)}, u32[]{:S(2)}) collective-permute-start(bf16[64,1152]{1,0:T(8,128)(2,1)S(1)} %get-tuple-element.70), channel_id=1, source_target_pairs={{0,16},{1,17},{2,18},{3,19},{4,20},{5,21},{6,22},{7,23},{8,24},{9,... | collective-permute-start | bytes 442376 | tf_op jit(solution)/shard_map/ppermute | solution.py:531
  79.9 7.7 %collective-permute-start.7 = (bf16[64,1152]{1,0:T(8,128)(2,1)S(1)}, bf16[64,1152]{1,0:T(8,128)(2,1)S(1)}, u32[]{:S(2)}, u32[]{:S(2)}) collective-permute-start(bf16[64,1152]{1,0:T(8,128)(2,1)S(1)} %get-tuple-element.69), channel_id=1, source_target_pairs={{0,24},{1,25},{2,26},{3,27},{4,28},{5,29},{6,30},{7,31},{8,16},{9,... | collective-permute-start | bytes 442376 | tf_op jit(solution)/shard_map/ppermute | solution.py:531
  82.3 5.3 %collective-permute-start.6 = (bf16[64,1152]{1,0:T(8,128)(2,1)S(1)}, bf16[64,1152]{1,0:T(8,128)(2,1)S(1)}, u32[]{:S(2)}, u32[]{:S(2)}) collective-permute-start(bf16[64,1152]{1,0:T(8,128)(2,1)S(1)} %get-tuple-element.69), channel_id=1, source_target_pairs={{0,8},{1,9},{2,10},{3,11},{4,12},{5,13},{6,14},{7,15},{8,0},{9,1},... | collective-permute-start | bytes 442376 | tf_op jit(solution)/shard_map/ppermute | solution.py:531
  87.7 6.8 %collective-permute-start.11 = (bf16[64,1152]{1,0:T(8,128)(2,1)S(1)}, bf16[64,1152]{1,0:T(8,128)(2,1)S(1)}, u32[]{:S(2)}, u32[]{:S(2)}) collective-permute-start(bf16[64,1152]{1,0:T(8,128)(2,1)S(1)} %add_convert_fusion.2.own_ref), channel_id=1, source_target_pairs={{0,64},{1,65},{2,66},{3,67},{4,68},{5,69},{6,70},{7,71},{8,72},{9,... | collective-permute-start | bytes 442376 | tf_op jit(solution)/shard_map/ppermute | solution.py:531
  88.6 7.4 %collective-permute-start.10 = (bf16[64,1152]{1,0:T(8,128)(2,1)S(1)}, bf16[64,1152]{1,0:T(8,128)(2,1)S(1)}, u32[]{:S(2)}, u32[]{:S(2)}) collective-permute-start(bf16[64,1152]{1,0:T(8,128)(2,1)S(1)} %add_convert_fusion.2.own_ref), channel_id=1, source_target_pairs={{0,96},{1,97},{2,98},{3,99},{4,100},{5,101},{6,102},{7,103},{8,104... | collective-permute-start | bytes 442376 | tf_op jit(solution)/shard_map/ppermute | solution.py:531
  90.8 5.2 %collective-permute-start.9 = (bf16[64,1152]{1,0:T(8,128)(2,1)S(1)}, bf16[64,1152]{1,0:T(8,128)(2,1)S(1)}, u32[]{:S(2)}, u32[]{:S(2)}) collective-permute-start(bf16[64,1152]{1,0:T(8,128)(2,1)S(1)} %add_convert_fusion.2.own_ref), channel_id=1, source_target_pairs={{0,32},{1,33},{2,34},{3,35},{4,36},{5,37},{6,38},{7,39},{8,40},{9,... | collective-permute-start | bytes 442376 | tf_op jit(solution)/shard_map/ppermute | solution.py:531

commit v9 on v8

--- a/solution.py
+++ b/solution.py
@@ -33,8 +33,8 @@
     return pl.CostEstimate(flops=flops, bytes_accessed=nbytes, transcendentals=trans)
 
 
-CHUNKS = (512, 512, 512, 256, 256)
-FCOLS = 512
+def chunk(ref, start):
+    return ref.at[pl.ds(start, ROWS)]
 
 
 def forward_kernel(
@@ -42,68 +42,47 @@
     weight_ref,
     out_weight_ref,
     forecast_ref,
-    hidden_out,
-    slope_out,
+    pre_out,
     padded_ref,
+    pre_ref,
     hidden_ref,
-    slope_ref,
     latent_copy,
     weight_copy,
     out_weight_copy,
     latent_sems,
-    weight_sems,
+    weight_sem,
     out_weight_sem,
-    hidden_sems,
-    slope_sems,
+    pre_sems,
 ):
     nodes, width = latent_ref.shape
     variables = out_weight_ref.shape[0]
+    weight_load = pltpu.make_async_copy(weight_ref, weight_copy, weight_sem)
     out_weight_load = pltpu.make_async_copy(out_weight_ref, out_weight_copy, out_weight_sem)
-    spans = []
-    for size in CHUNKS:
-        begin = spans[-1].stop if spans else 0
-        spans.append(slice(begin, begin + size))
-    weight_loads = [
-        pltpu.make_async_copy(
-            weight_ref.at[:, pl.ds(start, FCOLS)], weight_copy.at[:, pl.ds(start, FCOLS)], weight_sems.at[start // FCOLS]
-        )
-        for start in range(0, width, FCOLS)
+    latent_loads = [
+        pltpu.make_async_copy(chunk(latent_ref, start), chunk(latent_copy, start), latent_sems.at[start // ROWS])
+        for start in range(0, nodes, ROWS)
     ]
-
-    def chunk(ref, rows):
-        return ref.at[pl.ds(rows.start, rows.stop - rows.start)]
-
-    latent_loads = [
-        pltpu.make_async_copy(chunk(latent_ref, rows), chunk(latent_copy, rows), latent_sems.at[index])
-        for index, rows in enumerate(spans)
-    ]
-    weight_loads[0].start()
-    latent_loads[0].start()
-    for load in weight_loads[1:] + latent_loads[1:]:
+    out_weight_load.start()
+    weight_load.start()
+    for load in latent_loads:
         load.start()
-    out_weight_load.start()
     out_weight_load.wait()
     turned_weight = jnp.concatenate(
         [out_weight_copy[...], jnp.zeros((WIDE - variables, width), bf16)], axis=0
     )
     padded_ref[...] = turned_weight.T
+    weight_load.wait()
     stores = []
-    for index, rows in enumerate(spans):
-        latent_loads[index].wait()
-        for start in range(0, width, FCOLS):
-            columns = slice(start, start + FCOLS)
-            if index == 0:
-                weight_loads[start // FCOLS].wait()
-            pre = jnp.dot(latent_copy[rows, :], weight_copy[:, columns], preferred_element_type=f32)
-            sig = 0.5 * jnp.tanh(0.5 * pre) + 0.5
-            hidden = pre * sig
-            hidden_ref[rows, columns] = hidden.astype(bf16)
-            slope_ref[rows, columns] = (sig + hidden * (1.0 - sig)).astype(bf16)
-        for made, out, sems in ((hidden_ref, hidden_out, hidden_sems), (slope_ref, slope_out, slope_sems)):
-            store = pltpu.make_async_copy(chunk(made, rows), chunk(out, rows), sems.at[index])
-            store.start()
-            stores.append(store)
-        for share in range(rows.start // SHARE, rows.stop // SHARE):
+    for start in range(0, nodes, ROWS):
+        rows = slice(start, start + ROWS)
+        latent_loads[start // ROWS].wait()
+        pre = jnp.dot(latent_copy[rows, :], weight_copy[...], preferred_element_type=f32)
+        pre_ref[rows, :] = pre.astype(bf16)
+        hidden_ref[rows, :] = (pre * (0.5 * jnp.tanh(0.5 * pre) + 0.5)).astype(bf16)
+        store = pltpu.make_async_copy(chunk(pre_ref, start), chunk(pre_out, start), pre_sems.at[start // ROWS])
+        store.start()
+        stores.append(store)
+        for share in range(start // SHARE, (start + ROWS) // SHARE):
             forecast_ref[share] = lax.dot_general(
                 turned_weight[:TALL],
                 hidden_ref[share * SHARE : (share + 1) * SHARE, :],
@@ -123,10 +102,9 @@
     return pl.pallas_call(
         forward_kernel,
         in_specs=[anywhere] * 3,
-        out_specs=[vmem, anywhere, anywhere, vmem],
+        out_specs=[vmem, anywhere, vmem],
         out_shape=[
             jax.ShapeDtypeStruct((nodes // SHARE, TALL, SHARE), f32),
-            pltpu.HBM((nodes, width), bf16),
             pltpu.HBM((nodes, width), bf16),
             jax.ShapeDtypeStruct((width, WIDE), bf16),
         ],
@@ -136,11 +114,10 @@
             pltpu.VMEM((nodes, width), bf16),
             pltpu.VMEM((width, width), bf16),
             pltpu.VMEM(out_weight.shape, bf16),
-            pltpu.SemaphoreType.DMA((len(CHUNKS),)),
-            pltpu.SemaphoreType.DMA((width // FCOLS,)),
+            pltpu.SemaphoreType.DMA((nodes // ROWS,)),
             pltpu.SemaphoreType.DMA,
-            pltpu.SemaphoreType.DMA((len(CHUNKS),)),
-            pltpu.SemaphoreType.DMA((len(CHUNKS),)),
+            pltpu.SemaphoreType.DMA,
+            pltpu.SemaphoreType.DMA((nodes // ROWS,)),
         ],
         compiler_params=params(32),
         cost_estimate=cost(2 * nodes * width * (width + WIDE), 20 << 20),
@@ -148,11 +125,64 @@
     )(pinned(latent), pinned(weight), pinned(out_weight))
 
 
+def gate_kernel(pre_hbm, hidden_out, slope_out, pre_ref, hidden_ref, slope_ref, pre_sems, hidden_sems, slope_sems):
+    nodes, width = pre_hbm.shape
+    loads = [
+        pltpu.make_async_copy(chunk(pre_hbm, start), chunk(pre_ref, start), pre_sems.at[start // ROWS])
+        for start in range(0, nodes, ROWS)
+    ]
+    for load in loads:
+        load.start()
+    stores = []
+    for start in range(0, nodes, ROWS):
+        rows = slice(start, start + ROWS)
+        loads[start // ROWS].wait()
+        for group in range(width // 128):
+            columns = slice(group * 128, (group + 1) * 128)
+            pre = pre_ref[rows, columns].astype(f32)
+            sig = 0.5 * jnp.tanh(0.5 * pre) + 0.5
+            hidden = pre * sig
+            hidden_ref[group, rows, :] = hidden.astype(bf16)
+            slope_ref[rows, columns] = (sig + hidden * (1.0 - sig)).astype(bf16)
+        for store in (
+            pltpu.make_async_copy(
+                hidden_ref.at[:, pl.ds(start, ROWS)], hidden_out.at[:, pl.ds(start, ROWS)], hidden_sems.at[start // ROWS]
+            ),
+            pltpu.make_async_copy(chunk(slope_ref, start), chunk(slope_out, start), slope_sems.at[start // ROWS]),
+        ):
+            store.start()
+            stores.append(store)
+    for store in stores:
+        store.wait()
+
+
+def gates(pre):
+    nodes, width = pre.shape
+    sems = pltpu.SemaphoreType.DMA((nodes // ROWS,))
+    return pl.pallas_call(
+        gate_kernel,
+        in_specs=[anywhere],
+        out_specs=[anywhere] * 2,
+        out_shape=[pltpu.HBM((width // 128, nodes, 128), bf16), pltpu.HBM((nodes, width), bf16)],
+        scratch_shapes=[
+            pltpu.VMEM((nodes, width), bf16),
+            pltpu.VMEM((width // 128, nodes, 128), bf16),
+            pltpu.VMEM((nodes, width), bf16),
+            sems,
+            sems,
+            sems,
+        ],
+        compiler_params=params(20),
+        cost_estimate=cost(0, 12 << 20),
+        name="gates",
+    )(pinned(pre))
+
+
 def slope_function(diff):
     return diff * lax.rsqrt(diff * diff + smooth_sq)
 
 
-def pair_kernel(place_ref, blocks_ref, observed_ref, area_ref, low_ref, here_ref, weight_ref, sems):
+def pair_kernel(place_ref, blocks_ref, observed_ref, area_ref, low_ref, here_ref, weight_ref, totals_ref, sems):
     members = blocks_ref.shape[0]
     variables = observed_ref.shape[0]
     at = pl.multiple_of(place_ref[0] * SHARE, SHARE)
@@ -171,17 +201,20 @@
                 slope = slope_function(values[a] - values[b])
                 totals[a] = totals[a] + slope
                 totals[b] = totals[b] - slope
-        if start == 0:
-            for load in loads:
-                load.wait()
-        area = weight_ref[...]
+        for a in range(members):
+            totals_ref[a, rows, :] = totals[a]
+    for load in loads:
+        load.wait()
+    area = weight_ref[...]
+    for start in range(0, TALL, 16):
+        rows = slice(start, start + 16)
         real = min(16, variables - start)
         observed = here_ref[start : start + real, :]
         if real < 16:
             observed = jnp.concatenate([observed, jnp.zeros((16 - real, SHARE), f32)], axis=0)
         for a in range(members):
-            field = area * (slope_function(values[a] - observed) - totals[a] * (1.0 / (members - 1)))
-            low_ref[a, rows, :] = field.astype(bf16)
+            own = slope_function(blocks_ref[a, rows, :] - observed)
+            low_ref[a, rows, :] = (area * (own - totals_ref[a, rows, :] * (1.0 / (members - 1)))).astype(bf16)
 
 
 def pairs(place, blocks, observed, area):
@@ -195,6 +228,7 @@
         scratch_shapes=[
             pltpu.VMEM((variables, SHARE), f32),
             pltpu.VMEM((1, SHARE), f32),
+            pltpu.VMEM((members, TALL, SHARE), f32),
             pltpu.SemaphoreType.DMA((2,)),
         ],
         compiler_params=params(8),
@@ -253,8 +287,8 @@
     x_lo, z, core = position(grid_ref)
     return [
         pltpu.make_async_copy(
-            hidden_hbm.at[:, pl.ds(pl.multiple_of(owner(block, STEPS[part], x_lo, z) * 128, 128), 128)],
-            hidden_ref.at[:, pl.ds(block * 128, 128)],
+            hidden_hbm.at[owner(block, STEPS[part], x_lo, z)],
+            hidden_ref.at[block],
             sems.at[block],
         )
         for block in range(4)
@@ -272,10 +306,10 @@
 def second_product(grid_ref, flat_ref, hidden_ref, send_ref, second_ref, scratch_ref):
     width = send_ref.shape[1] - WIDE
     core = position(grid_ref)[2]
-    for start in (0, 256):
-        rows = slice(start, start + 256)
-        second = jnp.dot(flat_ref[...], hidden_ref[:, rows], preferred_element_type=f32)
-        scratch_ref[rows, :] = second.T.astype(bf16)
+    for block in (0, 2):
+        columns = jnp.concatenate([hidden_ref[block], hidden_ref[block + 1]], axis=1)
+        second = jnp.dot(flat_ref[...], columns, preferred_element_type=f32)
+        scratch_ref[block * 128 : (block + 2) * 128, :] = second.T.astype(bf16)
     for block in range(4):
         rows = slice(block * 64, (block + 1) * 64)
         mine = pl.multiple_of(block * 128 + core * 64, 64)
@@ -308,9 +342,9 @@
     nodes, width = pre_ref.shape
     slope_loads = [
         pltpu.make_async_copy(
-            slope_hbm.at[:, pl.ds(start, COLS)], slope_ref.at[:, pl.ds(start, COLS)], slope_sems.at[start // COLS]
+            slope_hbm.at[pl.ds(start, ROWS)], slope_ref.at[pl.ds(start, ROWS)], slope_sems.at[start // ROWS]
         )
-        for start in range(0, width, COLS)
+        for start in range(0, nodes, ROWS)
     ]
     turned_now = turned_load(turned_hbm, 0, turned_ref, turned_sems.at[0])
     turned_next = turned_load(turned_hbm, 256, next_turned_ref, turned_sems.at[1])
@@ -322,11 +356,11 @@
         low = jnp.concatenate([low_ref[share], jnp.zeros((WIDE - TALL, SHARE), bf16)], axis=0)
         flat_ref[:, columns] = low
         turn_ref[columns, :] = low.T
-    for column in range(0, width, COLS):
-        columns = slice(column, column + COLS)
-        slope_loads[column // COLS].wait()
-        for start in range(0, nodes, ROWS):
-            rows = slice(start, start + ROWS)
+    for start in range(0, nodes, ROWS):
+        rows = slice(start, start + ROWS)
+        slope_loads[start // ROWS].wait()
+        for column in range(0, width, COLS):
+            columns = slice(column, column + COLS)
             grad_hidden = lax.dot_general(turn_ref[rows, :], padded_ref[columns, :], NT, preferred_element_type=f32)
             pre_ref[rows, columns] = (grad_hidden * slope_ref[rows, columns].astype(f32)).astype(bf16)
     turned_now.wait()
@@ -408,12 +442,12 @@
         scratch_shapes=[
             pltpu.VMEM((nodes, WIDE), bf16),
             pltpu.VMEM((256, nodes), bf16),
-            pltpu.VMEM((nodes, 512), bf16),
+            pltpu.VMEM((4, nodes, 128), bf16),
             pltpu.VMEM((512, WIDE), bf16),
             pltpu.VMEM((nodes, width), bf16),
             pltpu.SemaphoreType.DMA((2,)),
             pltpu.SemaphoreType.DMA((4,)),
-            pltpu.SemaphoreType.DMA((width // COLS,)),
+            pltpu.SemaphoreType.DMA((nodes // ROWS,)),
         ],
         compiler_params=params(20),
         cost_estimate=cost(nodes * width * (width // 2 + 3 * WIDE), 8 << 20),
@@ -422,12 +456,12 @@
 
 
 def keep_a(grid, turned_latent, hidden, grad_pre, turned_now, second):
-    nodes, width = hidden.shape
+    nodes, width = grad_pre.shape
     return pl.pallas_call(
         keep_a_kernel,
         in_specs=[smem, anywhere, anywhere] + [vmem] * 3,
         out_specs=[vmem] * 3,
-        out_shape=[shape(256, width + WIDE), shape(256, nodes), shape(nodes, 512)],
+        out_shape=[shape(256, width + WIDE), shape(256, nodes), shape(4, nodes, 128)],
         scratch_shapes=[pltpu.SemaphoreType.DMA, pltpu.SemaphoreType.DMA((4,))],
         compiler_params=params(12),
         cost_estimate=cost(nodes * width * width // 2, 4 << 20),
@@ -572,12 +606,15 @@
     place = lax.axis_index("member").astype(jnp.int32).reshape(1)
     grid = lax.axis_index("grid").astype(jnp.int32).reshape(1)
 
-    forecast, hidden, slope, padded = forward(latent, hidden_weight, output_weight.T)
-    blocks, late_grid = lax.optimization_barrier(((0.25 * forecast).astype(f16), grid))
+    forecast, pre, padded = forward(latent, hidden_weight, output_weight.T)
+    blocks, pre = lax.optimization_barrier(((0.25 * forecast).astype(f16), pre))
     blocks = lax.all_to_all(blocks, "member", 0, 0, tiled=True)
+    hidden, slope = gates(pre)
+    blocks, hidden, slope = lax.optimization_barrier((blocks, hidden, slope))
+    low = pairs(place, 4.0 * blocks.astype(f32), observed, node_area_weight.reshape(1, nodes))
+    low, late_grid = lax.optimization_barrier((low, grid))
+    low = lax.all_to_all(low, "member", 0, 0, tiled=True)
     turned_latent = turned(late_grid, latent)
-    low = pairs(place, 4.0 * blocks.astype(f32), observed, node_area_weight.reshape(1, nodes))
-    low = lax.all_to_all(low, "member", 0, 0, tiled=True)
     grad_pre, rows_a, second_a, flat, turned_now = send_a(grid, low, turned_latent, slope, hidden, padded)
     kept_a, turned_now, hidden_now = keep_a(grid, turned_latent, hidden, grad_pre, turned_now, second_a)
     far, own = over_core(rows_a, kept_a).astype(bf16)

time: 97.2 us -> 94.8 us (0.975)
  waiting for transfers between devices: 30.3 us -> 24.3 us
  Pallas kernels: 33.8 us -> 37.4 us
    all_to_all x1, waiting for transfers between devices: 10.9 us -> 5.06 us  [body(): blocks = lax.all_to_all(blocks, 'member', 0, 0, tiled=True)]
    pallas_call x0 -> x1, Pallas kernels: none -> 5.79 us  [gates(): pl.pallas_call(gate_kernel, in_specs=[anywhere], out_specs=[anywhere] * 2...]
    pallas_call x1, Pallas kernels: 12.1 us -> 10.1 us  [forward(): pl.pallas_call(forward_kernel, in_specs=[anywhere] * 3, out_specs=[vmem,...]
  transfers between devices with their start and end apart: 14 -> 14, of which waited for: 9 -> 9; matrix products, arithmetic and copies ran while one was open for 0% -> 0% of each run, Pallas kernels for 12% -> 18%
where the time goes in v9:
time: 94.8 us; the launch traced here: 94.4 us
  Pallas kernels  37.4 us (39%)
  starting transfers between devices  25.9 us (27%)
  waiting for transfers between devices  24.3 us (26%)
  local copies, waits for them, and re-layouts  4.32 us (5%)
  other arithmetic  1.62 us (2%)
    ppermute x12, starting transfers between devices, moved(): return lax.ppermute(value, ('member', 'grid'), moves)  15.2 us
    ppermute x12, waiting for transfers between devices, moved(): return lax.ppermute(value, ('member', 'grid'), moves)  14.9 us
    pallas_call x1, Pallas kernels, forward(): pl.pallas_call(forward_kernel, in_specs=[anywhere] * 3, out_specs=[vmem,...  10.1 us
    all_to_all x1, starting transfers between devices, body(): blocks = lax.all_to_all(blocks, 'member', 0, 0, tiled=True)  7.02 us
    pallas_call x1, Pallas kernels, gates(): pl.pallas_call(gate_kernel, in_specs=[anywhere], out_specs=[anywhere] * 2...  5.79 us
    pallas_call x1, Pallas kernels, latent_gradient(): pl.pallas_call(latent_kernel, in_specs=[vmem, vmem], out_specs=anywhere,...  5.59 us
    pallas_call x1, Pallas kernels, send_a(): pl.pallas_call(send_a_kernel, in_specs=[smem, vmem, anywhere, anywhere, a...  5.34 us
    all_to_all x1, waiting for transfers between devices, body(): blocks = lax.all_to_all(blocks, 'member', 0, 0, tiled=True)  5.06 us
  transfers between devices with their start and end apart: 14, of which 9 were waited for; matrix products, arithmetic and copies ran while one was open for 0% of the time, Pallas kernels for 18%

profile of v9, /device:TPU:0, one launch (start us, length us, event | category | flops | bytes accessed | tf_op | source)
XLA Modules:
  0.0 94.4 jit_solution(10376509273627753006)
XLA Ops:
  0.6 10.1 %forward.1 = (f32[8,112,256]{2,1,0:T(8,128)S(1)}, bf16[2048,1024]{1,0:T(8,128)(2,1)}, bf16[1024,128]{1,0:T(8,128)(2,1)S(1)}) custom-call(bf16[2048,1024]{1,0:T(8,128)(2,1)} %bitcast.26, bf16[1024,1024]{1,0:T(8,128)(2,1)} %weight_hbm.1, bf16[100,1024]{1,0:T(8,128)(2,1)} %bitcast.31), custom_call_target="tpu_custom_call" | custom-call | flops 4831838208 | bytes 20971520 | tf_op jit(solution)/shard_map/forward/pallas_call | solution.py:102
  10.7 0.9 multiply_convert_fusion
  11.6 7.0 %all-to-all-start = ((f16[8,112,256]{2,1,0:T(8,128)(2,1)}), f16[8,112,256]{2,1,0:T(8,128)(2,1)S(1)}, u32[]{:S(2)}, u32[]{:S(2)}) async-start(f16[8,112,256]{2,1,0:T(8,128)(2,1)} %multiply_convert_fusion), calls=%async_computation | async-start | bytes 917504 | tf_op jit(solution)/shard_map/all_to_all | solution.py:611
  18.7 0.0 copy-start.2
  18.7 0.0 copy-start.3
  18.7 5.8 %gates.1 = (bf16[8,2048,128]{2,1,0:T(8,128)(2,1)}, bf16[2048,1024]{1,0:T(8,128)(2,1)}) custom-call(bf16[2048,1024]{1,0:T(8,128)(2,1)} %get-tuple-element.41.pre_hbm), custom_call_target="tpu_custom_call" | custom-call | bytes 12582912 | tf_op jit(solution)/shard_map/gates/pallas_call | solution.py:162
  24.5 5.1 %all-to-all-done = f16[8,112,256]{2,1,0:T(8,128)(2,1)S(1)} async-done(((f16[8,112,256]{2,1,0:T(8,128)(2,1)}), f16[8,112,256]{2,1,0:T(8,128)(2,1)S(1)}, u32[]{:S(2)}, u32[]{:S(2)}) %all-to-all-start) | async-done | bytes 458784 | tf_op jit(solution)/shard_map/all_to_all | solution.py:611
  29.5 0.1 convert_multiply_fusion.blocks_ref
  29.6 0.0 copy-done.2
  29.6 0.0 copy-done.3
  29.6 1.9 %pairs.1 = bf16[8,112,256]{2,1,0:T(8,128)(2,1)} custom-call(s32[1]{0:T(128)} %bitcast.1.place_ref, f32[8,112,256]{2,1,0:T(8,128)S(1)} %convert_multiply_fusion.blocks_ref, f32[100,2048]{1,0:T(8,128)S(1)} %copy-done.2, f32[1,2048]{1,0:T(1,128)S(1)} %bitcast.28), custom_call_target="tpu_custom_call" | custom-call | flops 4194304 | bytes 2097152 | tf_op jit(solution)/shard_map/pairs/pallas_call | solution.py:223
  31.5 3.7 %all-to-all-start.1 = ((bf16[8,112,256]{2,1,0:T(8,128)(2,1)}), bf16[8,112,256]{2,1,0:T(8,128)(2,1)S(1)}, u32[]{:S(2)}, u32[]{:S(2)}) async-start(bf16[8,112,256]{2,1,0:T(8,128)(2,1)} %pairs.1), calls=%async_computation.1 | async-start | bytes 917504 | tf_op jit(solution)/shard_map/all_to_all | solution.py:616
  35.2 0.0 copy-start.1
  35.2 2.2 %copy-done.1 = bf16[1,2048,1024]{2,1,0:T(8,128)(2,1)S(1)} copy-done((bf16[1,2048,1024]{2,1,0:T(8,128)(2,1)S(1)}, bf16[1,2048,1024]{2,1,0:T(8,128)(2,1)}, u32[]{:S(2)}) %copy-start.1) | copy-done | bytes 4194328
  37.4 1.1 %turned.1.turned_hbm = bf16[1024,2048]{1,0:T(8,128)(2,1)S(1)} custom-call(s32[1]{0:T(128)} %bitcast.grid_ref, bf16[2048,1024]{1,0:T(8,128)(2,1)S(1)} %bitcast.27), custom_call_target="tpu_custom_call" | custom-call | bytes 8388608 | tf_op jit(solution)/shard_map/turned/pallas_call | solution.py:271
  38.6 0.0 copy-start
  38.6 2.0 %copy-done = bf16[1024,2048]{1,0:T(8,128)(2,1)} copy-done((bf16[1024,2048]{1,0:T(8,128)(2,1)}, bf16[1024,2048]{1,0:T(8,128)(2,1)S(1)}, u32[]{:S(2)}) %copy-start) | copy-done | bytes 4194328
  40.6 4.4 %all-to-all-done.1.low_ref = bf16[8,112,256]{2,1,0:T(8,128)(2,1)S(1)} async-done(((bf16[8,112,256]{2,1,0:T(8,128)(2,1)}), bf16[8,112,256]{2,1,0:T(8,128)(2,1)S(1)}, u32[]{:S(2)}, u32[]{:S(2)}) %all-to-all-start.1) | async-done | bytes 458784 | tf_op jit(solution)/shard_map/all_to_all | solution.py:616
  44.9 5.3 %send_a.1 = (bf16[2048,1024]{1,0:T(8,128)(2,1)S(1)}, bf16[256,1152]{1,0:T(8,128)(2,1)S(1)}, bf16[256,128]{1,0:T(8,128)(2,1)S(1)}, bf16[128,2048]{1,0:T(8,128)(2,1)S(1)}, bf16[256,2048]{1,0:T(8,128)(2,1)S(1)}) custom-call(s32[1]{0:T(128)} %bitcast.grid_ref, bf16[8,112,256]{2,1,0:T(8,128)(2,1)S(1)} %all-to-all-done.1.low_ref, bf16[1024,2048]{1,0:T(8,128)(2,1)} %copy-done, ...), custom_call_target="tpu_custom_call" | custom-call | flops 1879048192 | bytes 8388608 | tf_op jit(solution)/shard_map/send_a/pallas_call | solution.py:431
  50.3 0.1 collective-permute-start
  50.4 2.9 %keep_a.1 = (bf16[256,1152]{1,0:T(8,128)(2,1)S(1)}, bf16[256,2048]{1,0:T(8,128)(2,1)S(1)}, bf16[4,2048,128]{2,1,0:T(8,128)(2,1)S(1)}) custom-call(s32[1]{0:T(128)} %bitcast.grid_ref, bf16[1024,2048]{1,0:T(8,128)(2,1)} %copy-done, bf16[8,2048,128]{2,1,0:T(8,128)(2,1)} %get-tuple-element.46.hidden_hbm, bf16[2048,1024]{1,0:T(8,128)(2,1)S(1)} %get-tuple-element.67.pre_ref, ...), custom_call_target="tpu_custom_call" | custom-call | flops 1073741824 | bytes 4194304 | tf_op jit(solution)/shard_map/keep_a/pallas_call | solution.py:460
  53.3 0.0 collective-permute-done
  53.3 0.1 add_convert_fusion
  53.5 2.3 %send_b.1 = (bf16[256,1152]{1,0:T(8,128)(2,1)S(1)}, bf16[256,128]{1,0:T(8,128)(2,1)S(1)}, bf16[256,2048]{1,0:T(8,128)(2,1)S(1)}) custom-call(s32[1]{0:T(128)} %bitcast.grid_ref, bf16[1024,2048]{1,0:T(8,128)(2,1)} %copy-done, bf16[2048,1024]{1,0:T(8,128)(2,1)S(1)} %get-tuple-element.67.pre_ref, bf16[128,2048]{1,0:T(8,128)(2,1)S(1)} %get-tuple-element.57.flat_ref, ...), custom_call_target="tpu_custom_call" | custom-call | flops 1073741824 | bytes 4194304 | tf_op jit(solution)/shard_map/send_b/pallas_call | solution.py:474
  55.8 0.6 collective-permute-start.1
  56.4 4.1 %collective-permute-start.3 = (bf16[64,1152]{1,0:T(8,128)(2,1)S(1)}, bf16[64,1152]{1,0:T(8,128)(2,1)S(1)}, u32[]{:S(2)}, u32[]{:S(2)}) collective-permute-start(bf16[64,1152]{1,0:T(8,128)(2,1)S(1)} %get-tuple-element.83), channel_id=1, source_target_pairs={{0,6},{1,7},{2,0},{3,1},{4,2},{5,3},{6,4},{7,5},{8,14},{9,15},{10,... | collective-permute-start | bytes 442376 | tf_op jit(solution)/shard_map/ppermute | solution.py:565
  60.6 0.0 collective-permute-start.2
  60.6 1.6 %keep_b.1 = (bf16[256,1152]{1,0:T(8,128)(2,1)S(1)}, bf16[1024,1024]{1,0:T(8,128)(2,1)S(1)}) custom-call(bf16[1024,1024]{1,0:T(8,128)(2,1)} %weight_hbm.1, bf16[2048,1024]{1,0:T(8,128)(2,1)S(1)} %get-tuple-element.67.pre_ref, bf16[256,2048]{1,0:T(8,128)(2,1)S(1)} %get-tuple-element.60.turned_ref, bf16[256,128]{1,0:T(8,128)(2,1)S(1)} %get-tuple-element.61.second_ref), custom_call_target="tpu_custom_call" | custom-call | flops 1073741824 | bytes 4194304 | tf_op jit(solution)/shard_map/keep_b/pallas_call | solution.py:488
  62.2 0.0 collective-permute-done.1
  62.2 0.2 convert_add_fusion
  62.4 1.5 %collective-permute-done.3 = bf16[64,1152]{1,0:T(8,128)(2,1)S(1)} collective-permute-done((bf16[64,1152]{1,0:T(8,128)(2,1)S(1)}, bf16[64,1152]{1,0:T(8,128)(2,1)S(1)}, u32[]{:S(2)}, u32[]{:S(2)}) %collective-permute-start.3) | collective-permute-done | bytes 147488 | tf_op jit(solution)/shard_map/ppermute | solution.py:565
  63.8 3.4 %collective-permute-done.2 = bf16[64,1152]{1,0:T(8,128)(2,1)S(1)} collective-permute-done((bf16[64,1152]{1,0:T(8,128)(2,1)S(1)}, bf16[64,1152]{1,0:T(8,128)(2,1)S(1)}, u32[]{:S(2)}, u32[]{:S(2)}) %collective-permute-start.2) | collective-permute-done | bytes 147488 | tf_op jit(solution)/shard_map/ppermute | solution.py:565
  67.3 0.1 fusion.3
  67.3 0.1 pad_maximum_fusion
  67.4 0.1 collective-permute-start.4
  67.5 3.2 %collective-permute-start.5 = (bf16[2,64,1152]{2,1,0:T(8,128)(2,1)S(1)}, bf16[2,64,1152]{2,1,0:T(8,128)(2,1)S(1)}, u32[]{:S(2)}, u32[]{:S(2)}) collective-permute-start(bf16[2,64,1152]{2,1,0:T(8,128)(2,1)S(1)} %get-tuple-element.66), channel_id=1, source_target_pairs={{0,6},{1,7},{2,0},{3,1},{4,2},{5,3},{6,4},{7,5},{8,14},{9,15},{10,... | collective-permute-start | bytes 884744 | tf_op jit(solution)/shard_map/ppermute | solution.py:565
  70.7 5.6 %latent_gradient.1 = bf16[2048,1024]{1,0:T(8,128)(2,1)} custom-call(bf16[2048,1024]{1,0:T(8,128)(2,1)S(1)} %get-tuple-element.67.pre_ref, bf16[1024,1024]{1,0:T(8,128)(2,1)S(1)} %get-tuple-element.68.weight_ref), custom_call_target="tpu_custom_call" | custom-call | flops 4294967296 | bytes 10485760 | tf_op jit(solution)/shard_map/latent_gradient/pallas_call | solution.py:521
  76.3 0.1 collective-permute-done.4
  76.4 0.0 collective-permute-done.5
  76.4 0.1 add_convert_fusion.1
  76.6 0.9 collective-permute-start.8
  77.5 2.5 %collective-permute-start.7 = (bf16[64,1152]{1,0:T(8,128)(2,1)S(1)}, bf16[64,1152]{1,0:T(8,128)(2,1)S(1)}, u32[]{:S(2)}, u32[]{:S(2)}) collective-permute-start(bf16[64,1152]{1,0:T(8,128)(2,1)S(1)} %get-tuple-element.81), channel_id=1, source_target_pairs={{0,24},{1,25},{2,26},{3,27},{4,28},{5,29},{6,30},{7,31},{8,16},{9,... | collective-permute-start | bytes 442376 | tf_op jit(solution)/shard_map/ppermute | solution.py:565
  80.0 0.2 collective-permute-start.6
  80.2 3.6 %collective-permute-done.8 = bf16[64,1152]{1,0:T(8,128)(2,1)S(1)} collective-permute-done((bf16[64,1152]{1,0:T(8,128)(2,1)S(1)}, bf16[64,1152]{1,0:T(8,128)(2,1)S(1)}, u32[]{:S(2)}, u32[]{:S(2)}) %collective-permute-start.8) | collective-permute-done | bytes 147488 | tf_op jit(solution)/shard_map/ppermute | solution.py:565
  83.8 1.5 %collective-permute-done.7 = bf16[64,1152]{1,0:T(8,128)(2,1)S(1)} collective-permute-done((bf16[64,1152]{1,0:T(8,128)(2,1)S(1)}, bf16[64,1152]{1,0:T(8,128)(2,1)S(1)}, u32[]{:S(2)}, u32[]{:S(2)}) %collective-permute-start.7) | collective-permute-done | bytes 147488 | tf_op jit(solution)/shard_map/ppermute | solution.py:565
  85.2 0.0 collective-permute-done.6
  85.3 0.1 add_convert_fusion.2.own_ref
  85.3 0.9 collective-permute-start.11
  86.3 2.1 %collective-permute-start.10 = (bf16[64,1152]{1,0:T(8,128)(2,1)S(1)}, bf16[64,1152]{1,0:T(8,128)(2,1)S(1)}, u32[]{:S(2)}, u32[]{:S(2)}) collective-permute-start(bf16[64,1152]{1,0:T(8,128)(2,1)S(1)} %add_convert_fusion.2.own_ref), channel_id=1, source_target_pairs={{0,96},{1,97},{2,98},{3,99},{4,100},{5,101},{6,102},{7,103},{8,104... | collective-permute-start | bytes 442376 | tf_op jit(solution)/shard_map/ppermute | solution.py:565
  88.4 0.5 collective-permute-start.9
  88.9 3.3 %collective-permute-done.11.refs_2_ = bf16[64,1152]{1,0:T(8,128)(2,1)S(1)} collective-permute-done((bf16[64,1152]{1,0:T(8,128)(2,1)S(1)}, bf16[64,1152]{1,0:T(8,128)(2,1)S(1)}, u32[]{:S(2)}, u32[]{:S(2)}) %collective-permute-start.11) | collective-permute-done | bytes 147488 | tf_op jit(solution)/shard_map/ppermute | solution.py:565
  92.2 1.5 %collective-permute-done.10.refs_1_ = bf16[64,1152]{1,0:T(8,128)(2,1)S(1)} collective-permute-done((bf16[64,1152]{1,0:T(8,128)(2,1)S(1)}, bf16[64,1152]{1,0:T(8,128)(2,1)S(1)}, u32[]{:S(2)}, u32[]{:S(2)}) %collective-permute-start.10) | collective-permute-done | bytes 147488 | tf_op jit(solution)/shard_map/ppermute | solution.py:565
  93.6 0.0 collective-permute-done.9.refs_0_
  93.6 0.8 finish.1
  (4 shorter events, 0.1 us)
Async XLA Ops:
  11.6 17.9 %all-to-all-start = ((f16[8,112,256]{2,1,0:T(8,128)(2,1)}), f16[8,112,256]{2,1,0:T(8,128)(2,1)S(1)}, u32[]{:S(2)}, u32[]{:S(2)}) async-start(f16[8,112,256]{2,1,0:T(8,128)(2,1)} %multiply_convert_fusion), calls=%async_computation | async-start | bytes 917504 | tf_op jit(solution)/shard_map/all_to_all | solution.py:611
  18.7 11.0 %copy-start.2 = (f32[100,2048]{1,0:T(8,128)S(1)}, f32[100,2048]{1,0:T(8,128)}, u32[]{:S(2)}) copy-start(f32[100,2048]{1,0:T(8,128)} %observed_ref.1) | copy-start | bytes 2457604
  18.7 11.0 %copy-start.3 = (f32[2048]{0:T(1024)S(1)}, f32[2048]{0:T(1024)}, u32[]{:S(2)}) copy-start(f32[2048]{0:T(1024)} %param.9) | copy-start | bytes 24580
  31.5 13.4 %all-to-all-start.1 = ((bf16[8,112,256]{2,1,0:T(8,128)(2,1)}), bf16[8,112,256]{2,1,0:T(8,128)(2,1)S(1)}, u32[]{:S(2)}, u32[]{:S(2)}) async-start(bf16[8,112,256]{2,1,0:T(8,128)(2,1)} %pairs.1), calls=%async_computation.1 | async-start | bytes 917504 | tf_op jit(solution)/shard_map/all_to_all | solution.py:616
  35.2 2.2 %copy-start.1 = (bf16[1,2048,1024]{2,1,0:T(8,128)(2,1)S(1)}, bf16[1,2048,1024]{2,1,0:T(8,128)(2,1)}, u32[]{:S(2)}) copy-start(bf16[1,2048,1024]{2,1,0:T(8,128)(2,1)} %param.5) | copy-start | bytes 12582916
  38.6 2.0 %copy-start = (bf16[1024,2048]{1,0:T(8,128)(2,1)}, bf16[1024,2048]{1,0:T(8,128)(2,1)S(1)}, u32[]{:S(2)}) copy-start(bf16[1024,2048]{1,0:T(8,128)(2,1)S(1)} %turned.1.turned_hbm) | copy-start | bytes 12582916
  50.3 3.0 %collective-permute-start = (bf16[256,1152]{1,0:T(8,128)(2,1)S(1)}, bf16[256,1152]{1,0:T(8,128)(2,1)S(1)}, u32[]{:S(2)}, u32[]{:S(2)}) collective-permute-start(bf16[256,1152]{1,0:T(8,128)(2,1)S(1)} %get-tuple-element.54), channel_id=1, source_target_pairs={{0,1},{1,0},{2,3},{3,2},{4,5},{5,4},{6,7},{7,6},{8,9},{9,8},{10,11... | collective-permute-start | bytes 1769480 | tf_op jit(solution)/shard_map/ppermute | solution.py:565
  55.8 6.3 %collective-permute-start.1 = (bf16[256,1152]{1,0:T(8,128)(2,1)S(1)}, bf16[256,1152]{1,0:T(8,128)(2,1)S(1)}, u32[]{:S(2)}, u32[]{:S(2)}) collective-permute-start(bf16[256,1152]{1,0:T(8,128)(2,1)S(1)} %get-tuple-element.63), channel_id=1, source_target_pairs={{0,1},{1,0},{2,3},{3,2},{4,5},{5,4},{6,7},{7,6},{8,9},{9,8},{10,11... | collective-permute-start | bytes 1769480 | tf_op jit(solution)/shard_map/ppermute | solution.py:565
  56.4 7.4 %collective-permute-start.3 = (bf16[64,1152]{1,0:T(8,128)(2,1)S(1)}, bf16[64,1152]{1,0:T(8,128)(2,1)S(1)}, u32[]{:S(2)}, u32[]{:S(2)}) collective-permute-start(bf16[64,1152]{1,0:T(8,128)(2,1)S(1)} %get-tuple-element.83), channel_id=1, source_target_pairs={{0,6},{1,7},{2,0},{3,1},{4,2},{5,3},{6,4},{7,5},{8,14},{9,15},{10,... | collective-permute-start | bytes 442376 | tf_op jit(solution)/shard_map/ppermute | solution.py:565
  60.6 6.7 %collective-permute-start.2 = (bf16[64,1152]{1,0:T(8,128)(2,1)S(1)}, bf16[64,1152]{1,0:T(8,128)(2,1)S(1)}, u32[]{:S(2)}, u32[]{:S(2)}) collective-permute-start(bf16[64,1152]{1,0:T(8,128)(2,1)S(1)} %get-tuple-element.84), channel_id=1, source_target_pairs={{0,2},{1,3},{2,4},{3,5},{4,6},{5,7},{6,0},{7,1},{8,10},{9,11},{10,... | collective-permute-start | bytes 442376 | tf_op jit(solution)/shard_map/ppermute | solution.py:565
  67.4 9.0 %collective-permute-start.4 = (bf16[2,64,1152]{2,1,0:T(8,128)(2,1)S(1)}, bf16[2,64,1152]{2,1,0:T(8,128)(2,1)S(1)}, u32[]{:S(2)}, u32[]{:S(2)}) collective-permute-start(bf16[2,64,1152]{2,1,0:T(8,128)(2,1)S(1)} %get-tuple-element.65), channel_id=1, source_target_pairs={{0,2},{1,3},{2,4},{3,5},{4,6},{5,7},{6,0},{7,1},{8,10},{9,11},{10,... | collective-permute-start | bytes 884744 | tf_op jit(solution)/shard_map/ppermute | solution.py:565
  67.5 9.0 %collective-permute-start.5 = (bf16[2,64,1152]{2,1,0:T(8,128)(2,1)S(1)}, bf16[2,64,1152]{2,1,0:T(8,128)(2,1)S(1)}, u32[]{:S(2)}, u32[]{:S(2)}) collective-permute-start(bf16[2,64,1152]{2,1,0:T(8,128)(2,1)S(1)} %get-tuple-element.66), channel_id=1, source_target_pairs={{0,6},{1,7},{2,0},{3,1},{4,2},{5,3},{6,4},{7,5},{8,14},{9,15},{10,... | collective-permute-start | bytes 884744 | tf_op jit(solution)/shard_map/ppermute | solution.py:565
  76.6 7.2 %collective-permute-start.8 = (bf16[64,1152]{1,0:T(8,128)(2,1)S(1)}, bf16[64,1152]{1,0:T(8,128)(2,1)S(1)}, u32[]{:S(2)}, u32[]{:S(2)}) collective-permute-start(bf16[64,1152]{1,0:T(8,128)(2,1)S(1)} %get-tuple-element.82), channel_id=1, source_target_pairs={{0,16},{1,17},{2,18},{3,19},{4,20},{5,21},{6,22},{7,23},{8,24},{9,... | collective-permute-start | bytes 442376 | tf_op jit(solution)/shard_map/ppermute | solution.py:565
  77.5 7.7 %collective-permute-start.7 = (bf16[64,1152]{1,0:T(8,128)(2,1)S(1)}, bf16[64,1152]{1,0:T(8,128)(2,1)S(1)}, u32[]{:S(2)}, u32[]{:S(2)}) collective-permute-start(bf16[64,1152]{1,0:T(8,128)(2,1)S(1)} %get-tuple-element.81), channel_id=1, source_target_pairs={{0,24},{1,25},{2,26},{3,27},{4,28},{5,29},{6,30},{7,31},{8,16},{9,... | collective-permute-start | bytes 442376 | tf_op jit(solution)/shard_map/ppermute | solution.py:565
  80.0 5.3 %collective-permute-start.6 = (bf16[64,1152]{1,0:T(8,128)(2,1)S(1)}, bf16[64,1152]{1,0:T(8,128)(2,1)S(1)}, u32[]{:S(2)}, u32[]{:S(2)}) collective-permute-start(bf16[64,1152]{1,0:T(8,128)(2,1)S(1)} %get-tuple-element.81), channel_id=1, source_target_pairs={{0,8},{1,9},{2,10},{3,11},{4,12},{5,13},{6,14},{7,15},{8,0},{9,1},... | collective-permute-start | bytes 442376 | tf_op jit(solution)/shard_map/ppermute | solution.py:565
  85.3 6.8 %collective-permute-start.11 = (bf16[64,1152]{1,0:T(8,128)(2,1)S(1)}, bf16[64,1152]{1,0:T(8,128)(2,1)S(1)}, u32[]{:S(2)}, u32[]{:S(2)}) collective-permute-start(bf16[64,1152]{1,0:T(8,128)(2,1)S(1)} %add_convert_fusion.2.own_ref), channel_id=1, source_target_pairs={{0,64},{1,65},{2,66},{3,67},{4,68},{5,69},{6,70},{7,71},{8,72},{9,... | collective-permute-start | bytes 442376 | tf_op jit(solution)/shard_map/ppermute | solution.py:565
  86.3 7.4 %collective-permute-start.10 = (bf16[64,1152]{1,0:T(8,128)(2,1)S(1)}, bf16[64,1152]{1,0:T(8,128)(2,1)S(1)}, u32[]{:S(2)}, u32[]{:S(2)}) collective-permute-start(bf16[64,1152]{1,0:T(8,128)(2,1)S(1)} %add_convert_fusion.2.own_ref), channel_id=1, source_target_pairs={{0,96},{1,97},{2,98},{3,99},{4,100},{5,101},{6,102},{7,103},{8,104... | collective-permute-start | bytes 442376 | tf_op jit(solution)/shard_map/ppermute | solution.py:565
  88.4 5.2 %collective-permute-start.9 = (bf16[64,1152]{1,0:T(8,128)(2,1)S(1)}, bf16[64,1152]{1,0:T(8,128)(2,1)S(1)}, u32[]{:S(2)}, u32[]{:S(2)}) collective-permute-start(bf16[64,1152]{1,0:T(8,128)(2,1)S(1)} %add_convert_fusion.2.own_ref), channel_id=1, source_target_pairs={{0,32},{1,33},{2,34},{3,35},{4,36},{5,37},{6,38},{7,39},{8,40},{9,... | collective-permute-start | bytes 442376 | tf_op jit(solution)/shard_map/ppermute | solution.py:565

commit v10 on v9

--- a/solution.py
+++ b/solution.py
@@ -497,18 +497,19 @@
     )(pinned(weight), grad_pre, turned_now, second)
 
 
-def latent_kernel(pre_ref, weight_ref, out_ref, result_ref, sems):
-    nodes, width = pre_ref.shape
+def latent_kernel(pre_ref, weight_ref, *refs, begin):
+    out_ref, result_ref, sems = refs[-3:]
+    width = pre_ref.shape[1]
     stores = []
-    for row in range(0, nodes, ROWS):
-        rows = slice(row, row + ROWS)
+    for row in range(0, result_ref.shape[0], ROWS):
+        rows = slice(begin + row, begin + row + ROWS)
         for start in range(0, width, COLS):
             columns = slice(start, start + COLS)
-            result_ref[rows, columns] = lax.dot_general(
+            result_ref[row : row + ROWS, columns] = lax.dot_general(
                 pre_ref[rows, :], weight_ref[columns, :], NT, preferred_element_type=f32
             ).astype(bf16)
         store = pltpu.make_async_copy(
-            result_ref.at[pl.ds(row, ROWS)], out_ref.at[pl.ds(row, ROWS)], sems.at[row // ROWS]
+            result_ref.at[pl.ds(row, ROWS)], out_ref.at[pl.ds(begin + row, ROWS)], sems.at[row // ROWS]
         )
         store.start()
         stores.append(store)
@@ -516,18 +517,21 @@
         store.wait()
 
 
-def latent_gradient(grad_pre, weight):
+def latent_gradient(grad_pre, weight, begin, so_far=None):
     nodes, width = grad_pre.shape
-    return pl.pallas_call(
-        latent_kernel,
-        in_specs=[vmem, vmem],
+    half = nodes // 2
+    more = [] if so_far is None else [so_far]
+    return pl.pallas_call(
+        functools.partial(latent_kernel, begin=begin),
+        in_specs=[vmem, vmem] + [anywhere] * len(more),
         out_specs=anywhere,
         out_shape=pltpu.HBM((nodes, width), bf16),
-        scratch_shapes=[pltpu.VMEM((nodes, width), bf16), pltpu.SemaphoreType.DMA((nodes // ROWS,))],
+        input_output_aliases={2: 0} if more else {},
+        scratch_shapes=[pltpu.VMEM((half, width), bf16), pltpu.SemaphoreType.DMA((half // ROWS,))],
         compiler_params=params(12),
-        cost_estimate=cost(2 * nodes * width * width, 10 << 20),
+        cost_estimate=cost(nodes * width * width, 5 << 20),
         name="latent_gradient",
-    )(grad_pre, weight)
+    )(grad_pre, weight, *more)
 
 
 def finish_kernel(own_ref, *refs, factor):
@@ -623,10 +627,12 @@
     rows_b, second_b, turned_now = send_b(grid, turned_latent, grad_pre, flat, turned_now, hidden_now)
     kept_b, weight_copy = keep_b(hidden_weight, grad_pre, turned_now, second_b)
     above, below = over_core(rows_b, kept_b)
+    grad_latent = latent_gradient(grad_pre, weight_copy, 0)
+    upward, downward, grad_latent = lax.optimization_barrier((upward, downward, grad_latent))
     above = jnp.stack([above[0] + upward.astype(f32), above[1]]).astype(bf16)
     below = jnp.stack([below[0], below[1] + downward.astype(f32)]).astype(bf16)
     above, below, grad_pre = lax.optimization_barrier((above, below, grad_pre))
-    grad_latent = latent_gradient(grad_pre, weight_copy)
+    grad_latent = latent_gradient(grad_pre, weight_copy, nodes // 2, grad_latent)
     blocks = summed(own, [up(above), down(below)]).astype(bf16)
     blocks, grad_latent = lax.optimization_barrier((blocks, grad_latent))
     block = over_x(blocks)

time: 94.8 us -> 94.9 us (level)
  Pallas kernels: 37.4 us -> 38.6 us
  waiting for transfers between devices: 24.3 us -> 23.2 us
    pallas_call x1 -> x2, Pallas kernels: 5.59 us -> 6.76 us  [latent_gradient(): pl.pallas_call(functools.partial(latent_kernel, begin=begin), in_specs=[v...]
    ppermute x12, waiting for transfers between devices: 14.9 us -> 13.8 us  [moved(): return lax.ppermute(value, ('member', 'grid'), moves)]
  transfers between devices with their start and end apart: 14 -> 14, of which waited for: 9 -> 9; matrix products, arithmetic and copies ran while one was open for 0% -> 0% of each run, Pallas kernels for 18% -> 19%
where the time goes in v10:
time: 94.9 us; the launch traced here: 94.5 us
  Pallas kernels  38.6 us (41%)
  starting transfers between devices  25.9 us (27%)
  waiting for transfers between devices  23.2 us (24%)
  local copies, waits for them, and re-layouts  4.32 us (5%)
  other arithmetic  1.63 us (2%)
    ppermute x12, starting transfers between devices, moved(): return lax.ppermute(value, ('member', 'grid'), moves)  15.2 us
    ppermute x12, waiting for transfers between devices, moved(): return lax.ppermute(value, ('member', 'grid'), moves)  13.8 us
    pallas_call x1, Pallas kernels, forward(): pl.pallas_call(forward_kernel, in_specs=[anywhere] * 3, out_specs=[vmem,...  10.1 us
    all_to_all x1, starting transfers between devices, body(): blocks = lax.all_to_all(blocks, 'member', 0, 0, tiled=True)  7.02 us
    pallas_call x2, Pallas kernels, latent_gradient(): pl.pallas_call(functools.partial(latent_kernel, begin=begin), in_specs=[v...  6.76 us
    pallas_call x1, Pallas kernels, gates(): pl.pallas_call(gate_kernel, in_specs=[anywhere], out_specs=[anywhere] * 2...  5.79 us
    pallas_call x1, Pallas kernels, send_a(): pl.pallas_call(send_a_kernel, in_specs=[smem, vmem, anywhere, anywhere, a...  5.34 us
    all_to_all x1, waiting for transfers between devices, body(): blocks = lax.all_to_all(blocks, 'member', 0, 0, tiled=True)  5.06 us
  transfers between devices with their start and end apart: 14, of which 9 were waited for; matrix products, arithmetic and copies ran while one was open for 0% of the time, Pallas kernels for 19%

profile of v10, /device:TPU:0, one launch (start us, length us, event | category | flops | bytes accessed | tf_op | source)
XLA Modules:
  0.0 94.5 jit_solution(17128390249443206953)
XLA Ops:
  0.6 10.1 %forward.1 = (f32[8,112,256]{2,1,0:T(8,128)S(1)}, bf16[2048,1024]{1,0:T(8,128)(2,1)}, bf16[1024,128]{1,0:T(8,128)(2,1)S(1)}) custom-call(bf16[2048,1024]{1,0:T(8,128)(2,1)} %bitcast.26, bf16[1024,1024]{1,0:T(8,128)(2,1)} %weight_hbm.1, bf16[100,1024]{1,0:T(8,128)(2,1)} %bitcast.32), custom_call_target="tpu_custom_call" | custom-call | flops 4831838208 | bytes 20971520 | tf_op jit(solution)/shard_map/forward/pallas_call | solution.py:102
  10.7 0.9 multiply_convert_fusion
  11.6 7.0 %all-to-all-start = ((f16[8,112,256]{2,1,0:T(8,128)(2,1)}), f16[8,112,256]{2,1,0:T(8,128)(2,1)S(1)}, u32[]{:S(2)}, u32[]{:S(2)}) async-start(f16[8,112,256]{2,1,0:T(8,128)(2,1)} %multiply_convert_fusion), calls=%async_computation | async-start | bytes 917504 | tf_op jit(solution)/shard_map/all_to_all | solution.py:615
  18.7 0.0 copy-start.2
  18.7 0.0 copy-start.3
  18.7 5.8 %gates.1 = (bf16[8,2048,128]{2,1,0:T(8,128)(2,1)}, bf16[2048,1024]{1,0:T(8,128)(2,1)}) custom-call(bf16[2048,1024]{1,0:T(8,128)(2,1)} %get-tuple-element.44.pre_hbm), custom_call_target="tpu_custom_call" | custom-call | bytes 12582912 | tf_op jit(solution)/shard_map/gates/pallas_call | solution.py:162
  24.5 5.1 %all-to-all-done = f16[8,112,256]{2,1,0:T(8,128)(2,1)S(1)} async-done(((f16[8,112,256]{2,1,0:T(8,128)(2,1)}), f16[8,112,256]{2,1,0:T(8,128)(2,1)S(1)}, u32[]{:S(2)}, u32[]{:S(2)}) %all-to-all-start) | async-done | bytes 458784 | tf_op jit(solution)/shard_map/all_to_all | solution.py:615
  29.5 0.1 convert_multiply_fusion.blocks_ref
  29.6 0.0 copy-done.2
  29.6 0.0 copy-done.3
  29.6 1.9 %pairs.1 = bf16[8,112,256]{2,1,0:T(8,128)(2,1)} custom-call(s32[1]{0:T(128)} %bitcast.1.place_ref, f32[8,112,256]{2,1,0:T(8,128)S(1)} %convert_multiply_fusion.blocks_ref, f32[100,2048]{1,0:T(8,128)S(1)} %copy-done.2, f32[1,2048]{1,0:T(1,128)S(1)} %bitcast.28), custom_call_target="tpu_custom_call" | custom-call | flops 4194304 | bytes 2097152 | tf_op jit(solution)/shard_map/pairs/pallas_call | solution.py:223
  31.5 3.7 %all-to-all-start.1 = ((bf16[8,112,256]{2,1,0:T(8,128)(2,1)}), bf16[8,112,256]{2,1,0:T(8,128)(2,1)S(1)}, u32[]{:S(2)}, u32[]{:S(2)}) async-start(bf16[8,112,256]{2,1,0:T(8,128)(2,1)} %pairs.1), calls=%async_computation.1 | async-start | bytes 917504 | tf_op jit(solution)/shard_map/all_to_all | solution.py:620
  35.2 0.0 copy-start.1
  35.2 2.2 %copy-done.1 = bf16[1,2048,1024]{2,1,0:T(8,128)(2,1)S(1)} copy-done((bf16[1,2048,1024]{2,1,0:T(8,128)(2,1)S(1)}, bf16[1,2048,1024]{2,1,0:T(8,128)(2,1)}, u32[]{:S(2)}) %copy-start.1) | copy-done | bytes 4194328
  37.4 1.1 %turned.1.turned_hbm = bf16[1024,2048]{1,0:T(8,128)(2,1)S(1)} custom-call(s32[1]{0:T(128)} %bitcast.grid_ref, bf16[2048,1024]{1,0:T(8,128)(2,1)S(1)} %bitcast.27), custom_call_target="tpu_custom_call" | custom-call | bytes 8388608 | tf_op jit(solution)/shard_map/turned/pallas_call | solution.py:271
  38.6 0.0 copy-start
  38.6 2.0 %copy-done = bf16[1024,2048]{1,0:T(8,128)(2,1)} copy-done((bf16[1024,2048]{1,0:T(8,128)(2,1)}, bf16[1024,2048]{1,0:T(8,128)(2,1)S(1)}, u32[]{:S(2)}) %copy-start) | copy-done | bytes 4194328
  40.6 4.4 %all-to-all-done.1.low_ref = bf16[8,112,256]{2,1,0:T(8,128)(2,1)S(1)} async-done(((bf16[8,112,256]{2,1,0:T(8,128)(2,1)}), bf16[8,112,256]{2,1,0:T(8,128)(2,1)S(1)}, u32[]{:S(2)}, u32[]{:S(2)}) %all-to-all-start.1) | async-done | bytes 458784 | tf_op jit(solution)/shard_map/all_to_all | solution.py:620
  44.9 5.3 %send_a.1 = (bf16[2048,1024]{1,0:T(8,128)(2,1)S(1)}, bf16[256,1152]{1,0:T(8,128)(2,1)S(1)}, bf16[256,128]{1,0:T(8,128)(2,1)S(1)}, bf16[128,2048]{1,0:T(8,128)(2,1)S(1)}, bf16[256,2048]{1,0:T(8,128)(2,1)S(1)}) custom-call(s32[1]{0:T(128)} %bitcast.grid_ref, bf16[8,112,256]{2,1,0:T(8,128)(2,1)S(1)} %all-to-all-done.1.low_ref, bf16[1024,2048]{1,0:T(8,128)(2,1)} %copy-done, ...), custom_call_target="tpu_custom_call" | custom-call | flops 1879048192 | bytes 8388608 | tf_op jit(solution)/shard_map/send_a/pallas_call | solution.py:431
  50.3 0.1 collective-permute-start
  50.4 2.9 %keep_a.1 = (bf16[256,1152]{1,0:T(8,128)(2,1)S(1)}, bf16[256,2048]{1,0:T(8,128)(2,1)S(1)}, bf16[4,2048,128]{2,1,0:T(8,128)(2,1)S(1)}) custom-call(s32[1]{0:T(128)} %bitcast.grid_ref, bf16[1024,2048]{1,0:T(8,128)(2,1)} %copy-done, bf16[8,2048,128]{2,1,0:T(8,128)(2,1)} %get-tuple-element.49.hidden_hbm, bf16[2048,1024]{1,0:T(8,128)(2,1)S(1)} %get-tuple-element.73.pre_ref, ...), custom_call_target="tpu_custom_call" | custom-call | flops 1073741824 | bytes 4194304 | tf_op jit(solution)/shard_map/keep_a/pallas_call | solution.py:460
  53.3 0.0 collective-permute-done
  53.3 0.1 add_convert_fusion
  53.5 2.3 %send_b.1 = (bf16[256,1152]{1,0:T(8,128)(2,1)S(1)}, bf16[256,128]{1,0:T(8,128)(2,1)S(1)}, bf16[256,2048]{1,0:T(8,128)(2,1)S(1)}) custom-call(s32[1]{0:T(128)} %bitcast.grid_ref, bf16[1024,2048]{1,0:T(8,128)(2,1)} %copy-done, bf16[2048,1024]{1,0:T(8,128)(2,1)S(1)} %get-tuple-element.73.pre_ref, bf16[128,2048]{1,0:T(8,128)(2,1)S(1)} %get-tuple-element.60.flat_ref, ...), custom_call_target="tpu_custom_call" | custom-call | flops 1073741824 | bytes 4194304 | tf_op jit(solution)/shard_map/send_b/pallas_call | solution.py:474
  55.8 0.6 collective-permute-start.1
  56.4 4.1 %collective-permute-start.3 = (bf16[64,1152]{1,0:T(8,128)(2,1)S(1)}, bf16[64,1152]{1,0:T(8,128)(2,1)S(1)}, u32[]{:S(2)}, u32[]{:S(2)}) collective-permute-start(bf16[64,1152]{1,0:T(8,128)(2,1)S(1)} %get-tuple-element.89), channel_id=1, source_target_pairs={{0,6},{1,7},{2,0},{3,1},{4,2},{5,3},{6,4},{7,5},{8,14},{9,15},{10,... | collective-permute-start | bytes 442376 | tf_op jit(solution)/shard_map/ppermute | solution.py:569
  60.6 0.0 collective-permute-start.2
  60.6 1.6 %keep_b.1 = (bf16[256,1152]{1,0:T(8,128)(2,1)S(1)}, bf16[1024,1024]{1,0:T(8,128)(2,1)S(1)}) custom-call(bf16[1024,1024]{1,0:T(8,128)(2,1)} %weight_hbm.1, bf16[2048,1024]{1,0:T(8,128)(2,1)S(1)} %get-tuple-element.73.pre_ref, bf16[256,2048]{1,0:T(8,128)(2,1)S(1)} %get-tuple-element.63.turned_ref, bf16[256,128]{1,0:T(8,128)(2,1)S(1)} %get-tuple-element.64.second_ref), custom_call_target="tpu_custom_call" | custom-call | flops 1073741824 | bytes 4194304 | tf_op jit(solution)/shard_map/keep_b/pallas_call | solution.py:488
  62.2 3.4 %latent_gradient.2.refs_0_ = bf16[2048,1024]{1,0:T(8,128)(2,1)} custom-call(bf16[2048,1024]{1,0:T(8,128)(2,1)S(1)} %get-tuple-element.73.pre_ref, bf16[1024,1024]{1,0:T(8,128)(2,1)S(1)} %get-tuple-element.68.weight_ref), custom_call_target="tpu_custom_call" | custom-call | flops 2147483648 | bytes 5242880 | tf_op jit(solution)/shard_map/latent_gradient/pallas_call | solution.py:524
  65.6 0.0 collective-permute-done.3
  65.6 1.7 %collective-permute-done.2 = bf16[64,1152]{1,0:T(8,128)(2,1)S(1)} collective-permute-done((bf16[64,1152]{1,0:T(8,128)(2,1)S(1)}, bf16[64,1152]{1,0:T(8,128)(2,1)S(1)}, u32[]{:S(2)}, u32[]{:S(2)}) %collective-permute-start.2) | collective-permute-done | bytes 147488 | tf_op jit(solution)/shard_map/ppermute | solution.py:569
  67.3 0.0 collective-permute-done.1
  67.3 0.2 convert_add_fusion
  67.5 0.1 fusion.3
  67.5 0.1 pad_maximum_fusion
  67.6 0.1 collective-permute-start.4
  67.7 3.2 %collective-permute-start.5 = (bf16[2,64,1152]{2,1,0:T(8,128)(2,1)S(1)}, bf16[2,64,1152]{2,1,0:T(8,128)(2,1)S(1)}, u32[]{:S(2)}, u32[]{:S(2)}) collective-permute-start(bf16[2,64,1152]{2,1,0:T(8,128)(2,1)S(1)} %get-tuple-element.72), channel_id=1, source_target_pairs={{0,6},{1,7},{2,0},{3,1},{4,2},{5,3},{6,4},{7,5},{8,14},{9,15},{10,... | collective-permute-start | bytes 884744 | tf_op jit(solution)/shard_map/ppermute | solution.py:569
  70.9 3.4 %latent_gradient.3 = bf16[2048,1024]{1,0:T(8,128)(2,1)} custom-call(bf16[2048,1024]{1,0:T(8,128)(2,1)S(1)} %get-tuple-element.73.pre_ref, bf16[1024,1024]{1,0:T(8,128)(2,1)S(1)} %get-tuple-element.68.weight_ref, bf16[2048,1024]{1,0:T(8,128)(2,1)} %latent_gradient.2.refs_0_), custom_call_target="tpu_custom_call", output_to_operand_aliasing={{}: (2, {})} | custom-call | flops 2147483648 | bytes 5242880 | tf_op jit(solution)/shard_map/latent_gradient/pallas_call | solution.py:524
  74.3 2.4 %collective-permute-done.4 = bf16[2,64,1152]{2,1,0:T(8,128)(2,1)S(1)} collective-permute-done((bf16[2,64,1152]{2,1,0:T(8,128)(2,1)S(1)}, bf16[2,64,1152]{2,1,0:T(8,128)(2,1)S(1)}, u32[]{:S(2)}, u32[]{:S(2)}) %collective-permute-start.4) | collective-permute-done | bytes 294944 | tf_op jit(solution)/shard_map/ppermute | solution.py:569
  76.6 0.0 collective-permute-done.5
  76.6 0.1 add_convert_fusion.1
  76.8 0.9 collective-permute-start.8
  77.7 2.5 %collective-permute-start.7 = (bf16[64,1152]{1,0:T(8,128)(2,1)S(1)}, bf16[64,1152]{1,0:T(8,128)(2,1)S(1)}, u32[]{:S(2)}, u32[]{:S(2)}) collective-permute-start(bf16[64,1152]{1,0:T(8,128)(2,1)S(1)} %get-tuple-element.87), channel_id=1, source_target_pairs={{0,24},{1,25},{2,26},{3,27},{4,28},{5,29},{6,30},{7,31},{8,16},{9,... | collective-permute-start | bytes 442376 | tf_op jit(solution)/shard_map/ppermute | solution.py:569
  80.2 0.2 collective-permute-start.6
  80.4 3.4 %collective-permute-done.8 = bf16[64,1152]{1,0:T(8,128)(2,1)S(1)} collective-permute-done((bf16[64,1152]{1,0:T(8,128)(2,1)S(1)}, bf16[64,1152]{1,0:T(8,128)(2,1)S(1)}, u32[]{:S(2)}, u32[]{:S(2)}) %collective-permute-start.8) | collective-permute-done | bytes 147488 | tf_op jit(solution)/shard_map/ppermute | solution.py:569
  83.8 1.5 %collective-permute-done.7 = bf16[64,1152]{1,0:T(8,128)(2,1)S(1)} collective-permute-done((bf16[64,1152]{1,0:T(8,128)(2,1)S(1)}, bf16[64,1152]{1,0:T(8,128)(2,1)S(1)}, u32[]{:S(2)}, u32[]{:S(2)}) %collective-permute-start.7) | collective-permute-done | bytes 147488 | tf_op jit(solution)/shard_map/ppermute | solution.py:569
  85.2 0.1 collective-permute-done.6
  85.4 0.1 add_convert_fusion.2.own_ref
  85.4 0.9 collective-permute-start.11
  86.4 2.2 %collective-permute-start.10 = (bf16[64,1152]{1,0:T(8,128)(2,1)S(1)}, bf16[64,1152]{1,0:T(8,128)(2,1)S(1)}, u32[]{:S(2)}, u32[]{:S(2)}) collective-permute-start(bf16[64,1152]{1,0:T(8,128)(2,1)S(1)} %add_convert_fusion.2.own_ref), channel_id=1, source_target_pairs={{0,96},{1,97},{2,98},{3,99},{4,100},{5,101},{6,102},{7,103},{8,104... | collective-permute-start | bytes 442376 | tf_op jit(solution)/shard_map/ppermute | solution.py:569
  88.5 0.5 collective-permute-start.9
  89.0 3.3 %collective-permute-done.11.refs_2_ = bf16[64,1152]{1,0:T(8,128)(2,1)S(1)} collective-permute-done((bf16[64,1152]{1,0:T(8,128)(2,1)S(1)}, bf16[64,1152]{1,0:T(8,128)(2,1)S(1)}, u32[]{:S(2)}, u32[]{:S(2)}) %collective-permute-start.11) | collective-permute-done | bytes 147488 | tf_op jit(solution)/shard_map/ppermute | solution.py:569
  92.3 1.5 %collective-permute-done.10.refs_1_ = bf16[64,1152]{1,0:T(8,128)(2,1)S(1)} collective-permute-done((bf16[64,1152]{1,0:T(8,128)(2,1)S(1)}, bf16[64,1152]{1,0:T(8,128)(2,1)S(1)}, u32[]{:S(2)}, u32[]{:S(2)}) %collective-permute-start.10) | collective-permute-done | bytes 147488 | tf_op jit(solution)/shard_map/ppermute | solution.py:569
  93.8 0.0 collective-permute-done.9.refs_0_
  93.8 0.8 finish.1
  (4 shorter events, 0.1 us)
Async XLA Ops:
  11.6 17.9 %all-to-all-start = ((f16[8,112,256]{2,1,0:T(8,128)(2,1)}), f16[8,112,256]{2,1,0:T(8,128)(2,1)S(1)}, u32[]{:S(2)}, u32[]{:S(2)}) async-start(f16[8,112,256]{2,1,0:T(8,128)(2,1)} %multiply_convert_fusion), calls=%async_computation | async-start | bytes 917504 | tf_op jit(solution)/shard_map/all_to_all | solution.py:615
  18.7 11.0 %copy-start.2 = (f32[100,2048]{1,0:T(8,128)S(1)}, f32[100,2048]{1,0:T(8,128)}, u32[]{:S(2)}) copy-start(f32[100,2048]{1,0:T(8,128)} %observed_ref.1) | copy-start | bytes 2457604
  18.7 11.0 %copy-start.3 = (f32[2048]{0:T(1024)S(1)}, f32[2048]{0:T(1024)}, u32[]{:S(2)}) copy-start(f32[2048]{0:T(1024)} %param.9) | copy-start | bytes 24580
  31.5 13.4 %all-to-all-start.1 = ((bf16[8,112,256]{2,1,0:T(8,128)(2,1)}), bf16[8,112,256]{2,1,0:T(8,128)(2,1)S(1)}, u32[]{:S(2)}, u32[]{:S(2)}) async-start(bf16[8,112,256]{2,1,0:T(8,128)(2,1)} %pairs.1), calls=%async_computation.1 | async-start | bytes 917504 | tf_op jit(solution)/shard_map/all_to_all | solution.py:620
  35.2 2.2 %copy-start.1 = (bf16[1,2048,1024]{2,1,0:T(8,128)(2,1)S(1)}, bf16[1,2048,1024]{2,1,0:T(8,128)(2,1)}, u32[]{:S(2)}) copy-start(bf16[1,2048,1024]{2,1,0:T(8,128)(2,1)} %param.5) | copy-start | bytes 12582916
  38.6 2.0 %copy-start = (bf16[1024,2048]{1,0:T(8,128)(2,1)}, bf16[1024,2048]{1,0:T(8,128)(2,1)S(1)}, u32[]{:S(2)}) copy-start(bf16[1024,2048]{1,0:T(8,128)(2,1)S(1)} %turned.1.turned_hbm) | copy-start | bytes 12582916
  50.3 3.0 %collective-permute-start = (bf16[256,1152]{1,0:T(8,128)(2,1)S(1)}, bf16[256,1152]{1,0:T(8,128)(2,1)S(1)}, u32[]{:S(2)}, u32[]{:S(2)}) collective-permute-start(bf16[256,1152]{1,0:T(8,128)(2,1)S(1)} %get-tuple-element.57), channel_id=1, source_target_pairs={{0,1},{1,0},{2,3},{3,2},{4,5},{5,4},{6,7},{7,6},{8,9},{9,8},{10,11... | collective-permute-start | bytes 1769480 | tf_op jit(solution)/shard_map/ppermute | solution.py:569
  55.8 11.4 %collective-permute-start.1 = (bf16[256,1152]{1,0:T(8,128)(2,1)S(1)}, bf16[256,1152]{1,0:T(8,128)(2,1)S(1)}, u32[]{:S(2)}, u32[]{:S(2)}) collective-permute-start(bf16[256,1152]{1,0:T(8,128)(2,1)S(1)} %get-tuple-element.66), channel_id=1, source_target_pairs={{0,1},{1,0},{2,3},{3,2},{4,5},{5,4},{6,7},{7,6},{8,9},{9,8},{10,11... | collective-permute-start | bytes 1769480 | tf_op jit(solution)/shard_map/ppermute | solution.py:569
  56.4 9.1 %collective-permute-start.3 = (bf16[64,1152]{1,0:T(8,128)(2,1)S(1)}, bf16[64,1152]{1,0:T(8,128)(2,1)S(1)}, u32[]{:S(2)}, u32[]{:S(2)}) collective-permute-start(bf16[64,1152]{1,0:T(8,128)(2,1)S(1)} %get-tuple-element.89), channel_id=1, source_target_pairs={{0,6},{1,7},{2,0},{3,1},{4,2},{5,3},{6,4},{7,5},{8,14},{9,15},{10,... | collective-permute-start | bytes 442376 | tf_op jit(solution)/shard_map/ppermute | solution.py:569
  60.6 6.7 %collective-permute-start.2 = (bf16[64,1152]{1,0:T(8,128)(2,1)S(1)}, bf16[64,1152]{1,0:T(8,128)(2,1)S(1)}, u32[]{:S(2)}, u32[]{:S(2)}) collective-permute-start(bf16[64,1152]{1,0:T(8,128)(2,1)S(1)} %get-tuple-element.90), channel_id=1, source_target_pairs={{0,2},{1,3},{2,4},{3,5},{4,6},{5,7},{6,0},{7,1},{8,10},{9,11},{10,... | collective-permute-start | bytes 442376 | tf_op jit(solution)/shard_map/ppermute | solution.py:569
  67.6 9.0 %collective-permute-start.4 = (bf16[2,64,1152]{2,1,0:T(8,128)(2,1)S(1)}, bf16[2,64,1152]{2,1,0:T(8,128)(2,1)S(1)}, u32[]{:S(2)}, u32[]{:S(2)}) collective-permute-start(bf16[2,64,1152]{2,1,0:T(8,128)(2,1)S(1)} %get-tuple-element.71), channel_id=1, source_target_pairs={{0,2},{1,3},{2,4},{3,5},{4,6},{5,7},{6,0},{7,1},{8,10},{9,11},{10,... | collective-permute-start | bytes 884744 | tf_op jit(solution)/shard_map/ppermute | solution.py:569
  67.7 9.0 %collective-permute-start.5 = (bf16[2,64,1152]{2,1,0:T(8,128)(2,1)S(1)}, bf16[2,64,1152]{2,1,0:T(8,128)(2,1)S(1)}, u32[]{:S(2)}, u32[]{:S(2)}) collective-permute-start(bf16[2,64,1152]{2,1,0:T(8,128)(2,1)S(1)} %get-tuple-element.72), channel_id=1, source_target_pairs={{0,6},{1,7},{2,0},{3,1},{4,2},{5,3},{6,4},{7,5},{8,14},{9,15},{10,... | collective-permute-start | bytes 884744 | tf_op jit(solution)/shard_map/ppermute | solution.py:569
  76.8 7.0 %collective-permute-start.8 = (bf16[64,1152]{1,0:T(8,128)(2,1)S(1)}, bf16[64,1152]{1,0:T(8,128)(2,1)S(1)}, u32[]{:S(2)}, u32[]{:S(2)}) collective-permute-start(bf16[64,1152]{1,0:T(8,128)(2,1)S(1)} %get-tuple-element.88), channel_id=1, source_target_pairs={{0,16},{1,17},{2,18},{3,19},{4,20},{5,21},{6,22},{7,23},{8,24},{9,... | collective-permute-start | bytes 442376 | tf_op jit(solution)/shard_map/ppermute | solution.py:569
  77.7 7.5 %collective-permute-start.7 = (bf16[64,1152]{1,0:T(8,128)(2,1)S(1)}, bf16[64,1152]{1,0:T(8,128)(2,1)S(1)}, u32[]{:S(2)}, u32[]{:S(2)}) collective-permute-start(bf16[64,1152]{1,0:T(8,128)(2,1)S(1)} %get-tuple-element.87), channel_id=1, source_target_pairs={{0,24},{1,25},{2,26},{3,27},{4,28},{5,29},{6,30},{7,31},{8,16},{9,... | collective-permute-start | bytes 442376 | tf_op jit(solution)/shard_map/ppermute | solution.py:569
  80.2 5.1 %collective-permute-start.6 = (bf16[64,1152]{1,0:T(8,128)(2,1)S(1)}, bf16[64,1152]{1,0:T(8,128)(2,1)S(1)}, u32[]{:S(2)}, u32[]{:S(2)}) collective-permute-start(bf16[64,1152]{1,0:T(8,128)(2,1)S(1)} %get-tuple-element.87), channel_id=1, source_target_pairs={{0,8},{1,9},{2,10},{3,11},{4,12},{5,13},{6,14},{7,15},{8,0},{9,1},... | collective-permute-start | bytes 442376 | tf_op jit(solution)/shard_map/ppermute | solution.py:569
  85.4 6.9 %collective-permute-start.11 = (bf16[64,1152]{1,0:T(8,128)(2,1)S(1)}, bf16[64,1152]{1,0:T(8,128)(2,1)S(1)}, u32[]{:S(2)}, u32[]{:S(2)}) collective-permute-start(bf16[64,1152]{1,0:T(8,128)(2,1)S(1)} %add_convert_fusion.2.own_ref), channel_id=1, source_target_pairs={{0,64},{1,65},{2,66},{3,67},{4,68},{5,69},{6,70},{7,71},{8,72},{9,... | collective-permute-start | bytes 442376 | tf_op jit(solution)/shard_map/ppermute | solution.py:569
  86.4 7.4 %collective-permute-start.10 = (bf16[64,1152]{1,0:T(8,128)(2,1)S(1)}, bf16[64,1152]{1,0:T(8,128)(2,1)S(1)}, u32[]{:S(2)}, u32[]{:S(2)}) collective-permute-start(bf16[64,1152]{1,0:T(8,128)(2,1)S(1)} %add_convert_fusion.2.own_ref), channel_id=1, source_target_pairs={{0,96},{1,97},{2,98},{3,99},{4,100},{5,101},{6,102},{7,103},{8,104... | collective-permute-start | bytes 442376 | tf_op jit(solution)/shard_map/ppermute | solution.py:569
  88.5 5.3 %collective-permute-start.9 = (bf16[64,1152]{1,0:T(8,128)(2,1)S(1)}, bf16[64,1152]{1,0:T(8,128)(2,1)S(1)}, u32[]{:S(2)}, u32[]{:S(2)}) collective-permute-start(bf16[64,1152]{1,0:T(8,128)(2,1)S(1)} %add_convert_fusion.2.own_ref), channel_id=1, source_target_pairs={{0,32},{1,33},{2,34},{3,35},{4,36},{5,37},{6,38},{7,39},{8,40},{9,... | collective-permute-start | bytes 442376 | tf_op jit(solution)/shard_map/ppermute | solution.py:569

commit v11 on v9

--- a/solution.py
+++ b/solution.py
@@ -242,11 +242,13 @@
     return grid >> 3, (grid >> 1) & 3, grid & 1
 
 
-STEPS = ((2, 0), (1, 3))
-
-
-def owner(block, steps, x_lo, z):
-    return ((block & 1) ^ x_lo) * 4 + ((z + steps[block >> 1]) & 3)
+FAR = 256
+NEAR = 384
+NEAR_STEPS = (1, 3, 0)
+
+
+def owner(step, other_x, x_lo, z):
+    return (other_x ^ x_lo) * 4 + ((z + step) & 3)
 
 
 def turn_kernel(grid_ref, latent_ref, turned_ref):
@@ -254,11 +256,14 @@
     x_lo, z, core = position(grid_ref)
     for group in range(8):
         step = (group - z) & 3
+        other_x = (group >> 2) ^ x_lo
         odd = step & 1
-        place = odd * (2 + (step >> 1)) + (1 - odd) * (1 - (step >> 1))
-        at = (place >> 1) * 512 + (place & 1) * 128 + ((group >> 2) ^ x_lo) * 64
-        first = pl.multiple_of(at + (1 - core) * 256, 64)
-        second = pl.multiple_of(at + core * 256, 64)
+        far = (step >> 1) * (1 - odd)
+        near = FAR + (odd * (step >> 1) + (1 - odd) * 2) * 128 + other_x * 64
+        first = far * (other_x * 128 + (1 - core) * 64) + (1 - far) * (near + (1 - core) * NEAR)
+        second = far * (other_x * 128 + core * 64) + (1 - far) * (near + core * NEAR)
+        first = pl.multiple_of(first, 64)
+        second = pl.multiple_of(second, 64)
         for row in range(0, nodes, ROWS):
             columns = slice(row, row + ROWS)
             block = latent_ref[columns, group * 128 : (group + 1) * 128].T
@@ -279,22 +284,6 @@
     )(grid, latent)
 
 
-def turned_load(turned_hbm, start, turned_ref, sem):
-    return pltpu.make_async_copy(turned_hbm.at[pl.ds(start, 256)], turned_ref, sem)
-
-
-def hidden_loads(part, grid_ref, hidden_hbm, hidden_ref, sems):
-    x_lo, z, core = position(grid_ref)
-    return [
-        pltpu.make_async_copy(
-            hidden_hbm.at[owner(block, STEPS[part], x_lo, z)],
-            hidden_ref.at[block],
-            sems.at[block],
-        )
-        for block in range(4)
-    ]
-
-
 def first_product(turned_ref, pre_ref, out_ref):
     width = pre_ref.shape[1]
     for column in range(0, width, 512):
@@ -303,22 +292,14 @@
         out_ref[:, columns] = part.astype(bf16)
 
 
-def second_product(grid_ref, flat_ref, hidden_ref, send_ref, second_ref, scratch_ref):
-    width = send_ref.shape[1] - WIDE
-    core = position(grid_ref)[2]
-    for block in (0, 2):
+def second_product(flat_ref, hidden_ref, scratch_ref):
+    for block in range(0, hidden_ref.shape[0], 2):
         columns = jnp.concatenate([hidden_ref[block], hidden_ref[block + 1]], axis=1)
         second = jnp.dot(flat_ref[...], columns, preferred_element_type=f32)
         scratch_ref[block * 128 : (block + 2) * 128, :] = second.T.astype(bf16)
-    for block in range(4):
-        rows = slice(block * 64, (block + 1) * 64)
-        mine = pl.multiple_of(block * 128 + core * 64, 64)
-        other = pl.multiple_of(block * 128 + (1 - core) * 64, 64)
-        second_ref[rows, :] = scratch_ref[pl.ds(mine, 64), :]
-        send_ref[rows, width:] = scratch_ref[pl.ds(other, 64), :]
-
-
-def send_a_kernel(
+
+
+def far_kernel(
     grid_ref,
     low_ref,
     turned_hbm,
@@ -326,30 +307,30 @@
     hidden_hbm,
     padded_ref,
     pre_ref,
-    send_ref,
-    second_ref,
+    up_ref,
+    down_ref,
     flat_ref,
-    next_turned_ref,
     turn_ref,
     turned_ref,
     hidden_ref,
     scratch_ref,
     slope_ref,
-    turned_sems,
+    turned_sem,
     hidden_sems,
     slope_sems,
 ):
     nodes, width = pre_ref.shape
+    x_lo, z, core = position(grid_ref)
     slope_loads = [
-        pltpu.make_async_copy(
-            slope_hbm.at[pl.ds(start, ROWS)], slope_ref.at[pl.ds(start, ROWS)], slope_sems.at[start // ROWS]
-        )
+        pltpu.make_async_copy(chunk(slope_hbm, start), chunk(slope_ref, start), slope_sems.at[start // ROWS])
         for start in range(0, nodes, ROWS)
     ]
-    turned_now = turned_load(turned_hbm, 0, turned_ref, turned_sems.at[0])
-    turned_next = turned_load(turned_hbm, 256, next_turned_ref, turned_sems.at[1])
-    hidden_now = hidden_loads(0, grid_ref, hidden_hbm, hidden_ref, hidden_sems)
-    for load in slope_loads + [turned_now] + hidden_now + [turned_next]:
+    turned_load = pltpu.make_async_copy(turned_hbm.at[pl.ds(0, FAR)], turned_ref, turned_sem)
+    hidden_loads = [
+        pltpu.make_async_copy(hidden_hbm.at[owner(2, other_x, x_lo, z)], hidden_ref.at[other_x], hidden_sems.at[other_x])
+        for other_x in (0, 1)
+    ]
+    for load in slope_loads + [turned_load] + hidden_loads:
         load.start()
     for share in range(low_ref.shape[0]):
         columns = slice(share * SHARE, (share + 1) * SHARE)
@@ -363,138 +344,120 @@
             columns = slice(column, column + COLS)
             grad_hidden = lax.dot_general(turn_ref[rows, :], padded_ref[columns, :], NT, preferred_element_type=f32)
             pre_ref[rows, columns] = (grad_hidden * slope_ref[rows, columns].astype(f32)).astype(bf16)
-    turned_now.wait()
-    first_product(turned_ref, pre_ref, send_ref)
-    for load in hidden_now:
+    turned_load.wait()
+    for column in range(0, width, 512):
+        columns = slice(column, column + 512)
+        part = jnp.dot(turned_ref[...], pre_ref[:, columns], preferred_element_type=f32).astype(bf16)
+        up_ref[:, columns] = part[:128]
+        down_ref[:, columns] = part[128:]
+    for load in hidden_loads:
         load.wait()
-    second_product(grid_ref, flat_ref, hidden_ref, send_ref, second_ref, scratch_ref)
-    turned_next.wait()
-
-
-def keep_a_kernel(
+    second_product(flat_ref, hidden_ref, scratch_ref)
+    for block, out_ref in enumerate((up_ref, down_ref)):
+        mine = pl.multiple_of(block * 128 + core * 64, 64)
+        other = pl.multiple_of(block * 128 + (1 - core) * 64, 64)
+        out_ref[:64, width:] = scratch_ref[pl.ds(other, 64), :]
+        out_ref[64:, width:] = scratch_ref[pl.ds(mine, 64), :]
+
+
+def near_kernel(
     grid_ref,
     turned_hbm,
     hidden_hbm,
-    pre_ref,
-    turned_ref,
-    second_ref,
-    keep_ref,
-    next_turned_ref,
-    next_hidden_ref,
-    turned_sem,
-    hidden_sems,
-):
-    loads = [turned_load(turned_hbm, 512, next_turned_ref, turned_sem)]
-    loads += hidden_loads(1, grid_ref, hidden_hbm, next_hidden_ref, hidden_sems)
-    for load in loads:
-        load.start()
-    first_product(turned_ref, pre_ref, keep_ref)
-    keep_ref[:, pre_ref.shape[1] :] = second_ref[...]
-    for load in loads:
-        load.wait()
-
-
-def send_b_kernel(
-    grid_ref,
-    turned_hbm,
+    weight_hbm,
     pre_ref,
     flat_ref,
+    send_ref,
+    keep_ref,
+    weight_ref,
     turned_ref,
     hidden_ref,
-    send_ref,
-    second_ref,
-    next_turned_ref,
     scratch_ref,
-    turned_sem,
+    turned_sems,
+    hidden_sems,
+    weight_sem,
 ):
-    load = turned_load(turned_hbm, 768, next_turned_ref, turned_sem)
-    load.start()
-    first_product(turned_ref, pre_ref, send_ref)
-    second_product(grid_ref, flat_ref, hidden_ref, send_ref, second_ref, scratch_ref)
-    load.wait()
-
-
-def keep_b_kernel(weight_hbm, pre_ref, turned_ref, second_ref, keep_ref, weight_ref, weight_sem):
-    load = pltpu.make_async_copy(weight_hbm, weight_ref, weight_sem)
-    load.start()
-    first_product(turned_ref, pre_ref, keep_ref)
-    keep_ref[:, pre_ref.shape[1] :] = second_ref[...]
-    load.wait()
+    width = pre_ref.shape[1]
+    x_lo, z, core = position(grid_ref)
+    turned_loads = [
+        pltpu.make_async_copy(turned_hbm.at[pl.ds(FAR + part * NEAR, NEAR)], turned_ref.at[part], turned_sems.at[part])
+        for part in (0, 1)
+    ]
+    hidden_loads = [
+        pltpu.make_async_copy(
+            hidden_hbm.at[owner(NEAR_STEPS[block // 2], block % 2, x_lo, z)], hidden_ref.at[block], hidden_sems.at[block]
+        )
+        for block in range(6)
+    ]
+    weight_load = pltpu.make_async_copy(weight_hbm, weight_ref, weight_sem)
+    for load in turned_loads + hidden_loads + [weight_load]:
+        load.start()
+    for part, out_ref in enumerate((send_ref, keep_ref)):
+        turned_loads[part].wait()
+        first_product(turned_ref.at[part], pre_ref, out_ref)
+    for load in hidden_loads:
+        load.wait()
+    second_product(flat_ref, hidden_ref, scratch_ref)
+    for block in range(6):
+        rows = slice(block * 64, (block + 1) * 64)
+        mine = pl.multiple_of(block * 128 + core * 64, 64)
+        other = pl.multiple_of(block * 128 + (1 - core) * 64, 64)
+        keep_ref[rows, width:] = scratch_ref[pl.ds(mine, 64), :]
+        send_ref[rows, width:] = scratch_ref[pl.ds(other, 64), :]
+    weight_load.wait()
 
 
 def shape(*dims):
     return jax.ShapeDtypeStruct(dims, bf16)
 
 
-def send_a(grid, low, turned_latent, slope, hidden, padded):
+def backward_far(grid, low, turned_latent, slope, hidden, padded):
     nodes, width = slope.shape
     return pl.pallas_call(
-        send_a_kernel,
+        far_kernel,
         in_specs=[smem, vmem, anywhere, anywhere, anywhere, vmem],
-        out_specs=[vmem] * 5,
+        out_specs=[vmem] * 4,
         out_shape=[
             shape(nodes, width),
-            shape(256, width + WIDE),
-            shape(256, WIDE),
+            shape(128, width + WIDE),
+            shape(128, width + WIDE),
             shape(WIDE, nodes),
-            shape(256, nodes),
         ],
         scratch_shapes=[
             pltpu.VMEM((nodes, WIDE), bf16),
-            pltpu.VMEM((256, nodes), bf16),
-            pltpu.VMEM((4, nodes, 128), bf16),
-            pltpu.VMEM((512, WIDE), bf16),
+            pltpu.VMEM((FAR, nodes), bf16),
+            pltpu.VMEM((2, nodes, 128), bf16),
+            pltpu.VMEM((256, WIDE), bf16),
             pltpu.VMEM((nodes, width), bf16),
+            pltpu.SemaphoreType.DMA,
             pltpu.SemaphoreType.DMA((2,)),
-            pltpu.SemaphoreType.DMA((4,)),
             pltpu.SemaphoreType.DMA((nodes // ROWS,)),
         ],
         compiler_params=params(20),
         cost_estimate=cost(nodes * width * (width // 2 + 3 * WIDE), 8 << 20),
-        name="send_a",
+        name="backward_far",
     )(grid, low, pinned(turned_latent), pinned(slope), pinned(hidden), padded)
 
 
-def keep_a(grid, turned_latent, hidden, grad_pre, turned_now, second):
+def backward_near(grid, turned_latent, hidden, weight, grad_pre, flat):
     nodes, width = grad_pre.shape
     return pl.pallas_call(
-        keep_a_kernel,
-        in_specs=[smem, anywhere, anywhere] + [vmem] * 3,
+        near_kernel,
+        in_specs=[smem, anywhere, anywhere, anywhere, vmem, vmem],
         out_specs=[vmem] * 3,
-        out_shape=[shape(256, width + WIDE), shape(256, nodes), shape(4, nodes, 128)],
-        scratch_shapes=[pltpu.SemaphoreType.DMA, pltpu.SemaphoreType.DMA((4,))],
-        compiler_params=params(12),
-        cost_estimate=cost(nodes * width * width // 2, 4 << 20),
-        name="keep_a",
-    )(grid, pinned(turned_latent), pinned(hidden), grad_pre, turned_now, second)
-
-
-def send_b(grid, turned_latent, grad_pre, flat, turned_now, hidden_now):
-    nodes, width = grad_pre.shape
-    return pl.pallas_call(
-        send_b_kernel,
-        in_specs=[smem, anywhere] + [vmem] * 4,
-        out_specs=[vmem] * 3,
-        out_shape=[shape(256, width + WIDE), shape(256, WIDE), shape(256, nodes)],
-        scratch_shapes=[pltpu.VMEM((512, WIDE), bf16), pltpu.SemaphoreType.DMA],
-        compiler_params=params(12),
-        cost_estimate=cost(nodes * width * width // 2, 4 << 20),
-        name="send_b",
-    )(grid, pinned(turned_latent), grad_pre, flat, turned_now, hidden_now)
-
-
-def keep_b(weight, grad_pre, turned_now, second):
-    nodes, width = grad_pre.shape
-    return pl.pallas_call(
-        keep_b_kernel,
-        in_specs=[anywhere] + [vmem] * 3,
-        out_specs=[vmem] * 2,
-        out_shape=[shape(256, width + WIDE), shape(width, width)],
-        scratch_shapes=[pltpu.SemaphoreType.DMA],
-        compiler_params=params(12),
-        cost_estimate=cost(nodes * width * width // 2, 4 << 20),
-        name="keep_b",
-    )(pinned(weight), grad_pre, turned_now, second)
+        out_shape=[shape(NEAR, width + WIDE), shape(NEAR, width + WIDE), shape(width, width)],
+        scratch_shapes=[
+            pltpu.VMEM((2, NEAR, nodes), bf16),
+            pltpu.VMEM((6, nodes, 128), bf16),
+            pltpu.VMEM((768, WIDE), bf16),
+            pltpu.SemaphoreType.DMA((2,)),
+            pltpu.SemaphoreType.DMA((6,)),
+            pltpu.SemaphoreType.DMA,
+        ],
+        compiler_params=params(20),
+        cost_estimate=cost(nodes * width * (3 * width // 2 + 2 * WIDE), 8 << 20),
+        name="backward_near",
+    )(grid, pinned(turned_latent), pinned(hidden), pinned(weight), grad_pre, flat)
 
 
 def latent_kernel(pre_ref, weight_ref, out_ref, result_ref, sems):
@@ -572,11 +535,6 @@
     return total
 
 
-def over_core(send, keep):
-    got = moved(send, lambda y, x, z, c: (y, x, z, 1 - c))
-    return summed(keep, [got]).reshape(2, 2, 64, send.shape[1])
-
-
 def up(value):
     return moved(value, lambda y, x, z, c: (y, x, (z + 1) % 4, c))
 
@@ -615,16 +573,18 @@
     low, late_grid = lax.optimization_barrier((low, grid))
     low = lax.all_to_all(low, "member", 0, 0, tiled=True)
     turned_latent = turned(late_grid, latent)
-    grad_pre, rows_a, second_a, flat, turned_now = send_a(grid, low, turned_latent, slope, hidden, padded)
-    kept_a, turned_now, hidden_now = keep_a(grid, turned_latent, hidden, grad_pre, turned_now, second_a)
-    far, own = over_core(rows_a, kept_a).astype(bf16)
-    far, own, flat = lax.optimization_barrier((far, own, flat))
-    upward, downward = up(far[0]), down(far[1])
-    rows_b, second_b, turned_now = send_b(grid, turned_latent, grad_pre, flat, turned_now, hidden_now)
-    kept_b, weight_copy = keep_b(hidden_weight, grad_pre, turned_now, second_b)
-    above, below = over_core(rows_b, kept_b)
-    above = jnp.stack([above[0] + upward.astype(f32), above[1]]).astype(bf16)
-    below = jnp.stack([below[0], below[1] + downward.astype(f32)]).astype(bf16)
+    grad_pre, upward, downward, flat = backward_far(grid, low, turned_latent, slope, hidden, padded)
+    upward, downward = up(upward).astype(f32), down(downward).astype(f32)
+    send, keep, weight_copy = backward_near(grid, turned_latent, hidden, hidden_weight, grad_pre, flat)
+
+    def joined(rows, at):
+        rows = rows.astype(f32).reshape(3, 2, 64, rows.shape[1])
+        above = jnp.stack([rows[0, 0] + upward[at : at + 64], rows[0, 1]])
+        below = jnp.stack([rows[1, 0], rows[1, 1] + downward[at : at + 64]])
+        return jnp.stack([above, below, rows[2]])
+
+    got = moved(joined(send, 0).astype(bf16), lambda y, x, z, c: (y, x, z, 1 - c))
+    above, below, own = (joined(keep, 64) + got.astype(f32)).astype(bf16)
     above, below, grad_pre = lax.optimization_barrier((above, below, grad_pre))
     grad_latent = latent_gradient(grad_pre, weight_copy)
     blocks = summed(own, [up(above), down(below)]).astype(bf16)

time: 94.8 us -> 102 us (1.076)
  waiting for transfers between devices: 24.3 us -> 30.9 us
    ppermute x12 -> x11, waiting for transfers between devices: 14.9 us -> 21.5 us  [moved(): return lax.ppermute(value, ('member', 'grid'), moves)]
    pallas_call x4 -> x2, Pallas kernels: 12.2 us -> 11.7 us  [the longest x1 6.78 us: backward_near(): pl.pallas_call(near_kernel, in_specs=[smem, anywhere, anywhere, anywhere,...]
    ppermute x12 -> x11, starting transfers between devices: 15.2 us -> 15 us  [moved(): return lax.ppermute(value, ('member', 'grid'), moves)]
  transfers between devices with their start and end apart: 14 -> 13, of which waited for: 9 -> 9; matrix products, arithmetic and copies ran while one was open for 0% -> 0% of each run, Pallas kernels for 18% -> 12%
where the time goes in v11:
time: 102 us; the launch traced here: 101 us
  Pallas kernels  36.9 us (36%)
  waiting for transfers between devices  30.9 us (30%)
  starting transfers between devices  25.7 us (25%)
  local copies, waits for them, and re-layouts  4.4 us (4%)
  other arithmetic  2.18 us (2%)
    ppermute x11, waiting for transfers between devices, moved(): return lax.ppermute(value, ('member', 'grid'), moves)  21.5 us
    ppermute x11, starting transfers between devices, moved(): return lax.ppermute(value, ('member', 'grid'), moves)  15 us
    pallas_call x1, Pallas kernels, forward(): pl.pallas_call(forward_kernel, in_specs=[anywhere] * 3, out_specs=[vmem,...  10.1 us
    all_to_all x1, starting transfers between devices, body(): blocks = lax.all_to_all(blocks, 'member', 0, 0, tiled=True)  7.02 us
    pallas_call x1, Pallas kernels, backward_near(): pl.pallas_call(near_kernel, in_specs=[smem, anywhere, anywhere, anywhere,...  6.78 us
    pallas_call x1, Pallas kernels, gates(): pl.pallas_call(gate_kernel, in_specs=[anywhere], out_specs=[anywhere] * 2...  5.78 us
    pallas_call x1, Pallas kernels, latent_gradient(): pl.pallas_call(latent_kernel, in_specs=[vmem, vmem], out_specs=anywhere,...  5.55 us
    all_to_all x1, waiting for transfers between devices, body(): blocks = lax.all_to_all(blocks, 'member', 0, 0, tiled=True)  5.07 us
  transfers between devices with their start and end apart: 13, of which 9 were waited for; matrix products, arithmetic and copies ran while one was open for 0% of the time, Pallas kernels for 12%

profile of v11, /device:TPU:0, one launch (start us, length us, event | category | flops | bytes accessed | tf_op | source)
XLA Modules:
  0.0 101.0 jit_solution(15535222368137985920)
XLA Ops:
  0.6 10.1 %forward.1 = (f32[8,112,256]{2,1,0:T(8,128)S(1)}, bf16[2048,1024]{1,0:T(8,128)(2,1)}, bf16[1024,128]{1,0:T(8,128)(2,1)S(1)}) custom-call(bf16[2048,1024]{1,0:T(8,128)(2,1)} %bitcast.69, bf16[1024,1024]{1,0:T(8,128)(2,1)} %weight_hbm.1, bf16[100,1024]{1,0:T(8,128)(2,1)} %bitcast.78), custom_call_target="tpu_custom_call" | custom-call | flops 4831838208 | bytes 20971520 | tf_op jit(solution)/shard_map/forward/pallas_call | solution.py:102
  10.7 0.9 multiply_convert_fusion
  11.6 7.0 %all-to-all-start = ((f16[8,112,256]{2,1,0:T(8,128)(2,1)}), f16[8,112,256]{2,1,0:T(8,128)(2,1)S(1)}, u32[]{:S(2)}, u32[]{:S(2)}) async-start(f16[8,112,256]{2,1,0:T(8,128)(2,1)} %multiply_convert_fusion), calls=%async_computation | async-start | bytes 917504 | tf_op jit(solution)/shard_map/all_to_all | solution.py:569
  18.7 0.0 copy-start.2
  18.7 0.0 copy-start.3
  18.7 5.8 %gates.1 = (bf16[8,2048,128]{2,1,0:T(8,128)(2,1)}, bf16[2048,1024]{1,0:T(8,128)(2,1)}) custom-call(bf16[2048,1024]{1,0:T(8,128)(2,1)} %get-tuple-element.32.pre_hbm), custom_call_target="tpu_custom_call" | custom-call | bytes 12582912 | tf_op jit(solution)/shard_map/gates/pallas_call | solution.py:162
  24.5 5.1 %all-to-all-done = f16[8,112,256]{2,1,0:T(8,128)(2,1)S(1)} async-done(((f16[8,112,256]{2,1,0:T(8,128)(2,1)}), f16[8,112,256]{2,1,0:T(8,128)(2,1)S(1)}, u32[]{:S(2)}, u32[]{:S(2)}) %all-to-all-start) | async-done | bytes 458784 | tf_op jit(solution)/shard_map/all_to_all | solution.py:569
  29.5 0.1 convert_multiply_fusion.blocks_ref
  29.6 0.0 copy-done.2
  29.6 0.0 copy-done.3
  29.6 1.9 %pairs.1 = bf16[8,112,256]{2,1,0:T(8,128)(2,1)} custom-call(s32[1]{0:T(128)} %bitcast.1.place_ref, f32[8,112,256]{2,1,0:T(8,128)S(1)} %convert_multiply_fusion.blocks_ref, f32[100,2048]{1,0:T(8,128)S(1)} %copy-done.2, f32[1,2048]{1,0:T(1,128)S(1)} %bitcast.73), custom_call_target="tpu_custom_call" | custom-call | flops 4194304 | bytes 2097152 | tf_op jit(solution)/shard_map/pairs/pallas_call | solution.py:223
  31.5 3.7 %all-to-all-start.1 = ((bf16[8,112,256]{2,1,0:T(8,128)(2,1)}), bf16[8,112,256]{2,1,0:T(8,128)(2,1)S(1)}, u32[]{:S(2)}, u32[]{:S(2)}) async-start(bf16[8,112,256]{2,1,0:T(8,128)(2,1)} %pairs.1), calls=%async_computation.1 | async-start | bytes 917504 | tf_op jit(solution)/shard_map/all_to_all | solution.py:574
  35.2 0.0 copy-start.1
  35.2 2.2 %copy-done.1 = bf16[1,2048,1024]{2,1,0:T(8,128)(2,1)S(1)} copy-done((bf16[1,2048,1024]{2,1,0:T(8,128)(2,1)S(1)}, bf16[1,2048,1024]{2,1,0:T(8,128)(2,1)}, u32[]{:S(2)}) %copy-start.1) | copy-done | bytes 4194328
  37.4 1.1 %turned.1.turned_hbm = bf16[1024,2048]{1,0:T(8,128)(2,1)S(1)} custom-call(s32[1]{0:T(128)} %bitcast.grid_ref, bf16[2048,1024]{1,0:T(8,128)(2,1)S(1)} %bitcast.70), custom_call_target="tpu_custom_call" | custom-call | bytes 8388608 | tf_op jit(solution)/shard_map/turned/pallas_call | solution.py:276
  38.6 0.0 copy-start
  38.6 2.0 %copy-done = bf16[1024,2048]{1,0:T(8,128)(2,1)} copy-done((bf16[1024,2048]{1,0:T(8,128)(2,1)}, bf16[1024,2048]{1,0:T(8,128)(2,1)S(1)}, u32[]{:S(2)}) %copy-start) | copy-done | bytes 4194328
  40.6 4.4 %all-to-all-done.1.low_ref = bf16[8,112,256]{2,1,0:T(8,128)(2,1)S(1)} async-done(((bf16[8,112,256]{2,1,0:T(8,128)(2,1)}), bf16[8,112,256]{2,1,0:T(8,128)(2,1)S(1)}, u32[]{:S(2)}, u32[]{:S(2)}) %all-to-all-start.1) | async-done | bytes 458784 | tf_op jit(solution)/shard_map/all_to_all | solution.py:574
  44.9 5.0 %backward_far.1 = (bf16[2048,1024]{1,0:T(8,128)(2,1)S(1)}, bf16[128,1152]{1,0:T(8,128)(2,1)S(1)}, bf16[128,1152]{1,0:T(8,128)(2,1)S(1)}, bf16[128,2048]{1,0:T(8,128)(2,1)S(1)}) custom-call(s32[1]{0:T(128)} %bitcast.grid_ref, bf16[8,112,256]{2,1,0:T(8,128)(2,1)S(1)} %all-to-all-done.1.low_ref, bf16[1024,2048]{1,0:T(8,128)(2,1)} %copy-done, ...), custom_call_target="tpu_custom_call" | custom-call | flops 1879048192 | bytes 8388608 | tf_op jit(solution)/shard_map/backward_far/pallas_call | solution.py:416
  49.9 6.8 %backward_near.1 = (bf16[384,1152]{1,0:T(8,128)(2,1)S(1)}, bf16[384,1152]{1,0:T(8,128)(2,1)S(1)}, bf16[1024,1024]{1,0:T(8,128)(2,1)S(1)}) custom-call(s32[1]{0:T(128)} %bitcast.grid_ref, bf16[1024,2048]{1,0:T(8,128)(2,1)} %copy-done, bf16[8,2048,128]{2,1,0:T(8,128)(2,1)} %get-tuple-element.37.hidden_hbm, bf16[1024,1024]{1,0:T(8,128)(2,1)} %weight_hbm.1, ...), custom_call_target="tpu_custom_call" | custom-call | flops 3758096384 | bytes 8388608 | tf_op jit(solution)/shard_map/backward_near/pallas_call | solution.py:444
  56.7 2.0 %collective-permute-start = (bf16[128,1152]{1,0:T(8,128)(2,1)S(1)}, bf16[128,1152]{1,0:T(8,128)(2,1)S(1)}, u32[]{:S(2)}, u32[]{:S(2)}) collective-permute-start(bf16[128,1152]{1,0:T(8,128)(2,1)S(1)} %get-tuple-element.44), channel_id=1, source_target_pairs={{0,2},{1,3},{2,4},{3,5},{4,6},{5,7},{6,0},{7,1},{8,10},{9,11},{10,... | collective-permute-start | bytes 884744 | tf_op jit(solution)/shard_map/ppermute | solution.py:528
  58.7 2.2 %collective-permute-start.1 = (bf16[128,1152]{1,0:T(8,128)(2,1)S(1)}, bf16[128,1152]{1,0:T(8,128)(2,1)S(1)}, u32[]{:S(2)}, u32[]{:S(2)}) collective-permute-start(bf16[128,1152]{1,0:T(8,128)(2,1)S(1)} %get-tuple-element.45), channel_id=1, source_target_pairs={{0,6},{1,7},{2,0},{3,1},{4,2},{5,3},{6,4},{7,5},{8,14},{9,15},{10,... | collective-permute-start | bytes 884744 | tf_op jit(solution)/shard_map/ppermute | solution.py:528
  60.9 0.1 convert_element_type.55
  61.0 0.1 reshape.34
  61.2 4.4 %collective-permute-done = bf16[128,1152]{1,0:T(8,128)(2,1)S(1)} collective-permute-done((bf16[128,1152]{1,0:T(8,128)(2,1)S(1)}, bf16[128,1152]{1,0:T(8,128)(2,1)S(1)}, u32[]{:S(2)}, u32[]{:S(2)}) %collective-permute-start) | collective-permute-done | bytes 294944 | tf_op jit(solution)/shard_map/ppermute | solution.py:528
  65.6 0.0 collective-permute-done.1
  65.7 0.2 fusion.6
  65.8 0.1 maximum_bitcast_fusion.2
  65.9 0.1 pad_maximum_fusion
  66.0 0.1 collective-permute-start.2
  66.2 0.1 maximum_bitcast_fusion
  66.3 2.2 %collective-permute-done.2 = bf16[3,2,64,1152]{3,2,1,0:T(8,128)(2,1)S(1)} collective-permute-done((bf16[3,2,64,1152]{3,2,1,0:T(8,128)(2,1)S(1)}, bf16[3,2,64,1152]{3,2,1,0:T(8,128)(2,1)S(1)}, u32[]{:S(2)}, u32[]{:S(2)}) %collective-permute-start.2) | collective-permute-done | bytes 884768 | tf_op jit(solution)/shard_map/ppermute | solution.py:528
  68.6 0.2 fusion
  68.9 1.8 %collective-permute-start.3 = (bf16[2,64,1152]{2,1,0:T(8,128)(2,1)S(1)}, bf16[2,64,1152]{2,1,0:T(8,128)(2,1)S(1)}, u32[]{:S(2)}, u32[]{:S(2)}) collective-permute-start(bf16[2,64,1152]{2,1,0:T(8,128)(2,1)S(1)} %get-tuple-element.47), channel_id=1, source_target_pairs={{0,2},{1,3},{2,4},{3,5},{4,6},{5,7},{6,0},{7,1},{8,10},{9,11},{10,... | collective-permute-start | bytes 884744 | tf_op jit(solution)/shard_map/ppermute | solution.py:528
  70.6 1.8 %collective-permute-start.4 = (bf16[2,64,1152]{2,1,0:T(8,128)(2,1)S(1)}, bf16[2,64,1152]{2,1,0:T(8,128)(2,1)S(1)}, u32[]{:S(2)}, u32[]{:S(2)}) collective-permute-start(bf16[2,64,1152]{2,1,0:T(8,128)(2,1)S(1)} %get-tuple-element.48), channel_id=1, source_target_pairs={{0,6},{1,7},{2,0},{3,1},{4,2},{5,3},{6,4},{7,5},{8,14},{9,15},{10,... | collective-permute-start | bytes 884744 | tf_op jit(solution)/shard_map/ppermute | solution.py:528
  72.4 5.5 %latent_gradient.1 = bf16[2048,1024]{1,0:T(8,128)(2,1)} custom-call(bf16[2048,1024]{1,0:T(8,128)(2,1)S(1)} %get-tuple-element.49.pre_ref, bf16[1024,1024]{1,0:T(8,128)(2,1)S(1)} %get-tuple-element.50.weight_ref), custom_call_target="tpu_custom_call" | custom-call | flops 4294967296 | bytes 10485760 | tf_op jit(solution)/shard_map/latent_gradient/pallas_call | solution.py:484
  78.0 1.5 %collective-permute-done.3 = bf16[2,64,1152]{2,1,0:T(8,128)(2,1)S(1)} collective-permute-done((bf16[2,64,1152]{2,1,0:T(8,128)(2,1)S(1)}, bf16[2,64,1152]{2,1,0:T(8,128)(2,1)S(1)}, u32[]{:S(2)}, u32[]{:S(2)}) %collective-permute-start.3) | collective-permute-done | bytes 294944 | tf_op jit(solution)/shard_map/ppermute | solution.py:528
  79.4 0.0 collective-permute-done.4
  79.5 0.1 fusion.2
  79.6 0.9 collective-permute-start.7
  80.5 2.5 %collective-permute-start.6 = (bf16[64,1152]{1,0:T(8,128)(2,1)S(1)}, bf16[64,1152]{1,0:T(8,128)(2,1)S(1)}, u32[]{:S(2)}, u32[]{:S(2)}) collective-permute-start(bf16[64,1152]{1,0:T(8,128)(2,1)S(1)} %get-tuple-element.67), channel_id=1, source_target_pairs={{0,24},{1,25},{2,26},{3,27},{4,28},{5,29},{6,30},{7,31},{8,16},{9,... | collective-permute-start | bytes 442376 | tf_op jit(solution)/shard_map/ppermute | solution.py:528
  83.0 0.2 collective-permute-start.5
  83.2 4.8 %collective-permute-done.7 = bf16[64,1152]{1,0:T(8,128)(2,1)S(1)} collective-permute-done((bf16[64,1152]{1,0:T(8,128)(2,1)S(1)}, bf16[64,1152]{1,0:T(8,128)(2,1)S(1)}, u32[]{:S(2)}, u32[]{:S(2)}) %collective-permute-start.7) | collective-permute-done | bytes 147488 | tf_op jit(solution)/shard_map/ppermute | solution.py:528
  88.0 1.7 %collective-permute-done.6 = bf16[64,1152]{1,0:T(8,128)(2,1)S(1)} collective-permute-done((bf16[64,1152]{1,0:T(8,128)(2,1)S(1)}, bf16[64,1152]{1,0:T(8,128)(2,1)S(1)}, u32[]{:S(2)}, u32[]{:S(2)}) %collective-permute-start.6) | collective-permute-done | bytes 147488 | tf_op jit(solution)/shard_map/ppermute | solution.py:528
  89.7 0.0 collective-permute-done.5
  89.7 0.1 add_convert_fusion.own_ref
  89.8 1.0 collective-permute-start.10
  90.7 2.1 %collective-permute-start.9 = (bf16[64,1152]{1,0:T(8,128)(2,1)S(1)}, bf16[64,1152]{1,0:T(8,128)(2,1)S(1)}, u32[]{:S(2)}, u32[]{:S(2)}) collective-permute-start(bf16[64,1152]{1,0:T(8,128)(2,1)S(1)} %add_convert_fusion.own_ref), channel_id=1, source_target_pairs={{0,96},{1,97},{2,98},{3,99},{4,100},{5,101},{6,102},{7,103},{8,104... | collective-permute-start | bytes 442376 | tf_op jit(solution)/shard_map/ppermute | solution.py:528
  92.8 0.6 collective-permute-start.8
  93.4 4.8 %collective-permute-done.10.refs_2_ = bf16[64,1152]{1,0:T(8,128)(2,1)S(1)} collective-permute-done((bf16[64,1152]{1,0:T(8,128)(2,1)S(1)}, bf16[64,1152]{1,0:T(8,128)(2,1)S(1)}, u32[]{:S(2)}, u32[]{:S(2)}) %collective-permute-start.10) | collective-permute-done | bytes 147488 | tf_op jit(solution)/shard_map/ppermute | solution.py:528
  98.1 2.1 %collective-permute-done.9.refs_1_ = bf16[64,1152]{1,0:T(8,128)(2,1)S(1)} collective-permute-done((bf16[64,1152]{1,0:T(8,128)(2,1)S(1)}, bf16[64,1152]{1,0:T(8,128)(2,1)S(1)}, u32[]{:S(2)}, u32[]{:S(2)}) %collective-permute-start.9) | collective-permute-done | bytes 147488 | tf_op jit(solution)/shard_map/ppermute | solution.py:528
  100.3 0.0 collective-permute-done.8.refs_0_
  100.3 0.8 finish.1
  (8 shorter events, 0.3 us)
Async XLA Ops:
  11.6 17.9 %all-to-all-start = ((f16[8,112,256]{2,1,0:T(8,128)(2,1)}), f16[8,112,256]{2,1,0:T(8,128)(2,1)S(1)}, u32[]{:S(2)}, u32[]{:S(2)}) async-start(f16[8,112,256]{2,1,0:T(8,128)(2,1)} %multiply_convert_fusion), calls=%async_computation | async-start | bytes 917504 | tf_op jit(solution)/shard_map/all_to_all | solution.py:569
  18.7 11.0 %copy-start.2 = (f32[100,2048]{1,0:T(8,128)S(1)}, f32[100,2048]{1,0:T(8,128)}, u32[]{:S(2)}) copy-start(f32[100,2048]{1,0:T(8,128)} %observed_ref.1) | copy-start | bytes 2457604
  18.7 11.0 %copy-start.3 = (f32[2048]{0:T(1024)S(1)}, f32[2048]{0:T(1024)}, u32[]{:S(2)}) copy-start(f32[2048]{0:T(1024)} %param.9) | copy-start | bytes 24580
  31.5 13.4 %all-to-all-start.1 = ((bf16[8,112,256]{2,1,0:T(8,128)(2,1)}), bf16[8,112,256]{2,1,0:T(8,128)(2,1)S(1)}, u32[]{:S(2)}, u32[]{:S(2)}) async-start(bf16[8,112,256]{2,1,0:T(8,128)(2,1)} %pairs.1), calls=%async_computation.1 | async-start | bytes 917504 | tf_op jit(solution)/shard_map/all_to_all | solution.py:574
  35.2 2.2 %copy-start.1 = (bf16[1,2048,1024]{2,1,0:T(8,128)(2,1)S(1)}, bf16[1,2048,1024]{2,1,0:T(8,128)(2,1)}, u32[]{:S(2)}) copy-start(bf16[1,2048,1024]{2,1,0:T(8,128)(2,1)} %param.5) | copy-start | bytes 12582916
  38.6 2.0 %copy-start = (bf16[1024,2048]{1,0:T(8,128)(2,1)}, bf16[1024,2048]{1,0:T(8,128)(2,1)S(1)}, u32[]{:S(2)}) copy-start(bf16[1024,2048]{1,0:T(8,128)(2,1)S(1)} %turned.1.turned_hbm) | copy-start | bytes 12582916
  56.7 8.9 %collective-permute-start = (bf16[128,1152]{1,0:T(8,128)(2,1)S(1)}, bf16[128,1152]{1,0:T(8,128)(2,1)S(1)}, u32[]{:S(2)}, u32[]{:S(2)}) collective-permute-start(bf16[128,1152]{1,0:T(8,128)(2,1)S(1)} %get-tuple-element.44), channel_id=1, source_target_pairs={{0,2},{1,3},{2,4},{3,5},{4,6},{5,7},{6,0},{7,1},{8,10},{9,11},{10,... | collective-permute-start | bytes 884744 | tf_op jit(solution)/shard_map/ppermute | solution.py:528
  58.7 6.9 %collective-permute-start.1 = (bf16[128,1152]{1,0:T(8,128)(2,1)S(1)}, bf16[128,1152]{1,0:T(8,128)(2,1)S(1)}, u32[]{:S(2)}, u32[]{:S(2)}) collective-permute-start(bf16[128,1152]{1,0:T(8,128)(2,1)S(1)} %get-tuple-element.45), channel_id=1, source_target_pairs={{0,6},{1,7},{2,0},{3,1},{4,2},{5,3},{6,4},{7,5},{8,14},{9,15},{10,... | collective-permute-start | bytes 884744 | tf_op jit(solution)/shard_map/ppermute | solution.py:528
  66.0 2.5 %collective-permute-start.2 = (bf16[3,2,64,1152]{3,2,1,0:T(8,128)(2,1)S(1)}, bf16[3,2,64,1152]{3,2,1,0:T(8,128)(2,1)S(1)}, u32[]{:S(2)}, u32[]{:S(2)}) collective-permute-start(bf16[3,2,64,1152]{3,2,1,0:T(8,128)(2,1)S(1)} %pad_maximum_fusion), channel_id=1, source_target_pairs={{0,1},{1,0},{2,3},{3,2},{4,5},{5,4},{6,7},{7,6},{8,9},{9,8},{10,11... | collective-permute-start | bytes 2654216 | tf_op jit(solution)/shard_map/ppermute | solution.py:528
  68.9 10.6 %collective-permute-start.3 = (bf16[2,64,1152]{2,1,0:T(8,128)(2,1)S(1)}, bf16[2,64,1152]{2,1,0:T(8,128)(2,1)S(1)}, u32[]{:S(2)}, u32[]{:S(2)}) collective-permute-start(bf16[2,64,1152]{2,1,0:T(8,128)(2,1)S(1)} %get-tuple-element.47), channel_id=1, source_target_pairs={{0,2},{1,3},{2,4},{3,5},{4,6},{5,7},{6,0},{7,1},{8,10},{9,11},{10,... | collective-permute-start | bytes 884744 | tf_op jit(solution)/shard_map/ppermute | solution.py:528
  70.6 8.8 %collective-permute-start.4 = (bf16[2,64,1152]{2,1,0:T(8,128)(2,1)S(1)}, bf16[2,64,1152]{2,1,0:T(8,128)(2,1)S(1)}, u32[]{:S(2)}, u32[]{:S(2)}) collective-permute-start(bf16[2,64,1152]{2,1,0:T(8,128)(2,1)S(1)} %get-tuple-element.48), channel_id=1, source_target_pairs={{0,6},{1,7},{2,0},{3,1},{4,2},{5,3},{6,4},{7,5},{8,14},{9,15},{10,... | collective-permute-start | bytes 884744 | tf_op jit(solution)/shard_map/ppermute | solution.py:528
  79.6 8.4 %collective-permute-start.7 = (bf16[64,1152]{1,0:T(8,128)(2,1)S(1)}, bf16[64,1152]{1,0:T(8,128)(2,1)S(1)}, u32[]{:S(2)}, u32[]{:S(2)}) collective-permute-start(bf16[64,1152]{1,0:T(8,128)(2,1)S(1)} %get-tuple-element.68), channel_id=1, source_target_pairs={{0,16},{1,17},{2,18},{3,19},{4,20},{5,21},{6,22},{7,23},{8,24},{9,... | collective-permute-start | bytes 442376 | tf_op jit(solution)/shard_map/ppermute | solution.py:528
  80.5 9.2 %collective-permute-start.6 = (bf16[64,1152]{1,0:T(8,128)(2,1)S(1)}, bf16[64,1152]{1,0:T(8,128)(2,1)S(1)}, u32[]{:S(2)}, u32[]{:S(2)}) collective-permute-start(bf16[64,1152]{1,0:T(8,128)(2,1)S(1)} %get-tuple-element.67), channel_id=1, source_target_pairs={{0,24},{1,25},{2,26},{3,27},{4,28},{5,29},{6,30},{7,31},{8,16},{9,... | collective-permute-start | bytes 442376 | tf_op jit(solution)/shard_map/ppermute | solution.py:528
  83.0 6.7 %collective-permute-start.5 = (bf16[64,1152]{1,0:T(8,128)(2,1)S(1)}, bf16[64,1152]{1,0:T(8,128)(2,1)S(1)}, u32[]{:S(2)}, u32[]{:S(2)}) collective-permute-start(bf16[64,1152]{1,0:T(8,128)(2,1)S(1)} %get-tuple-element.67), channel_id=1, source_target_pairs={{0,8},{1,9},{2,10},{3,11},{4,12},{5,13},{6,14},{7,15},{8,0},{9,1},... | collective-permute-start | bytes 442376 | tf_op jit(solution)/shard_map/ppermute | solution.py:528
  89.8 8.3 %collective-permute-start.10 = (bf16[64,1152]{1,0:T(8,128)(2,1)S(1)}, bf16[64,1152]{1,0:T(8,128)(2,1)S(1)}, u32[]{:S(2)}, u32[]{:S(2)}) collective-permute-start(bf16[64,1152]{1,0:T(8,128)(2,1)S(1)} %add_convert_fusion.own_ref), channel_id=1, source_target_pairs={{0,64},{1,65},{2,66},{3,67},{4,68},{5,69},{6,70},{7,71},{8,72},{9,... | collective-permute-start | bytes 442376 | tf_op jit(solution)/shard_map/ppermute | solution.py:528
  90.7 9.5 %collective-permute-start.9 = (bf16[64,1152]{1,0:T(8,128)(2,1)S(1)}, bf16[64,1152]{1,0:T(8,128)(2,1)S(1)}, u32[]{:S(2)}, u32[]{:S(2)}) collective-permute-start(bf16[64,1152]{1,0:T(8,128)(2,1)S(1)} %add_convert_fusion.own_ref), channel_id=1, source_target_pairs={{0,96},{1,97},{2,98},{3,99},{4,100},{5,101},{6,102},{7,103},{8,104... | collective-permute-start | bytes 442376 | tf_op jit(solution)/shard_map/ppermute | solution.py:528
  92.8 7.5 %collective-permute-start.8 = (bf16[64,1152]{1,0:T(8,128)(2,1)S(1)}, bf16[64,1152]{1,0:T(8,128)(2,1)S(1)}, u32[]{:S(2)}, u32[]{:S(2)}) collective-permute-start(bf16[64,1152]{1,0:T(8,128)(2,1)S(1)} %add_convert_fusion.own_ref), channel_id=1, source_target_pairs={{0,32},{1,33},{2,34},{3,35},{4,36},{5,37},{6,38},{7,39},{8,40},{9,... | collective-permute-start | bytes 442376 | tf_op jit(solution)/shard_map/ppermute | solution.py:528

commit v12 on v9

--- a/solution.py
+++ b/solution.py
@@ -242,11 +242,7 @@
     return grid >> 3, (grid >> 1) & 3, grid & 1
 
 
-STEPS = ((2, 0), (1, 3))
-
-
-def owner(block, steps, x_lo, z):
-    return ((block & 1) ^ x_lo) * 4 + ((z + steps[block >> 1]) & 3)
+PARTS = (((2, 0), (2, 1), (1, 1), (3, 0)), ((1, 0), (3, 1), (0, 0), (0, 1)))
 
 
 def turn_kernel(grid_ref, latent_ref, turned_ref):
@@ -254,9 +250,11 @@
     x_lo, z, core = position(grid_ref)
     for group in range(8):
         step = (group - z) & 3
-        odd = step & 1
-        place = odd * (2 + (step >> 1)) + (1 - odd) * (1 - (step >> 1))
-        at = (place >> 1) * 512 + (place & 1) * 128 + ((group >> 2) ^ x_lo) * 64
+        other_x = (group >> 2) ^ x_lo
+        odd, back = step & 1, step >> 1
+        part = odd * (1 - (other_x ^ back)) + (1 - odd) * (1 - back)
+        place = odd * (back + 2 * (1 - part)) + (1 - odd) * (other_x + 2 * part)
+        at = part * 512 + place * 64
         first = pl.multiple_of(at + (1 - core) * 256, 64)
         second = pl.multiple_of(at + core * 256, 64)
         for row in range(0, nodes, ROWS):
@@ -287,11 +285,9 @@
     x_lo, z, core = position(grid_ref)
     return [
         pltpu.make_async_copy(
-            hidden_hbm.at[owner(block, STEPS[part], x_lo, z)],
-            hidden_ref.at[block],
-            sems.at[block],
+            hidden_hbm.at[(other_x ^ x_lo) * 4 + ((z + step) & 3)], hidden_ref.at[block], sems.at[block]
         )
-        for block in range(4)
+        for block, (step, other_x) in enumerate(PARTS[part])
     ]
 
 
@@ -574,7 +570,7 @@
 
 def over_core(send, keep):
     got = moved(send, lambda y, x, z, c: (y, x, z, 1 - c))
-    return summed(keep, [got]).reshape(2, 2, 64, send.shape[1])
+    return summed(keep, [got]).reshape(4, 64, send.shape[1])
 
 
 def up(value):
@@ -617,17 +613,20 @@
     turned_latent = turned(late_grid, latent)
     grad_pre, rows_a, second_a, flat, turned_now = send_a(grid, low, turned_latent, slope, hidden, padded)
     kept_a, turned_now, hidden_now = keep_a(grid, turned_latent, hidden, grad_pre, turned_now, second_a)
-    far, own = over_core(rows_a, kept_a).astype(bf16)
-    far, own, flat = lax.optimization_barrier((far, own, flat))
-    upward, downward = up(far[0]), down(far[1])
+    far_up, far_down, near_up, near_down = over_core(rows_a, kept_a).astype(bf16)
+    far_up, far_down, near_up, near_down, flat = lax.optimization_barrier((far_up, far_down, near_up, near_down, flat))
+    upward, downward = up(far_up), down(far_down)
+    from_below, from_above = up(near_up), down(near_down)
     rows_b, second_b, turned_now = send_b(grid, turned_latent, grad_pre, flat, turned_now, hidden_now)
     kept_b, weight_copy = keep_b(hidden_weight, grad_pre, turned_now, second_b)
-    above, below = over_core(rows_b, kept_b)
-    above = jnp.stack([above[0] + upward.astype(f32), above[1]]).astype(bf16)
-    below = jnp.stack([below[0], below[1] + downward.astype(f32)]).astype(bf16)
+    above, below, own, other = over_core(rows_b, kept_b)
+    above = (above + upward.astype(f32)).astype(bf16)
+    below = (below + downward.astype(f32)).astype(bf16)
     above, below, grad_pre = lax.optimization_barrier((above, below, grad_pre))
     grad_latent = latent_gradient(grad_pre, weight_copy)
-    blocks = summed(own, [up(above), down(below)]).astype(bf16)
+    own = summed(own, [up(above), from_above])
+    other = summed(other, [from_below, down(below)])
+    blocks = jnp.stack([own, other]).astype(bf16)
     blocks, grad_latent = lax.optimization_barrier((blocks, grad_latent))
     block = over_x(blocks)
     factor = 1.0 / math.sqrt(members * nodes * groups)

time: 94.8 us -> 92.7 us (0.978)
  waiting for transfers between devices: 24.3 us -> 20.2 us
  starting transfers between devices: 25.9 us -> 28.2 us
    ppermute x12 -> x14, waiting for transfers between devices: 14.9 us -> 10.8 us  [moved(): return lax.ppermute(value, ('member', 'grid'), moves)]
    ppermute x12 -> x14, starting transfers between devices: 15.2 us -> 17.6 us  [moved(): return lax.ppermute(value, ('member', 'grid'), moves)]
  transfers between devices with their start and end apart: 14 -> 16, of which waited for: 9 -> 8; matrix products, arithmetic and copies ran while one was open for 0% -> 0% of each run, Pallas kernels for 18% -> 18%
where the time goes in v12:
time: 92.7 us; the launch traced here: 92.3 us
  Pallas kernels  37.1 us (40%)
  starting transfers between devices  28.2 us (30%)
  waiting for transfers between devices  20.2 us (22%)
  local copies, waits for them, and re-layouts  4.27 us (5%)
  other arithmetic  1.54 us (2%)
    ppermute x14, starting transfers between devices, moved(): return lax.ppermute(value, ('member', 'grid'), moves)  17.6 us
    ppermute x14, waiting for transfers between devices, moved(): return lax.ppermute(value, ('member', 'grid'), moves)  10.8 us
    pallas_call x1, Pallas kernels, forward(): pl.pallas_call(forward_kernel, in_specs=[anywhere] * 3, out_specs=[vmem,...  10.1 us
    all_to_all x1, starting transfers between devices, body(): blocks = lax.all_to_all(blocks, 'member', 0, 0, tiled=True)  7.02 us
    pallas_call x1, Pallas kernels, gates(): pl.pallas_call(gate_kernel, in_specs=[anywhere], out_specs=[anywhere] * 2...  5.78 us
    pallas_call x1, Pallas kernels, latent_gradient(): pl.pallas_call(latent_kernel, in_specs=[vmem, vmem], out_specs=anywhere,...  5.59 us
    all_to_all x1, waiting for transfers between devices, body(): blocks = lax.all_to_all(blocks, 'member', 0, 0, tiled=True)  5.07 us
    pallas_call x1, Pallas kernels, send_a(): pl.pallas_call(send_a_kernel, in_specs=[smem, vmem, anywhere, anywhere, a...  5.02 us
  transfers between devices with their start and end apart: 16, of which 8 were waited for; matrix products, arithmetic and copies ran while one was open for 0% of the time, Pallas kernels for 18%

profile of v12, /device:TPU:0, one launch (start us, length us, event | category | flops | bytes accessed | tf_op | source)
XLA Modules:
  0.0 92.3 jit_solution(11606557535863839926)
XLA Ops:
  0.6 10.1 %forward.1 = (f32[8,112,256]{2,1,0:T(8,128)S(1)}, bf16[2048,1024]{1,0:T(8,128)(2,1)}, bf16[1024,128]{1,0:T(8,128)(2,1)S(1)}) custom-call(bf16[2048,1024]{1,0:T(8,128)(2,1)} %bitcast.16, bf16[1024,1024]{1,0:T(8,128)(2,1)} %weight_hbm.1, bf16[100,1024]{1,0:T(8,128)(2,1)} %bitcast.19), custom_call_target="tpu_custom_call" | custom-call | flops 4831838208 | bytes 20971520 | tf_op jit(solution)/shard_map/forward/pallas_call | solution.py:102
  10.7 0.9 %multiply_convert_fusion = f16[8,112,256]{2,1,0:T(8,128)(2,1)} fusion(f32[8,112,256]{2,1,0:T(8,128)S(1)} %get-tuple-element.40), kind=kLoop, calls=%fused_computation.3 | loop fusion | flops 458752 | bytes 1376256 | tf_op jit(solution)/shard_map/convert_element_type | solution.py:606
  11.6 7.0 %all-to-all-start = ((f16[8,112,256]{2,1,0:T(8,128)(2,1)}), f16[8,112,256]{2,1,0:T(8,128)(2,1)S(1)}, u32[]{:S(2)}, u32[]{:S(2)}) async-start(f16[8,112,256]{2,1,0:T(8,128)(2,1)} %multiply_convert_fusion), calls=%async_computation | async-start | bytes 917504 | tf_op jit(solution)/shard_map/all_to_all | solution.py:607
  18.7 0.0 copy-start.2
  18.7 0.0 copy-start.3
  18.7 5.8 %gates.1 = (bf16[8,2048,128]{2,1,0:T(8,128)(2,1)}, bf16[2048,1024]{1,0:T(8,128)(2,1)}) custom-call(bf16[2048,1024]{1,0:T(8,128)(2,1)} %get-tuple-element.43.pre_hbm), custom_call_target="tpu_custom_call" | custom-call | bytes 12582912 | tf_op jit(solution)/shard_map/gates/pallas_call | solution.py:162
  24.5 5.1 %all-to-all-done = f16[8,112,256]{2,1,0:T(8,128)(2,1)S(1)} async-done(((f16[8,112,256]{2,1,0:T(8,128)(2,1)}), f16[8,112,256]{2,1,0:T(8,128)(2,1)S(1)}, u32[]{:S(2)}, u32[]{:S(2)}) %all-to-all-start) | async-done | bytes 458784 | tf_op jit(solution)/shard_map/all_to_all | solution.py:607
  29.5 0.1 convert_multiply_fusion.blocks_ref
  29.6 0.0 copy-done.2
  29.6 0.0 copy-done.3
  29.6 1.9 %pairs.1 = bf16[8,112,256]{2,1,0:T(8,128)(2,1)} custom-call(s32[1]{0:T(128)} %bitcast.1.place_ref, f32[8,112,256]{2,1,0:T(8,128)S(1)} %convert_multiply_fusion.blocks_ref, f32[100,2048]{1,0:T(8,128)S(1)} %copy-done.2, f32[1,2048]{1,0:T(1,128)S(1)} %bitcast.18), custom_call_target="tpu_custom_call" | custom-call | flops 4194304 | bytes 2097152 | tf_op jit(solution)/shard_map/pairs/pallas_call | solution.py:223
  31.6 3.7 %all-to-all-start.1 = ((bf16[8,112,256]{2,1,0:T(8,128)(2,1)}), bf16[8,112,256]{2,1,0:T(8,128)(2,1)S(1)}, u32[]{:S(2)}, u32[]{:S(2)}) async-start(bf16[8,112,256]{2,1,0:T(8,128)(2,1)} %pairs.1), calls=%async_computation.1 | async-start | bytes 917504 | tf_op jit(solution)/shard_map/all_to_all | solution.py:612
  35.2 0.0 copy-start.1
  35.2 2.2 %copy-done.1 = bf16[1,2048,1024]{2,1,0:T(8,128)(2,1)S(1)} copy-done((bf16[1,2048,1024]{2,1,0:T(8,128)(2,1)S(1)}, bf16[1,2048,1024]{2,1,0:T(8,128)(2,1)}, u32[]{:S(2)}) %copy-start.1) | copy-done | bytes 4194328
  37.4 1.1 %turned.1.turned_hbm = bf16[1024,2048]{1,0:T(8,128)(2,1)S(1)} custom-call(s32[1]{0:T(128)} %bitcast.grid_ref, bf16[2048,1024]{1,0:T(8,128)(2,1)S(1)} %bitcast.17), custom_call_target="tpu_custom_call" | custom-call | bytes 8388608 | tf_op jit(solution)/shard_map/turned/pallas_call | solution.py:269
  38.6 0.0 copy-start
  38.6 2.0 %copy-done = bf16[1024,2048]{1,0:T(8,128)(2,1)} copy-done((bf16[1024,2048]{1,0:T(8,128)(2,1)}, bf16[1024,2048]{1,0:T(8,128)(2,1)S(1)}, u32[]{:S(2)}) %copy-start) | copy-done | bytes 4194328
  40.6 4.4 %all-to-all-done.1.low_ref = bf16[8,112,256]{2,1,0:T(8,128)(2,1)S(1)} async-done(((bf16[8,112,256]{2,1,0:T(8,128)(2,1)}), bf16[8,112,256]{2,1,0:T(8,128)(2,1)S(1)}, u32[]{:S(2)}, u32[]{:S(2)}) %all-to-all-start.1) | async-done | bytes 458784 | tf_op jit(solution)/shard_map/all_to_all | solution.py:612
  44.9 5.0 %send_a.1 = (bf16[2048,1024]{1,0:T(8,128)(2,1)S(1)}, bf16[256,1152]{1,0:T(8,128)(2,1)S(1)}, bf16[256,128]{1,0:T(8,128)(2,1)S(1)}, bf16[128,2048]{1,0:T(8,128)(2,1)S(1)}, bf16[256,2048]{1,0:T(8,128)(2,1)S(1)}) custom-call(s32[1]{0:T(128)} %bitcast.grid_ref, bf16[8,112,256]{2,1,0:T(8,128)(2,1)S(1)} %all-to-all-done.1.low_ref, bf16[1024,2048]{1,0:T(8,128)(2,1)} %copy-done, ...), custom_call_target="tpu_custom_call" | custom-call | flops 1879048192 | bytes 8388608 | tf_op jit(solution)/shard_map/send_a/pallas_call | solution.py:427
  50.0 0.1 collective-permute-start
  50.1 2.9 %keep_a.1 = (bf16[256,1152]{1,0:T(8,128)(2,1)S(1)}, bf16[256,2048]{1,0:T(8,128)(2,1)S(1)}, bf16[4,2048,128]{2,1,0:T(8,128)(2,1)S(1)}) custom-call(s32[1]{0:T(128)} %bitcast.grid_ref, bf16[1024,2048]{1,0:T(8,128)(2,1)} %copy-done, bf16[8,2048,128]{2,1,0:T(8,128)(2,1)} %get-tuple-element.50.hidden_hbm, bf16[2048,1024]{1,0:T(8,128)(2,1)S(1)} %get-tuple-element.71.pre_ref, ...), custom_call_target="tpu_custom_call" | custom-call | flops 1073741824 | bytes 4194304 | tf_op jit(solution)/shard_map/keep_a/pallas_call | solution.py:456
  53.0 0.0 collective-permute-done
  53.0 0.1 add_convert_fusion
  53.2 2.3 %send_b.1 = (bf16[256,1152]{1,0:T(8,128)(2,1)S(1)}, bf16[256,128]{1,0:T(8,128)(2,1)S(1)}, bf16[256,2048]{1,0:T(8,128)(2,1)S(1)}) custom-call(s32[1]{0:T(128)} %bitcast.grid_ref, bf16[1024,2048]{1,0:T(8,128)(2,1)} %copy-done, bf16[2048,1024]{1,0:T(8,128)(2,1)S(1)} %get-tuple-element.71.pre_ref, bf16[128,2048]{1,0:T(8,128)(2,1)S(1)} %get-tuple-element.58.flat_ref, ...), custom_call_target="tpu_custom_call" | custom-call | flops 1073741824 | bytes 4194304 | tf_op jit(solution)/shard_map/send_b/pallas_call | solution.py:470
  55.5 0.6 collective-permute-start.1
  56.1 1.9 %collective-permute-start.2 = (bf16[64,1152]{1,0:T(8,128)(2,1)S(1)}, bf16[64,1152]{1,0:T(8,128)(2,1)S(1)}, u32[]{:S(2)}, u32[]{:S(2)}) collective-permute-start(bf16[64,1152]{1,0:T(8,128)(2,1)S(1)} %get-tuple-element.65), channel_id=1, source_target_pairs={{0,2},{1,3},{2,4},{3,5},{4,6},{5,7},{6,0},{7,1},{8,10},{9,11},{10,... | collective-permute-start | bytes 442376 | tf_op jit(solution)/shard_map/ppermute | solution.py:561
  58.0 2.1 %collective-permute-start.3 = (bf16[64,1152]{1,0:T(8,128)(2,1)S(1)}, bf16[64,1152]{1,0:T(8,128)(2,1)S(1)}, u32[]{:S(2)}, u32[]{:S(2)}) collective-permute-start(bf16[64,1152]{1,0:T(8,128)(2,1)S(1)} %get-tuple-element.66), channel_id=1, source_target_pairs={{0,6},{1,7},{2,0},{3,1},{4,2},{5,3},{6,4},{7,5},{8,14},{9,15},{10,... | collective-permute-start | bytes 442376 | tf_op jit(solution)/shard_map/ppermute | solution.py:561
  60.2 2.0 %collective-permute-start.5 = (bf16[64,1152]{1,0:T(8,128)(2,1)S(1)}, bf16[64,1152]{1,0:T(8,128)(2,1)S(1)}, u32[]{:S(2)}, u32[]{:S(2)}) collective-permute-start(bf16[64,1152]{1,0:T(8,128)(2,1)S(1)} %get-tuple-element.68), channel_id=1, source_target_pairs={{0,6},{1,7},{2,0},{3,1},{4,2},{5,3},{6,4},{7,5},{8,14},{9,15},{10,... | collective-permute-start | bytes 442376 | tf_op jit(solution)/shard_map/ppermute | solution.py:561
  62.2 0.0 collective-permute-start.6
  62.2 1.6 %keep_b.1 = (bf16[256,1152]{1,0:T(8,128)(2,1)S(1)}, bf16[1024,1024]{1,0:T(8,128)(2,1)S(1)}) custom-call(bf16[1024,1024]{1,0:T(8,128)(2,1)} %weight_hbm.1, bf16[2048,1024]{1,0:T(8,128)(2,1)S(1)} %get-tuple-element.71.pre_ref, bf16[256,2048]{1,0:T(8,128)(2,1)S(1)} %get-tuple-element.61.turned_ref, bf16[256,128]{1,0:T(8,128)(2,1)S(1)} %get-tuple-element.62.second_ref), custom_call_target="tpu_custom_call" | custom-call | flops 1073741824 | bytes 4194304 | tf_op jit(solution)/shard_map/keep_b/pallas_call | solution.py:484
  63.8 0.0 collective-permute-done.1
  63.8 0.1 convert_add_fusion
  63.9 0.3 collective-permute-done.2
  64.2 0.5 collective-permute-done.3
  64.7 0.1 fusion.2
  64.8 2.0 %collective-permute-start.4 = (bf16[64,1152]{1,0:T(8,128)(2,1)S(1)}, bf16[64,1152]{1,0:T(8,128)(2,1)S(1)}, u32[]{:S(2)}, u32[]{:S(2)}) collective-permute-start(bf16[64,1152]{1,0:T(8,128)(2,1)S(1)} %get-tuple-element.67), channel_id=1, source_target_pairs={{0,2},{1,3},{2,4},{3,5},{4,6},{5,7},{6,0},{7,1},{8,10},{9,11},{10,... | collective-permute-start | bytes 442376 | tf_op jit(solution)/shard_map/ppermute | solution.py:561
  66.8 1.7 %collective-permute-start.7 = (bf16[64,1152]{1,0:T(8,128)(2,1)S(1)}, bf16[64,1152]{1,0:T(8,128)(2,1)S(1)}, u32[]{:S(2)}, u32[]{:S(2)}) collective-permute-start(bf16[64,1152]{1,0:T(8,128)(2,1)S(1)} %get-tuple-element.70), channel_id=1, source_target_pairs={{0,6},{1,7},{2,0},{3,1},{4,2},{5,3},{6,4},{7,5},{8,14},{9,15},{10,... | collective-permute-start | bytes 442376 | tf_op jit(solution)/shard_map/ppermute | solution.py:561
  68.5 5.6 %latent_gradient.1 = bf16[2048,1024]{1,0:T(8,128)(2,1)} custom-call(bf16[2048,1024]{1,0:T(8,128)(2,1)S(1)} %get-tuple-element.71.pre_ref, bf16[1024,1024]{1,0:T(8,128)(2,1)S(1)} %get-tuple-element.72.weight_ref), custom_call_target="tpu_custom_call" | custom-call | flops 4294967296 | bytes 10485760 | tf_op jit(solution)/shard_map/latent_gradient/pallas_call | solution.py:517
  74.1 0.0 collective-permute-done.5
  74.1 0.0 collective-permute-done.6
  74.1 0.0 collective-permute-done.4
  74.1 0.0 collective-permute-done.7
  74.1 0.1 fusion.6
  74.3 0.9 %collective-permute-start.10 = (bf16[64,1152]{1,0:T(8,128)(2,1)S(1)}, bf16[64,1152]{1,0:T(8,128)(2,1)S(1)}, u32[]{:S(2)}, u32[]{:S(2)}) collective-permute-start(bf16[64,1152]{1,0:T(8,128)(2,1)S(1)} %get-tuple-element.86), channel_id=1, source_target_pairs={{0,16},{1,17},{2,18},{3,19},{4,20},{5,21},{6,22},{7,23},{8,24},{9,... | collective-permute-start | bytes 442376 | tf_op jit(solution)/shard_map/ppermute | solution.py:561
  75.2 2.5 %collective-permute-start.9 = (bf16[64,1152]{1,0:T(8,128)(2,1)S(1)}, bf16[64,1152]{1,0:T(8,128)(2,1)S(1)}, u32[]{:S(2)}, u32[]{:S(2)}) collective-permute-start(bf16[64,1152]{1,0:T(8,128)(2,1)S(1)} %get-tuple-element.85), channel_id=1, source_target_pairs={{0,24},{1,25},{2,26},{3,27},{4,28},{5,29},{6,30},{7,31},{8,16},{9,... | collective-permute-start | bytes 442376 | tf_op jit(solution)/shard_map/ppermute | solution.py:561
  77.7 0.2 collective-permute-start.8
  77.9 3.7 %collective-permute-done.10 = bf16[64,1152]{1,0:T(8,128)(2,1)S(1)} collective-permute-done((bf16[64,1152]{1,0:T(8,128)(2,1)S(1)}, bf16[64,1152]{1,0:T(8,128)(2,1)S(1)}, u32[]{:S(2)}, u32[]{:S(2)}) %collective-permute-start.10) | collective-permute-done | bytes 147488 | tf_op jit(solution)/shard_map/ppermute | solution.py:561
  81.6 1.5 %collective-permute-done.9 = bf16[64,1152]{1,0:T(8,128)(2,1)S(1)} collective-permute-done((bf16[64,1152]{1,0:T(8,128)(2,1)S(1)}, bf16[64,1152]{1,0:T(8,128)(2,1)S(1)}, u32[]{:S(2)}, u32[]{:S(2)}) %collective-permute-start.9) | collective-permute-done | bytes 147488 | tf_op jit(solution)/shard_map/ppermute | solution.py:561
  83.1 0.0 collective-permute-done.8
  83.1 0.1 add_convert_fusion.1.own_ref
  83.2 0.9 %collective-permute-start.13 = (bf16[64,1152]{1,0:T(8,128)(2,1)S(1)}, bf16[64,1152]{1,0:T(8,128)(2,1)S(1)}, u32[]{:S(2)}, u32[]{:S(2)}) collective-permute-start(bf16[64,1152]{1,0:T(8,128)(2,1)S(1)} %add_convert_fusion.1.own_ref), channel_id=1, source_target_pairs={{0,64},{1,65},{2,66},{3,67},{4,68},{5,69},{6,70},{7,71},{8,72},{9,... | collective-permute-start | bytes 442376 | tf_op jit(solution)/shard_map/ppermute | solution.py:561
  84.1 2.1 %collective-permute-start.12 = (bf16[64,1152]{1,0:T(8,128)(2,1)S(1)}, bf16[64,1152]{1,0:T(8,128)(2,1)S(1)}, u32[]{:S(2)}, u32[]{:S(2)}) collective-permute-start(bf16[64,1152]{1,0:T(8,128)(2,1)S(1)} %add_convert_fusion.1.own_ref), channel_id=1, source_target_pairs={{0,96},{1,97},{2,98},{3,99},{4,100},{5,101},{6,102},{7,103},{8,104... | collective-permute-start | bytes 442376 | tf_op jit(solution)/shard_map/ppermute | solution.py:561
  86.2 0.6 collective-permute-start.11
  86.7 3.3 %collective-permute-done.13.refs_2_ = bf16[64,1152]{1,0:T(8,128)(2,1)S(1)} collective-permute-done((bf16[64,1152]{1,0:T(8,128)(2,1)S(1)}, bf16[64,1152]{1,0:T(8,128)(2,1)S(1)}, u32[]{:S(2)}, u32[]{:S(2)}) %collective-permute-start.13) | collective-permute-done | bytes 147488 | tf_op jit(solution)/shard_map/ppermute | solution.py:561
  90.0 1.5 %collective-permute-done.12.refs_1_ = bf16[64,1152]{1,0:T(8,128)(2,1)S(1)} collective-permute-done((bf16[64,1152]{1,0:T(8,128)(2,1)S(1)}, bf16[64,1152]{1,0:T(8,128)(2,1)S(1)}, u32[]{:S(2)}, u32[]{:S(2)}) %collective-permute-start.12) | collective-permute-done | bytes 147488 | tf_op jit(solution)/shard_map/ppermute | solution.py:561
  91.5 0.0 collective-permute-done.11.refs_0_
  91.5 0.8 finish.1
  (3 shorter events, 0.1 us)
Async XLA Ops:
  11.6 17.9 %all-to-all-start = ((f16[8,112,256]{2,1,0:T(8,128)(2,1)}), f16[8,112,256]{2,1,0:T(8,128)(2,1)S(1)}, u32[]{:S(2)}, u32[]{:S(2)}) async-start(f16[8,112,256]{2,1,0:T(8,128)(2,1)} %multiply_convert_fusion), calls=%async_computation | async-start | bytes 917504 | tf_op jit(solution)/shard_map/all_to_all | solution.py:607
  18.7 11.0 %copy-start.2 = (f32[100,2048]{1,0:T(8,128)S(1)}, f32[100,2048]{1,0:T(8,128)}, u32[]{:S(2)}) copy-start(f32[100,2048]{1,0:T(8,128)} %observed_ref.1) | copy-start | bytes 2457604
  18.7 11.0 %copy-start.3 = (f32[2048]{0:T(1024)S(1)}, f32[2048]{0:T(1024)}, u32[]{:S(2)}) copy-start(f32[2048]{0:T(1024)} %param.9) | copy-start | bytes 24580
  31.6 13.4 %all-to-all-start.1 = ((bf16[8,112,256]{2,1,0:T(8,128)(2,1)}), bf16[8,112,256]{2,1,0:T(8,128)(2,1)S(1)}, u32[]{:S(2)}, u32[]{:S(2)}) async-start(bf16[8,112,256]{2,1,0:T(8,128)(2,1)} %pairs.1), calls=%async_computation.1 | async-start | bytes 917504 | tf_op jit(solution)/shard_map/all_to_all | solution.py:612
  35.2 2.2 %copy-start.1 = (bf16[1,2048,1024]{2,1,0:T(8,128)(2,1)S(1)}, bf16[1,2048,1024]{2,1,0:T(8,128)(2,1)}, u32[]{:S(2)}) copy-start(bf16[1,2048,1024]{2,1,0:T(8,128)(2,1)} %param.5) | copy-start | bytes 12582916
  38.6 2.0 %copy-start = (bf16[1024,2048]{1,0:T(8,128)(2,1)}, bf16[1024,2048]{1,0:T(8,128)(2,1)S(1)}, u32[]{:S(2)}) copy-start(bf16[1024,2048]{1,0:T(8,128)(2,1)S(1)} %turned.1.turned_hbm) | copy-start | bytes 12582916
  50.0 3.0 %collective-permute-start = (bf16[256,1152]{1,0:T(8,128)(2,1)S(1)}, bf16[256,1152]{1,0:T(8,128)(2,1)S(1)}, u32[]{:S(2)}, u32[]{:S(2)}) collective-permute-start(bf16[256,1152]{1,0:T(8,128)(2,1)S(1)} %get-tuple-element.56), channel_id=1, source_target_pairs={{0,1},{1,0},{2,3},{3,2},{4,5},{5,4},{6,7},{7,6},{8,9},{9,8},{10,11... | collective-permute-start | bytes 1769480 | tf_op jit(solution)/shard_map/ppermute | solution.py:561
  55.5 8.3 %collective-permute-start.1 = (bf16[256,1152]{1,0:T(8,128)(2,1)S(1)}, bf16[256,1152]{1,0:T(8,128)(2,1)S(1)}, u32[]{:S(2)}, u32[]{:S(2)}) collective-permute-start(bf16[256,1152]{1,0:T(8,128)(2,1)S(1)} %get-tuple-element.64), channel_id=1, source_target_pairs={{0,1},{1,0},{2,3},{3,2},{4,5},{5,4},{6,7},{7,6},{8,9},{9,8},{10,11... | collective-permute-start | bytes 1769480 | tf_op jit(solution)/shard_map/ppermute | solution.py:561
  56.1 8.1 %collective-permute-start.2 = (bf16[64,1152]{1,0:T(8,128)(2,1)S(1)}, bf16[64,1152]{1,0:T(8,128)(2,1)S(1)}, u32[]{:S(2)}, u32[]{:S(2)}) collective-permute-start(bf16[64,1152]{1,0:T(8,128)(2,1)S(1)} %get-tuple-element.65), channel_id=1, source_target_pairs={{0,2},{1,3},{2,4},{3,5},{4,6},{5,7},{6,0},{7,1},{8,10},{9,11},{10,... | collective-permute-start | bytes 442376 | tf_op jit(solution)/shard_map/ppermute | solution.py:561
  58.0 6.7 %collective-permute-start.3 = (bf16[64,1152]{1,0:T(8,128)(2,1)S(1)}, bf16[64,1152]{1,0:T(8,128)(2,1)S(1)}, u32[]{:S(2)}, u32[]{:S(2)}) collective-permute-start(bf16[64,1152]{1,0:T(8,128)(2,1)S(1)} %get-tuple-element.66), channel_id=1, source_target_pairs={{0,6},{1,7},{2,0},{3,1},{4,2},{5,3},{6,4},{7,5},{8,14},{9,15},{10,... | collective-permute-start | bytes 442376 | tf_op jit(solution)/shard_map/ppermute | solution.py:561
  60.2 13.9 %collective-permute-start.5 = (bf16[64,1152]{1,0:T(8,128)(2,1)S(1)}, bf16[64,1152]{1,0:T(8,128)(2,1)S(1)}, u32[]{:S(2)}, u32[]{:S(2)}) collective-permute-start(bf16[64,1152]{1,0:T(8,128)(2,1)S(1)} %get-tuple-element.68), channel_id=1, source_target_pairs={{0,6},{1,7},{2,0},{3,1},{4,2},{5,3},{6,4},{7,5},{8,14},{9,15},{10,... | collective-permute-start | bytes 442376 | tf_op jit(solution)/shard_map/ppermute | solution.py:561
  62.2 11.9 %collective-permute-start.6 = (bf16[64,1152]{1,0:T(8,128)(2,1)S(1)}, bf16[64,1152]{1,0:T(8,128)(2,1)S(1)}, u32[]{:S(2)}, u32[]{:S(2)}) collective-permute-start(bf16[64,1152]{1,0:T(8,128)(2,1)S(1)} %get-tuple-element.69), channel_id=1, source_target_pairs={{0,2},{1,3},{2,4},{3,5},{4,6},{5,7},{6,0},{7,1},{8,10},{9,11},{10,... | collective-permute-start | bytes 442376 | tf_op jit(solution)/shard_map/ppermute | solution.py:561
  64.8 9.3 %collective-permute-start.4 = (bf16[64,1152]{1,0:T(8,128)(2,1)S(1)}, bf16[64,1152]{1,0:T(8,128)(2,1)S(1)}, u32[]{:S(2)}, u32[]{:S(2)}) collective-permute-start(bf16[64,1152]{1,0:T(8,128)(2,1)S(1)} %get-tuple-element.67), channel_id=1, source_target_pairs={{0,2},{1,3},{2,4},{3,5},{4,6},{5,7},{6,0},{7,1},{8,10},{9,11},{10,... | collective-permute-start | bytes 442376 | tf_op jit(solution)/shard_map/ppermute | solution.py:561
  66.8 7.3 %collective-permute-start.7 = (bf16[64,1152]{1,0:T(8,128)(2,1)S(1)}, bf16[64,1152]{1,0:T(8,128)(2,1)S(1)}, u32[]{:S(2)}, u32[]{:S(2)}) collective-permute-start(bf16[64,1152]{1,0:T(8,128)(2,1)S(1)} %get-tuple-element.70), channel_id=1, source_target_pairs={{0,6},{1,7},{2,0},{3,1},{4,2},{5,3},{6,4},{7,5},{8,14},{9,15},{10,... | collective-permute-start | bytes 442376 | tf_op jit(solution)/shard_map/ppermute | solution.py:561
  74.3 7.3 %collective-permute-start.10 = (bf16[64,1152]{1,0:T(8,128)(2,1)S(1)}, bf16[64,1152]{1,0:T(8,128)(2,1)S(1)}, u32[]{:S(2)}, u32[]{:S(2)}) collective-permute-start(bf16[64,1152]{1,0:T(8,128)(2,1)S(1)} %get-tuple-element.86), channel_id=1, source_target_pairs={{0,16},{1,17},{2,18},{3,19},{4,20},{5,21},{6,22},{7,23},{8,24},{9,... | collective-permute-start | bytes 442376 | tf_op jit(solution)/shard_map/ppermute | solution.py:561
  75.2 7.8 %collective-permute-start.9 = (bf16[64,1152]{1,0:T(8,128)(2,1)S(1)}, bf16[64,1152]{1,0:T(8,128)(2,1)S(1)}, u32[]{:S(2)}, u32[]{:S(2)}) collective-permute-start(bf16[64,1152]{1,0:T(8,128)(2,1)S(1)} %get-tuple-element.85), channel_id=1, source_target_pairs={{0,24},{1,25},{2,26},{3,27},{4,28},{5,29},{6,30},{7,31},{8,16},{9,... | collective-permute-start | bytes 442376 | tf_op jit(solution)/shard_map/ppermute | solution.py:561
  77.7 5.4 %collective-permute-start.8 = (bf16[64,1152]{1,0:T(8,128)(2,1)S(1)}, bf16[64,1152]{1,0:T(8,128)(2,1)S(1)}, u32[]{:S(2)}, u32[]{:S(2)}) collective-permute-start(bf16[64,1152]{1,0:T(8,128)(2,1)S(1)} %get-tuple-element.85), channel_id=1, source_target_pairs={{0,8},{1,9},{2,10},{3,11},{4,12},{5,13},{6,14},{7,15},{8,0},{9,1},... | collective-permute-start | bytes 442376 | tf_op jit(solution)/shard_map/ppermute | solution.py:561
  83.2 6.8 %collective-permute-start.13 = (bf16[64,1152]{1,0:T(8,128)(2,1)S(1)}, bf16[64,1152]{1,0:T(8,128)(2,1)S(1)}, u32[]{:S(2)}, u32[]{:S(2)}) collective-permute-start(bf16[64,1152]{1,0:T(8,128)(2,1)S(1)} %add_convert_fusion.1.own_ref), channel_id=1, source_target_pairs={{0,64},{1,65},{2,66},{3,67},{4,68},{5,69},{6,70},{7,71},{8,72},{9,... | collective-permute-start | bytes 442376 | tf_op jit(solution)/shard_map/ppermute | solution.py:561
  84.1 7.4 %collective-permute-start.12 = (bf16[64,1152]{1,0:T(8,128)(2,1)S(1)}, bf16[64,1152]{1,0:T(8,128)(2,1)S(1)}, u32[]{:S(2)}, u32[]{:S(2)}) collective-permute-start(bf16[64,1152]{1,0:T(8,128)(2,1)S(1)} %add_convert_fusion.1.own_ref), channel_id=1, source_target_pairs={{0,96},{1,97},{2,98},{3,99},{4,100},{5,101},{6,102},{7,103},{8,104... | collective-permute-start | bytes 442376 | tf_op jit(solution)/shard_map/ppermute | solution.py:561
  86.2 5.3 %collective-permute-start.11 = (bf16[64,1152]{1,0:T(8,128)(2,1)S(1)}, bf16[64,1152]{1,0:T(8,128)(2,1)S(1)}, u32[]{:S(2)}, u32[]{:S(2)}) collective-permute-start(bf16[64,1152]{1,0:T(8,128)(2,1)S(1)} %add_convert_fusion.1.own_ref), channel_id=1, source_target_pairs={{0,32},{1,33},{2,34},{3,35},{4,36},{5,37},{6,38},{7,39},{8,40},{9,... | collective-permute-start | bytes 442376 | tf_op jit(solution)/shard_map/ppermute | solution.py:561

commit v13 on v12

--- a/solution.py
+++ b/solution.py
@@ -493,18 +493,19 @@
     )(pinned(weight), grad_pre, turned_now, second)
 
 
-def latent_kernel(pre_ref, weight_ref, out_ref, result_ref, sems):
-    nodes, width = pre_ref.shape
+def latent_kernel(pre_ref, weight_ref, *refs, begin):
+    out_ref, result_ref, sems = refs[-3:]
+    width = pre_ref.shape[1]
     stores = []
-    for row in range(0, nodes, ROWS):
-        rows = slice(row, row + ROWS)
+    for row in range(0, result_ref.shape[0], ROWS):
+        rows = slice(begin + row, begin + row + ROWS)
         for start in range(0, width, COLS):
             columns = slice(start, start + COLS)
-            result_ref[rows, columns] = lax.dot_general(
+            result_ref[row : row + ROWS, columns] = lax.dot_general(
                 pre_ref[rows, :], weight_ref[columns, :], NT, preferred_element_type=f32
             ).astype(bf16)
         store = pltpu.make_async_copy(
-            result_ref.at[pl.ds(row, ROWS)], out_ref.at[pl.ds(row, ROWS)], sems.at[row // ROWS]
+            result_ref.at[pl.ds(row, ROWS)], out_ref.at[pl.ds(begin + row, ROWS)], sems.at[row // ROWS]
         )
         store.start()
         stores.append(store)
@@ -512,18 +513,21 @@
         store.wait()
 
 
-def latent_gradient(grad_pre, weight):
+def latent_gradient(grad_pre, weight, begin, so_far=None):
     nodes, width = grad_pre.shape
-    return pl.pallas_call(
-        latent_kernel,
-        in_specs=[vmem, vmem],
+    half = nodes // 2
+    more = [] if so_far is None else [so_far]
+    return pl.pallas_call(
+        functools.partial(latent_kernel, begin=begin),
+        in_specs=[vmem, vmem] + [anywhere] * len(more),
         out_specs=anywhere,
         out_shape=pltpu.HBM((nodes, width), bf16),
-        scratch_shapes=[pltpu.VMEM((nodes, width), bf16), pltpu.SemaphoreType.DMA((nodes // ROWS,))],
+        input_output_aliases={2: 0} if more else {},
+        scratch_shapes=[pltpu.VMEM((half, width), bf16), pltpu.SemaphoreType.DMA((half // ROWS,))],
         compiler_params=params(12),
-        cost_estimate=cost(2 * nodes * width * width, 10 << 20),
+        cost_estimate=cost(nodes * width * width, 5 << 20),
         name="latent_gradient",
-    )(grad_pre, weight)
+    )(grad_pre, weight, *more)
 
 
 def finish_kernel(own_ref, *refs, factor):
@@ -623,12 +627,13 @@
     above = (above + upward.astype(f32)).astype(bf16)
     below = (below + downward.astype(f32)).astype(bf16)
     above, below, grad_pre = lax.optimization_barrier((above, below, grad_pre))
-    grad_latent = latent_gradient(grad_pre, weight_copy)
+    grad_latent = latent_gradient(grad_pre, weight_copy, 0)
     own = summed(own, [up(above), from_above])
     other = summed(other, [from_below, down(below)])
     blocks = jnp.stack([own, other]).astype(bf16)
     blocks, grad_latent = lax.optimization_barrier((blocks, grad_latent))
-    block = over_x(blocks)
+    grad_latent = latent_gradient(grad_pre, weight_copy, nodes // 2, grad_latent)
+    block, grad_latent = lax.optimization_barrier((over_x(blocks), grad_latent))
     factor = 1.0 / math.sqrt(members * nodes * groups)
     first, second = finish(block, over_y(block), width, variables, factor)
     return grad_latent[None], first, second

time: 92.7 us -> 91.9 us (level)
  waiting for transfers between devices: 20.2 us -> 17.1 us
  starting transfers between devices: 28.2 us -> 29.4 us
  Pallas kernels: 37.1 us -> 38.3 us
    ppermute x14, waiting for transfers between devices: 10.8 us -> 7.68 us  [moved(): return lax.ppermute(value, ('member', 'grid'), moves)]
    ppermute x14, starting transfers between devices: 17.6 us -> 18.8 us  [moved(): return lax.ppermute(value, ('member', 'grid'), moves)]
    pallas_call x1 -> x2, Pallas kernels: 5.59 us -> 6.76 us  [latent_gradient(): pl.pallas_call(functools.partial(latent_kernel, begin=begin), in_specs=[v...]
  transfers between devices with their start and end apart: 16 -> 16, of which waited for: 8 -> 8; matrix products, arithmetic and copies ran while one was open for 0% -> 0% of each run, Pallas kernels for 18% -> 20%
where the time goes in v13:
time: 91.9 us; the launch traced here: 91.5 us
  Pallas kernels  38.3 us (42%)
  starting transfers between devices  29.4 us (32%)
  waiting for transfers between devices  17.1 us (19%)
  local copies, waits for them, and re-layouts  4.27 us (5%)
  other arithmetic  1.54 us (2%)
    ppermute x14, starting transfers between devices, moved(): return lax.ppermute(value, ('member', 'grid'), moves)  18.8 us
    pallas_call x1, Pallas kernels, forward(): pl.pallas_call(forward_kernel, in_specs=[anywhere] * 3, out_specs=[vmem,...  10.1 us
    ppermute x14, waiting for transfers between devices, moved(): return lax.ppermute(value, ('member', 'grid'), moves)  7.68 us
    all_to_all x1, starting transfers between devices, body(): blocks = lax.all_to_all(blocks, 'member', 0, 0, tiled=True)  7.02 us
    pallas_call x2, Pallas kernels, latent_gradient(): pl.pallas_call(functools.partial(latent_kernel, begin=begin), in_specs=[v...  6.76 us
    pallas_call x1, Pallas kernels, gates(): pl.pallas_call(gate_kernel, in_specs=[anywhere], out_specs=[anywhere] * 2...  5.78 us
    all_to_all x1, waiting for transfers between devices, body(): blocks = lax.all_to_all(blocks, 'member', 0, 0, tiled=True)  5.07 us
    pallas_call x1, Pallas kernels, send_a(): pl.pallas_call(send_a_kernel, in_specs=[smem, vmem, anywhere, anywhere, a...  5.02 us
  transfers between devices with their start and end apart: 16, of which 8 were waited for; matrix products, arithmetic and copies ran while one was open for 0% of the time, Pallas kernels for 20%

profile of v13, /device:TPU:0, one launch (start us, length us, event | category | flops | bytes accessed | tf_op | source)
XLA Modules:
  0.0 91.5 jit_solution(13876503265621997640)
XLA Ops:
  0.6 10.1 %forward.1 = (f32[8,112,256]{2,1,0:T(8,128)S(1)}, bf16[2048,1024]{1,0:T(8,128)(2,1)}, bf16[1024,128]{1,0:T(8,128)(2,1)S(1)}) custom-call(bf16[2048,1024]{1,0:T(8,128)(2,1)} %bitcast.16, bf16[1024,1024]{1,0:T(8,128)(2,1)} %weight_hbm.1, bf16[100,1024]{1,0:T(8,128)(2,1)} %bitcast.20), custom_call_target="tpu_custom_call" | custom-call | flops 4831838208 | bytes 20971520 | tf_op jit(solution)/shard_map/forward/pallas_call | solution.py:102
  10.7 0.9 %multiply_convert_fusion = f16[8,112,256]{2,1,0:T(8,128)(2,1)} fusion(f32[8,112,256]{2,1,0:T(8,128)S(1)} %get-tuple-element.42), kind=kLoop, calls=%fused_computation.3 | loop fusion | flops 458752 | bytes 1376256 | tf_op jit(solution)/shard_map/convert_element_type | solution.py:610
  11.6 7.0 %all-to-all-start = ((f16[8,112,256]{2,1,0:T(8,128)(2,1)}), f16[8,112,256]{2,1,0:T(8,128)(2,1)S(1)}, u32[]{:S(2)}, u32[]{:S(2)}) async-start(f16[8,112,256]{2,1,0:T(8,128)(2,1)} %multiply_convert_fusion), calls=%async_computation | async-start | bytes 917504 | tf_op jit(solution)/shard_map/all_to_all | solution.py:611
  18.7 0.0 copy-start.2
  18.7 0.0 copy-start.3
  18.7 5.8 %gates.1 = (bf16[8,2048,128]{2,1,0:T(8,128)(2,1)}, bf16[2048,1024]{1,0:T(8,128)(2,1)}) custom-call(bf16[2048,1024]{1,0:T(8,128)(2,1)} %get-tuple-element.45.pre_hbm), custom_call_target="tpu_custom_call" | custom-call | bytes 12582912 | tf_op jit(solution)/shard_map/gates/pallas_call | solution.py:162
  24.5 5.1 %all-to-all-done = f16[8,112,256]{2,1,0:T(8,128)(2,1)S(1)} async-done(((f16[8,112,256]{2,1,0:T(8,128)(2,1)}), f16[8,112,256]{2,1,0:T(8,128)(2,1)S(1)}, u32[]{:S(2)}, u32[]{:S(2)}) %all-to-all-start) | async-done | bytes 458784 | tf_op jit(solution)/shard_map/all_to_all | solution.py:611
  29.5 0.1 convert_multiply_fusion.blocks_ref
  29.6 0.0 copy-done.2
  29.6 0.0 copy-done.3
  29.6 1.9 %pairs.1 = bf16[8,112,256]{2,1,0:T(8,128)(2,1)} custom-call(s32[1]{0:T(128)} %bitcast.1.place_ref, f32[8,112,256]{2,1,0:T(8,128)S(1)} %convert_multiply_fusion.blocks_ref, f32[100,2048]{1,0:T(8,128)S(1)} %copy-done.2, f32[1,2048]{1,0:T(1,128)S(1)} %bitcast.18), custom_call_target="tpu_custom_call" | custom-call | flops 4194304 | bytes 2097152 | tf_op jit(solution)/shard_map/pairs/pallas_call | solution.py:223
  31.6 3.7 %all-to-all-start.1 = ((bf16[8,112,256]{2,1,0:T(8,128)(2,1)}), bf16[8,112,256]{2,1,0:T(8,128)(2,1)S(1)}, u32[]{:S(2)}, u32[]{:S(2)}) async-start(bf16[8,112,256]{2,1,0:T(8,128)(2,1)} %pairs.1), calls=%async_computation.1 | async-start | bytes 917504 | tf_op jit(solution)/shard_map/all_to_all | solution.py:616
  35.2 0.0 copy-start.1
  35.2 2.2 %copy-done.1 = bf16[1,2048,1024]{2,1,0:T(8,128)(2,1)S(1)} copy-done((bf16[1,2048,1024]{2,1,0:T(8,128)(2,1)S(1)}, bf16[1,2048,1024]{2,1,0:T(8,128)(2,1)}, u32[]{:S(2)}) %copy-start.1) | copy-done | bytes 4194328
  37.4 1.1 %turned.1.turned_hbm = bf16[1024,2048]{1,0:T(8,128)(2,1)S(1)} custom-call(s32[1]{0:T(128)} %bitcast.grid_ref, bf16[2048,1024]{1,0:T(8,128)(2,1)S(1)} %bitcast.17), custom_call_target="tpu_custom_call" | custom-call | bytes 8388608 | tf_op jit(solution)/shard_map/turned/pallas_call | solution.py:269
  38.6 0.0 copy-start
  38.6 2.0 %copy-done = bf16[1024,2048]{1,0:T(8,128)(2,1)} copy-done((bf16[1024,2048]{1,0:T(8,128)(2,1)}, bf16[1024,2048]{1,0:T(8,128)(2,1)S(1)}, u32[]{:S(2)}) %copy-start) | copy-done | bytes 4194328
  40.6 4.4 %all-to-all-done.1.low_ref = bf16[8,112,256]{2,1,0:T(8,128)(2,1)S(1)} async-done(((bf16[8,112,256]{2,1,0:T(8,128)(2,1)}), bf16[8,112,256]{2,1,0:T(8,128)(2,1)S(1)}, u32[]{:S(2)}, u32[]{:S(2)}) %all-to-all-start.1) | async-done | bytes 458784 | tf_op jit(solution)/shard_map/all_to_all | solution.py:616
  44.9 5.0 %send_a.1 = (bf16[2048,1024]{1,0:T(8,128)(2,1)S(1)}, bf16[256,1152]{1,0:T(8,128)(2,1)S(1)}, bf16[256,128]{1,0:T(8,128)(2,1)S(1)}, bf16[128,2048]{1,0:T(8,128)(2,1)S(1)}, bf16[256,2048]{1,0:T(8,128)(2,1)S(1)}) custom-call(s32[1]{0:T(128)} %bitcast.grid_ref, bf16[8,112,256]{2,1,0:T(8,128)(2,1)S(1)} %all-to-all-done.1.low_ref, bf16[1024,2048]{1,0:T(8,128)(2,1)} %copy-done, ...), custom_call_target="tpu_custom_call" | custom-call | flops 1879048192 | bytes 8388608 | tf_op jit(solution)/shard_map/send_a/pallas_call | solution.py:427
  50.0 0.1 collective-permute-start
  50.1 2.9 %keep_a.1 = (bf16[256,1152]{1,0:T(8,128)(2,1)S(1)}, bf16[256,2048]{1,0:T(8,128)(2,1)S(1)}, bf16[4,2048,128]{2,1,0:T(8,128)(2,1)S(1)}) custom-call(s32[1]{0:T(128)} %bitcast.grid_ref, bf16[1024,2048]{1,0:T(8,128)(2,1)} %copy-done, bf16[8,2048,128]{2,1,0:T(8,128)(2,1)} %get-tuple-element.52.hidden_hbm, bf16[2048,1024]{1,0:T(8,128)(2,1)S(1)} %get-tuple-element.73.pre_ref, ...), custom_call_target="tpu_custom_call" | custom-call | flops 1073741824 | bytes 4194304 | tf_op jit(solution)/shard_map/keep_a/pallas_call | solution.py:456
  53.0 0.0 collective-permute-done
  53.0 0.1 add_convert_fusion
  53.2 2.3 %send_b.1 = (bf16[256,1152]{1,0:T(8,128)(2,1)S(1)}, bf16[256,128]{1,0:T(8,128)(2,1)S(1)}, bf16[256,2048]{1,0:T(8,128)(2,1)S(1)}) custom-call(s32[1]{0:T(128)} %bitcast.grid_ref, bf16[1024,2048]{1,0:T(8,128)(2,1)} %copy-done, bf16[2048,1024]{1,0:T(8,128)(2,1)S(1)} %get-tuple-element.73.pre_ref, bf16[128,2048]{1,0:T(8,128)(2,1)S(1)} %get-tuple-element.60.flat_ref, ...), custom_call_target="tpu_custom_call" | custom-call | flops 1073741824 | bytes 4194304 | tf_op jit(solution)/shard_map/send_b/pallas_call | solution.py:470
  55.5 0.6 collective-permute-start.1
  56.1 1.9 %collective-permute-start.2 = (bf16[64,1152]{1,0:T(8,128)(2,1)S(1)}, bf16[64,1152]{1,0:T(8,128)(2,1)S(1)}, u32[]{:S(2)}, u32[]{:S(2)}) collective-permute-start(bf16[64,1152]{1,0:T(8,128)(2,1)S(1)} %get-tuple-element.67), channel_id=1, source_target_pairs={{0,2},{1,3},{2,4},{3,5},{4,6},{5,7},{6,0},{7,1},{8,10},{9,11},{10,... | collective-permute-start | bytes 442376 | tf_op jit(solution)/shard_map/ppermute | solution.py:565
  58.0 2.1 %collective-permute-start.3 = (bf16[64,1152]{1,0:T(8,128)(2,1)S(1)}, bf16[64,1152]{1,0:T(8,128)(2,1)S(1)}, u32[]{:S(2)}, u32[]{:S(2)}) collective-permute-start(bf16[64,1152]{1,0:T(8,128)(2,1)S(1)} %get-tuple-element.68), channel_id=1, source_target_pairs={{0,6},{1,7},{2,0},{3,1},{4,2},{5,3},{6,4},{7,5},{8,14},{9,15},{10,... | collective-permute-start | bytes 442376 | tf_op jit(solution)/shard_map/ppermute | solution.py:565
  60.2 2.0 %collective-permute-start.5 = (bf16[64,1152]{1,0:T(8,128)(2,1)S(1)}, bf16[64,1152]{1,0:T(8,128)(2,1)S(1)}, u32[]{:S(2)}, u32[]{:S(2)}) collective-permute-start(bf16[64,1152]{1,0:T(8,128)(2,1)S(1)} %get-tuple-element.70), channel_id=1, source_target_pairs={{0,6},{1,7},{2,0},{3,1},{4,2},{5,3},{6,4},{7,5},{8,14},{9,15},{10,... | collective-permute-start | bytes 442376 | tf_op jit(solution)/shard_map/ppermute | solution.py:565
  62.2 0.0 collective-permute-start.6
  62.2 1.6 %keep_b.1 = (bf16[256,1152]{1,0:T(8,128)(2,1)S(1)}, bf16[1024,1024]{1,0:T(8,128)(2,1)S(1)}) custom-call(bf16[1024,1024]{1,0:T(8,128)(2,1)} %weight_hbm.1, bf16[2048,1024]{1,0:T(8,128)(2,1)S(1)} %get-tuple-element.73.pre_ref, bf16[256,2048]{1,0:T(8,128)(2,1)S(1)} %get-tuple-element.63.turned_ref, bf16[256,128]{1,0:T(8,128)(2,1)S(1)} %get-tuple-element.64.second_ref), custom_call_target="tpu_custom_call" | custom-call | flops 1073741824 | bytes 4194304 | tf_op jit(solution)/shard_map/keep_b/pallas_call | solution.py:484
  63.8 0.0 collective-permute-done.1
  63.8 0.1 convert_add_fusion
  63.9 0.3 collective-permute-done.2
  64.2 0.5 collective-permute-done.3
  64.7 0.1 fusion.2
  64.8 2.0 %collective-permute-start.4 = (bf16[64,1152]{1,0:T(8,128)(2,1)S(1)}, bf16[64,1152]{1,0:T(8,128)(2,1)S(1)}, u32[]{:S(2)}, u32[]{:S(2)}) collective-permute-start(bf16[64,1152]{1,0:T(8,128)(2,1)S(1)} %get-tuple-element.69), channel_id=1, source_target_pairs={{0,2},{1,3},{2,4},{3,5},{4,6},{5,7},{6,0},{7,1},{8,10},{9,11},{10,... | collective-permute-start | bytes 442376 | tf_op jit(solution)/shard_map/ppermute | solution.py:565
  66.8 1.4 %collective-permute-start.7 = (bf16[64,1152]{1,0:T(8,128)(2,1)S(1)}, bf16[64,1152]{1,0:T(8,128)(2,1)S(1)}, u32[]{:S(2)}, u32[]{:S(2)}) collective-permute-start(bf16[64,1152]{1,0:T(8,128)(2,1)S(1)} %get-tuple-element.72), channel_id=1, source_target_pairs={{0,6},{1,7},{2,0},{3,1},{4,2},{5,3},{6,4},{7,5},{8,14},{9,15},{10,... | collective-permute-start | bytes 442376 | tf_op jit(solution)/shard_map/ppermute | solution.py:565
  68.3 3.4 %latent_gradient.2.refs_0_ = bf16[2048,1024]{1,0:T(8,128)(2,1)} custom-call(bf16[2048,1024]{1,0:T(8,128)(2,1)S(1)} %get-tuple-element.73.pre_ref, bf16[1024,1024]{1,0:T(8,128)(2,1)S(1)} %get-tuple-element.74.weight_ref), custom_call_target="tpu_custom_call" | custom-call | flops 2147483648 | bytes 5242880 | tf_op jit(solution)/shard_map/latent_gradient/pallas_call | solution.py:520
  71.7 0.0 collective-permute-done.5
  71.7 0.0 collective-permute-done.6
  71.7 0.0 collective-permute-done.4
  71.7 0.3 collective-permute-done.7
  72.0 0.1 fusion.6
  72.1 0.9 collective-permute-start.9
  73.0 0.2 collective-permute-start.8
  73.3 3.9 %collective-permute-start.10 = (bf16[64,1152]{1,0:T(8,128)(2,1)S(1)}, bf16[64,1152]{1,0:T(8,128)(2,1)S(1)}, u32[]{:S(2)}, u32[]{:S(2)}) collective-permute-start(bf16[64,1152]{1,0:T(8,128)(2,1)S(1)} %get-tuple-element.90), channel_id=1, source_target_pairs={{0,16},{1,17},{2,18},{3,19},{4,20},{5,21},{6,22},{7,23},{8,24},{9,... | collective-permute-start | bytes 442376 | tf_op jit(solution)/shard_map/ppermute | solution.py:565
  77.1 3.4 %latent_gradient.3 = bf16[2048,1024]{1,0:T(8,128)(2,1)} custom-call(bf16[2048,1024]{1,0:T(8,128)(2,1)S(1)} %get-tuple-element.73.pre_ref, bf16[1024,1024]{1,0:T(8,128)(2,1)S(1)} %get-tuple-element.74.weight_ref, bf16[2048,1024]{1,0:T(8,128)(2,1)} %latent_gradient.2.refs_0_), custom_call_target="tpu_custom_call", output_to_operand_aliasing={{}: (2, {})} | custom-call | flops 2147483648 | bytes 5242880 | tf_op jit(solution)/shard_map/latent_gradient/pallas_call | solution.py:520
  80.5 1.8 %collective-permute-done.10 = bf16[64,1152]{1,0:T(8,128)(2,1)S(1)} collective-permute-done((bf16[64,1152]{1,0:T(8,128)(2,1)S(1)}, bf16[64,1152]{1,0:T(8,128)(2,1)S(1)}, u32[]{:S(2)}, u32[]{:S(2)}) %collective-permute-start.10) | collective-permute-done | bytes 147488 | tf_op jit(solution)/shard_map/ppermute | solution.py:565
  82.4 0.0 collective-permute-done.9
  82.4 0.0 collective-permute-done.8
  82.4 0.1 add_convert_fusion.1.own_ref
  82.4 0.9 %collective-permute-start.13 = (bf16[64,1152]{1,0:T(8,128)(2,1)S(1)}, bf16[64,1152]{1,0:T(8,128)(2,1)S(1)}, u32[]{:S(2)}, u32[]{:S(2)}) collective-permute-start(bf16[64,1152]{1,0:T(8,128)(2,1)S(1)} %add_convert_fusion.1.own_ref), channel_id=1, source_target_pairs={{0,64},{1,65},{2,66},{3,67},{4,68},{5,69},{6,70},{7,71},{8,72},{9,... | collective-permute-start | bytes 442376 | tf_op jit(solution)/shard_map/ppermute | solution.py:565
  83.4 2.1 %collective-permute-start.12 = (bf16[64,1152]{1,0:T(8,128)(2,1)S(1)}, bf16[64,1152]{1,0:T(8,128)(2,1)S(1)}, u32[]{:S(2)}, u32[]{:S(2)}) collective-permute-start(bf16[64,1152]{1,0:T(8,128)(2,1)S(1)} %add_convert_fusion.1.own_ref), channel_id=1, source_target_pairs={{0,96},{1,97},{2,98},{3,99},{4,100},{5,101},{6,102},{7,103},{8,104... | collective-permute-start | bytes 442376 | tf_op jit(solution)/shard_map/ppermute | solution.py:565
  85.4 0.6 collective-permute-start.11
  86.0 3.3 %collective-permute-done.13.refs_2_ = bf16[64,1152]{1,0:T(8,128)(2,1)S(1)} collective-permute-done((bf16[64,1152]{1,0:T(8,128)(2,1)S(1)}, bf16[64,1152]{1,0:T(8,128)(2,1)S(1)}, u32[]{:S(2)}, u32[]{:S(2)}) %collective-permute-start.13) | collective-permute-done | bytes 147488 | tf_op jit(solution)/shard_map/ppermute | solution.py:565
  89.3 1.5 %collective-permute-done.12.refs_1_ = bf16[64,1152]{1,0:T(8,128)(2,1)S(1)} collective-permute-done((bf16[64,1152]{1,0:T(8,128)(2,1)S(1)}, bf16[64,1152]{1,0:T(8,128)(2,1)S(1)}, u32[]{:S(2)}, u32[]{:S(2)}) %collective-permute-start.12) | collective-permute-done | bytes 147488 | tf_op jit(solution)/shard_map/ppermute | solution.py:565
  90.8 0.0 collective-permute-done.11.refs_0_
  90.8 0.8 finish.1
  (3 shorter events, 0.1 us)
Async XLA Ops:
  11.6 17.9 %all-to-all-start = ((f16[8,112,256]{2,1,0:T(8,128)(2,1)}), f16[8,112,256]{2,1,0:T(8,128)(2,1)S(1)}, u32[]{:S(2)}, u32[]{:S(2)}) async-start(f16[8,112,256]{2,1,0:T(8,128)(2,1)} %multiply_convert_fusion), calls=%async_computation | async-start | bytes 917504 | tf_op jit(solution)/shard_map/all_to_all | solution.py:611
  18.7 11.0 %copy-start.2 = (f32[100,2048]{1,0:T(8,128)S(1)}, f32[100,2048]{1,0:T(8,128)}, u32[]{:S(2)}) copy-start(f32[100,2048]{1,0:T(8,128)} %observed_ref.1) | copy-start | bytes 2457604
  18.7 11.0 %copy-start.3 = (f32[2048]{0:T(1024)S(1)}, f32[2048]{0:T(1024)}, u32[]{:S(2)}) copy-start(f32[2048]{0:T(1024)} %param.9) | copy-start | bytes 24580
  31.6 13.4 %all-to-all-start.1 = ((bf16[8,112,256]{2,1,0:T(8,128)(2,1)}), bf16[8,112,256]{2,1,0:T(8,128)(2,1)S(1)}, u32[]{:S(2)}, u32[]{:S(2)}) async-start(bf16[8,112,256]{2,1,0:T(8,128)(2,1)} %pairs.1), calls=%async_computation.1 | async-start | bytes 917504 | tf_op jit(solution)/shard_map/all_to_all | solution.py:616
  35.2 2.2 %copy-start.1 = (bf16[1,2048,1024]{2,1,0:T(8,128)(2,1)S(1)}, bf16[1,2048,1024]{2,1,0:T(8,128)(2,1)}, u32[]{:S(2)}) copy-start(bf16[1,2048,1024]{2,1,0:T(8,128)(2,1)} %param.5) | copy-start | bytes 12582916
  38.6 2.0 %copy-start = (bf16[1024,2048]{1,0:T(8,128)(2,1)}, bf16[1024,2048]{1,0:T(8,128)(2,1)S(1)}, u32[]{:S(2)}) copy-start(bf16[1024,2048]{1,0:T(8,128)(2,1)S(1)} %turned.1.turned_hbm) | copy-start | bytes 12582916
  50.0 3.0 %collective-permute-start = (bf16[256,1152]{1,0:T(8,128)(2,1)S(1)}, bf16[256,1152]{1,0:T(8,128)(2,1)S(1)}, u32[]{:S(2)}, u32[]{:S(2)}) collective-permute-start(bf16[256,1152]{1,0:T(8,128)(2,1)S(1)} %get-tuple-element.58), channel_id=1, source_target_pairs={{0,1},{1,0},{2,3},{3,2},{4,5},{5,4},{6,7},{7,6},{8,9},{9,8},{10,11... | collective-permute-start | bytes 1769480 | tf_op jit(solution)/shard_map/ppermute | solution.py:565
  55.5 8.3 %collective-permute-start.1 = (bf16[256,1152]{1,0:T(8,128)(2,1)S(1)}, bf16[256,1152]{1,0:T(8,128)(2,1)S(1)}, u32[]{:S(2)}, u32[]{:S(2)}) collective-permute-start(bf16[256,1152]{1,0:T(8,128)(2,1)S(1)} %get-tuple-element.66), channel_id=1, source_target_pairs={{0,1},{1,0},{2,3},{3,2},{4,5},{5,4},{6,7},{7,6},{8,9},{9,8},{10,11... | collective-permute-start | bytes 1769480 | tf_op jit(solution)/shard_map/ppermute | solution.py:565
  56.1 8.1 %collective-permute-start.2 = (bf16[64,1152]{1,0:T(8,128)(2,1)S(1)}, bf16[64,1152]{1,0:T(8,128)(2,1)S(1)}, u32[]{:S(2)}, u32[]{:S(2)}) collective-permute-start(bf16[64,1152]{1,0:T(8,128)(2,1)S(1)} %get-tuple-element.67), channel_id=1, source_target_pairs={{0,2},{1,3},{2,4},{3,5},{4,6},{5,7},{6,0},{7,1},{8,10},{9,11},{10,... | collective-permute-start | bytes 442376 | tf_op jit(solution)/shard_map/ppermute | solution.py:565
  58.0 6.7 %collective-permute-start.3 = (bf16[64,1152]{1,0:T(8,128)(2,1)S(1)}, bf16[64,1152]{1,0:T(8,128)(2,1)S(1)}, u32[]{:S(2)}, u32[]{:S(2)}) collective-permute-start(bf16[64,1152]{1,0:T(8,128)(2,1)S(1)} %get-tuple-element.68), channel_id=1, source_target_pairs={{0,6},{1,7},{2,0},{3,1},{4,2},{5,3},{6,4},{7,5},{8,14},{9,15},{10,... | collective-permute-start | bytes 442376 | tf_op jit(solution)/shard_map/ppermute | solution.py:565
  60.2 11.5 %collective-permute-start.5 = (bf16[64,1152]{1,0:T(8,128)(2,1)S(1)}, bf16[64,1152]{1,0:T(8,128)(2,1)S(1)}, u32[]{:S(2)}, u32[]{:S(2)}) collective-permute-start(bf16[64,1152]{1,0:T(8,128)(2,1)S(1)} %get-tuple-element.70), channel_id=1, source_target_pairs={{0,6},{1,7},{2,0},{3,1},{4,2},{5,3},{6,4},{7,5},{8,14},{9,15},{10,... | collective-permute-start | bytes 442376 | tf_op jit(solution)/shard_map/ppermute | solution.py:565
  62.2 9.5 %collective-permute-start.6 = (bf16[64,1152]{1,0:T(8,128)(2,1)S(1)}, bf16[64,1152]{1,0:T(8,128)(2,1)S(1)}, u32[]{:S(2)}, u32[]{:S(2)}) collective-permute-start(bf16[64,1152]{1,0:T(8,128)(2,1)S(1)} %get-tuple-element.71), channel_id=1, source_target_pairs={{0,2},{1,3},{2,4},{3,5},{4,6},{5,7},{6,0},{7,1},{8,10},{9,11},{10,... | collective-permute-start | bytes 442376 | tf_op jit(solution)/shard_map/ppermute | solution.py:565
  64.8 6.9 %collective-permute-start.4 = (bf16[64,1152]{1,0:T(8,128)(2,1)S(1)}, bf16[64,1152]{1,0:T(8,128)(2,1)S(1)}, u32[]{:S(2)}, u32[]{:S(2)}) collective-permute-start(bf16[64,1152]{1,0:T(8,128)(2,1)S(1)} %get-tuple-element.69), channel_id=1, source_target_pairs={{0,2},{1,3},{2,4},{3,5},{4,6},{5,7},{6,0},{7,1},{8,10},{9,11},{10,... | collective-permute-start | bytes 442376 | tf_op jit(solution)/shard_map/ppermute | solution.py:565
  66.8 5.1 %collective-permute-start.7 = (bf16[64,1152]{1,0:T(8,128)(2,1)S(1)}, bf16[64,1152]{1,0:T(8,128)(2,1)S(1)}, u32[]{:S(2)}, u32[]{:S(2)}) collective-permute-start(bf16[64,1152]{1,0:T(8,128)(2,1)S(1)} %get-tuple-element.72), channel_id=1, source_target_pairs={{0,6},{1,7},{2,0},{3,1},{4,2},{5,3},{6,4},{7,5},{8,14},{9,15},{10,... | collective-permute-start | bytes 442376 | tf_op jit(solution)/shard_map/ppermute | solution.py:565
  72.1 10.2 %collective-permute-start.9 = (bf16[64,1152]{1,0:T(8,128)(2,1)S(1)}, bf16[64,1152]{1,0:T(8,128)(2,1)S(1)}, u32[]{:S(2)}, u32[]{:S(2)}) collective-permute-start(bf16[64,1152]{1,0:T(8,128)(2,1)S(1)} %get-tuple-element.89), channel_id=1, source_target_pairs={{0,24},{1,25},{2,26},{3,27},{4,28},{5,29},{6,30},{7,31},{8,16},{9,... | collective-permute-start | bytes 442376 | tf_op jit(solution)/shard_map/ppermute | solution.py:565
  73.0 9.3 %collective-permute-start.8 = (bf16[64,1152]{1,0:T(8,128)(2,1)S(1)}, bf16[64,1152]{1,0:T(8,128)(2,1)S(1)}, u32[]{:S(2)}, u32[]{:S(2)}) collective-permute-start(bf16[64,1152]{1,0:T(8,128)(2,1)S(1)} %get-tuple-element.89), channel_id=1, source_target_pairs={{0,8},{1,9},{2,10},{3,11},{4,12},{5,13},{6,14},{7,15},{8,0},{9,1},... | collective-permute-start | bytes 442376 | tf_op jit(solution)/shard_map/ppermute | solution.py:565
  73.3 9.1 %collective-permute-start.10 = (bf16[64,1152]{1,0:T(8,128)(2,1)S(1)}, bf16[64,1152]{1,0:T(8,128)(2,1)S(1)}, u32[]{:S(2)}, u32[]{:S(2)}) collective-permute-start(bf16[64,1152]{1,0:T(8,128)(2,1)S(1)} %get-tuple-element.90), channel_id=1, source_target_pairs={{0,16},{1,17},{2,18},{3,19},{4,20},{5,21},{6,22},{7,23},{8,24},{9,... | collective-permute-start | bytes 442376 | tf_op jit(solution)/shard_map/ppermute | solution.py:565
  82.4 6.8 %collective-permute-start.13 = (bf16[64,1152]{1,0:T(8,128)(2,1)S(1)}, bf16[64,1152]{1,0:T(8,128)(2,1)S(1)}, u32[]{:S(2)}, u32[]{:S(2)}) collective-permute-start(bf16[64,1152]{1,0:T(8,128)(2,1)S(1)} %add_convert_fusion.1.own_ref), channel_id=1, source_target_pairs={{0,64},{1,65},{2,66},{3,67},{4,68},{5,69},{6,70},{7,71},{8,72},{9,... | collective-permute-start | bytes 442376 | tf_op jit(solution)/shard_map/ppermute | solution.py:565
  83.4 7.4 %collective-permute-start.12 = (bf16[64,1152]{1,0:T(8,128)(2,1)S(1)}, bf16[64,1152]{1,0:T(8,128)(2,1)S(1)}, u32[]{:S(2)}, u32[]{:S(2)}) collective-permute-start(bf16[64,1152]{1,0:T(8,128)(2,1)S(1)} %add_convert_fusion.1.own_ref), channel_id=1, source_target_pairs={{0,96},{1,97},{2,98},{3,99},{4,100},{5,101},{6,102},{7,103},{8,104... | collective-permute-start | bytes 442376 | tf_op jit(solution)/shard_map/ppermute | solution.py:565
  85.4 5.3 %collective-permute-start.11 = (bf16[64,1152]{1,0:T(8,128)(2,1)S(1)}, bf16[64,1152]{1,0:T(8,128)(2,1)S(1)}, u32[]{:S(2)}, u32[]{:S(2)}) collective-permute-start(bf16[64,1152]{1,0:T(8,128)(2,1)S(1)} %add_convert_fusion.1.own_ref), channel_id=1, source_target_pairs={{0,32},{1,33},{2,34},{3,35},{4,36},{5,37},{6,38},{7,39},{8,40},{9,... | collective-permute-start | bytes 442376 | tf_op jit(solution)/shard_map/ppermute | solution.py:565

commit v14 on v13

--- a/solution.py
+++ b/solution.py
@@ -632,10 +632,12 @@
     other = summed(other, [from_below, down(below)])
     blocks = jnp.stack([own, other]).astype(bf16)
     blocks, grad_latent = lax.optimization_barrier((blocks, grad_latent))
+    block, grad_latent = lax.optimization_barrier((over_x(blocks), grad_latent))
+    others = over_y(block)
     grad_latent = latent_gradient(grad_pre, weight_copy, nodes // 2, grad_latent)
-    block, grad_latent = lax.optimization_barrier((over_x(blocks), grad_latent))
+    *others, grad_latent = lax.optimization_barrier((*others, grad_latent))
     factor = 1.0 / math.sqrt(members * nodes * groups)
-    first, second = finish(block, over_y(block), width, variables, factor)
+    first, second = finish(block, others, width, variables, factor)
     return grad_latent[None], first, second
 
 

time: 91.9 us -> 92.3 us (level)
  waiting for transfers between devices: 17.1 us -> 18.5 us
  starting transfers between devices: 29.4 us -> 28.2 us
    ppermute x14, waiting for transfers between devices: 7.68 us -> 9.05 us  [moved(): return lax.ppermute(value, ('member', 'grid'), moves)]
    ppermute x14, starting transfers between devices: 18.8 us -> 17.6 us  [moved(): return lax.ppermute(value, ('member', 'grid'), moves)]
  transfers between devices with their start and end apart: 16 -> 16, of which waited for: 8 -> 9; matrix products, arithmetic and copies ran while one was open for 0% -> 0% of each run, Pallas kernels for 20% -> 20%
where the time goes in v14:
time: 92.3 us; the launch traced here: 91.7 us
  Pallas kernels  38.3 us (41%)
  starting transfers between devices  28.2 us (31%)
  waiting for transfers between devices  18.5 us (20%)
  local copies, waits for them, and re-layouts  4.27 us (5%)
  other arithmetic  1.54 us (2%)
    ppermute x14, starting transfers between devices, moved(): return lax.ppermute(value, ('member', 'grid'), moves)  17.6 us
    pallas_call x1, Pallas kernels, forward(): pl.pallas_call(forward_kernel, in_specs=[anywhere] * 3, out_specs=[vmem,...  10.1 us
    ppermute x14, waiting for transfers between devices, moved(): return lax.ppermute(value, ('member', 'grid'), moves)  9.05 us
    all_to_all x1, starting transfers between devices, body(): blocks = lax.all_to_all(blocks, 'member', 0, 0, tiled=True)  7.02 us
    pallas_call x2, Pallas kernels, latent_gradient(): pl.pallas_call(functools.partial(latent_kernel, begin=begin), in_specs=[v...  6.76 us
    pallas_call x1, Pallas kernels, gates(): pl.pallas_call(gate_kernel, in_specs=[anywhere], out_specs=[anywhere] * 2...  5.78 us
    all_to_all x1, waiting for transfers between devices, body(): blocks = lax.all_to_all(blocks, 'member', 0, 0, tiled=True)  5.07 us
    pallas_call x1, Pallas kernels, send_a(): pl.pallas_call(send_a_kernel, in_specs=[smem, vmem, anywhere, anywhere, a...  5.02 us
  transfers between devices with their start and end apart: 16, of which 9 were waited for; matrix products, arithmetic and copies ran while one was open for 0% of the time, Pallas kernels for 20%

profile of v14, /device:TPU:0, one launch (start us, length us, event | category | flops | bytes accessed | tf_op | source)
XLA Modules:
  0.0 91.7 jit_solution(13717419101418095241)
XLA Ops:
  0.6 10.1 %forward.1 = (f32[8,112,256]{2,1,0:T(8,128)S(1)}, bf16[2048,1024]{1,0:T(8,128)(2,1)}, bf16[1024,128]{1,0:T(8,128)(2,1)S(1)}) custom-call(bf16[2048,1024]{1,0:T(8,128)(2,1)} %bitcast.16, bf16[1024,1024]{1,0:T(8,128)(2,1)} %weight_hbm.1, bf16[100,1024]{1,0:T(8,128)(2,1)} %bitcast.20), custom_call_target="tpu_custom_call" | custom-call | flops 4831838208 | bytes 20971520 | tf_op jit(solution)/shard_map/forward/pallas_call | solution.py:102
  10.7 0.9 %multiply_convert_fusion = f16[8,112,256]{2,1,0:T(8,128)(2,1)} fusion(f32[8,112,256]{2,1,0:T(8,128)S(1)} %get-tuple-element.46), kind=kLoop, calls=%fused_computation.3 | loop fusion | flops 458752 | bytes 1376256 | tf_op jit(solution)/shard_map/convert_element_type | solution.py:610
  11.6 7.0 %all-to-all-start = ((f16[8,112,256]{2,1,0:T(8,128)(2,1)}), f16[8,112,256]{2,1,0:T(8,128)(2,1)S(1)}, u32[]{:S(2)}, u32[]{:S(2)}) async-start(f16[8,112,256]{2,1,0:T(8,128)(2,1)} %multiply_convert_fusion), calls=%async_computation | async-start | bytes 917504 | tf_op jit(solution)/shard_map/all_to_all | solution.py:611
  18.7 0.0 copy-start.2
  18.7 0.0 copy-start.3
  18.7 5.8 %gates.1 = (bf16[8,2048,128]{2,1,0:T(8,128)(2,1)}, bf16[2048,1024]{1,0:T(8,128)(2,1)}) custom-call(bf16[2048,1024]{1,0:T(8,128)(2,1)} %get-tuple-element.49.pre_hbm), custom_call_target="tpu_custom_call" | custom-call | bytes 12582912 | tf_op jit(solution)/shard_map/gates/pallas_call | solution.py:162
  24.5 5.1 %all-to-all-done = f16[8,112,256]{2,1,0:T(8,128)(2,1)S(1)} async-done(((f16[8,112,256]{2,1,0:T(8,128)(2,1)}), f16[8,112,256]{2,1,0:T(8,128)(2,1)S(1)}, u32[]{:S(2)}, u32[]{:S(2)}) %all-to-all-start) | async-done | bytes 458784 | tf_op jit(solution)/shard_map/all_to_all | solution.py:611
  29.5 0.1 convert_multiply_fusion.blocks_ref
  29.6 0.0 copy-done.2
  29.6 0.0 copy-done.3
  29.6 1.9 %pairs.1 = bf16[8,112,256]{2,1,0:T(8,128)(2,1)} custom-call(s32[1]{0:T(128)} %bitcast.1.place_ref, f32[8,112,256]{2,1,0:T(8,128)S(1)} %convert_multiply_fusion.blocks_ref, f32[100,2048]{1,0:T(8,128)S(1)} %copy-done.2, f32[1,2048]{1,0:T(1,128)S(1)} %bitcast.18), custom_call_target="tpu_custom_call" | custom-call | flops 4194304 | bytes 2097152 | tf_op jit(solution)/shard_map/pairs/pallas_call | solution.py:223
  31.6 3.7 %all-to-all-start.1 = ((bf16[8,112,256]{2,1,0:T(8,128)(2,1)}), bf16[8,112,256]{2,1,0:T(8,128)(2,1)S(1)}, u32[]{:S(2)}, u32[]{:S(2)}) async-start(bf16[8,112,256]{2,1,0:T(8,128)(2,1)} %pairs.1), calls=%async_computation.1 | async-start | bytes 917504 | tf_op jit(solution)/shard_map/all_to_all | solution.py:616
  35.2 0.0 copy-start.1
  35.2 2.2 %copy-done.1 = bf16[1,2048,1024]{2,1,0:T(8,128)(2,1)S(1)} copy-done((bf16[1,2048,1024]{2,1,0:T(8,128)(2,1)S(1)}, bf16[1,2048,1024]{2,1,0:T(8,128)(2,1)}, u32[]{:S(2)}) %copy-start.1) | copy-done | bytes 4194328
  37.4 1.1 %turned.1.turned_hbm = bf16[1024,2048]{1,0:T(8,128)(2,1)S(1)} custom-call(s32[1]{0:T(128)} %bitcast.grid_ref, bf16[2048,1024]{1,0:T(8,128)(2,1)S(1)} %bitcast.17), custom_call_target="tpu_custom_call" | custom-call | bytes 8388608 | tf_op jit(solution)/shard_map/turned/pallas_call | solution.py:269
  38.6 0.0 copy-start
  38.6 2.0 %copy-done = bf16[1024,2048]{1,0:T(8,128)(2,1)} copy-done((bf16[1024,2048]{1,0:T(8,128)(2,1)}, bf16[1024,2048]{1,0:T(8,128)(2,1)S(1)}, u32[]{:S(2)}) %copy-start) | copy-done | bytes 4194328
  40.6 4.4 %all-to-all-done.1.low_ref = bf16[8,112,256]{2,1,0:T(8,128)(2,1)S(1)} async-done(((bf16[8,112,256]{2,1,0:T(8,128)(2,1)}), bf16[8,112,256]{2,1,0:T(8,128)(2,1)S(1)}, u32[]{:S(2)}, u32[]{:S(2)}) %all-to-all-start.1) | async-done | bytes 458784 | tf_op jit(solution)/shard_map/all_to_all | solution.py:616
  44.9 5.0 %send_a.1 = (bf16[2048,1024]{1,0:T(8,128)(2,1)S(1)}, bf16[256,1152]{1,0:T(8,128)(2,1)S(1)}, bf16[256,128]{1,0:T(8,128)(2,1)S(1)}, bf16[128,2048]{1,0:T(8,128)(2,1)S(1)}, bf16[256,2048]{1,0:T(8,128)(2,1)S(1)}) custom-call(s32[1]{0:T(128)} %bitcast.grid_ref, bf16[8,112,256]{2,1,0:T(8,128)(2,1)S(1)} %all-to-all-done.1.low_ref, bf16[1024,2048]{1,0:T(8,128)(2,1)} %copy-done, ...), custom_call_target="tpu_custom_call" | custom-call | flops 1879048192 | bytes 8388608 | tf_op jit(solution)/shard_map/send_a/pallas_call | solution.py:427
  50.0 0.1 collective-permute-start
  50.1 2.9 %keep_a.1 = (bf16[256,1152]{1,0:T(8,128)(2,1)S(1)}, bf16[256,2048]{1,0:T(8,128)(2,1)S(1)}, bf16[4,2048,128]{2,1,0:T(8,128)(2,1)S(1)}) custom-call(s32[1]{0:T(128)} %bitcast.grid_ref, bf16[1024,2048]{1,0:T(8,128)(2,1)} %copy-done, bf16[8,2048,128]{2,1,0:T(8,128)(2,1)} %get-tuple-element.56.hidden_hbm, bf16[2048,1024]{1,0:T(8,128)(2,1)S(1)} %get-tuple-element.77.pre_ref, ...), custom_call_target="tpu_custom_call" | custom-call | flops 1073741824 | bytes 4194304 | tf_op jit(solution)/shard_map/keep_a/pallas_call | solution.py:456
  53.0 0.0 collective-permute-done
  53.0 0.1 add_convert_fusion
  53.2 2.3 %send_b.1 = (bf16[256,1152]{1,0:T(8,128)(2,1)S(1)}, bf16[256,128]{1,0:T(8,128)(2,1)S(1)}, bf16[256,2048]{1,0:T(8,128)(2,1)S(1)}) custom-call(s32[1]{0:T(128)} %bitcast.grid_ref, bf16[1024,2048]{1,0:T(8,128)(2,1)} %copy-done, bf16[2048,1024]{1,0:T(8,128)(2,1)S(1)} %get-tuple-element.77.pre_ref, bf16[128,2048]{1,0:T(8,128)(2,1)S(1)} %get-tuple-element.64.flat_ref, ...), custom_call_target="tpu_custom_call" | custom-call | flops 1073741824 | bytes 4194304 | tf_op jit(solution)/shard_map/send_b/pallas_call | solution.py:470
  55.5 0.6 collective-permute-start.1
  56.1 1.9 %collective-permute-start.2 = (bf16[64,1152]{1,0:T(8,128)(2,1)S(1)}, bf16[64,1152]{1,0:T(8,128)(2,1)S(1)}, u32[]{:S(2)}, u32[]{:S(2)}) collective-permute-start(bf16[64,1152]{1,0:T(8,128)(2,1)S(1)} %get-tuple-element.71), channel_id=1, source_target_pairs={{0,2},{1,3},{2,4},{3,5},{4,6},{5,7},{6,0},{7,1},{8,10},{9,11},{10,... | collective-permute-start | bytes 442376 | tf_op jit(solution)/shard_map/ppermute | solution.py:565
  58.0 2.1 %collective-permute-start.3 = (bf16[64,1152]{1,0:T(8,128)(2,1)S(1)}, bf16[64,1152]{1,0:T(8,128)(2,1)S(1)}, u32[]{:S(2)}, u32[]{:S(2)}) collective-permute-start(bf16[64,1152]{1,0:T(8,128)(2,1)S(1)} %get-tuple-element.72), channel_id=1, source_target_pairs={{0,6},{1,7},{2,0},{3,1},{4,2},{5,3},{6,4},{7,5},{8,14},{9,15},{10,... | collective-permute-start | bytes 442376 | tf_op jit(solution)/shard_map/ppermute | solution.py:565
  60.2 2.0 %collective-permute-start.5 = (bf16[64,1152]{1,0:T(8,128)(2,1)S(1)}, bf16[64,1152]{1,0:T(8,128)(2,1)S(1)}, u32[]{:S(2)}, u32[]{:S(2)}) collective-permute-start(bf16[64,1152]{1,0:T(8,128)(2,1)S(1)} %get-tuple-element.74), channel_id=1, source_target_pairs={{0,6},{1,7},{2,0},{3,1},{4,2},{5,3},{6,4},{7,5},{8,14},{9,15},{10,... | collective-permute-start | bytes 442376 | tf_op jit(solution)/shard_map/ppermute | solution.py:565
  62.2 0.0 collective-permute-start.6
  62.2 1.6 %keep_b.1 = (bf16[256,1152]{1,0:T(8,128)(2,1)S(1)}, bf16[1024,1024]{1,0:T(8,128)(2,1)S(1)}) custom-call(bf16[1024,1024]{1,0:T(8,128)(2,1)} %weight_hbm.1, bf16[2048,1024]{1,0:T(8,128)(2,1)S(1)} %get-tuple-element.77.pre_ref, bf16[256,2048]{1,0:T(8,128)(2,1)S(1)} %get-tuple-element.67.turned_ref, bf16[256,128]{1,0:T(8,128)(2,1)S(1)} %get-tuple-element.68.second_ref), custom_call_target="tpu_custom_call" | custom-call | flops 1073741824 | bytes 4194304 | tf_op jit(solution)/shard_map/keep_b/pallas_call | solution.py:484
  63.8 0.0 collective-permute-done.1
  63.8 0.1 convert_add_fusion
  63.9 0.3 collective-permute-done.2
  64.2 0.5 collective-permute-done.3
  64.7 0.1 fusion.2
  64.8 2.0 %collective-permute-start.4 = (bf16[64,1152]{1,0:T(8,128)(2,1)S(1)}, bf16[64,1152]{1,0:T(8,128)(2,1)S(1)}, u32[]{:S(2)}, u32[]{:S(2)}) collective-permute-start(bf16[64,1152]{1,0:T(8,128)(2,1)S(1)} %get-tuple-element.73), channel_id=1, source_target_pairs={{0,2},{1,3},{2,4},{3,5},{4,6},{5,7},{6,0},{7,1},{8,10},{9,11},{10,... | collective-permute-start | bytes 442376 | tf_op jit(solution)/shard_map/ppermute | solution.py:565
  66.8 1.4 %collective-permute-start.7 = (bf16[64,1152]{1,0:T(8,128)(2,1)S(1)}, bf16[64,1152]{1,0:T(8,128)(2,1)S(1)}, u32[]{:S(2)}, u32[]{:S(2)}) collective-permute-start(bf16[64,1152]{1,0:T(8,128)(2,1)S(1)} %get-tuple-element.76), channel_id=1, source_target_pairs={{0,6},{1,7},{2,0},{3,1},{4,2},{5,3},{6,4},{7,5},{8,14},{9,15},{10,... | collective-permute-start | bytes 442376 | tf_op jit(solution)/shard_map/ppermute | solution.py:565
  68.3 3.4 %latent_gradient.2.refs_0_ = bf16[2048,1024]{1,0:T(8,128)(2,1)} custom-call(bf16[2048,1024]{1,0:T(8,128)(2,1)S(1)} %get-tuple-element.77.pre_ref, bf16[1024,1024]{1,0:T(8,128)(2,1)S(1)} %get-tuple-element.78.weight_ref), custom_call_target="tpu_custom_call" | custom-call | flops 2147483648 | bytes 5242880 | tf_op jit(solution)/shard_map/latent_gradient/pallas_call | solution.py:520
  71.7 0.0 collective-permute-done.5
  71.7 0.0 collective-permute-done.6
  71.7 0.0 collective-permute-done.4
  71.7 0.3 collective-permute-done.7
  72.0 0.1 fusion.6
  72.1 1.1 %collective-permute-start.10 = (bf16[64,1152]{1,0:T(8,128)(2,1)S(1)}, bf16[64,1152]{1,0:T(8,128)(2,1)S(1)}, u32[]{:S(2)}, u32[]{:S(2)}) collective-permute-start(bf16[64,1152]{1,0:T(8,128)(2,1)S(1)} %get-tuple-element.98), channel_id=1, source_target_pairs={{0,16},{1,17},{2,18},{3,19},{4,20},{5,21},{6,22},{7,23},{8,24},{9,... | collective-permute-start | bytes 442376 | tf_op jit(solution)/shard_map/ppermute | solution.py:565
  73.3 2.5 %collective-permute-start.9 = (bf16[64,1152]{1,0:T(8,128)(2,1)S(1)}, bf16[64,1152]{1,0:T(8,128)(2,1)S(1)}, u32[]{:S(2)}, u32[]{:S(2)}) collective-permute-start(bf16[64,1152]{1,0:T(8,128)(2,1)S(1)} %get-tuple-element.97), channel_id=1, source_target_pairs={{0,24},{1,25},{2,26},{3,27},{4,28},{5,29},{6,30},{7,31},{8,16},{9,... | collective-permute-start | bytes 442376 | tf_op jit(solution)/shard_map/ppermute | solution.py:565
  75.8 0.2 collective-permute-start.8
  75.9 4.0 %collective-permute-done.10 = bf16[64,1152]{1,0:T(8,128)(2,1)S(1)} collective-permute-done((bf16[64,1152]{1,0:T(8,128)(2,1)S(1)}, bf16[64,1152]{1,0:T(8,128)(2,1)S(1)}, u32[]{:S(2)}, u32[]{:S(2)}) %collective-permute-start.10) | collective-permute-done | bytes 147488 | tf_op jit(solution)/shard_map/ppermute | solution.py:565
  79.9 1.5 %collective-permute-done.9 = bf16[64,1152]{1,0:T(8,128)(2,1)S(1)} collective-permute-done((bf16[64,1152]{1,0:T(8,128)(2,1)S(1)}, bf16[64,1152]{1,0:T(8,128)(2,1)S(1)}, u32[]{:S(2)}, u32[]{:S(2)}) %collective-permute-start.9) | collective-permute-done | bytes 147488 | tf_op jit(solution)/shard_map/ppermute | solution.py:565
  81.4 0.0 collective-permute-done.8
  81.4 0.1 add_convert_fusion.1.own_ref
  81.5 0.9 %collective-permute-start.13 = (bf16[64,1152]{1,0:T(8,128)(2,1)S(1)}, bf16[64,1152]{1,0:T(8,128)(2,1)S(1)}, u32[]{:S(2)}, u32[]{:S(2)}) collective-permute-start(bf16[64,1152]{1,0:T(8,128)(2,1)S(1)} %add_convert_fusion.1.own_ref), channel_id=1, source_target_pairs={{0,64},{1,65},{2,66},{3,67},{4,68},{5,69},{6,70},{7,71},{8,72},{9,... | collective-permute-start | bytes 442376 | tf_op jit(solution)/shard_map/ppermute | solution.py:565
  82.4 2.1 %collective-permute-start.12 = (bf16[64,1152]{1,0:T(8,128)(2,1)S(1)}, bf16[64,1152]{1,0:T(8,128)(2,1)S(1)}, u32[]{:S(2)}, u32[]{:S(2)}) collective-permute-start(bf16[64,1152]{1,0:T(8,128)(2,1)S(1)} %add_convert_fusion.1.own_ref), channel_id=1, source_target_pairs={{0,96},{1,97},{2,98},{3,99},{4,100},{5,101},{6,102},{7,103},{8,104... | collective-permute-start | bytes 442376 | tf_op jit(solution)/shard_map/ppermute | solution.py:565
  84.5 0.6 collective-permute-start.11
  85.1 3.4 %latent_gradient.3 = bf16[2048,1024]{1,0:T(8,128)(2,1)} custom-call(bf16[2048,1024]{1,0:T(8,128)(2,1)S(1)} %get-tuple-element.77.pre_ref, bf16[1024,1024]{1,0:T(8,128)(2,1)S(1)} %get-tuple-element.78.weight_ref, bf16[2048,1024]{1,0:T(8,128)(2,1)} %latent_gradient.2.refs_0_), custom_call_target="tpu_custom_call", output_to_operand_aliasing={{}: (2, {})} | custom-call | flops 2147483648 | bytes 5242880 | tf_op jit(solution)/shard_map/latent_gradient/pallas_call | solution.py:520
  88.5 0.9 %collective-permute-done.13.refs_2_ = bf16[64,1152]{1,0:T(8,128)(2,1)S(1)} collective-permute-done((bf16[64,1152]{1,0:T(8,128)(2,1)S(1)}, bf16[64,1152]{1,0:T(8,128)(2,1)S(1)}, u32[]{:S(2)}, u32[]{:S(2)}) %collective-permute-start.13) | collective-permute-done | bytes 147488 | tf_op jit(solution)/shard_map/ppermute | solution.py:565
  89.4 1.5 %collective-permute-done.12.refs_1_ = bf16[64,1152]{1,0:T(8,128)(2,1)S(1)} collective-permute-done((bf16[64,1152]{1,0:T(8,128)(2,1)S(1)}, bf16[64,1152]{1,0:T(8,128)(2,1)S(1)}, u32[]{:S(2)}, u32[]{:S(2)}) %collective-permute-start.12) | collective-permute-done | bytes 147488 | tf_op jit(solution)/shard_map/ppermute | solution.py:565
  90.9 0.0 collective-permute-done.11.refs_0_
  90.9 0.8 finish.1
  (3 shorter events, 0.1 us)
Async XLA Ops:
  11.6 17.9 %all-to-all-start = ((f16[8,112,256]{2,1,0:T(8,128)(2,1)}), f16[8,112,256]{2,1,0:T(8,128)(2,1)S(1)}, u32[]{:S(2)}, u32[]{:S(2)}) async-start(f16[8,112,256]{2,1,0:T(8,128)(2,1)} %multiply_convert_fusion), calls=%async_computation | async-start | bytes 917504 | tf_op jit(solution)/shard_map/all_to_all | solution.py:611
  18.7 11.0 %copy-start.2 = (f32[100,2048]{1,0:T(8,128)S(1)}, f32[100,2048]{1,0:T(8,128)}, u32[]{:S(2)}) copy-start(f32[100,2048]{1,0:T(8,128)} %observed_ref.1) | copy-start | bytes 2457604
  18.7 11.0 %copy-start.3 = (f32[2048]{0:T(1024)S(1)}, f32[2048]{0:T(1024)}, u32[]{:S(2)}) copy-start(f32[2048]{0:T(1024)} %param.9) | copy-start | bytes 24580
  31.6 13.4 %all-to-all-start.1 = ((bf16[8,112,256]{2,1,0:T(8,128)(2,1)}), bf16[8,112,256]{2,1,0:T(8,128)(2,1)S(1)}, u32[]{:S(2)}, u32[]{:S(2)}) async-start(bf16[8,112,256]{2,1,0:T(8,128)(2,1)} %pairs.1), calls=%async_computation.1 | async-start | bytes 917504 | tf_op jit(solution)/shard_map/all_to_all | solution.py:616
  35.2 2.2 %copy-start.1 = (bf16[1,2048,1024]{2,1,0:T(8,128)(2,1)S(1)}, bf16[1,2048,1024]{2,1,0:T(8,128)(2,1)}, u32[]{:S(2)}) copy-start(bf16[1,2048,1024]{2,1,0:T(8,128)(2,1)} %param.5) | copy-start | bytes 12582916
  38.6 2.0 %copy-start = (bf16[1024,2048]{1,0:T(8,128)(2,1)}, bf16[1024,2048]{1,0:T(8,128)(2,1)S(1)}, u32[]{:S(2)}) copy-start(bf16[1024,2048]{1,0:T(8,128)(2,1)S(1)} %turned.1.turned_hbm) | copy-start | bytes 12582916
  50.0 3.0 %collective-permute-start = (bf16[256,1152]{1,0:T(8,128)(2,1)S(1)}, bf16[256,1152]{1,0:T(8,128)(2,1)S(1)}, u32[]{:S(2)}, u32[]{:S(2)}) collective-permute-start(bf16[256,1152]{1,0:T(8,128)(2,1)S(1)} %get-tuple-element.62), channel_id=1, source_target_pairs={{0,1},{1,0},{2,3},{3,2},{4,5},{5,4},{6,7},{7,6},{8,9},{9,8},{10,11... | collective-permute-start | bytes 1769480 | tf_op jit(solution)/shard_map/ppermute | solution.py:565
  55.5 8.3 %collective-permute-start.1 = (bf16[256,1152]{1,0:T(8,128)(2,1)S(1)}, bf16[256,1152]{1,0:T(8,128)(2,1)S(1)}, u32[]{:S(2)}, u32[]{:S(2)}) collective-permute-start(bf16[256,1152]{1,0:T(8,128)(2,1)S(1)} %get-tuple-element.70), channel_id=1, source_target_pairs={{0,1},{1,0},{2,3},{3,2},{4,5},{5,4},{6,7},{7,6},{8,9},{9,8},{10,11... | collective-permute-start | bytes 1769480 | tf_op jit(solution)/shard_map/ppermute | solution.py:565
  56.1 8.1 %collective-permute-start.2 = (bf16[64,1152]{1,0:T(8,128)(2,1)S(1)}, bf16[64,1152]{1,0:T(8,128)(2,1)S(1)}, u32[]{:S(2)}, u32[]{:S(2)}) collective-permute-start(bf16[64,1152]{1,0:T(8,128)(2,1)S(1)} %get-tuple-element.71), channel_id=1, source_target_pairs={{0,2},{1,3},{2,4},{3,5},{4,6},{5,7},{6,0},{7,1},{8,10},{9,11},{10,... | collective-permute-start | bytes 442376 | tf_op jit(solution)/shard_map/ppermute | solution.py:565
  58.0 6.7 %collective-permute-start.3 = (bf16[64,1152]{1,0:T(8,128)(2,1)S(1)}, bf16[64,1152]{1,0:T(8,128)(2,1)S(1)}, u32[]{:S(2)}, u32[]{:S(2)}) collective-permute-start(bf16[64,1152]{1,0:T(8,128)(2,1)S(1)} %get-tuple-element.72), channel_id=1, source_target_pairs={{0,6},{1,7},{2,0},{3,1},{4,2},{5,3},{6,4},{7,5},{8,14},{9,15},{10,... | collective-permute-start | bytes 442376 | tf_op jit(solution)/shard_map/ppermute | solution.py:565
  60.2 11.5 %collective-permute-start.5 = (bf16[64,1152]{1,0:T(8,128)(2,1)S(1)}, bf16[64,1152]{1,0:T(8,128)(2,1)S(1)}, u32[]{:S(2)}, u32[]{:S(2)}) collective-permute-start(bf16[64,1152]{1,0:T(8,128)(2,1)S(1)} %get-tuple-element.74), channel_id=1, source_target_pairs={{0,6},{1,7},{2,0},{3,1},{4,2},{5,3},{6,4},{7,5},{8,14},{9,15},{10,... | collective-permute-start | bytes 442376 | tf_op jit(solution)/shard_map/ppermute | solution.py:565
  62.2 9.5 %collective-permute-start.6 = (bf16[64,1152]{1,0:T(8,128)(2,1)S(1)}, bf16[64,1152]{1,0:T(8,128)(2,1)S(1)}, u32[]{:S(2)}, u32[]{:S(2)}) collective-permute-start(bf16[64,1152]{1,0:T(8,128)(2,1)S(1)} %get-tuple-element.75), channel_id=1, source_target_pairs={{0,2},{1,3},{2,4},{3,5},{4,6},{5,7},{6,0},{7,1},{8,10},{9,11},{10,... | collective-permute-start | bytes 442376 | tf_op jit(solution)/shard_map/ppermute | solution.py:565
  64.8 6.9 %collective-permute-start.4 = (bf16[64,1152]{1,0:T(8,128)(2,1)S(1)}, bf16[64,1152]{1,0:T(8,128)(2,1)S(1)}, u32[]{:S(2)}, u32[]{:S(2)}) collective-permute-start(bf16[64,1152]{1,0:T(8,128)(2,1)S(1)} %get-tuple-element.73), channel_id=1, source_target_pairs={{0,2},{1,3},{2,4},{3,5},{4,6},{5,7},{6,0},{7,1},{8,10},{9,11},{10,... | collective-permute-start | bytes 442376 | tf_op jit(solution)/shard_map/ppermute | solution.py:565
  66.8 5.1 %collective-permute-start.7 = (bf16[64,1152]{1,0:T(8,128)(2,1)S(1)}, bf16[64,1152]{1,0:T(8,128)(2,1)S(1)}, u32[]{:S(2)}, u32[]{:S(2)}) collective-permute-start(bf16[64,1152]{1,0:T(8,128)(2,1)S(1)} %get-tuple-element.76), channel_id=1, source_target_pairs={{0,6},{1,7},{2,0},{3,1},{4,2},{5,3},{6,4},{7,5},{8,14},{9,15},{10,... | collective-permute-start | bytes 442376 | tf_op jit(solution)/shard_map/ppermute | solution.py:565
  72.1 7.8 %collective-permute-start.10 = (bf16[64,1152]{1,0:T(8,128)(2,1)S(1)}, bf16[64,1152]{1,0:T(8,128)(2,1)S(1)}, u32[]{:S(2)}, u32[]{:S(2)}) collective-permute-start(bf16[64,1152]{1,0:T(8,128)(2,1)S(1)} %get-tuple-element.98), channel_id=1, source_target_pairs={{0,16},{1,17},{2,18},{3,19},{4,20},{5,21},{6,22},{7,23},{8,24},{9,... | collective-permute-start | bytes 442376 | tf_op jit(solution)/shard_map/ppermute | solution.py:565
  73.3 8.1 %collective-permute-start.9 = (bf16[64,1152]{1,0:T(8,128)(2,1)S(1)}, bf16[64,1152]{1,0:T(8,128)(2,1)S(1)}, u32[]{:S(2)}, u32[]{:S(2)}) collective-permute-start(bf16[64,1152]{1,0:T(8,128)(2,1)S(1)} %get-tuple-element.97), channel_id=1, source_target_pairs={{0,24},{1,25},{2,26},{3,27},{4,28},{5,29},{6,30},{7,31},{8,16},{9,... | collective-permute-start | bytes 442376 | tf_op jit(solution)/shard_map/ppermute | solution.py:565
  75.8 5.7 %collective-permute-start.8 = (bf16[64,1152]{1,0:T(8,128)(2,1)S(1)}, bf16[64,1152]{1,0:T(8,128)(2,1)S(1)}, u32[]{:S(2)}, u32[]{:S(2)}) collective-permute-start(bf16[64,1152]{1,0:T(8,128)(2,1)S(1)} %get-tuple-element.97), channel_id=1, source_target_pairs={{0,8},{1,9},{2,10},{3,11},{4,12},{5,13},{6,14},{7,15},{8,0},{9,1},... | collective-permute-start | bytes 442376 | tf_op jit(solution)/shard_map/ppermute | solution.py:565
  81.5 7.9 %collective-permute-start.13 = (bf16[64,1152]{1,0:T(8,128)(2,1)S(1)}, bf16[64,1152]{1,0:T(8,128)(2,1)S(1)}, u32[]{:S(2)}, u32[]{:S(2)}) collective-permute-start(bf16[64,1152]{1,0:T(8,128)(2,1)S(1)} %add_convert_fusion.1.own_ref), channel_id=1, source_target_pairs={{0,64},{1,65},{2,66},{3,67},{4,68},{5,69},{6,70},{7,71},{8,72},{9,... | collective-permute-start | bytes 442376 | tf_op jit(solution)/shard_map/ppermute | solution.py:565
  82.4 8.5 %collective-permute-start.12 = (bf16[64,1152]{1,0:T(8,128)(2,1)S(1)}, bf16[64,1152]{1,0:T(8,128)(2,1)S(1)}, u32[]{:S(2)}, u32[]{:S(2)}) collective-permute-start(bf16[64,1152]{1,0:T(8,128)(2,1)S(1)} %add_convert_fusion.1.own_ref), channel_id=1, source_target_pairs={{0,96},{1,97},{2,98},{3,99},{4,100},{5,101},{6,102},{7,103},{8,104... | collective-permute-start | bytes 442376 | tf_op jit(solution)/shard_map/ppermute | solution.py:565
  84.5 6.4 %collective-permute-start.11 = (bf16[64,1152]{1,0:T(8,128)(2,1)S(1)}, bf16[64,1152]{1,0:T(8,128)(2,1)S(1)}, u32[]{:S(2)}, u32[]{:S(2)}) collective-permute-start(bf16[64,1152]{1,0:T(8,128)(2,1)S(1)} %add_convert_fusion.1.own_ref), channel_id=1, source_target_pairs={{0,32},{1,33},{2,34},{3,35},{4,36},{5,37},{6,38},{7,39},{8,40},{9,... | collective-permute-start | bytes 442376 | tf_op jit(solution)/shard_map/ppermute | solution.py:565

commit v15 on v13

--- a/solution.py
+++ b/solution.py
@@ -182,7 +182,7 @@
     return diff * lax.rsqrt(diff * diff + smooth_sq)
 
 
-def pair_kernel(place_ref, blocks_ref, observed_ref, area_ref, low_ref, here_ref, weight_ref, totals_ref, sems):
+def pair_kernel(place_ref, blocks_ref, observed_ref, area_ref, low_out, here_ref, weight_ref, totals_ref, low_ref, sems):
     members = blocks_ref.shape[0]
     variables = observed_ref.shape[0]
     at = pl.multiple_of(place_ref[0] * SHARE, SHARE)
@@ -205,6 +205,12 @@
             totals_ref[a, rows, :] = totals[a]
     for load in loads:
         load.wait()
+    stores = [
+        pltpu.make_async_copy(
+            low_ref.at[:, pl.ds(first, count)], low_out.at[:, pl.ds(first, count)], sems.at[2 + index]
+        )
+        for index, (first, count) in enumerate(((0, 64), (64, TALL - 64)))
+    ]
     area = weight_ref[...]
     for start in range(0, TALL, 16):
         rows = slice(start, start + 16)
@@ -215,6 +221,11 @@
         for a in range(members):
             own = slope_function(blocks_ref[a, rows, :] - observed)
             low_ref[a, rows, :] = (area * (own - totals_ref[a, rows, :] * (1.0 / (members - 1)))).astype(bf16)
+        if start == 48:
+            stores[0].start()
+    stores[1].start()
+    for store in stores:
+        store.wait()
 
 
 def pairs(place, blocks, observed, area):
@@ -223,13 +234,14 @@
     return pl.pallas_call(
         pair_kernel,
         in_specs=[smem, vmem, anywhere, anywhere],
-        out_specs=vmem,
-        out_shape=jax.ShapeDtypeStruct((members, TALL, SHARE), bf16),
+        out_specs=anywhere,
+        out_shape=pltpu.HBM((members, TALL, SHARE), bf16),
         scratch_shapes=[
             pltpu.VMEM((variables, SHARE), f32),
             pltpu.VMEM((1, SHARE), f32),
             pltpu.VMEM((members, TALL, SHARE), f32),
-            pltpu.SemaphoreType.DMA((2,)),
+            pltpu.VMEM((members, TALL, SHARE), bf16),
+            pltpu.SemaphoreType.DMA((4,)),
         ],
         compiler_params=params(8),
         cost_estimate=cost(4 << 20, 2 << 20),
@@ -367,47 +379,38 @@
     turned_next.wait()
 
 
-def keep_a_kernel(
+def keep_a_kernel(turned_hbm, pre_ref, turned_ref, second_ref, keep_ref, next_turned_ref, turned_sem):
+    load = turned_load(turned_hbm, 512, next_turned_ref, turned_sem)
+    load.start()
+    first_product(turned_ref, pre_ref, keep_ref)
+    keep_ref[:, pre_ref.shape[1] :] = second_ref[...]
+    load.wait()
+
+
+def send_b_kernel(
     grid_ref,
     turned_hbm,
     hidden_hbm,
     pre_ref,
+    flat_ref,
     turned_ref,
+    send_ref,
     second_ref,
-    keep_ref,
     next_turned_ref,
-    next_hidden_ref,
+    hidden_ref,
+    scratch_ref,
     turned_sem,
     hidden_sems,
 ):
-    loads = [turned_load(turned_hbm, 512, next_turned_ref, turned_sem)]
-    loads += hidden_loads(1, grid_ref, hidden_hbm, next_hidden_ref, hidden_sems)
+    loads = hidden_loads(1, grid_ref, hidden_hbm, hidden_ref, hidden_sems)
+    loads.append(turned_load(turned_hbm, 768, next_turned_ref, turned_sem))
     for load in loads:
         load.start()
-    first_product(turned_ref, pre_ref, keep_ref)
-    keep_ref[:, pre_ref.shape[1] :] = second_ref[...]
-    for load in loads:
+    first_product(turned_ref, pre_ref, send_ref)
+    for load in loads[:-1]:
         load.wait()
-
-
-def send_b_kernel(
-    grid_ref,
-    turned_hbm,
-    pre_ref,
-    flat_ref,
-    turned_ref,
-    hidden_ref,
-    send_ref,
-    second_ref,
-    next_turned_ref,
-    scratch_ref,
-    turned_sem,
-):
-    load = turned_load(turned_hbm, 768, next_turned_ref, turned_sem)
-    load.start()
-    first_product(turned_ref, pre_ref, send_ref)
     second_product(grid_ref, flat_ref, hidden_ref, send_ref, second_ref, scratch_ref)
-    load.wait()
+    loads[-1].wait()
 
 
 def keep_b_kernel(weight_hbm, pre_ref, turned_ref, second_ref, keep_ref, weight_ref, weight_sem):
@@ -451,32 +454,37 @@
     )(grid, low, pinned(turned_latent), pinned(slope), pinned(hidden), padded)
 
 
-def keep_a(grid, turned_latent, hidden, grad_pre, turned_now, second):
+def keep_a(turned_latent, grad_pre, turned_now, second):
     nodes, width = grad_pre.shape
     return pl.pallas_call(
         keep_a_kernel,
-        in_specs=[smem, anywhere, anywhere] + [vmem] * 3,
-        out_specs=[vmem] * 3,
-        out_shape=[shape(256, width + WIDE), shape(256, nodes), shape(4, nodes, 128)],
-        scratch_shapes=[pltpu.SemaphoreType.DMA, pltpu.SemaphoreType.DMA((4,))],
+        in_specs=[anywhere] + [vmem] * 3,
+        out_specs=[vmem] * 2,
+        out_shape=[shape(256, width + WIDE), shape(256, nodes)],
+        scratch_shapes=[pltpu.SemaphoreType.DMA],
         compiler_params=params(12),
         cost_estimate=cost(nodes * width * width // 2, 4 << 20),
         name="keep_a",
-    )(grid, pinned(turned_latent), pinned(hidden), grad_pre, turned_now, second)
-
-
-def send_b(grid, turned_latent, grad_pre, flat, turned_now, hidden_now):
+    )(pinned(turned_latent), grad_pre, turned_now, second)
+
+
+def send_b(grid, turned_latent, hidden, grad_pre, flat, turned_now):
     nodes, width = grad_pre.shape
     return pl.pallas_call(
         send_b_kernel,
-        in_specs=[smem, anywhere] + [vmem] * 4,
+        in_specs=[smem, anywhere, anywhere] + [vmem] * 3,
         out_specs=[vmem] * 3,
         out_shape=[shape(256, width + WIDE), shape(256, WIDE), shape(256, nodes)],
-        scratch_shapes=[pltpu.VMEM((512, WIDE), bf16), pltpu.SemaphoreType.DMA],
+        scratch_shapes=[
+            pltpu.VMEM((4, nodes, 128), bf16),
+            pltpu.VMEM((512, WIDE), bf16),
+            pltpu.SemaphoreType.DMA,
+            pltpu.SemaphoreType.DMA((4,)),
+        ],
         compiler_params=params(12),
         cost_estimate=cost(nodes * width * width // 2, 4 << 20),
         name="send_b",
-    )(grid, pinned(turned_latent), grad_pre, flat, turned_now, hidden_now)
+    )(grid, pinned(turned_latent), pinned(hidden), grad_pre, flat, turned_now)
 
 
 def keep_b(weight, grad_pre, turned_now, second):
@@ -616,12 +624,12 @@
     low = lax.all_to_all(low, "member", 0, 0, tiled=True)
     turned_latent = turned(late_grid, latent)
     grad_pre, rows_a, second_a, flat, turned_now = send_a(grid, low, turned_latent, slope, hidden, padded)
-    kept_a, turned_now, hidden_now = keep_a(grid, turned_latent, hidden, grad_pre, turned_now, second_a)
+    kept_a, turned_now = keep_a(turned_latent, grad_pre, turned_now, second_a)
     far_up, far_down, near_up, near_down = over_core(rows_a, kept_a).astype(bf16)
     far_up, far_down, near_up, near_down, flat = lax.optimization_barrier((far_up, far_down, near_up, near_down, flat))
     upward, downward = up(far_up), down(far_down)
     from_below, from_above = up(near_up), down(near_down)
-    rows_b, second_b, turned_now = send_b(grid, turned_latent, grad_pre, flat, turned_now, hidden_now)
+    rows_b, second_b, turned_now = send_b(grid, turned_latent, hidden, grad_pre, flat, turned_now)
     kept_b, weight_copy = keep_b(hidden_weight, grad_pre, turned_now, second_b)
     above, below, own, other = over_core(rows_b, kept_b)
     above = (above + upward.astype(f32)).astype(bf16)

time: 91.9 us -> 91.4 us (level)
  transfers between devices with their start and end apart: 16 -> 16, of which waited for: 8 -> 8; matrix products, arithmetic and copies ran while one was open for 0% -> 0% of each run, Pallas kernels for 20% -> 18%
where the time goes in v15:
time: 91.4 us; the launch traced here: 91 us
  Pallas kernels  37.4 us (41%)
  starting transfers between devices  29.1 us (32%)
  waiting for transfers between devices  17.8 us (19%)
  local copies, waits for them, and re-layouts  4.27 us (5%)
  other arithmetic  1.53 us (2%)
    ppermute x14, starting transfers between devices, moved(): return lax.ppermute(value, ('member', 'grid'), moves)  18.5 us
    pallas_call x1, Pallas kernels, forward(): pl.pallas_call(forward_kernel, in_specs=[anywhere] * 3, out_specs=[vmem,...  10.1 us
    ppermute x14, waiting for transfers between devices, moved(): return lax.ppermute(value, ('member', 'grid'), moves)  8.38 us
    all_to_all x1, starting transfers between devices, body(): blocks = lax.all_to_all(blocks, 'member', 0, 0, tiled=True)  7.02 us
    pallas_call x2, Pallas kernels, latent_gradient(): pl.pallas_call(functools.partial(latent_kernel, begin=begin), in_specs=[v...  6.75 us
    pallas_call x1, Pallas kernels, gates(): pl.pallas_call(gate_kernel, in_specs=[anywhere], out_specs=[anywhere] * 2...  5.78 us
    all_to_all x1, waiting for transfers between devices, body(): blocks = lax.all_to_all(blocks, 'member', 0, 0, tiled=True)  5.07 us
    pallas_call x1, Pallas kernels, send_a(): pl.pallas_call(send_a_kernel, in_specs=[smem, vmem, anywhere, anywhere, a...  5.02 us
  transfers between devices with their start and end apart: 16, of which 8 were waited for; matrix products, arithmetic and copies ran while one was open for 0% of the time, Pallas kernels for 18%

profile of v15, /device:TPU:0, one launch (start us, length us, event | category | flops | bytes accessed | tf_op | source)
XLA Modules:
  0.0 91.0 jit_solution(7253898062810441933)
XLA Ops:
  0.6 10.1 %forward.1 = (f32[8,112,256]{2,1,0:T(8,128)S(1)}, bf16[2048,1024]{1,0:T(8,128)(2,1)}, bf16[1024,128]{1,0:T(8,128)(2,1)S(1)}) custom-call(bf16[2048,1024]{1,0:T(8,128)(2,1)} %bitcast.16, bf16[1024,1024]{1,0:T(8,128)(2,1)} %weight_hbm.1, bf16[100,1024]{1,0:T(8,128)(2,1)} %bitcast.20), custom_call_target="tpu_custom_call" | custom-call | flops 4831838208 | bytes 20971520 | tf_op jit(solution)/shard_map/forward/pallas_call | solution.py:102
  10.7 0.9 %multiply_convert_fusion = f16[8,112,256]{2,1,0:T(8,128)(2,1)} fusion(f32[8,112,256]{2,1,0:T(8,128)S(1)} %get-tuple-element.41), kind=kLoop, calls=%fused_computation.3 | loop fusion | flops 458752 | bytes 1376256 | tf_op jit(solution)/shard_map/convert_element_type | solution.py:618
  11.6 7.0 %all-to-all-start = ((f16[8,112,256]{2,1,0:T(8,128)(2,1)}), f16[8,112,256]{2,1,0:T(8,128)(2,1)S(1)}, u32[]{:S(2)}, u32[]{:S(2)}) async-start(f16[8,112,256]{2,1,0:T(8,128)(2,1)} %multiply_convert_fusion), calls=%async_computation | async-start | bytes 917504 | tf_op jit(solution)/shard_map/all_to_all | solution.py:619
  18.7 0.0 copy-start.2
  18.7 0.0 copy-start.3
  18.7 5.8 %gates.1 = (bf16[8,2048,128]{2,1,0:T(8,128)(2,1)}, bf16[2048,1024]{1,0:T(8,128)(2,1)}) custom-call(bf16[2048,1024]{1,0:T(8,128)(2,1)} %get-tuple-element.44.pre_hbm), custom_call_target="tpu_custom_call" | custom-call | bytes 12582912 | tf_op jit(solution)/shard_map/gates/pallas_call | solution.py:162
  24.5 5.1 %all-to-all-done = f16[8,112,256]{2,1,0:T(8,128)(2,1)S(1)} async-done(((f16[8,112,256]{2,1,0:T(8,128)(2,1)}), f16[8,112,256]{2,1,0:T(8,128)(2,1)S(1)}, u32[]{:S(2)}, u32[]{:S(2)}) %all-to-all-start) | async-done | bytes 458784 | tf_op jit(solution)/shard_map/all_to_all | solution.py:619
  29.5 0.1 convert_multiply_fusion.blocks_ref
  29.6 0.0 copy-done.2
  29.6 0.0 copy-done.3
  29.6 1.8 %pairs.1 = bf16[8,112,256]{2,1,0:T(8,128)(2,1)} custom-call(s32[1]{0:T(128)} %bitcast.1.place_ref, f32[8,112,256]{2,1,0:T(8,128)S(1)} %convert_multiply_fusion.blocks_ref, f32[100,2048]{1,0:T(8,128)S(1)} %copy-done.2, f32[1,2048]{1,0:T(1,128)S(1)} %bitcast.18), custom_call_target="tpu_custom_call" | custom-call | flops 4194304 | bytes 2097152 | tf_op jit(solution)/shard_map/pairs/pallas_call | solution.py:234
  31.5 3.7 %all-to-all-start.1 = ((bf16[8,112,256]{2,1,0:T(8,128)(2,1)}), bf16[8,112,256]{2,1,0:T(8,128)(2,1)S(1)}, u32[]{:S(2)}, u32[]{:S(2)}) async-start(bf16[8,112,256]{2,1,0:T(8,128)(2,1)} %pairs.1), calls=%async_computation.1 | async-start | bytes 917504 | tf_op jit(solution)/shard_map/all_to_all | solution.py:624
  35.1 0.0 copy-start.1
  35.1 2.2 %copy-done.1 = bf16[1,2048,1024]{2,1,0:T(8,128)(2,1)S(1)} copy-done((bf16[1,2048,1024]{2,1,0:T(8,128)(2,1)S(1)}, bf16[1,2048,1024]{2,1,0:T(8,128)(2,1)}, u32[]{:S(2)}) %copy-start.1) | copy-done | bytes 4194328
  37.3 1.1 %turned.1.turned_hbm = bf16[1024,2048]{1,0:T(8,128)(2,1)S(1)} custom-call(s32[1]{0:T(128)} %bitcast.grid_ref, bf16[2048,1024]{1,0:T(8,128)(2,1)S(1)} %bitcast.17), custom_call_target="tpu_custom_call" | custom-call | bytes 8388608 | tf_op jit(solution)/shard_map/turned/pallas_call | solution.py:281
  38.5 0.0 copy-start
  38.5 2.0 %copy-done = bf16[1024,2048]{1,0:T(8,128)(2,1)} copy-done((bf16[1024,2048]{1,0:T(8,128)(2,1)}, bf16[1024,2048]{1,0:T(8,128)(2,1)S(1)}, u32[]{:S(2)}) %copy-start) | copy-done | bytes 4194328
  40.5 4.4 %all-to-all-done.1.low_ref = bf16[8,112,256]{2,1,0:T(8,128)(2,1)S(1)} async-done(((bf16[8,112,256]{2,1,0:T(8,128)(2,1)}), bf16[8,112,256]{2,1,0:T(8,128)(2,1)S(1)}, u32[]{:S(2)}, u32[]{:S(2)}) %all-to-all-start.1) | async-done | bytes 458784 | tf_op jit(solution)/shard_map/all_to_all | solution.py:624
  44.8 5.0 %send_a.1 = (bf16[2048,1024]{1,0:T(8,128)(2,1)S(1)}, bf16[256,1152]{1,0:T(8,128)(2,1)S(1)}, bf16[256,128]{1,0:T(8,128)(2,1)S(1)}, bf16[128,2048]{1,0:T(8,128)(2,1)S(1)}, bf16[256,2048]{1,0:T(8,128)(2,1)S(1)}) custom-call(s32[1]{0:T(128)} %bitcast.grid_ref, bf16[8,112,256]{2,1,0:T(8,128)(2,1)S(1)} %all-to-all-done.1.low_ref, bf16[1024,2048]{1,0:T(8,128)(2,1)} %copy-done, ...), custom_call_target="tpu_custom_call" | custom-call | flops 1879048192 | bytes 8388608 | tf_op jit(solution)/shard_map/send_a/pallas_call | solution.py:430
  49.9 0.1 collective-permute-start
  50.0 1.3 %keep_a.1 = (bf16[256,1152]{1,0:T(8,128)(2,1)S(1)}, bf16[256,2048]{1,0:T(8,128)(2,1)S(1)}) custom-call(bf16[1024,2048]{1,0:T(8,128)(2,1)} %copy-done, bf16[2048,1024]{1,0:T(8,128)(2,1)S(1)} %get-tuple-element.71.pre_ref, bf16[256,2048]{1,0:T(8,128)(2,1)S(1)} %get-tuple-element.54.turned_ref, bf16[256,128]{1,0:T(8,128)(2,1)S(1)} %get-tuple-element.55.second_ref), custom_call_target="tpu_custom_call" | custom-call | flops 1073741824 | bytes 4194304 | tf_op jit(solution)/shard_map/keep_a/pallas_call | solution.py:459
  51.2 0.7 collective-permute-done
  52.0 0.1 add_convert_fusion
  52.2 3.2 %send_b.1 = (bf16[256,1152]{1,0:T(8,128)(2,1)S(1)}, bf16[256,128]{1,0:T(8,128)(2,1)S(1)}, bf16[256,2048]{1,0:T(8,128)(2,1)S(1)}) custom-call(s32[1]{0:T(128)} %bitcast.grid_ref, bf16[1024,2048]{1,0:T(8,128)(2,1)} %copy-done, bf16[8,2048,128]{2,1,0:T(8,128)(2,1)} %get-tuple-element.51.hidden_hbm, bf16[2048,1024]{1,0:T(8,128)(2,1)S(1)} %get-tuple-element.71.pre_ref, ...), custom_call_target="tpu_custom_call" | custom-call | flops 1073741824 | bytes 4194304 | tf_op jit(solution)/shard_map/send_b/pallas_call | solution.py:473
  55.3 0.2 collective-permute-start.1
  55.5 1.9 %collective-permute-start.2 = (bf16[64,1152]{1,0:T(8,128)(2,1)S(1)}, bf16[64,1152]{1,0:T(8,128)(2,1)S(1)}, u32[]{:S(2)}, u32[]{:S(2)}) collective-permute-start(bf16[64,1152]{1,0:T(8,128)(2,1)S(1)} %get-tuple-element.65), channel_id=1, source_target_pairs={{0,2},{1,3},{2,4},{3,5},{4,6},{5,7},{6,0},{7,1},{8,10},{9,11},{10,... | collective-permute-start | bytes 442376 | tf_op jit(solution)/shard_map/ppermute | solution.py:573
  57.5 2.1 %collective-permute-start.3 = (bf16[64,1152]{1,0:T(8,128)(2,1)S(1)}, bf16[64,1152]{1,0:T(8,128)(2,1)S(1)}, u32[]{:S(2)}, u32[]{:S(2)}) collective-permute-start(bf16[64,1152]{1,0:T(8,128)(2,1)S(1)} %get-tuple-element.66), channel_id=1, source_target_pairs={{0,6},{1,7},{2,0},{3,1},{4,2},{5,3},{6,4},{7,5},{8,14},{9,15},{10,... | collective-permute-start | bytes 442376 | tf_op jit(solution)/shard_map/ppermute | solution.py:573
  59.6 2.0 %collective-permute-start.5 = (bf16[64,1152]{1,0:T(8,128)(2,1)S(1)}, bf16[64,1152]{1,0:T(8,128)(2,1)S(1)}, u32[]{:S(2)}, u32[]{:S(2)}) collective-permute-start(bf16[64,1152]{1,0:T(8,128)(2,1)S(1)} %get-tuple-element.68), channel_id=1, source_target_pairs={{0,6},{1,7},{2,0},{3,1},{4,2},{5,3},{6,4},{7,5},{8,14},{9,15},{10,... | collective-permute-start | bytes 442376 | tf_op jit(solution)/shard_map/ppermute | solution.py:573
  61.6 0.0 collective-permute-start.6
  61.6 1.6 %keep_b.1 = (bf16[256,1152]{1,0:T(8,128)(2,1)S(1)}, bf16[1024,1024]{1,0:T(8,128)(2,1)S(1)}) custom-call(bf16[1024,1024]{1,0:T(8,128)(2,1)} %weight_hbm.1, bf16[2048,1024]{1,0:T(8,128)(2,1)S(1)} %get-tuple-element.71.pre_ref, bf16[256,2048]{1,0:T(8,128)(2,1)S(1)} %get-tuple-element.61.turned_ref, bf16[256,128]{1,0:T(8,128)(2,1)S(1)} %get-tuple-element.62.second_ref), custom_call_target="tpu_custom_call" | custom-call | flops 1073741824 | bytes 4194304 | tf_op jit(solution)/shard_map/keep_b/pallas_call | solution.py:492
  63.2 0.0 collective-permute-done.1
  63.3 0.1 convert_add_fusion
  63.4 0.6 collective-permute-done.2
  64.0 0.2 collective-permute-done.3
  64.1 0.1 fusion.2
  64.2 2.0 %collective-permute-start.4 = (bf16[64,1152]{1,0:T(8,128)(2,1)S(1)}, bf16[64,1152]{1,0:T(8,128)(2,1)S(1)}, u32[]{:S(2)}, u32[]{:S(2)}) collective-permute-start(bf16[64,1152]{1,0:T(8,128)(2,1)S(1)} %get-tuple-element.67), channel_id=1, source_target_pairs={{0,2},{1,3},{2,4},{3,5},{4,6},{5,7},{6,0},{7,1},{8,10},{9,11},{10,... | collective-permute-start | bytes 442376 | tf_op jit(solution)/shard_map/ppermute | solution.py:573
  66.2 1.7 %collective-permute-start.7 = (bf16[64,1152]{1,0:T(8,128)(2,1)S(1)}, bf16[64,1152]{1,0:T(8,128)(2,1)S(1)}, u32[]{:S(2)}, u32[]{:S(2)}) collective-permute-start(bf16[64,1152]{1,0:T(8,128)(2,1)S(1)} %get-tuple-element.70), channel_id=1, source_target_pairs={{0,6},{1,7},{2,0},{3,1},{4,2},{5,3},{6,4},{7,5},{8,14},{9,15},{10,... | collective-permute-start | bytes 442376 | tf_op jit(solution)/shard_map/ppermute | solution.py:573
  67.9 3.4 %latent_gradient.2.refs_0_ = bf16[2048,1024]{1,0:T(8,128)(2,1)} custom-call(bf16[2048,1024]{1,0:T(8,128)(2,1)S(1)} %get-tuple-element.71.pre_ref, bf16[1024,1024]{1,0:T(8,128)(2,1)S(1)} %get-tuple-element.72.weight_ref), custom_call_target="tpu_custom_call" | custom-call | flops 2147483648 | bytes 5242880 | tf_op jit(solution)/shard_map/latent_gradient/pallas_call | solution.py:528
  71.3 0.0 collective-permute-done.5
  71.3 0.0 collective-permute-done.6
  71.3 0.0 collective-permute-done.4
  71.3 0.0 collective-permute-done.7
  71.4 0.1 fusion.6
  71.6 0.7 collective-permute-start.9
  72.2 0.2 collective-permute-start.8
  72.4 3.9 %collective-permute-start.10 = (bf16[64,1152]{1,0:T(8,128)(2,1)S(1)}, bf16[64,1152]{1,0:T(8,128)(2,1)S(1)}, u32[]{:S(2)}, u32[]{:S(2)}) collective-permute-start(bf16[64,1152]{1,0:T(8,128)(2,1)S(1)} %get-tuple-element.88), channel_id=1, source_target_pairs={{0,16},{1,17},{2,18},{3,19},{4,20},{5,21},{6,22},{7,23},{8,24},{9,... | collective-permute-start | bytes 442376 | tf_op jit(solution)/shard_map/ppermute | solution.py:573
  76.3 3.4 %latent_gradient.3 = bf16[2048,1024]{1,0:T(8,128)(2,1)} custom-call(bf16[2048,1024]{1,0:T(8,128)(2,1)S(1)} %get-tuple-element.71.pre_ref, bf16[1024,1024]{1,0:T(8,128)(2,1)S(1)} %get-tuple-element.72.weight_ref, bf16[2048,1024]{1,0:T(8,128)(2,1)} %latent_gradient.2.refs_0_), custom_call_target="tpu_custom_call", output_to_operand_aliasing={{}: (2, {})} | custom-call | flops 2147483648 | bytes 5242880 | tf_op jit(solution)/shard_map/latent_gradient/pallas_call | solution.py:528
  79.7 2.1 %collective-permute-done.10 = bf16[64,1152]{1,0:T(8,128)(2,1)S(1)} collective-permute-done((bf16[64,1152]{1,0:T(8,128)(2,1)S(1)}, bf16[64,1152]{1,0:T(8,128)(2,1)S(1)}, u32[]{:S(2)}, u32[]{:S(2)}) %collective-permute-start.10) | collective-permute-done | bytes 147488 | tf_op jit(solution)/shard_map/ppermute | solution.py:573
  81.8 0.0 collective-permute-done.9
  81.8 0.0 collective-permute-done.8
  81.8 0.1 add_convert_fusion.1.own_ref
  81.9 0.9 %collective-permute-start.13 = (bf16[64,1152]{1,0:T(8,128)(2,1)S(1)}, bf16[64,1152]{1,0:T(8,128)(2,1)S(1)}, u32[]{:S(2)}, u32[]{:S(2)}) collective-permute-start(bf16[64,1152]{1,0:T(8,128)(2,1)S(1)} %add_convert_fusion.1.own_ref), channel_id=1, source_target_pairs={{0,64},{1,65},{2,66},{3,67},{4,68},{5,69},{6,70},{7,71},{8,72},{9,... | collective-permute-start | bytes 442376 | tf_op jit(solution)/shard_map/ppermute | solution.py:573
  82.8 2.1 %collective-permute-start.12 = (bf16[64,1152]{1,0:T(8,128)(2,1)S(1)}, bf16[64,1152]{1,0:T(8,128)(2,1)S(1)}, u32[]{:S(2)}, u32[]{:S(2)}) collective-permute-start(bf16[64,1152]{1,0:T(8,128)(2,1)S(1)} %add_convert_fusion.1.own_ref), channel_id=1, source_target_pairs={{0,96},{1,97},{2,98},{3,99},{4,100},{5,101},{6,102},{7,103},{8,104... | collective-permute-start | bytes 442376 | tf_op jit(solution)/shard_map/ppermute | solution.py:573
  84.9 0.6 collective-permute-start.11
  85.5 3.3 %collective-permute-done.13.refs_2_ = bf16[64,1152]{1,0:T(8,128)(2,1)S(1)} collective-permute-done((bf16[64,1152]{1,0:T(8,128)(2,1)S(1)}, bf16[64,1152]{1,0:T(8,128)(2,1)S(1)}, u32[]{:S(2)}, u32[]{:S(2)}) %collective-permute-start.13) | collective-permute-done | bytes 147488 | tf_op jit(solution)/shard_map/ppermute | solution.py:573
  88.7 1.5 %collective-permute-done.12.refs_1_ = bf16[64,1152]{1,0:T(8,128)(2,1)S(1)} collective-permute-done((bf16[64,1152]{1,0:T(8,128)(2,1)S(1)}, bf16[64,1152]{1,0:T(8,128)(2,1)S(1)}, u32[]{:S(2)}, u32[]{:S(2)}) %collective-permute-start.12) | collective-permute-done | bytes 147488 | tf_op jit(solution)/shard_map/ppermute | solution.py:573
  90.2 0.0 collective-permute-done.11.refs_0_
  90.2 0.8 finish.1
  (3 shorter events, 0.1 us)
Async XLA Ops:
  11.6 17.9 %all-to-all-start = ((f16[8,112,256]{2,1,0:T(8,128)(2,1)}), f16[8,112,256]{2,1,0:T(8,128)(2,1)S(1)}, u32[]{:S(2)}, u32[]{:S(2)}) async-start(f16[8,112,256]{2,1,0:T(8,128)(2,1)} %multiply_convert_fusion), calls=%async_computation | async-start | bytes 917504 | tf_op jit(solution)/shard_map/all_to_all | solution.py:619
  18.7 11.0 %copy-start.2 = (f32[100,2048]{1,0:T(8,128)S(1)}, f32[100,2048]{1,0:T(8,128)}, u32[]{:S(2)}) copy-start(f32[100,2048]{1,0:T(8,128)} %observed_ref.1) | copy-start | bytes 2457604
  18.7 11.0 %copy-start.3 = (f32[2048]{0:T(1024)S(1)}, f32[2048]{0:T(1024)}, u32[]{:S(2)}) copy-start(f32[2048]{0:T(1024)} %param.9) | copy-start | bytes 24580
  31.5 13.4 %all-to-all-start.1 = ((bf16[8,112,256]{2,1,0:T(8,128)(2,1)}), bf16[8,112,256]{2,1,0:T(8,128)(2,1)S(1)}, u32[]{:S(2)}, u32[]{:S(2)}) async-start(bf16[8,112,256]{2,1,0:T(8,128)(2,1)} %pairs.1), calls=%async_computation.1 | async-start | bytes 917504 | tf_op jit(solution)/shard_map/all_to_all | solution.py:624
  35.1 2.2 %copy-start.1 = (bf16[1,2048,1024]{2,1,0:T(8,128)(2,1)S(1)}, bf16[1,2048,1024]{2,1,0:T(8,128)(2,1)}, u32[]{:S(2)}) copy-start(bf16[1,2048,1024]{2,1,0:T(8,128)(2,1)} %param.5) | copy-start | bytes 12582916
  38.5 2.0 %copy-start = (bf16[1024,2048]{1,0:T(8,128)(2,1)}, bf16[1024,2048]{1,0:T(8,128)(2,1)S(1)}, u32[]{:S(2)}) copy-start(bf16[1024,2048]{1,0:T(8,128)(2,1)S(1)} %turned.1.turned_hbm) | copy-start | bytes 12582916
  49.9 2.1 %collective-permute-start = (bf16[256,1152]{1,0:T(8,128)(2,1)S(1)}, bf16[256,1152]{1,0:T(8,128)(2,1)S(1)}, u32[]{:S(2)}, u32[]{:S(2)}) collective-permute-start(bf16[256,1152]{1,0:T(8,128)(2,1)S(1)} %get-tuple-element.57), channel_id=1, source_target_pairs={{0,1},{1,0},{2,3},{3,2},{4,5},{5,4},{6,7},{7,6},{8,9},{9,8},{10,11... | collective-permute-start | bytes 1769480 | tf_op jit(solution)/shard_map/ppermute | solution.py:573
  55.3 7.9 %collective-permute-start.1 = (bf16[256,1152]{1,0:T(8,128)(2,1)S(1)}, bf16[256,1152]{1,0:T(8,128)(2,1)S(1)}, u32[]{:S(2)}, u32[]{:S(2)}) collective-permute-start(bf16[256,1152]{1,0:T(8,128)(2,1)S(1)} %get-tuple-element.64), channel_id=1, source_target_pairs={{0,1},{1,0},{2,3},{3,2},{4,5},{5,4},{6,7},{7,6},{8,9},{9,8},{10,11... | collective-permute-start | bytes 1769480 | tf_op jit(solution)/shard_map/ppermute | solution.py:573
  55.5 8.4 %collective-permute-start.2 = (bf16[64,1152]{1,0:T(8,128)(2,1)S(1)}, bf16[64,1152]{1,0:T(8,128)(2,1)S(1)}, u32[]{:S(2)}, u32[]{:S(2)}) collective-permute-start(bf16[64,1152]{1,0:T(8,128)(2,1)S(1)} %get-tuple-element.65), channel_id=1, source_target_pairs={{0,2},{1,3},{2,4},{3,5},{4,6},{5,7},{6,0},{7,1},{8,10},{9,11},{10,... | collective-permute-start | bytes 442376 | tf_op jit(solution)/shard_map/ppermute | solution.py:573
  57.5 6.7 %collective-permute-start.3 = (bf16[64,1152]{1,0:T(8,128)(2,1)S(1)}, bf16[64,1152]{1,0:T(8,128)(2,1)S(1)}, u32[]{:S(2)}, u32[]{:S(2)}) collective-permute-start(bf16[64,1152]{1,0:T(8,128)(2,1)S(1)} %get-tuple-element.66), channel_id=1, source_target_pairs={{0,6},{1,7},{2,0},{3,1},{4,2},{5,3},{6,4},{7,5},{8,14},{9,15},{10,... | collective-permute-start | bytes 442376 | tf_op jit(solution)/shard_map/ppermute | solution.py:573
  59.6 11.7 %collective-permute-start.5 = (bf16[64,1152]{1,0:T(8,128)(2,1)S(1)}, bf16[64,1152]{1,0:T(8,128)(2,1)S(1)}, u32[]{:S(2)}, u32[]{:S(2)}) collective-permute-start(bf16[64,1152]{1,0:T(8,128)(2,1)S(1)} %get-tuple-element.68), channel_id=1, source_target_pairs={{0,6},{1,7},{2,0},{3,1},{4,2},{5,3},{6,4},{7,5},{8,14},{9,15},{10,... | collective-permute-start | bytes 442376 | tf_op jit(solution)/shard_map/ppermute | solution.py:573
  61.6 9.7 %collective-permute-start.6 = (bf16[64,1152]{1,0:T(8,128)(2,1)S(1)}, bf16[64,1152]{1,0:T(8,128)(2,1)S(1)}, u32[]{:S(2)}, u32[]{:S(2)}) collective-permute-start(bf16[64,1152]{1,0:T(8,128)(2,1)S(1)} %get-tuple-element.69), channel_id=1, source_target_pairs={{0,2},{1,3},{2,4},{3,5},{4,6},{5,7},{6,0},{7,1},{8,10},{9,11},{10,... | collective-permute-start | bytes 442376 | tf_op jit(solution)/shard_map/ppermute | solution.py:573
  64.2 7.1 %collective-permute-start.4 = (bf16[64,1152]{1,0:T(8,128)(2,1)S(1)}, bf16[64,1152]{1,0:T(8,128)(2,1)S(1)}, u32[]{:S(2)}, u32[]{:S(2)}) collective-permute-start(bf16[64,1152]{1,0:T(8,128)(2,1)S(1)} %get-tuple-element.67), channel_id=1, source_target_pairs={{0,2},{1,3},{2,4},{3,5},{4,6},{5,7},{6,0},{7,1},{8,10},{9,11},{10,... | collective-permute-start | bytes 442376 | tf_op jit(solution)/shard_map/ppermute | solution.py:573
  66.2 5.1 %collective-permute-start.7 = (bf16[64,1152]{1,0:T(8,128)(2,1)S(1)}, bf16[64,1152]{1,0:T(8,128)(2,1)S(1)}, u32[]{:S(2)}, u32[]{:S(2)}) collective-permute-start(bf16[64,1152]{1,0:T(8,128)(2,1)S(1)} %get-tuple-element.70), channel_id=1, source_target_pairs={{0,6},{1,7},{2,0},{3,1},{4,2},{5,3},{6,4},{7,5},{8,14},{9,15},{10,... | collective-permute-start | bytes 442376 | tf_op jit(solution)/shard_map/ppermute | solution.py:573
  71.6 10.3 %collective-permute-start.9 = (bf16[64,1152]{1,0:T(8,128)(2,1)S(1)}, bf16[64,1152]{1,0:T(8,128)(2,1)S(1)}, u32[]{:S(2)}, u32[]{:S(2)}) collective-permute-start(bf16[64,1152]{1,0:T(8,128)(2,1)S(1)} %get-tuple-element.87), channel_id=1, source_target_pairs={{0,24},{1,25},{2,26},{3,27},{4,28},{5,29},{6,30},{7,31},{8,16},{9,... | collective-permute-start | bytes 442376 | tf_op jit(solution)/shard_map/ppermute | solution.py:573
  72.2 9.6 %collective-permute-start.8 = (bf16[64,1152]{1,0:T(8,128)(2,1)S(1)}, bf16[64,1152]{1,0:T(8,128)(2,1)S(1)}, u32[]{:S(2)}, u32[]{:S(2)}) collective-permute-start(bf16[64,1152]{1,0:T(8,128)(2,1)S(1)} %get-tuple-element.87), channel_id=1, source_target_pairs={{0,8},{1,9},{2,10},{3,11},{4,12},{5,13},{6,14},{7,15},{8,0},{9,1},... | collective-permute-start | bytes 442376 | tf_op jit(solution)/shard_map/ppermute | solution.py:573
  72.4 9.4 %collective-permute-start.10 = (bf16[64,1152]{1,0:T(8,128)(2,1)S(1)}, bf16[64,1152]{1,0:T(8,128)(2,1)S(1)}, u32[]{:S(2)}, u32[]{:S(2)}) collective-permute-start(bf16[64,1152]{1,0:T(8,128)(2,1)S(1)} %get-tuple-element.88), channel_id=1, source_target_pairs={{0,16},{1,17},{2,18},{3,19},{4,20},{5,21},{6,22},{7,23},{8,24},{9,... | collective-permute-start | bytes 442376 | tf_op jit(solution)/shard_map/ppermute | solution.py:573
  81.9 6.8 %collective-permute-start.13 = (bf16[64,1152]{1,0:T(8,128)(2,1)S(1)}, bf16[64,1152]{1,0:T(8,128)(2,1)S(1)}, u32[]{:S(2)}, u32[]{:S(2)}) collective-permute-start(bf16[64,1152]{1,0:T(8,128)(2,1)S(1)} %add_convert_fusion.1.own_ref), channel_id=1, source_target_pairs={{0,64},{1,65},{2,66},{3,67},{4,68},{5,69},{6,70},{7,71},{8,72},{9,... | collective-permute-start | bytes 442376 | tf_op jit(solution)/shard_map/ppermute | solution.py:573
  82.8 7.4 %collective-permute-start.12 = (bf16[64,1152]{1,0:T(8,128)(2,1)S(1)}, bf16[64,1152]{1,0:T(8,128)(2,1)S(1)}, u32[]{:S(2)}, u32[]{:S(2)}) collective-permute-start(bf16[64,1152]{1,0:T(8,128)(2,1)S(1)} %add_convert_fusion.1.own_ref), channel_id=1, source_target_pairs={{0,96},{1,97},{2,98},{3,99},{4,100},{5,101},{6,102},{7,103},{8,104... | collective-permute-start | bytes 442376 | tf_op jit(solution)/shard_map/ppermute | solution.py:573
  84.9 5.3 %collective-permute-start.11 = (bf16[64,1152]{1,0:T(8,128)(2,1)S(1)}, bf16[64,1152]{1,0:T(8,128)(2,1)S(1)}, u32[]{:S(2)}, u32[]{:S(2)}) collective-permute-start(bf16[64,1152]{1,0:T(8,128)(2,1)S(1)} %add_convert_fusion.1.own_ref), channel_id=1, source_target_pairs={{0,32},{1,33},{2,34},{3,35},{4,36},{5,37},{6,38},{7,39},{8,40},{9,... | collective-permute-start | bytes 442376 | tf_op jit(solution)/shard_map/ppermute | solution.py:573

commit v16 on v15

--- a/solution.py
+++ b/solution.py
@@ -379,38 +379,38 @@
     turned_next.wait()
 
 
-def keep_a_kernel(turned_hbm, pre_ref, turned_ref, second_ref, keep_ref, next_turned_ref, turned_sem):
-    load = turned_load(turned_hbm, 512, next_turned_ref, turned_sem)
-    load.start()
+def keep_a_kernel(turned_hbm, pre_ref, turned_ref, second_ref, keep_ref, next_turned_ref, last_turned_ref, turned_sems):
+    loads = [
+        turned_load(turned_hbm, 512, next_turned_ref, turned_sems.at[0]),
+        turned_load(turned_hbm, 768, last_turned_ref, turned_sems.at[1]),
+    ]
+    for load in loads:
+        load.start()
     first_product(turned_ref, pre_ref, keep_ref)
     keep_ref[:, pre_ref.shape[1] :] = second_ref[...]
-    load.wait()
+    for load in loads:
+        load.wait()
 
 
 def send_b_kernel(
     grid_ref,
-    turned_hbm,
     hidden_hbm,
     pre_ref,
     flat_ref,
     turned_ref,
     send_ref,
     second_ref,
-    next_turned_ref,
     hidden_ref,
     scratch_ref,
-    turned_sem,
     hidden_sems,
 ):
     loads = hidden_loads(1, grid_ref, hidden_hbm, hidden_ref, hidden_sems)
-    loads.append(turned_load(turned_hbm, 768, next_turned_ref, turned_sem))
     for load in loads:
         load.start()
     first_product(turned_ref, pre_ref, send_ref)
-    for load in loads[:-1]:
+    for load in loads:
         load.wait()
     second_product(grid_ref, flat_ref, hidden_ref, send_ref, second_ref, scratch_ref)
-    loads[-1].wait()
 
 
 def keep_b_kernel(weight_hbm, pre_ref, turned_ref, second_ref, keep_ref, weight_ref, weight_sem):
@@ -459,32 +459,31 @@
     return pl.pallas_call(
         keep_a_kernel,
         in_specs=[anywhere] + [vmem] * 3,
-        out_specs=[vmem] * 2,
-        out_shape=[shape(256, width + WIDE), shape(256, nodes)],
-        scratch_shapes=[pltpu.SemaphoreType.DMA],
+        out_specs=[vmem] * 3,
+        out_shape=[shape(256, width + WIDE), shape(256, nodes), shape(256, nodes)],
+        scratch_shapes=[pltpu.SemaphoreType.DMA((2,))],
         compiler_params=params(12),
         cost_estimate=cost(nodes * width * width // 2, 4 << 20),
         name="keep_a",
     )(pinned(turned_latent), grad_pre, turned_now, second)
 
 
-def send_b(grid, turned_latent, hidden, grad_pre, flat, turned_now):
+def send_b(grid, hidden, grad_pre, flat, turned_now):
     nodes, width = grad_pre.shape
     return pl.pallas_call(
         send_b_kernel,
-        in_specs=[smem, anywhere, anywhere] + [vmem] * 3,
-        out_specs=[vmem] * 3,
-        out_shape=[shape(256, width + WIDE), shape(256, WIDE), shape(256, nodes)],
+        in_specs=[smem, anywhere] + [vmem] * 3,
+        out_specs=[vmem] * 2,
+        out_shape=[shape(256, width + WIDE), shape(256, WIDE)],
         scratch_shapes=[
             pltpu.VMEM((4, nodes, 128), bf16),
             pltpu.VMEM((512, WIDE), bf16),
-            pltpu.SemaphoreType.DMA,
             pltpu.SemaphoreType.DMA((4,)),
         ],
         compiler_params=params(12),
         cost_estimate=cost(nodes * width * width // 2, 4 << 20),
         name="send_b",
-    )(grid, pinned(turned_latent), pinned(hidden), grad_pre, flat, turned_now)
+    )(grid, pinned(hidden), grad_pre, flat, turned_now)
 
 
 def keep_b(weight, grad_pre, turned_now, second):
@@ -624,13 +623,13 @@
     low = lax.all_to_all(low, "member", 0, 0, tiled=True)
     turned_latent = turned(late_grid, latent)
     grad_pre, rows_a, second_a, flat, turned_now = send_a(grid, low, turned_latent, slope, hidden, padded)
-    kept_a, turned_now = keep_a(turned_latent, grad_pre, turned_now, second_a)
+    kept_a, turned_now, turned_last = keep_a(turned_latent, grad_pre, turned_now, second_a)
     far_up, far_down, near_up, near_down = over_core(rows_a, kept_a).astype(bf16)
     far_up, far_down, near_up, near_down, flat = lax.optimization_barrier((far_up, far_down, near_up, near_down, flat))
     upward, downward = up(far_up), down(far_down)
     from_below, from_above = up(near_up), down(near_down)
-    rows_b, second_b, turned_now = send_b(grid, turned_latent, hidden, grad_pre, flat, turned_now)
-    kept_b, weight_copy = keep_b(hidden_weight, grad_pre, turned_now, second_b)
+    rows_b, second_b = send_b(grid, hidden, grad_pre, flat, turned_now)
+    kept_b, weight_copy = keep_b(hidden_weight, grad_pre, turned_last, second_b)
     above, below, own, other = over_core(rows_b, kept_b)
     above = (above + upward.astype(f32)).astype(bf16)
     below = (below + downward.astype(f32)).astype(bf16)

time: 91.4 us -> 91.4 us (level)
  no operation moved by 1% of the time
where the time goes in v16:
time: 91.4 us; the launch traced here: 91 us
  Pallas kernels  37.7 us (41%)
  starting transfers between devices  29.1 us (32%)
  waiting for transfers between devices  17.6 us (19%)
  local copies, waits for them, and re-layouts  4.27 us (5%)
  other arithmetic  1.53 us (2%)
    ppermute x14, starting transfers between devices, moved(): return lax.ppermute(value, ('member', 'grid'), moves)  18.5 us
    pallas_call x1, Pallas kernels, forward(): pl.pallas_call(forward_kernel, in_specs=[anywhere] * 3, out_specs=[vmem,...  10.1 us
    ppermute x14, waiting for transfers between devices, moved(): return lax.ppermute(value, ('member', 'grid'), moves)  8.11 us
    all_to_all x1, starting transfers between devices, body(): blocks = lax.all_to_all(blocks, 'member', 0, 0, tiled=True)  7.02 us
    pallas_call x2, Pallas kernels, latent_gradient(): pl.pallas_call(functools.partial(latent_kernel, begin=begin), in_specs=[v...  6.75 us
    pallas_call x1, Pallas kernels, gates(): pl.pallas_call(gate_kernel, in_specs=[anywhere], out_specs=[anywhere] * 2...  5.78 us
    all_to_all x1, waiting for transfers between devices, body(): blocks = lax.all_to_all(blocks, 'member', 0, 0, tiled=True)  5.07 us
    pallas_call x1, Pallas kernels, send_a(): pl.pallas_call(send_a_kernel, in_specs=[smem, vmem, anywhere, anywhere, a...  5.02 us
  transfers between devices with their start and end apart: 16, of which 8 were waited for; matrix products, arithmetic and copies ran while one was open for 0% of the time, Pallas kernels for 18%

profile of v16, /device:TPU:0, one launch (start us, length us, event | category | flops | bytes accessed | tf_op | source)
XLA Modules:
  0.0 91.0 jit_solution(13664228082760917259)
XLA Ops:
  0.6 10.1 %forward.1 = (f32[8,112,256]{2,1,0:T(8,128)S(1)}, bf16[2048,1024]{1,0:T(8,128)(2,1)}, bf16[1024,128]{1,0:T(8,128)(2,1)S(1)}) custom-call(bf16[2048,1024]{1,0:T(8,128)(2,1)} %bitcast.16, bf16[1024,1024]{1,0:T(8,128)(2,1)} %weight_hbm.1, bf16[100,1024]{1,0:T(8,128)(2,1)} %bitcast.20), custom_call_target="tpu_custom_call" | custom-call | flops 4831838208 | bytes 20971520 | tf_op jit(solution)/shard_map/forward/pallas_call | solution.py:102
  10.7 0.9 %multiply_convert_fusion = f16[8,112,256]{2,1,0:T(8,128)(2,1)} fusion(f32[8,112,256]{2,1,0:T(8,128)S(1)} %get-tuple-element.41), kind=kLoop, calls=%fused_computation.3 | loop fusion | flops 458752 | bytes 1376256 | tf_op jit(solution)/shard_map/convert_element_type | solution.py:617
  11.6 7.0 %all-to-all-start = ((f16[8,112,256]{2,1,0:T(8,128)(2,1)}), f16[8,112,256]{2,1,0:T(8,128)(2,1)S(1)}, u32[]{:S(2)}, u32[]{:S(2)}) async-start(f16[8,112,256]{2,1,0:T(8,128)(2,1)} %multiply_convert_fusion), calls=%async_computation | async-start | bytes 917504 | tf_op jit(solution)/shard_map/all_to_all | solution.py:618
  18.7 0.0 copy-start.2
  18.7 0.0 copy-start.3
  18.7 5.8 %gates.1 = (bf16[8,2048,128]{2,1,0:T(8,128)(2,1)}, bf16[2048,1024]{1,0:T(8,128)(2,1)}) custom-call(bf16[2048,1024]{1,0:T(8,128)(2,1)} %get-tuple-element.44.pre_hbm), custom_call_target="tpu_custom_call" | custom-call | bytes 12582912 | tf_op jit(solution)/shard_map/gates/pallas_call | solution.py:162
  24.5 5.1 %all-to-all-done = f16[8,112,256]{2,1,0:T(8,128)(2,1)S(1)} async-done(((f16[8,112,256]{2,1,0:T(8,128)(2,1)}), f16[8,112,256]{2,1,0:T(8,128)(2,1)S(1)}, u32[]{:S(2)}, u32[]{:S(2)}) %all-to-all-start) | async-done | bytes 458784 | tf_op jit(solution)/shard_map/all_to_all | solution.py:618
  29.5 0.1 convert_multiply_fusion.blocks_ref
  29.6 0.0 copy-done.2
  29.6 0.0 copy-done.3
  29.6 1.8 %pairs.1 = bf16[8,112,256]{2,1,0:T(8,128)(2,1)} custom-call(s32[1]{0:T(128)} %bitcast.1.place_ref, f32[8,112,256]{2,1,0:T(8,128)S(1)} %convert_multiply_fusion.blocks_ref, f32[100,2048]{1,0:T(8,128)S(1)} %copy-done.2, f32[1,2048]{1,0:T(1,128)S(1)} %bitcast.18), custom_call_target="tpu_custom_call" | custom-call | flops 4194304 | bytes 2097152 | tf_op jit(solution)/shard_map/pairs/pallas_call | solution.py:234
  31.5 3.7 %all-to-all-start.1 = ((bf16[8,112,256]{2,1,0:T(8,128)(2,1)}), bf16[8,112,256]{2,1,0:T(8,128)(2,1)S(1)}, u32[]{:S(2)}, u32[]{:S(2)}) async-start(bf16[8,112,256]{2,1,0:T(8,128)(2,1)} %pairs.1), calls=%async_computation.1 | async-start | bytes 917504 | tf_op jit(solution)/shard_map/all_to_all | solution.py:623
  35.1 0.0 copy-start.1
  35.1 2.2 %copy-done.1 = bf16[1,2048,1024]{2,1,0:T(8,128)(2,1)S(1)} copy-done((bf16[1,2048,1024]{2,1,0:T(8,128)(2,1)S(1)}, bf16[1,2048,1024]{2,1,0:T(8,128)(2,1)}, u32[]{:S(2)}) %copy-start.1) | copy-done | bytes 4194328
  37.3 1.1 %turned.1.turned_hbm = bf16[1024,2048]{1,0:T(8,128)(2,1)S(1)} custom-call(s32[1]{0:T(128)} %bitcast.grid_ref, bf16[2048,1024]{1,0:T(8,128)(2,1)S(1)} %bitcast.17), custom_call_target="tpu_custom_call" | custom-call | bytes 8388608 | tf_op jit(solution)/shard_map/turned/pallas_call | solution.py:281
  38.5 0.0 copy-start
  38.5 2.0 %copy-done = bf16[1024,2048]{1,0:T(8,128)(2,1)} copy-done((bf16[1024,2048]{1,0:T(8,128)(2,1)}, bf16[1024,2048]{1,0:T(8,128)(2,1)S(1)}, u32[]{:S(2)}) %copy-start) | copy-done | bytes 4194328
  40.5 4.4 %all-to-all-done.1.low_ref = bf16[8,112,256]{2,1,0:T(8,128)(2,1)S(1)} async-done(((bf16[8,112,256]{2,1,0:T(8,128)(2,1)}), bf16[8,112,256]{2,1,0:T(8,128)(2,1)S(1)}, u32[]{:S(2)}, u32[]{:S(2)}) %all-to-all-start.1) | async-done | bytes 458784 | tf_op jit(solution)/shard_map/all_to_all | solution.py:623
  44.8 5.0 %send_a.1 = (bf16[2048,1024]{1,0:T(8,128)(2,1)S(1)}, bf16[256,1152]{1,0:T(8,128)(2,1)S(1)}, bf16[256,128]{1,0:T(8,128)(2,1)S(1)}, bf16[128,2048]{1,0:T(8,128)(2,1)S(1)}, bf16[256,2048]{1,0:T(8,128)(2,1)S(1)}) custom-call(s32[1]{0:T(128)} %bitcast.grid_ref, bf16[8,112,256]{2,1,0:T(8,128)(2,1)S(1)} %all-to-all-done.1.low_ref, bf16[1024,2048]{1,0:T(8,128)(2,1)} %copy-done, ...), custom_call_target="tpu_custom_call" | custom-call | flops 1879048192 | bytes 8388608 | tf_op jit(solution)/shard_map/send_a/pallas_call | solution.py:430
  49.9 0.1 collective-permute-start
  50.0 1.6 %keep_a.1 = (bf16[256,1152]{1,0:T(8,128)(2,1)S(1)}, bf16[256,2048]{1,0:T(8,128)(2,1)S(1)}, bf16[256,2048]{1,0:T(8,128)(2,1)S(1)}) custom-call(bf16[1024,2048]{1,0:T(8,128)(2,1)} %copy-done, bf16[2048,1024]{1,0:T(8,128)(2,1)S(1)} %get-tuple-element.71.pre_ref, bf16[256,2048]{1,0:T(8,128)(2,1)S(1)} %get-tuple-element.54.turned_ref, ...), custom_call_target="tpu_custom_call" | custom-call | flops 1073741824 | bytes 4194304 | tf_op jit(solution)/shard_map/keep_a/pallas_call | solution.py:459
  51.5 0.4 collective-permute-done
  52.0 0.1 add_convert_fusion
  52.2 3.2 %send_b.1 = (bf16[256,1152]{1,0:T(8,128)(2,1)S(1)}, bf16[256,128]{1,0:T(8,128)(2,1)S(1)}) custom-call(s32[1]{0:T(128)} %bitcast.grid_ref, bf16[8,2048,128]{2,1,0:T(8,128)(2,1)} %get-tuple-element.51.hidden_hbm, bf16[2048,1024]{1,0:T(8,128)(2,1)S(1)} %get-tuple-element.71.pre_ref, bf16[128,2048]{1,0:T(8,128)(2,1)S(1)} %get-tuple-element.60.flat_ref, ...), custom_call_target="tpu_custom_call" | custom-call | flops 1073741824 | bytes 4194304 | tf_op jit(solution)/shard_map/send_b/pallas_call | solution.py:473
  55.3 0.2 collective-permute-start.1
  55.6 1.9 %collective-permute-start.2 = (bf16[64,1152]{1,0:T(8,128)(2,1)S(1)}, bf16[64,1152]{1,0:T(8,128)(2,1)S(1)}, u32[]{:S(2)}, u32[]{:S(2)}) collective-permute-start(bf16[64,1152]{1,0:T(8,128)(2,1)S(1)} %get-tuple-element.65), channel_id=1, source_target_pairs={{0,2},{1,3},{2,4},{3,5},{4,6},{5,7},{6,0},{7,1},{8,10},{9,11},{10,... | collective-permute-start | bytes 442376 | tf_op jit(solution)/shard_map/ppermute | solution.py:572
  57.5 2.1 %collective-permute-start.3 = (bf16[64,1152]{1,0:T(8,128)(2,1)S(1)}, bf16[64,1152]{1,0:T(8,128)(2,1)S(1)}, u32[]{:S(2)}, u32[]{:S(2)}) collective-permute-start(bf16[64,1152]{1,0:T(8,128)(2,1)S(1)} %get-tuple-element.66), channel_id=1, source_target_pairs={{0,6},{1,7},{2,0},{3,1},{4,2},{5,3},{6,4},{7,5},{8,14},{9,15},{10,... | collective-permute-start | bytes 442376 | tf_op jit(solution)/shard_map/ppermute | solution.py:572
  59.6 2.0 %collective-permute-start.5 = (bf16[64,1152]{1,0:T(8,128)(2,1)S(1)}, bf16[64,1152]{1,0:T(8,128)(2,1)S(1)}, u32[]{:S(2)}, u32[]{:S(2)}) collective-permute-start(bf16[64,1152]{1,0:T(8,128)(2,1)S(1)} %get-tuple-element.68), channel_id=1, source_target_pairs={{0,6},{1,7},{2,0},{3,1},{4,2},{5,3},{6,4},{7,5},{8,14},{9,15},{10,... | collective-permute-start | bytes 442376 | tf_op jit(solution)/shard_map/ppermute | solution.py:572
  61.7 0.0 collective-permute-start.6
  61.7 1.6 %keep_b.1 = (bf16[256,1152]{1,0:T(8,128)(2,1)S(1)}, bf16[1024,1024]{1,0:T(8,128)(2,1)S(1)}) custom-call(bf16[1024,1024]{1,0:T(8,128)(2,1)} %weight_hbm.1, bf16[2048,1024]{1,0:T(8,128)(2,1)S(1)} %get-tuple-element.71.pre_ref, bf16[256,2048]{1,0:T(8,128)(2,1)S(1)} %get-tuple-element.56.turned_ref, bf16[256,128]{1,0:T(8,128)(2,1)S(1)} %get-tuple-element.62.second_ref), custom_call_target="tpu_custom_call" | custom-call | flops 1073741824 | bytes 4194304 | tf_op jit(solution)/shard_map/keep_b/pallas_call | solution.py:491
  63.3 0.0 collective-permute-done.1
  63.3 0.1 convert_add_fusion
  63.4 0.6 collective-permute-done.2
  64.0 0.2 collective-permute-done.3
  64.2 0.1 fusion.2
  64.2 2.0 %collective-permute-start.4 = (bf16[64,1152]{1,0:T(8,128)(2,1)S(1)}, bf16[64,1152]{1,0:T(8,128)(2,1)S(1)}, u32[]{:S(2)}, u32[]{:S(2)}) collective-permute-start(bf16[64,1152]{1,0:T(8,128)(2,1)S(1)} %get-tuple-element.67), channel_id=1, source_target_pairs={{0,2},{1,3},{2,4},{3,5},{4,6},{5,7},{6,0},{7,1},{8,10},{9,11},{10,... | collective-permute-start | bytes 442376 | tf_op jit(solution)/shard_map/ppermute | solution.py:572
  66.3 1.7 %collective-permute-start.7 = (bf16[64,1152]{1,0:T(8,128)(2,1)S(1)}, bf16[64,1152]{1,0:T(8,128)(2,1)S(1)}, u32[]{:S(2)}, u32[]{:S(2)}) collective-permute-start(bf16[64,1152]{1,0:T(8,128)(2,1)S(1)} %get-tuple-element.70), channel_id=1, source_target_pairs={{0,6},{1,7},{2,0},{3,1},{4,2},{5,3},{6,4},{7,5},{8,14},{9,15},{10,... | collective-permute-start | bytes 442376 | tf_op jit(solution)/shard_map/ppermute | solution.py:572
  67.9 3.4 %latent_gradient.2.refs_0_ = bf16[2048,1024]{1,0:T(8,128)(2,1)} custom-call(bf16[2048,1024]{1,0:T(8,128)(2,1)S(1)} %get-tuple-element.71.pre_ref, bf16[1024,1024]{1,0:T(8,128)(2,1)S(1)} %get-tuple-element.72.weight_ref), custom_call_target="tpu_custom_call" | custom-call | flops 2147483648 | bytes 5242880 | tf_op jit(solution)/shard_map/latent_gradient/pallas_call | solution.py:527
  71.3 0.0 collective-permute-done.5
  71.3 0.0 collective-permute-done.6
  71.3 0.0 collective-permute-done.4
  71.4 0.0 collective-permute-done.7
  71.4 0.1 fusion.6
  71.6 0.7 collective-permute-start.9
  72.2 0.2 collective-permute-start.8
  72.5 3.9 %collective-permute-start.10 = (bf16[64,1152]{1,0:T(8,128)(2,1)S(1)}, bf16[64,1152]{1,0:T(8,128)(2,1)S(1)}, u32[]{:S(2)}, u32[]{:S(2)}) collective-permute-start(bf16[64,1152]{1,0:T(8,128)(2,1)S(1)} %get-tuple-element.88), channel_id=1, source_target_pairs={{0,16},{1,17},{2,18},{3,19},{4,20},{5,21},{6,22},{7,23},{8,24},{9,... | collective-permute-start | bytes 442376 | tf_op jit(solution)/shard_map/ppermute | solution.py:572
  76.3 3.4 %latent_gradient.3 = bf16[2048,1024]{1,0:T(8,128)(2,1)} custom-call(bf16[2048,1024]{1,0:T(8,128)(2,1)S(1)} %get-tuple-element.71.pre_ref, bf16[1024,1024]{1,0:T(8,128)(2,1)S(1)} %get-tuple-element.72.weight_ref, bf16[2048,1024]{1,0:T(8,128)(2,1)} %latent_gradient.2.refs_0_), custom_call_target="tpu_custom_call", output_to_operand_aliasing={{}: (2, {})} | custom-call | flops 2147483648 | bytes 5242880 | tf_op jit(solution)/shard_map/latent_gradient/pallas_call | solution.py:527
  79.7 2.1 %collective-permute-done.10 = bf16[64,1152]{1,0:T(8,128)(2,1)S(1)} collective-permute-done((bf16[64,1152]{1,0:T(8,128)(2,1)S(1)}, bf16[64,1152]{1,0:T(8,128)(2,1)S(1)}, u32[]{:S(2)}, u32[]{:S(2)}) %collective-permute-start.10) | collective-permute-done | bytes 147488 | tf_op jit(solution)/shard_map/ppermute | solution.py:572
  81.9 0.0 collective-permute-done.9
  81.9 0.0 collective-permute-done.8
  81.9 0.1 add_convert_fusion.1.own_ref
  81.9 0.9 %collective-permute-start.13 = (bf16[64,1152]{1,0:T(8,128)(2,1)S(1)}, bf16[64,1152]{1,0:T(8,128)(2,1)S(1)}, u32[]{:S(2)}, u32[]{:S(2)}) collective-permute-start(bf16[64,1152]{1,0:T(8,128)(2,1)S(1)} %add_convert_fusion.1.own_ref), channel_id=1, source_target_pairs={{0,64},{1,65},{2,66},{3,67},{4,68},{5,69},{6,70},{7,71},{8,72},{9,... | collective-permute-start | bytes 442376 | tf_op jit(solution)/shard_map/ppermute | solution.py:572
  82.9 2.1 %collective-permute-start.12 = (bf16[64,1152]{1,0:T(8,128)(2,1)S(1)}, bf16[64,1152]{1,0:T(8,128)(2,1)S(1)}, u32[]{:S(2)}, u32[]{:S(2)}) collective-permute-start(bf16[64,1152]{1,0:T(8,128)(2,1)S(1)} %add_convert_fusion.1.own_ref), channel_id=1, source_target_pairs={{0,96},{1,97},{2,98},{3,99},{4,100},{5,101},{6,102},{7,103},{8,104... | collective-permute-start | bytes 442376 | tf_op jit(solution)/shard_map/ppermute | solution.py:572
  84.9 0.6 collective-permute-start.11
  85.5 3.3 %collective-permute-done.13.refs_2_ = bf16[64,1152]{1,0:T(8,128)(2,1)S(1)} collective-permute-done((bf16[64,1152]{1,0:T(8,128)(2,1)S(1)}, bf16[64,1152]{1,0:T(8,128)(2,1)S(1)}, u32[]{:S(2)}, u32[]{:S(2)}) %collective-permute-start.13) | collective-permute-done | bytes 147488 | tf_op jit(solution)/shard_map/ppermute | solution.py:572
  88.8 1.5 %collective-permute-done.12.refs_1_ = bf16[64,1152]{1,0:T(8,128)(2,1)S(1)} collective-permute-done((bf16[64,1152]{1,0:T(8,128)(2,1)S(1)}, bf16[64,1152]{1,0:T(8,128)(2,1)S(1)}, u32[]{:S(2)}, u32[]{:S(2)}) %collective-permute-start.12) | collective-permute-done | bytes 147488 | tf_op jit(solution)/shard_map/ppermute | solution.py:572
  90.2 0.0 collective-permute-done.11.refs_0_
  90.2 0.8 finish.1
  (3 shorter events, 0.1 us)
Async XLA Ops:
  11.6 17.9 %all-to-all-start = ((f16[8,112,256]{2,1,0:T(8,128)(2,1)}), f16[8,112,256]{2,1,0:T(8,128)(2,1)S(1)}, u32[]{:S(2)}, u32[]{:S(2)}) async-start(f16[8,112,256]{2,1,0:T(8,128)(2,1)} %multiply_convert_fusion), calls=%async_computation | async-start | bytes 917504 | tf_op jit(solution)/shard_map/all_to_all | solution.py:618
  18.7 11.0 %copy-start.2 = (f32[100,2048]{1,0:T(8,128)S(1)}, f32[100,2048]{1,0:T(8,128)}, u32[]{:S(2)}) copy-start(f32[100,2048]{1,0:T(8,128)} %observed_ref.1) | copy-start | bytes 2457604
  18.7 11.0 %copy-start.3 = (f32[2048]{0:T(1024)S(1)}, f32[2048]{0:T(1024)}, u32[]{:S(2)}) copy-start(f32[2048]{0:T(1024)} %param.9) | copy-start | bytes 24580
  31.5 13.4 %all-to-all-start.1 = ((bf16[8,112,256]{2,1,0:T(8,128)(2,1)}), bf16[8,112,256]{2,1,0:T(8,128)(2,1)S(1)}, u32[]{:S(2)}, u32[]{:S(2)}) async-start(bf16[8,112,256]{2,1,0:T(8,128)(2,1)} %pairs.1), calls=%async_computation.1 | async-start | bytes 917504 | tf_op jit(solution)/shard_map/all_to_all | solution.py:623
  35.1 2.2 %copy-start.1 = (bf16[1,2048,1024]{2,1,0:T(8,128)(2,1)S(1)}, bf16[1,2048,1024]{2,1,0:T(8,128)(2,1)}, u32[]{:S(2)}) copy-start(bf16[1,2048,1024]{2,1,0:T(8,128)(2,1)} %param.5) | copy-start | bytes 12582916
  38.5 2.0 %copy-start = (bf16[1024,2048]{1,0:T(8,128)(2,1)}, bf16[1024,2048]{1,0:T(8,128)(2,1)S(1)}, u32[]{:S(2)}) copy-start(bf16[1024,2048]{1,0:T(8,128)(2,1)S(1)} %turned.1.turned_hbm) | copy-start | bytes 12582916
  49.9 2.1 %collective-permute-start = (bf16[256,1152]{1,0:T(8,128)(2,1)S(1)}, bf16[256,1152]{1,0:T(8,128)(2,1)S(1)}, u32[]{:S(2)}, u32[]{:S(2)}) collective-permute-start(bf16[256,1152]{1,0:T(8,128)(2,1)S(1)} %get-tuple-element.58), channel_id=1, source_target_pairs={{0,1},{1,0},{2,3},{3,2},{4,5},{5,4},{6,7},{7,6},{8,9},{9,8},{10,11... | collective-permute-start | bytes 1769480 | tf_op jit(solution)/shard_map/ppermute | solution.py:572
  55.3 7.9 %collective-permute-start.1 = (bf16[256,1152]{1,0:T(8,128)(2,1)S(1)}, bf16[256,1152]{1,0:T(8,128)(2,1)S(1)}, u32[]{:S(2)}, u32[]{:S(2)}) collective-permute-start(bf16[256,1152]{1,0:T(8,128)(2,1)S(1)} %get-tuple-element.64), channel_id=1, source_target_pairs={{0,1},{1,0},{2,3},{3,2},{4,5},{5,4},{6,7},{7,6},{8,9},{9,8},{10,11... | collective-permute-start | bytes 1769480 | tf_op jit(solution)/shard_map/ppermute | solution.py:572
  55.6 8.4 %collective-permute-start.2 = (bf16[64,1152]{1,0:T(8,128)(2,1)S(1)}, bf16[64,1152]{1,0:T(8,128)(2,1)S(1)}, u32[]{:S(2)}, u32[]{:S(2)}) collective-permute-start(bf16[64,1152]{1,0:T(8,128)(2,1)S(1)} %get-tuple-element.65), channel_id=1, source_target_pairs={{0,2},{1,3},{2,4},{3,5},{4,6},{5,7},{6,0},{7,1},{8,10},{9,11},{10,... | collective-permute-start | bytes 442376 | tf_op jit(solution)/shard_map/ppermute | solution.py:572
  57.5 6.7 %collective-permute-start.3 = (bf16[64,1152]{1,0:T(8,128)(2,1)S(1)}, bf16[64,1152]{1,0:T(8,128)(2,1)S(1)}, u32[]{:S(2)}, u32[]{:S(2)}) collective-permute-start(bf16[64,1152]{1,0:T(8,128)(2,1)S(1)} %get-tuple-element.66), channel_id=1, source_target_pairs={{0,6},{1,7},{2,0},{3,1},{4,2},{5,3},{6,4},{7,5},{8,14},{9,15},{10,... | collective-permute-start | bytes 442376 | tf_op jit(solution)/shard_map/ppermute | solution.py:572
  59.6 11.7 %collective-permute-start.5 = (bf16[64,1152]{1,0:T(8,128)(2,1)S(1)}, bf16[64,1152]{1,0:T(8,128)(2,1)S(1)}, u32[]{:S(2)}, u32[]{:S(2)}) collective-permute-start(bf16[64,1152]{1,0:T(8,128)(2,1)S(1)} %get-tuple-element.68), channel_id=1, source_target_pairs={{0,6},{1,7},{2,0},{3,1},{4,2},{5,3},{6,4},{7,5},{8,14},{9,15},{10,... | collective-permute-start | bytes 442376 | tf_op jit(solution)/shard_map/ppermute | solution.py:572
  61.7 9.7 %collective-permute-start.6 = (bf16[64,1152]{1,0:T(8,128)(2,1)S(1)}, bf16[64,1152]{1,0:T(8,128)(2,1)S(1)}, u32[]{:S(2)}, u32[]{:S(2)}) collective-permute-start(bf16[64,1152]{1,0:T(8,128)(2,1)S(1)} %get-tuple-element.69), channel_id=1, source_target_pairs={{0,2},{1,3},{2,4},{3,5},{4,6},{5,7},{6,0},{7,1},{8,10},{9,11},{10,... | collective-permute-start | bytes 442376 | tf_op jit(solution)/shard_map/ppermute | solution.py:572
  64.2 7.1 %collective-permute-start.4 = (bf16[64,1152]{1,0:T(8,128)(2,1)S(1)}, bf16[64,1152]{1,0:T(8,128)(2,1)S(1)}, u32[]{:S(2)}, u32[]{:S(2)}) collective-permute-start(bf16[64,1152]{1,0:T(8,128)(2,1)S(1)} %get-tuple-element.67), channel_id=1, source_target_pairs={{0,2},{1,3},{2,4},{3,5},{4,6},{5,7},{6,0},{7,1},{8,10},{9,11},{10,... | collective-permute-start | bytes 442376 | tf_op jit(solution)/shard_map/ppermute | solution.py:572
  66.3 5.1 %collective-permute-start.7 = (bf16[64,1152]{1,0:T(8,128)(2,1)S(1)}, bf16[64,1152]{1,0:T(8,128)(2,1)S(1)}, u32[]{:S(2)}, u32[]{:S(2)}) collective-permute-start(bf16[64,1152]{1,0:T(8,128)(2,1)S(1)} %get-tuple-element.70), channel_id=1, source_target_pairs={{0,6},{1,7},{2,0},{3,1},{4,2},{5,3},{6,4},{7,5},{8,14},{9,15},{10,... | collective-permute-start | bytes 442376 | tf_op jit(solution)/shard_map/ppermute | solution.py:572
  71.6 10.3 %collective-permute-start.9 = (bf16[64,1152]{1,0:T(8,128)(2,1)S(1)}, bf16[64,1152]{1,0:T(8,128)(2,1)S(1)}, u32[]{:S(2)}, u32[]{:S(2)}) collective-permute-start(bf16[64,1152]{1,0:T(8,128)(2,1)S(1)} %get-tuple-element.87), channel_id=1, source_target_pairs={{0,24},{1,25},{2,26},{3,27},{4,28},{5,29},{6,30},{7,31},{8,16},{9,... | collective-permute-start | bytes 442376 | tf_op jit(solution)/shard_map/ppermute | solution.py:572
  72.2 9.6 %collective-permute-start.8 = (bf16[64,1152]{1,0:T(8,128)(2,1)S(1)}, bf16[64,1152]{1,0:T(8,128)(2,1)S(1)}, u32[]{:S(2)}, u32[]{:S(2)}) collective-permute-start(bf16[64,1152]{1,0:T(8,128)(2,1)S(1)} %get-tuple-element.87), channel_id=1, source_target_pairs={{0,8},{1,9},{2,10},{3,11},{4,12},{5,13},{6,14},{7,15},{8,0},{9,1},... | collective-permute-start | bytes 442376 | tf_op jit(solution)/shard_map/ppermute | solution.py:572
  72.5 9.4 %collective-permute-start.10 = (bf16[64,1152]{1,0:T(8,128)(2,1)S(1)}, bf16[64,1152]{1,0:T(8,128)(2,1)S(1)}, u32[]{:S(2)}, u32[]{:S(2)}) collective-permute-start(bf16[64,1152]{1,0:T(8,128)(2,1)S(1)} %get-tuple-element.88), channel_id=1, source_target_pairs={{0,16},{1,17},{2,18},{3,19},{4,20},{5,21},{6,22},{7,23},{8,24},{9,... | collective-permute-start | bytes 442376 | tf_op jit(solution)/shard_map/ppermute | solution.py:572
  81.9 6.8 %collective-permute-start.13 = (bf16[64,1152]{1,0:T(8,128)(2,1)S(1)}, bf16[64,1152]{1,0:T(8,128)(2,1)S(1)}, u32[]{:S(2)}, u32[]{:S(2)}) collective-permute-start(bf16[64,1152]{1,0:T(8,128)(2,1)S(1)} %add_convert_fusion.1.own_ref), channel_id=1, source_target_pairs={{0,64},{1,65},{2,66},{3,67},{4,68},{5,69},{6,70},{7,71},{8,72},{9,... | collective-permute-start | bytes 442376 | tf_op jit(solution)/shard_map/ppermute | solution.py:572
  82.9 7.4 %collective-permute-start.12 = (bf16[64,1152]{1,0:T(8,128)(2,1)S(1)}, bf16[64,1152]{1,0:T(8,128)(2,1)S(1)}, u32[]{:S(2)}, u32[]{:S(2)}) collective-permute-start(bf16[64,1152]{1,0:T(8,128)(2,1)S(1)} %add_convert_fusion.1.own_ref), channel_id=1, source_target_pairs={{0,96},{1,97},{2,98},{3,99},{4,100},{5,101},{6,102},{7,103},{8,104... | collective-permute-start | bytes 442376 | tf_op jit(solution)/shard_map/ppermute | solution.py:572
  84.9 5.3 %collective-permute-start.11 = (bf16[64,1152]{1,0:T(8,128)(2,1)S(1)}, bf16[64,1152]{1,0:T(8,128)(2,1)S(1)}, u32[]{:S(2)}, u32[]{:S(2)}) collective-permute-start(bf16[64,1152]{1,0:T(8,128)(2,1)S(1)} %add_convert_fusion.1.own_ref), channel_id=1, source_target_pairs={{0,32},{1,33},{2,34},{3,35},{4,36},{5,37},{6,38},{7,39},{8,40},{9,... | collective-permute-start | bytes 442376 | tf_op jit(solution)/shard_map/ppermute | solution.py:572
